TPU v7x, 32 devices: a whole 2x2x4 slice. The times are simulated.
32 devices in a mesh: ctx: 4 (over y, x), fsdp: 8 (over z, core).
Axes of the slice: x: 2, y: 2, z: 4, core: 2. Of those that a mesh axis runs over, the one named last changes fastest.
Arguments:
- tokens: bfloat16 [16384, 2048], P(('ctx', 'fsdp')), may hold values from -6 to 6
- cotangent: float32 [16384, 2048], P(('ctx', 'fsdp')), may hold values from -6 to 6
- lengths: int32 [8, 2], P('fsdp'), may hold values from 8 to 8, as said below
- span_place: int32 [8, 16], P('fsdp'), may hold values from 0 to 15, as said below
- ln1_gain: float32 [2048], P('fsdp'), may hold values from 0.1 to 1.9
- ln1_shift: float32 [2048], P('fsdp'), may hold values from -2.5 to 2.5
- qkv_weight: float32 [2048, 6144], P('fsdp'), may hold values from -0.125 to 0.125
- q_bias: float32 [2048], P('fsdp'), may hold values from -2.5 to 2.5
- v_bias: float32 [2048], P('fsdp'), may hold values from -2.5 to 2.5
- out_weight: float32 [2048, 2048], P('fsdp'), may hold values from -0.5 to 0.5
- out_bias: float32 [2048], P('fsdp'), may hold values from -2.5 to 2.5
- ln2_gain: float32 [2048], P('fsdp'), may hold values from 0.1 to 1.9
- ln2_shift: float32 [2048], P('fsdp'), may hold values from -2.5 to 2.5
- up_weight: float32 [2048, 8192], P('fsdp'), may hold values from -0.125 to 0.125
- up_bias: float32 [8192], P('fsdp'), may hold values from -3 to 3
- down_weight: float32 [8192, 2048], P('fsdp'), may hold values from -0.0625 to 0.0625
- down_bias: float32 [2048], P('fsdp'), may hold values from -2.5 to 2.5
Outputs:
- mixed: float32 [16384, 2048], P(('ctx', 'fsdp'))
- input_grad: float32 [16384, 2048], P(('ctx', 'fsdp'))
- ln1_gain_grad: float32 [2048], P('fsdp')
- ln1_shift_grad: float32 [2048], P('fsdp')
- qkv_weight_grad: float32 [2048, 6144], P('fsdp')
- q_bias_grad: float32 [2048], P('fsdp')
- v_bias_grad: float32 [2048], P('fsdp')
- out_weight_grad: float32 [2048, 2048], P('fsdp')
- out_bias_grad: float32 [2048], P('fsdp')
- ln2_gain_grad: float32 [2048], P('fsdp')
- ln2_shift_grad: float32 [2048], P('fsdp')
- up_weight_grad: float32 [2048, 8192], P('fsdp')
- up_bias_grad: float32 [8192], P('fsdp')
- down_weight_grad: float32 [8192, 2048], P('fsdp')
- down_bias_grad: float32 [2048], P('fsdp')
Inputs may be any that keep to these rules, and one draw needn't show every extreme that they name: Each row holds two lengths in blocks, each 8 or more, that sum to 16; the first is at least as long as the second; in some row the first is exactly 8. `span_place`: each row is a permutation of the 16 blocks of a group.
All inputs are finite; a program needn't handle non-finite values.
Results may differ from a plain program's by a relative error of at most 0.02.
Values may be sent and summed in bfloat16 or wider, within the bound.
A program may use at most 512 MiB of HBM per device.

v0:
```python
import functools
import math

import jax
import jax.numpy as jnp
from jax import lax
from jax.experimental import pallas as pl
from jax.experimental.pallas import tpu as pltpu
from jax.sharding import PartitionSpec as P

HEADS = 16
SPAN = 128
SEQ_BLOCKS = 8

norm_eps = 1e-05
gelu_coef = 0.7978845608028654
LOG2E = 1.4426950408889634

half = jnp.bfloat16
single = jnp.float32


def dot_nn(a, b):
    return lax.dot_general(a, b, (((1,), (0,)), ((), ())), preferred_element_type=single)


def dot_nt(a, b):
    return lax.dot_general(a, b, (((1,), (1,)), ((), ())), preferred_element_type=single)


def dot_tn(a, b):
    return lax.dot_general(a, b, (((0,), (0,)), ((), ())), preferred_element_type=single)


def norm_parts(values):
    center = values - jnp.mean(values, axis=-1, keepdims=True)
    spread = jnp.mean(center * center, axis=-1, keepdims=True)
    inv = lax.rsqrt(spread + norm_eps)
    return center * inv, inv


def norm_back(normed, inv, gain, grad):
    dn = grad * gain
    return inv * (
        dn
        - jnp.mean(dn, axis=-1, keepdims=True)
        - normed * jnp.mean(dn * normed, axis=-1, keepdims=True)
    )


def gelu_both(v):
    t = jnp.tanh(gelu_coef * (v + 0.044715 * v * v * v))
    value = 0.5 * v * (1.0 + t)
    slope = 0.5 * (1.0 + t) + 0.5 * v * (1.0 - t * t) * gelu_coef * (1.0 + 3 * 0.044715 * v * v)
    return value, slope


def swap(x, mask):
    n = lax.axis_size("ctx")
    return lax.ppermute(x, "ctx", [(i, i ^ mask) for i in range(n)])


def gather_first(x):
    count = lax.axis_size("ctx")
    return [swap(x, j) for j in range(1, 3 if count == 4 else count)]


def gather_second(x, arrived):
    if lax.axis_size("ctx") != 4:
        return [[x]] + [[p] for p in arrived]
    one, two = arrived
    n = x.shape[0] // 2
    return [[x], [one], [two], [swap(one[:n], 2), swap(two[n:], 1)]]


def gather_ctx(x):
    return gather_second(x, gather_first(x))


def scatter_first(far):
    if lax.axis_size("ctx") != 4:
        return None
    return swap(far[0], 1), swap(far[1], 2)


def scatter_second(pieces, first):
    if first is None:
        return pieces[1:]
    p1, p2 = pieces[1], pieces[2]
    n = p1.shape[0] // 2
    from_x, from_y = first
    p1 = jnp.concatenate(
        [p1[:n], (p1[n:].astype(single) + from_y.astype(single)).astype(half)], axis=0
    )
    p2 = jnp.concatenate(
        [(p2[:n].astype(single) + from_x.astype(single)).astype(half), p2[n:]], axis=0
    )
    return [p1, p2]


def scatter_send(sent):
    return [swap(x, j + 1) for j, x in enumerate(sent)]


def total_of(own, arrived):
    for x in arrived:
        own = own + x.astype(single)
    return own


def xor_order(items, c):
    bit = 1
    while bit < len(items):
        on = (c & bit) == bit
        items = [jnp.where(on, items[i ^ bit], items[i]) for i in range(len(items))]
        bit *= 2
    return items


TILE = 256


def attn_scores(q_refs, k_refs, i, scale, slope):
    q = jnp.concatenate([q_refs[2 * i][...], q_refs[2 * i + 1][...]], axis=0)
    k = jnp.concatenate([r[...] for r in k_refs[: 2 * i + 2]], axis=0)
    n = TILE * (i + 1)
    col = lax.broadcasted_iota(jnp.int32, (1, n), 1) - (n - 1)
    s = dot_nt(q, k) * (scale * LOG2E) + (slope * LOG2E) * col.astype(single)
    row_at = lax.broadcasted_iota(jnp.int32, (TILE, TILE), 0)
    col_at = lax.broadcasted_iota(jnp.int32, (TILE, TILE), 1)
    last = jnp.where(col_at <= row_at, s[:, n - TILE :], -1e30)
    s = last if i == 0 else jnp.concatenate([s[:, : n - TILE], last], axis=1)
    e = jnp.exp2(s - jnp.max(s, axis=1, keepdims=True))
    return q, k, e, 1.0 / jnp.sum(e, axis=1, keepdims=True)


class Rows:
    def __init__(self, inv_ref, stage, out, sems, kinds):
        self.inv, self.stage, self.out, self.sems, self.kinds = inv_ref, stage, out, sems, kinds
        self.heads = pl.num_programs(1)
        self.step = pl.program_id(0) * self.heads + pl.program_id(1)
        self.slot = lax.rem(self.step, 2)

    def copies(self, step):
        slot = lax.rem(step, 2)
        seq, head = step // self.heads, lax.rem(step, self.heads)
        for kind in range(self.kinds):
            col = pl.multiple_of((kind * self.heads + head) * 128, 128)
            for j in range(SEQ_BLOCKS):
                row = pl.multiple_of(self.inv[seq * SEQ_BLOCKS + j] * SPAN, SPAN)
                yield pltpu.make_async_copy(
                    self.stage.at[slot, kind, pl.ds(j * SPAN, SPAN)],
                    self.out.at[pl.ds(row, SPAN), pl.ds(col, 128)],
                    self.sems.at[slot, kind * SEQ_BLOCKS + j],
                )

    def wait(self, step):
        for copy in self.copies(step):
            copy.wait()

    def open(self):
        @pl.when(self.step >= 2)
        def _():
            self.wait(self.step - 2)

    def close(self):
        for copy in self.copies(self.step):
            copy.start()

        @pl.when(self.step == 2 * self.heads - 1)
        def _():
            self.wait(self.step - 1)
            self.wait(self.step)


def attn_fwd_kernel(scale, inv_ref, slope_ref, *refs):
    q_refs, k_refs, v_refs = refs[:8], refs[8:16], refs[16:24]
    out, stage, sems = refs[24:]
    slope = slope_ref[pl.program_id(1)]
    rows = Rows(inv_ref, stage, out, sems, 1)
    rows.open()
    for i in range(4):
        q, k, e, r = attn_scores(q_refs, k_refs, i, scale, slope)
        v = jnp.concatenate([x[...] for x in v_refs[: 2 * i + 2]], axis=0)
        o = dot_nn((e * r).astype(half), v)
        stage[rows.slot, 0, TILE * i : TILE * (i + 1), :] = o.astype(half)
    rows.close()


def attn_bwd_kernel(scale, inv_ref, slope_ref, *refs):
    q_refs, k_refs, v_refs, g_refs = refs[:8], refs[8:16], refs[16:24], refs[24:32]
    out, stage, sems, dk_acc, dv_acc = refs[32:]
    slope = slope_ref[pl.program_id(1)]
    rows = Rows(inv_ref, stage, out, sems, 3)
    rows.open()
    for i in (3, 2, 1, 0):
        q, k, e, r = attn_scores(q_refs, k_refs, i, scale, slope)
        n = TILE * (i + 1)
        v = jnp.concatenate([x[...] for x in v_refs[: 2 * i + 2]], axis=0)
        g = jnp.concatenate([g_refs[2 * i][...], g_refs[2 * i + 1][...]], axis=0)
        p = e * r
        dp = dot_nt(g, v)
        delta = jnp.sum(p * dp, axis=1, keepdims=True)
        ds = (p * (dp - delta)).astype(half)
        pb = p.astype(half)
        dq = (dot_nn(ds, k) * scale).astype(half)
        stage[rows.slot, 0, TILE * i : TILE * (i + 1), :] = dq
        dk = dot_tn(ds, q)
        dv = dot_tn(pb, g)
        if i == 3:
            dk_acc[...] = dk
            dv_acc[...] = dv
        else:
            dk_acc[:n, :] += dk
            dv_acc[:n, :] += dv
    stage[rows.slot, 1] = (dk_acc[...] * scale).astype(half)
    stage[rows.slot, 2] = dv_acc[...].astype(half)
    rows.close()


def block_specs(offset):
    def one(j):
        return pl.BlockSpec(
            (SPAN, 128), lambda s, h, inv, slope: (inv[s * SEQ_BLOCKS + j], offset + h)
        )

    return [one(j) for j in range(SEQ_BLOCKS)]


def attn_call(kernel, kinds, joined, extra, extra_specs, scratch, inv, slopes, heads, cost, name):
    rows = joined.shape[0]
    specs = block_specs(0) + block_specs(heads) + block_specs(2 * heads) + extra_specs
    return pl.pallas_call(
        kernel,
        grid_spec=pltpu.PrefetchScalarGridSpec(
            num_scalar_prefetch=2,
            grid=(2, heads),
            in_specs=specs,
            out_specs=pl.BlockSpec(memory_space=pl.ANY),
            scratch_shapes=[
                pltpu.VMEM((2, kinds, rows // 2, 128), half),
                pltpu.SemaphoreType.DMA((2, kinds * SEQ_BLOCKS)),
            ]
            + scratch,
        ),
        out_shape=jax.ShapeDtypeStruct((rows, kinds * heads * 128), half),
        compiler_params=pltpu.CompilerParams(vmem_limit_bytes=48 * 1024 * 1024),
        cost_estimate=cost,
        name=name,
    )(inv, slopes, *([joined] * 24), *extra)


def attn_forward(joined, inv, slopes, heads, scale):
    kernel = functools.partial(attn_fwd_kernel, scale)
    cost = hint(20 * 10**9, joined.shape[0] * heads * 128 * 8)
    return attn_call(
        kernel, 1, joined, [], [], [], inv, slopes, heads, cost, "attn_forward"
    )


def attn_backward(joined, grad, inv, slopes, heads, scale):
    kernel = functools.partial(attn_bwd_kernel, scale)
    cost = hint(40 * 10**9, joined.shape[0] * heads * 128 * 14)
    sums = [pltpu.VMEM((joined.shape[0] // 2, 128), single)] * 2
    return attn_call(
        kernel,
        3,
        joined,
        [grad] * 8,
        block_specs(0),
        sums,
        inv,
        slopes,
        heads,
        cost,
        "attn_backward",
    )


HINT = 0.001


def block_of(x):
    return x if isinstance(x, tuple) else (x, x.shape[0], 0)


def hint(flops, bytes_accessed):
    return pl.CostEstimate(
        flops=int(HINT * flops), bytes_accessed=int(HINT * bytes_accessed), transcendentals=0
    )


def rows_kernel(dot, epilogue, count, extra, *refs):
    left, w_ref = refs[:count], refs[count]
    extras = refs[count + 1 : count + 1 + extra]
    outs = refs[count + 1 + extra :]
    for i in range(count):
        epilogue(i, dot(left[i][...], w_ref[...]), extras, outs)


def rows_matmul(blocks, w, transposed, extras, outs, epilogue, name, tile=512):
    blocks = [block_of(x) for x in blocks]
    extras = [block_of(x) for x in extras]
    n = w.shape[0] if transposed else w.shape[1]
    k = w.shape[1] if transposed else w.shape[0]
    t = math.gcd(n, tile)
    w_spec = (
        pl.BlockSpec((t, k), lambda i: (i, 0)) if transposed else pl.BlockSpec((k, t), lambda i: (0, i))
    )
    rows = sum(x[1] for x in blocks)
    return pl.pallas_call(
        functools.partial(
            rows_kernel, dot_nt if transposed else dot_nn, epilogue, len(blocks), len(extras)
        ),
        grid=(n // t,),
        in_specs=[pl.BlockSpec((x[1], k), lambda i, at=x[2]: (at, 0)) for x in blocks]
        + [w_spec]
        + [pl.BlockSpec((x[1], t), lambda i, at=x[2]: (at, i)) for x in extras],
        out_specs=[pl.BlockSpec((r, t), lambda i: (0, i)) for r, _ in outs],
        out_shape=[jax.ShapeDtypeStruct((r, n), d) for r, d in outs],
        compiler_params=pltpu.CompilerParams(vmem_limit_bytes=52 * 1024 * 1024),
        cost_estimate=hint(2 * rows * n * k, 2 * n * k + 4 * rows * (n + k)),
        name=name,
    )(*[x[0] for x in blocks], w, *[x[0] for x in extras])


def plain(blocks, w, transposed, dtype, name):
    def epilogue(i, x, extras, outs):
        outs[i][...] = x.astype(dtype)

    outs = [(block_of(x)[1], dtype) for x in blocks]
    return rows_matmul(blocks, w, transposed, [], outs, epilogue, name)


def joined_rows(blocks, w, bias, name):
    sizes = [block_of(x)[1] for x in blocks]

    def epilogue(i, x, extras, outs):
        at = sum(sizes[:i])
        outs[0][at : at + sizes[i], :] = (x + extras[0][...]).astype(half)

    bias = bias.reshape(1, -1)
    return rows_matmul(blocks, w, False, [bias], [(sum(sizes), half)], epilogue, name)[0]


def up_gelu(blocks, w, bias, name):
    count = len(blocks)

    def epilogue(i, x, extras, outs):
        value, slope = gelu_both(x + extras[0][...])
        outs[i][...] = value.astype(half)
        outs[count + i][...] = slope.astype(half)

    outs = [(block_of(x)[1], half) for x in blocks] * 2
    out = rows_matmul(blocks, w, False, [bias.reshape(1, -1)], outs, epilogue, name)
    return out[:count], out[count:]


def hidden_back(blocks, w, slopes, name):
    def epilogue(i, x, extras, outs):
        x = x.astype(half).astype(single) * extras[i][...].astype(single)
        outs[i][...] = x.astype(half)

    outs = [(block_of(x)[1], half) for x in blocks]
    return rows_matmul(blocks, w, True, slopes, outs, epilogue, name)


def outer_kernel(count, *refs):
    out = refs[-1]
    total = None
    for i in range(count):
        x = dot_tn(refs[i][...], refs[count + i][...])
        total = x if total is None else total + x
    out[...] = total.astype(half)


def outer(left, right, name):
    left = [block_of(x) for x in left]
    right = [block_of(x) for x in right]
    m, n = left[0][0].shape[1], right[0][0].shape[1]
    tm = math.gcd(m, 1024)
    tn = n // 2 if n % 256 == 0 and n > 1024 else n
    rows = sum(x[1] for x in left)
    return pl.pallas_call(
        functools.partial(outer_kernel, len(left)),
        grid=(m // tm, n // tn),
        in_specs=[pl.BlockSpec((x[1], tm), lambda i, j, at=x[2]: (at, i)) for x in left]
        + [pl.BlockSpec((x[1], tn), lambda i, j, at=x[2]: (at, j)) for x in right],
        out_specs=pl.BlockSpec((tm, tn), lambda i, j: (i, j)),
        out_shape=jax.ShapeDtypeStruct((m, n), half),
        compiler_params=pltpu.CompilerParams(vmem_limit_bytes=52 * 1024 * 1024),
        cost_estimate=hint(2 * rows * m * n, 2 * rows * (m + n) + 2 * m * n),
        name=name,
    )(*[x[0] for x in left], *[x[0] for x in right])


def partner(mask):
    c = lax.axis_index("ctx")
    if mask == 1:
        return c + 1 - 2 * lax.rem(c, 2)
    return lax.rem(c + 2, 4) if mask == 2 else 3 - c


def greet(masks):
    barrier = pltpu.get_barrier_semaphore()
    for mask in masks:
        pl.semaphore_signal(
            barrier,
            inc=1,
            device_id={"ctx": partner(mask)},
            device_id_type=pl.DeviceIdType.MESH,
        )
    pl.semaphore_wait(barrier, len(masks))


class Moves:
    def __init__(self, send_sem, recv_sem):
        self.send_sem, self.recv_sem, self.used = send_sem, recv_sem, 0

    def start(self, src, dst, mask):
        copy = pltpu.make_async_remote_copy(
            src_ref=src,
            dst_ref=dst,
            send_sem=self.send_sem.at[self.used],
            recv_sem=self.recv_sem.at[self.used],
            device_id={"ctx": partner(mask)},
            device_id_type=pl.DeviceIdType.MESH,
        )
        self.used += 1
        copy.start()
        return copy


def multiply(lefts, w, transposed, extras, outs, epilogue, tile=512):
    k = lefts[0].shape[1]
    n = w.shape[0] if transposed else w.shape[1]
    t = math.gcd(n, tile)
    w_spec = (
        pl.BlockSpec((t, k), lambda i: (i, 0)) if transposed else pl.BlockSpec((k, t), lambda i: (0, i))
    )
    dot = dot_nt if transposed else dot_nn

    def body(*refs):
        rows_kernel(dot, epilogue, len(lefts), len(extras), *refs)

    pltpu.emit_pipeline(
        body,
        grid=(n // t,),
        in_specs=[pl.BlockSpec((x.shape[0], k), lambda i: (0, 0)) for x in lefts]
        + [w_spec]
        + [pl.BlockSpec((x.shape[0], t), lambda i: (0, i)) for x in extras],
        out_specs=[pl.BlockSpec((x.shape[0], t), lambda i: (0, i)) for x in outs],
    )(*lefts, w, *extras, *outs)


def store(i, x, extras, outs):
    outs[i][...] = x.astype(outs[i].dtype)


def store_sum(i, x, extras, outs):
    outs[i][...] = (x + extras[i][...].astype(single)).astype(outs[i].dtype)


def store_passed(i, x, extras, outs):
    if i in (1, 2):
        x = x + extras[i - 1][...].astype(single)
    outs[i][...] = x.astype(outs[i].dtype)


def store_hidden(i, x, extras, outs):
    outs[i][...] = (x.astype(half).astype(single) * extras[i][...].astype(single)).astype(half)


def outer_on(lefts, rights, out):
    m, n = out.shape
    tm = math.gcd(m, 1024)
    tn = n // 2 if n % 256 == 0 and n > 1024 else n

    def body(*refs):
        outer_kernel(len(lefts), *refs)

    pltpu.emit_pipeline(
        body,
        grid=(m // tm, n // tn),
        in_specs=[pl.BlockSpec((x.shape[0], tm), lambda i, j: (0, i)) for x in lefts]
        + [pl.BlockSpec((x.shape[0], tn), lambda i, j: (0, j)) for x in rights],
        out_specs=[pl.BlockSpec((tm, tn), lambda i, j: (i, j))],
    )(*lefts, *rights, out)


def halves(ref):
    n = ref.shape[0] // 2
    return ref.at[pl.ds(0, n)], ref.at[pl.ds(n, n)]


def moving_call(kernel, operands, outs, moves, call, flops, name):
    anywhere = pl.BlockSpec(memory_space=pl.ANY)
    sems = pltpu.SemaphoreType.DMA((moves,))
    return pl.pallas_call(
        kernel,
        in_specs=[anywhere] * len(operands),
        out_specs=[anywhere] * len(outs),
        out_shape=[jax.ShapeDtypeStruct(shape, dtype) for shape, dtype in outs],
        scratch_shapes=[sems, sems],
        compiler_params=pltpu.CompilerParams(
            collective_id=call, has_side_effects=True, vmem_limit_bytes=52 * 1024 * 1024
        ),
        cost_estimate=hint(flops, 0),
        name=name,
    )(*operands)


def store_biased(i, x, extras, outs):
    outs[i][...] = (x + extras[0][...]).astype(half)


def qkv_kernel(*refs):
    tok, gain, shift, a1, w_qkv, bias = refs[0:2], refs[2], refs[3], refs[4:7], refs[7], refs[8]
    dz_lo, dz_hi = refs[9:11]
    joined, far, one_lo, two_hi = refs[11], refs[12:14], refs[14], refs[15]
    moves = Moves(*refs[16:18])
    n, width = tok[0].shape
    greet((1, 2))
    copies = [moves.start(dz_lo, one_lo, 1), moves.start(dz_hi, two_hi, 2)]

    def norm(x_lo, x_hi, g, s, o_lo, o_hi):
        for x, o in ((x_lo, o_lo), (x_hi, o_hi)):
            normed, _ = norm_parts(x[...].astype(single))
            o[...] = (normed * g[...] + s[...]).astype(half)

    t = math.gcd(n, 64)
    block = pl.BlockSpec((t, width), lambda i: (i, 0))
    row = pl.BlockSpec((1, width), lambda i: (0, 0))
    pltpu.emit_pipeline(
        norm, grid=(n // t,), in_specs=[block, block, row, row], out_specs=[block, block]
    )(*tok, gain, shift, *far)
    lefts, outs, at = [*a1, *far], [], 0
    for x in lefts:
        outs.append(joined.at[pl.ds(at, x.shape[0])])
        at += x.shape[0]
    multiply(lefts, w_qkv, False, [bias], outs, store_biased)
    for copy in copies:
        copy.wait()


def qkv_forward(tok, gain, shift, a1, w_qkv, bias, dz_lo, dz_hi):
    n, width = tok[0].shape
    k = w_qkv.shape[1]
    outs = [((8 * n, k), half)] + [((n, width), half)] * 4
    out = moving_call(
        qkv_kernel,
        [*tok, gain.reshape(1, -1), shift.reshape(1, -1), *a1, w_qkv, bias.reshape(1, -1), dz_lo, dz_hi],
        outs,
        2,
        7,
        16 * n * width * k,
        "qkv",
    )
    return out[0], out[1:3], out[3:5]


def feed_pass(dz, slope, w_down, w_up, du, total):
    n, width = dz[0].shape
    wide = w_down.shape[0]
    t = math.gcd(wide, 512)
    total[...] = jnp.zeros_like(total)

    def body(dz_lo, dz_hi, down, up, slope_lo, slope_hi, du_lo, du_hi):
        for i, x, s, d in ((0, dz_lo, slope_lo, du_lo), (1, dz_hi, slope_hi, du_hi)):
            grad = dot_nt(x[...], down[...]).astype(half).astype(single)
            grad = (grad * s[...].astype(single)).astype(half)
            d[...] = grad
            total[i * n : (i + 1) * n, :] += dot_nt(grad, up[...])

    pltpu.emit_pipeline(
        body,
        grid=(wide // t,),
        in_specs=[pl.BlockSpec((n, width), lambda i: (0, 0))] * 2
        + [pl.BlockSpec((t, width), lambda i: (i, 0)), pl.BlockSpec((width, t), lambda i: (0, i))]
        + [pl.BlockSpec((n, t), lambda i: (0, i))] * 2,
        out_specs=[pl.BlockSpec((n, t), lambda i: (0, i))] * 2,
    )(*dz, w_down, w_up, *slope, *du)


def feed_back_kernel(*refs):
    dz, slope, (w_down, w_up) = refs[0:8], refs[8:13], refs[13:15]
    du, own, p1_hi, p2_lo, land1_lo, land2_hi = refs[15:20], *refs[20:25]
    total, far, near, rest, from_x, from_y = refs[25:31]
    moves = Moves(*refs[31:33])
    local = refs[33]
    n = from_x.shape[0]
    lo, hi = pl.ds(0, n), pl.ds(n, n)
    (s1_lo, s1_hi), (s2_lo, s2_hi) = halves(slope[1]), halves(slope[2])
    (d1_lo, d1_hi), (d2_lo, d2_hi) = halves(du[1]), halves(du[2])
    greet((1, 2))
    feed_pass(dz[6:8], slope[3:5], w_down, w_up, du[3:5], total)
    far[...] = total[...].astype(half)
    first = [moves.start(far.at[lo], from_x, 1), moves.start(far.at[hi], from_y, 2)]
    feed_pass([dz[2], dz[5]], [s1_lo, s2_hi], w_down, w_up, [d1_lo, d2_hi], total)
    near[...] = total[...].astype(half)
    second = [moves.start(near.at[lo], land1_lo, 1), moves.start(near.at[hi], land2_hi, 2)]
    feed_pass([dz[3], dz[4]], [s1_hi, s2_lo], w_down, w_up, [d1_hi, d2_lo], total)
    for copy in first:
        copy.wait()
    rest[lo] = (total[lo] + from_y[...].astype(single)).astype(half)
    rest[hi] = (total[hi] + from_x[...].astype(single)).astype(half)
    stores = [
        pltpu.make_async_copy(rest.at[lo], p1_hi, local.at[0]),
        pltpu.make_async_copy(rest.at[hi], p2_lo, local.at[1]),
    ]
    for copy in stores:
        copy.start()
    feed_pass(dz[0:2], halves(slope[0]), w_down, w_up, halves(du[0]), total)
    stores.append(pltpu.make_async_copy(total, own, local.at[2]))
    stores[-1].start()
    for copy in second + stores:
        copy.wait()


def feed_back(dz, slope, w_down, w_up):
    n, width = dz[0].shape
    rows, wide = 2 * n, w_down.shape[0]
    anywhere = pl.BlockSpec(memory_space=pl.ANY)
    outs = [((r, wide), half) for r in (rows, rows, rows, n, n)]
    outs += [((rows, width), single)] + [((n, width), half)] * 4
    sems = pltpu.SemaphoreType.DMA((4,))
    out = pl.pallas_call(
        feed_back_kernel,
        in_specs=[anywhere] * 15,
        out_specs=[anywhere] * len(outs),
        out_shape=[jax.ShapeDtypeStruct(shape, dtype) for shape, dtype in outs],
        scratch_shapes=[pltpu.VMEM((rows, width), single)]
        + [pltpu.VMEM((rows, width), half)] * 3
        + [pltpu.VMEM((n, width), half)] * 2
        + [sems, sems, pltpu.SemaphoreType.DMA((3,))],
        compiler_params=pltpu.CompilerParams(
            collective_id=3, has_side_effects=True, vmem_limit_bytes=56 * 1024 * 1024
        ),
        cost_estimate=hint(16 * rows * width * wide, 0),
        name="feed_back",
    )(*dz, *slope, w_down, w_up)
    return out[0:5], out[5], out[6:8], out[8:10]


def up_back_kernel(*refs):
    p1_hi, p2_lo, a2, du = refs[0], refs[1], refs[2:7], refs[7:12]
    land1_hi, land2_lo, up_grad = refs[12:15]
    moves = Moves(*refs[15:17])
    greet((1, 2))
    copies = [moves.start(p1_hi, land1_hi, 1), moves.start(p2_lo, land2_lo, 2)]
    outer_on(a2, du, up_grad)
    for copy in copies:
        copy.wait()


def up_back(p1_hi, p2_lo, a2, du):
    m, n = a2[0].shape[1], du[0].shape[1]
    outs = [(p1_hi.shape, half)] * 2 + [((m, n), half)]
    flops = 8 * a2[0].shape[0] * m * n
    return moving_call(up_back_kernel, [p1_hi, p2_lo, *a2, *du], outs, 2, 6, flops, "up_back")


def heads_back_kernel(part, *refs):
    dattn, ob, dz1, gb1, gb2, w_down, mix_x, mix_y = refs[0:8]
    got, out_grad = refs[8:10]
    mix = refs[10:14]
    moves = Moves(*refs[14:16])
    local = refs[16]
    rows = dattn.shape[0]
    c = lax.axis_index("ctx")

    def columns(of):
        return dattn.at[:, pl.ds(pl.multiple_of(of * part, part), part)]

    greet((1, 2, 3))
    copies = []
    for mask in (3, 1, 2):
        at = got.at[pl.ds(mask * rows, rows)]
        copies.append(moves.start(columns(partner(mask)), at, mask))
    own = pltpu.make_async_copy(columns(c), got.at[pl.ds(0, rows)], local)
    own.start()
    outer_on([ob], [dz1], out_grad)
    multiply(
        [*halves(gb1), *halves(gb2)],
        w_down,
        False,
        [mix_y, mix_x],
        mix,
        store_passed,
    )
    own.wait()
    for copy in copies:
        copy.wait()


def heads_back(dattn, ob, dz1, gb1, gb2, w_down, mix_x, mix_y, part):
    rows, width = dattn.shape
    anywhere = pl.BlockSpec(memory_space=pl.ANY)
    sems = pltpu.SemaphoreType.DMA((3,))
    outs = [((4 * rows, part), half), ((width, width), half)] + [((rows // 2, width), half)] * 4
    return pl.pallas_call(
        functools.partial(heads_back_kernel, part),
        in_specs=[anywhere] * 8,
        out_specs=[anywhere] * len(outs),
        out_shape=[jax.ShapeDtypeStruct(shape, dtype) for shape, dtype in outs],
        scratch_shapes=[sems, sems, pltpu.SemaphoreType.DMA],
        compiler_params=pltpu.CompilerParams(
            collective_id=4, has_side_effects=True, vmem_limit_bytes=52 * 1024 * 1024
        ),
        cost_estimate=hint(10 * rows * width * width, 0),
        name="heads_back",
    )(dattn, ob, dz1, gb1, gb2, w_down, mix_x, mix_y)


def qkv_back_kernel(*refs):
    dqkv, w_qkv = refs[0:2]
    a1, gb_own, w_down = refs[2:7], refs[7], refs[8]
    own, p3, p1, p2, from_x, from_y, land1, land2, qkv_grad, mix_own = refs[9:19]
    moves = Moves(*refs[19:21])
    rows = own.shape[0]
    n = rows // 2

    def block(k):
        return dqkv.at[pl.ds(k * n, n)]

    greet((1, 2))
    (p3_lo, p3_hi), (p1_lo, p1_hi), (p2_lo, p2_hi) = halves(p3), halves(p1), halves(p2)
    (land1_lo, land1_hi), (land2_lo, land2_hi) = halves(land1), halves(land2)
    multiply([block(6), block(7)], w_qkv, True, [], [p3_lo, p3_hi], store)
    first = [moves.start(p3_lo, from_x, 1), moves.start(p3_hi, from_y, 2)]
    multiply([block(2), block(5)], w_qkv, True, [], [p1_lo, p2_hi], store)
    second = [moves.start(p1_lo, land1_lo, 1), moves.start(p2_hi, land2_hi, 2)]
    multiply([dqkv.at[pl.ds(0, rows)]], w_qkv, True, [], [own], store)
    multiply([gb_own], w_down, False, [], [mix_own], store)
    for copy in first:
        copy.wait()
    multiply([block(3), block(4)], w_qkv, True, [from_y, from_x], [p1_hi, p2_lo], store_sum)
    second += [moves.start(p1_hi, land1_hi, 1), moves.start(p2_lo, land2_lo, 2)]
    rights, at = [], 0
    for x in a1:
        rights.append(dqkv.at[pl.ds(at, x.shape[0])])
        at += x.shape[0]
    outer_on(a1, rights, qkv_grad)
    for copy in second:
        copy.wait()


def qkv_back(dqkv, w_qkv, a1, gb_own, w_down):
    rows, width = a1[0].shape
    wide = gb_own.shape[1]
    n = rows // 2
    outs = [((rows, width), single)] + [((rows, width), half)] * 3
    outs += [((n, width), half)] * 2 + [((rows, width), half)] * 2
    outs += [((width, dqkv.shape[1]), half), ((rows, width), single)]
    out = moving_call(
        qkv_back_kernel,
        [dqkv, w_qkv, *a1, gb_own, w_down],
        outs,
        6,
        5,
        16 * rows * width * dqkv.shape[1] + 2 * rows * width * wide,
        "qkv_back",
    )
    return out[0], out[6:8], out[8], out[9]


def lay_out_kernel(axis, layout, c_ref, *refs):
    out = refs[-1]
    for (j, row), ref in zip(layout, refs):
        x = ref[...].astype(single)
        r, w = x.shape
        if axis == 0:
            n = sum(ref.shape[0] for (k, _), ref in zip(layout, refs) if k == j)
            out[pl.ds(pl.multiple_of((c_ref[0] ^ j) * n + row, r), r), :] = x
        else:
            out[row : row + r, pl.ds(pl.multiple_of((c_ref[0] ^ j) * w, w), w)] = x


def lay_out(axis, pieces, c, groups):
    count = len(pieces)
    r = sum(x.shape[0] for x in pieces[0])
    n = pieces[0][0].shape[1]
    w = n // groups
    if w % 128:
        whole = xor_order([jnp.concatenate(p, axis=0).astype(single) for p in pieces], c)
        whole = jnp.stack([p.reshape(r, groups, w) for p in whole], axis=2)
        return whole.reshape(r, count * n)
    layout, blocks = [], []
    for j, p in enumerate(pieces):
        row = 0
        for x in p:
            layout.append((j, row))
            blocks.append(x)
            row += x.shape[0]
    out = (count * r, w) if axis == 0 else (r, count * w)
    return pl.pallas_call(
        functools.partial(lay_out_kernel, axis, layout),
        grid_spec=pltpu.PrefetchScalarGridSpec(
            num_scalar_prefetch=1,
            grid=(groups,),
            in_specs=[pl.BlockSpec((x.shape[0], w), lambda k, c: (0, k)) for x in blocks],
            out_specs=pl.BlockSpec(out, lambda k, c: (0, k)),
        ),
        out_shape=jax.ShapeDtypeStruct((out[0], out[1] * groups), single),
        compiler_params=pltpu.CompilerParams(vmem_limit_bytes=48 * 1024 * 1024),
        cost_estimate=hint(0, 6 * r * n * count),
        name="lay_out",
    )(c.reshape(1), *blocks)


def gather_small_kernel(nf, x_ref, o_ref, send_sem, recv_sem):
    f = lax.axis_index("fsdp")
    barrier = pltpu.get_barrier_semaphore()
    for d in range(1, nf):
        pl.semaphore_signal(
            barrier,
            inc=1,
            device_id={"fsdp": lax.rem(f + d, nf)},
            device_id_type=pl.DeviceIdType.MESH,
        )
    pl.semaphore_wait(barrier, nf - 1)
    copies = []
    for d in range(1, nf):
        copies.append(
            pltpu.make_async_remote_copy(
                src_ref=x_ref,
                dst_ref=o_ref.at[f],
                send_sem=send_sem.at[d],
                recv_sem=recv_sem.at[d],
                device_id={"fsdp": lax.rem(f + d, nf)},
                device_id_type=pl.DeviceIdType.MESH,
            )
        )
        copies[-1].start()
    o_ref[f] = x_ref[...]
    for copy in copies:
        copy.wait()


def gather_small(x, nf):
    return pl.pallas_call(
        functools.partial(gather_small_kernel, nf),
        out_shape=jax.ShapeDtypeStruct((nf,) + x.shape, single),
        in_specs=[pl.BlockSpec(memory_space=pltpu.VMEM)],
        out_specs=pl.BlockSpec(memory_space=pltpu.VMEM),
        scratch_shapes=[pltpu.SemaphoreType.DMA((nf,)), pltpu.SemaphoreType.DMA((nf,))],
        compiler_params=pltpu.CompilerParams(collective_id=1, has_side_effects=True),
        name="gather_small",
    )(x)


def reduce_small_kernel(nf, nc, x_ref, o_ref, land, stage, send_sem, recv_sem):
    f = lax.axis_index("fsdp")
    c = lax.axis_index("ctx")
    barrier = pltpu.get_barrier_semaphore()
    for d in range(1, nf):
        pl.semaphore_signal(
            barrier,
            inc=1,
            device_id={"fsdp": lax.rem(f + d, nf)},
            device_id_type=pl.DeviceIdType.MESH,
        )
    for d in range(1, nc):
        pl.semaphore_signal(
            barrier,
            inc=1,
            device_id={"ctx": lax.rem(c + d, nc)},
            device_id_type=pl.DeviceIdType.MESH,
        )
    pl.semaphore_wait(barrier, nf + nc - 2)
    copies = []
    for d in range(1, nf):
        to = lax.rem(f + d, nf)
        copies.append(
            pltpu.make_async_remote_copy(
                src_ref=x_ref.at[to],
                dst_ref=land.at[d],
                send_sem=send_sem.at[d],
                recv_sem=recv_sem.at[d],
                device_id={"fsdp": to},
                device_id_type=pl.DeviceIdType.MESH,
            )
        )
        copies[-1].start()
    total = x_ref[f]
    for d in range(1, nf):
        copies[d - 1].wait()
        total = total + land[d]
    stage[0] = total
    copies = []
    for d in range(1, nc):
        copies.append(
            pltpu.make_async_remote_copy(
                src_ref=stage.at[0],
                dst_ref=stage.at[d],
                send_sem=send_sem.at[nf + d],
                recv_sem=recv_sem.at[nf + d],
                device_id={"ctx": lax.rem(c + d, nc)},
                device_id_type=pl.DeviceIdType.MESH,
            )
        )
        copies[-1].start()
    for d in range(1, nc):
        copies[d - 1].wait()
        total = total + stage[d]
    o_ref[...] = total


def reduce_small(x, nf, nc, call):
    block = x.shape[1:]
    sems = pltpu.SemaphoreType.DMA((nf + nc,))
    return pl.pallas_call(
        functools.partial(reduce_small_kernel, nf, nc),
        out_shape=jax.ShapeDtypeStruct(block, single),
        in_specs=[pl.BlockSpec(memory_space=pltpu.VMEM)],
        out_specs=pl.BlockSpec(memory_space=pltpu.VMEM),
        scratch_shapes=[
            pltpu.VMEM((nf,) + block, single),
            pltpu.VMEM((nc,) + block, single),
            sems,
            sems,
        ],
        compiler_params=pltpu.CompilerParams(collective_id=call, has_side_effects=True),
        name="reduce_small",
    )(x)


def per_device(
    tokens,
    cotangent,
    lengths,
    span_place,
    ln1_gain,
    ln1_shift,
    qkv_weight,
    q_bias,
    v_bias,
    out_weight,
    out_bias,
    ln2_gain,
    ln2_shift,
    up_weight,
    up_bias,
    down_weight,
    down_bias,
):
    rows, width = tokens.shape
    CTX = lax.axis_size("ctx")
    c = lax.axis_index("ctx")
    f = lax.axis_index("fsdp")
    nf = lax.axis_size("fsdp")
    wide = up_weight.shape[1]
    part = width // CTX
    heads = HEADS // CTX
    scale = 1.0 / math.sqrt(width // HEADS)
    shard = width // nf
    fpart = wide // nf // CTX
    wpart = wide // CTX

    def columns(x, width_each, stride, count):
        return jnp.concatenate(
            [
                lax.dynamic_slice_in_dim(x, k * stride + c * width_each, width_each, axis=1)
                for k in range(count)
            ],
            axis=1,
        )

    def after(x, *others):
        return lax.optimization_barrier((x, others))[0]

    def pick(x, axis):
        return lax.dynamic_index_in_dim(x, c, axis, keepdims=False)

    def gather_f(x):
        return lax.all_gather(x, "fsdp", axis=0, tiled=True)

    qkv_own = columns(qkv_weight, part, width, 3)
    up_own = columns(up_weight, fpart, wide // nf, nf)
    down_own = lax.dynamic_slice_in_dim(down_weight, c * fpart, fpart, axis=0)
    w_qkv = gather_f(qkv_own.astype(half))
    small = jnp.concatenate(
        [ln1_gain, ln1_shift, q_bias, v_bias, out_bias, ln2_gain, ln2_shift, down_bias, up_bias]
    )
    small_len = small.shape[0]
    small = jnp.pad(small, (0, -small_len % 1024)).reshape(-1, 128)
    small_all = gather_small(small, nf).reshape(nf, -1)[:, :small_len]
    small_all = small_all.astype(half).astype(single)

    def vector(k):
        return small_all[:, k * shard : (k + 1) * shard].reshape(width)

    gain1, shift1, bias_q, bias_v, bias_o, gain2, shift2, bias_d = [vector(k) for k in range(8)]
    bias_u = pick(small_all[:, 8 * shard :].reshape(nf, CTX, fpart), 1).reshape(wpart)
    bias_qkv = jnp.concatenate(
        [pick(bias_q.reshape(CTX, part), 0), jnp.zeros((part,), single), pick(bias_v.reshape(CTX, part), 0)]
    )
    w_out = gather_f(out_weight.astype(half))

    per = rows // SPAN
    table = jnp.arange(CTX * per, dtype=jnp.int32)
    source = ((table // per) ^ c) * per + table % per
    place = jnp.sum(jnp.where(source[:, None] == table[None, :], span_place[0][None, :], 0), axis=1)
    inv = jnp.sum(jnp.where(place[None, :] == table[:, None], table[None, :], 0), axis=1)
    slopes = 2.0 ** (-8.0 * ((c * heads + jnp.arange(heads)).astype(single) + 1.0) / HEADS)

    def flat(pieces):
        return [x for p in pieces for x in p]

    def scatter_f(x):
        return lax.psum_scatter(x, "fsdp", scatter_dimension=0, tiled=True)

    far = CTX - 1
    mid = list(range(1, far))

    def first_norm(x):
        normed, _ = norm_parts(x.astype(single))
        return (normed * gain1 + shift1).astype(half)

    tok_near = after(gather_first(tokens), small_all, place, inv, slopes)
    tok = gather_second(tokens, tok_near)
    near = [[first_norm(x) for x in p] for p in tok[:far]]
    tok = after(tok, near)
    n = rows // 2
    if CTX == 4:
        cot = after(cotangent, tok)
        dz2_lo, dz2_hi = cot[:n].astype(half), cot[n:].astype(half)
    else:
        dz2_own = after(cotangent, tok).astype(half)
        dz2_rest = gather_first(dz2_own)
    w_up = gather_f(after(up_own.astype(half), tok))
    a1 = flat(near)
    if CTX == 4:
        joined, a1_far, dz2_first = qkv_forward(
            tok[far], gain1, shift1, a1, w_qkv, bias_qkv, dz2_lo, dz2_hi
        )
        a1 = a1 + list(a1_far)
        dz2_rest = after((dz2_hi, dz2_lo), joined)
        dz2_rest = [swap(dz2_rest[0], 1), swap(dz2_rest[1], 2)]
    else:
        a1 = a1 + [first_norm(x) for x in tok[far]]
        joined = joined_rows(a1, w_qkv, bias_qkv, "qkv")
    w_down = gather_f(after(down_own.astype(half), joined))
    attended = attn_forward(joined, inv, slopes, heads, scale)
    mine = [attended[j * rows : (j + 1) * rows] for j in range(CTX)]
    mine = after(mine, dz2_rest)
    mine = [mine[0]] + [swap(mine[j], j) for j in range(1, CTX)]
    ob = jnp.concatenate(xor_order(mine, c), axis=1)
    y1 = tokens.astype(single) + dot_nn(ob, w_out) + bias_o

    normed2, inv2 = norm_parts(y1)
    if CTX == 4:
        one_lo, two_hi = after(dz2_first, ob)
        one_hi, two_lo = dz2_rest
        dz2 = [[dz2_lo, dz2_hi], [one_lo, one_hi], [two_lo, two_hi], [swap(one_lo, 2), swap(two_hi, 1)]]
    else:
        dz2 = [[dz2_own]] + [[x] for x in dz2_rest]
    a2_own = (normed2 * gain2 + shift2).astype(half)
    gb, slope = [None] * CTX, [None] * CTX
    gb[0], slope[0] = up_gelu([a2_own], w_up, bias_u, "up_gelu_0")
    last = gb[0]
    a2 = gather_second(a2_own, after(gather_first(a2_own), last))
    for j in range(1, CTX):
        gb[j], slope[j] = up_gelu(after(a2[j], last), w_up, bias_u, f"up_gelu_{j}")
        last = gb[j]
    gb_blocks = flat(gb)
    if CTX == 4:
        gb_blocks = [(g[0], n, i) for g in gb[:far] for i in (0, 1)] + list(gb[far])
    down_grad = outer(gb_blocks, flat(dz2), "down_grad")
    down_part = scatter_f(down_grad)
    w_down = after(w_down, down_grad)

    du, dh2, mix = [None] * CTX, [None] * CTX, [None] * CTX
    if CTX == 4:
        du, dh2, (p1_hi, p2_lo), (x_lo, y_hi) = feed_back(flat(dz2), flat(slope), w_down, w_up)
        x_hi, y_lo, up_grad = up_back(p1_hi, p2_lo, flat(a2), du)
        mix_far = plain(after(gb[far], up_grad), w_down, False, half, "mix_far")
        mix_first = swap(mix_far[0], 1), swap(mix_far[1], 2)
        lows = total_of(dh2[:n], [x_lo, y_lo])
        dh2 = jnp.concatenate([lows, total_of(dh2[n:], [x_hi, y_hi])], axis=0)
        dh2 = after(dh2, mix_far)
        du = [du]
    else:
        for j in range(CTX):
            du[j] = hidden_back(dz2[j], w_down, slope[j], f"du_{j}")
            dh2[j] = plain(du[j], w_up, True, half if j else single, f"dh2_{j}")[0]
        arrived = scatter_send(dh2[1:])
        dh2 = dh2[0]
        up_grad = outer(flat(a2), flat(du), "up_grad")
        mix[far] = plain(gb[far], w_down, False, half, "mix_far")[0]
        dh2 = total_of(dh2, arrived)
    up_part = scatter_f(up_grad)
    up_bias_grad = sum(jnp.sum(x.astype(single), axis=0) for x in flat(du))
    down_bias_grad = sum(jnp.sum(x.astype(single), axis=0) for x in dz2[0])
    gain2_grad = jnp.sum(dh2 * normed2, axis=0)
    shift2_grad = jnp.sum(dh2, axis=0)
    dy1 = cotangent + norm_back(normed2, inv2, gain2, dh2)

    dz1 = dy1.astype(half)
    dattn = dot_nt(dz1, w_out).astype(half)
    out_bias_grad = jnp.sum(dz1.astype(single), axis=0)
    if CTX == 4:
        dattn, out_grad, one_lo, one_hi, two_lo, two_hi = heads_back(
            dattn, ob, dz1, gb[1][0], gb[2][0], w_down, *mix_first, part
        )
    else:
        dattn = xor_order([dattn[:, s * part : (s + 1) * part] for s in range(CTX)], c)
        dattn = [dattn[0]] + [swap(dattn[j], j) for j in range(1, CTX)]
        dattn = jnp.concatenate(dattn, axis=0)
        out_grad = outer([ob], [dz1], "out_grad")
        for j in mid:
            mix[j] = plain(gb[j], w_down, False, half, f"mix_{j}")[0]
    out_part = scatter_f(out_grad)
    down_own = after(down_part, dattn)
    down_near = gather_first(down_own)
    dqkv = attn_backward(joined, dattn, inv, slopes, heads, scale)
    if CTX == 4:
        lows = [swap(one_lo, 1), swap(two_lo, 2)]
        dqkv = after(dqkv, lows, up_part)
        dh1, arrived, qkv_grad, mix[0] = qkv_back(dqkv, w_qkv, a1, gb[0][0], w_down)
    else:
        dh1 = [
            plain([(dqkv, rows, j)], w_qkv, True, half if j else single, f"dh1_{j}")[0]
            for j in range(CTX)
        ]
        arrived = scatter_send(dh1[1:])
        dh1 = dh1[0]
        qkv_grad = outer(a1, [(dqkv, rows, j) for j in range(CTX)], "qkv_grad")
        mix[0] = plain(gb[0], w_down, False, single, "mix_0")[0]
    dh1 = total_of(after(dh1, down_near), arrived)
    down_out = gather_second(down_own, after(down_near, dh1))
    mixed = y1 + bias_d + mix[0]
    if CTX == 4:
        one_hi, two_hi = after((one_hi, two_hi), dh1)
        lows = total_of(mixed[:n], lows)
        mixed = jnp.concatenate([lows, total_of(mixed[n:], [swap(one_hi, 1), swap(two_hi, 2)])])
    else:
        mixed = total_of(mixed, scatter_send(mix[1:]))
    down_out = lay_out(0, down_out, c, width // min(width, 512))
    up_out = gather_ctx(after(up_part, dh1))
    out_part = after(out_part, up_out)
    up_out = lay_out(1, up_out, c, nf)
    sums = jnp.sum(dqkv.astype(single), axis=0)
    normed1_own, inv1_own = norm_parts(tokens.astype(single))
    gain1_grad = jnp.sum(dh1 * normed1_own, axis=0)
    shift1_grad = jnp.sum(dh1, axis=0)
    input_grad = dy1 + norm_back(normed1_own, inv1_own, gain1, dh1)

    qkv_part = scatter_f(after(qkv_grad, input_grad))
    bit = 1
    while bit < CTX:
        out_part = out_part.astype(half)
        out_part = out_part.astype(single) + swap(out_part, bit).astype(single)
        bit *= 2
    out_out = out_part
    qkv_out = lay_out(1, gather_ctx(qkv_part), c, 3)

    def spread(x, inner):
        x = x.reshape(-1, 1, inner)
        mask = (jnp.arange(CTX) == c)[None, :, None]
        return jnp.where(mask, x, 0.0).reshape(-1)

    def reduced(items, call):
        sizes = [x.shape[0] // nf for x in items]
        x = jnp.concatenate([x.reshape(nf, -1) for x in items], axis=1)
        x = jnp.pad(x, ((0, 0), (0, -x.shape[1] % 1024))).reshape(nf, -1, 128)
        x = reduce_small(x, nf, CTX, call).reshape(-1)
        out, at = [], 0
        for n in sizes:
            out.append(x[at : at + n])
            at += n
        return out

    sums_in = [out_bias_grad, gain2_grad, shift2_grad, down_bias_grad, spread(up_bias_grad, fpart)]
    gain1_grad = after(gain1_grad, qkv_part)
    sums_in += [gain1_grad, shift1_grad, spread(sums[:part], part), spread(sums[2 * part :], part)]
    sums_out = reduced(sums_in, 2)
    out_bias_out, gain2_out, shift2_out, down_bias_out, up_bias_out = sums_out[:5]
    gain1_out, shift1_out, q_bias_out, v_bias_out = sums_out[5:]
    return (
        mixed,
        input_grad,
        gain1_out,
        shift1_out,
        qkv_out,
        q_bias_out,
        v_bias_out,
        out_out,
        out_bias_out,
        gain2_out,
        shift2_out,
        up_out,
        up_bias_out,
        down_out,
        down_bias_out,
    )


def solution(mesh):
    rows, flat = P(("ctx", "fsdp"), None), P("fsdp")
    mat = P("fsdp", None)
    in_specs = (
        rows,
        rows,
        mat,
        mat,
        flat,
        flat,
        mat,
        flat,
        flat,
        mat,
        flat,
        flat,
        flat,
        mat,
        flat,
        mat,
        flat,
    )
    out_specs = (
        rows,
        rows,
        flat,
        flat,
        mat,
        flat,
        flat,
        mat,
        flat,
        flat,
        flat,
        mat,
        flat,
        mat,
        flat,
    )
    return jax.shard_map(
        per_device, mesh=mesh, in_specs=in_specs, out_specs=out_specs, check_vma=False
    )
```

profile of v0, /device:TPU:0, one launch (start us, length us, event | category | flops | bytes accessed | tf_op | source)
XLA Modules:
  0.0 766.7 jit_solution(11271077121290635600)
XLA Ops:
  18.1 9.1 %gather_small.1 = f32[8,24,128]{2,1,0:T(8,128)} custom-call(f32[24,128]{1,0:T(8,128)} %bitcast.92), custom_call_target="tpu_custom_call" | custom-call | tf_op jit(solution)/shard_map/gather_small/pallas_call | solution.py:841
  37.9 23.6 %collective-permute-done = bf16[512,2048]{1,0:T(8,128)(2,1)} collective-permute-done((bf16[512,2048]{1,0:T(8,128)(2,1)S(1)}, bf16[512,2048]{1,0:T(8,128)(2,1)}, u32[]{:S(2)}, u32[]{:S(2)}) %collective-permute-start) | collective-permute-done | bytes 2097184 | tf_op jit(solution)/shard_map/ppermute | solution.py:60
  75.3 5.8 fusion.21
  81.0 8.5 %collective-permute-done.3.refs_1_ = bf16[256,2048]{1,0:T(8,128)(2,1)} collective-permute-done((bf16[256,2048]{1,0:T(8,128)(2,1)S(1)}, bf16[256,2048]{1,0:T(8,128)(2,1)}, u32[]{:S(2)}, u32[]{:S(2)}) %collective-permute-start.3) | collective-permute-done | bytes 1048608 | tf_op jit(solution)/shard_map/ppermute | solution.py:60
  98.2 28.8 %qkv.1 = (bf16[2048,1536]{1,0:T(8,128)(2,1)}, bf16[256,2048]{1,0:T(8,128)(2,1)S(1)}, bf16[256,2048]{1,0:T(8,128)(2,1)}, bf16[256,2048]{1,0:T(8,128)(2,1)}, bf16[256,2048]{1,0:T(8,128)(2,1)}) custom-call(bf16[256,2048]{1,0:T(8,128)(2,1)} %collective-permute-done.2.refs_0_, bf16[256,2048]{1,0:T(8,128)(2,1)} %collective-permute-done.3.refs_1_, ...), custom_call_target="tpu_custom_call" | custom-call | flops 12884901 | tf_op jit(solution)/shard_map/qkv/pallas_call | solution.py:499
  130.2 24.3 %attn_forward.1 = bf16[2048,512]{1,0:T(8,128)(2,1)S(1)} custom-call(s32[16]{0:T(128)S(1)} %select_reduce_fusion.inv_ref, f32[4]{0:T(128)S(1)} %multiply_power_fusion.slope_ref, ...), custom_call_target="tpu_custom_call" | custom-call | flops 20000000 | bytes 8388 | tf_op jit(solution)/shard_map/attn_forward/pallas_call | solution.py:233
  161.5 12.5 %collective-permute-done.6 = bf16[512,512]{1,0:T(8,128)(2,1)S(1)} collective-permute-done((bf16[512,512]{1,0:T(8,128)(2,1)}, bf16[512,512]{1,0:T(8,128)(2,1)S(1)}, u32[]{:S(2)}, u32[]{:S(2)}) %collective-permute-start.6) | collective-permute-done | bytes 524320 | tf_op jit(solution)/shard_map/ppermute | solution.py:60
  174.0 7.0 collective-permute-done.7
  184.4 7.8 %fusion.43 = (f32[512]{0:T(512)S(1)}, f32[512,2048]{1,0:T(8,128)S(1)}) fusion(f32[2048]{0:T(1024)S(1)} %bitcast.95, bf16[2048,2048]{1,0:T(8,128)(2,1)} %all-gather.7.cloned.1.call-done, bf16[512,512]{1,0:T(8,128)(2,1)} %get-tuple-element.199, bf16[512,512]{1,0:T(8,128)(2,1)} %get-tuple-element.198, bf16[512,512]{1,0:T(8,128)(2,1)S(1)} %get-tuple-element.197, ...), kind=kOutput, calls=%fused_computation.166 | convolution fusion | flops 4307549696 | bytes 16787456 | tf_op jit(solution)/shard_map/dot_general | solution.py:24
  196.5 47.7 %all-gather.9.cloned.1.call-done.refs_1_.refs_2_.refs_14_ = bf16[2048,2048]{1,0:T(8,128)(2,1)} async-done(((bf16[256,2048]{1,0:T(8,128)(2,1)}), bf16[2048,2048]{1,0:T(8,128)(2,1)}) %all-gather.9.cloned.1.call-update) | async-done | bytes 8388624 | tf_op jit(solution)/shard_map/all_gather | solution.py:976
  244.2 10.9 %up_gelu_0.1 = (bf16[512,2048]{1,0:T(8,128)(2,1)}, bf16[512,2048]{1,0:T(8,128)(2,1)}) custom-call(bf16[512,2048]{1,0:T(8,128)(2,1)} %copy-done.13, bf16[2048,2048]{1,0:T(8,128)(2,1)} %all-gather.9.cloned.1.call-done.refs_1_.refs_2_.refs_14_, f32[1,2048]{1,0:T(1,128)S(1)} %bitcast.69), custom_call_target="tpu_custom_call" | custom-call | flops 4294967 | bytes 16777 | tf_op jit(solution)/shard_map/up_gelu_0/pallas_call | solution.py:311
  263.8 10.9 %up_gelu_1.1 = (bf16[512,2048]{1,0:T(8,128)(2,1)}, bf16[512,2048]{1,0:T(8,128)(2,1)}) custom-call(bf16[512,2048]{1,0:T(8,128)(2,1)} %collective-permute-done.11.refs_0_.refs_3_, bf16[2048,2048]{1,0:T(8,128)(2,1)} %all-gather.9.cloned.1.call-done.refs_1_.refs_2_.refs_14_, f32[1,2048]{1,0:T(1,128)S(1)} %bitcast.70), custom_call_target="tpu_custom_call" | custom-call | flops 4294967 | bytes 16777 | tf_op jit(solution)/shard_map/up_gelu_1/pallas_call | solution.py:311
  274.7 11.0 %up_gelu_2.1 = (bf16[512,2048]{1,0:T(8,128)(2,1)}, bf16[512,2048]{1,0:T(8,128)(2,1)}) custom-call(bf16[512,2048]{1,0:T(8,128)(2,1)} %collective-permute-done.12.refs_0_.refs_4_, bf16[2048,2048]{1,0:T(8,128)(2,1)} %all-gather.9.cloned.1.call-done.refs_1_.refs_2_.refs_14_, f32[1,2048]{1,0:T(1,128)S(1)} %bitcast.71), custom_call_target="tpu_custom_call" | custom-call | flops 4294967 | bytes 16777 | tf_op jit(solution)/shard_map/up_gelu_2/pallas_call | solution.py:311
  287.0 20.5 %up_gelu_3.1 = (bf16[256,2048]{1,0:T(8,128)(2,1)S(1)}, bf16[256,2048]{1,0:T(8,128)(2,1)}, bf16[256,2048]{1,0:T(8,128)(2,1)}, bf16[256,2048]{1,0:T(8,128)(2,1)}) custom-call(bf16[256,2048]{1,0:T(8,128)(2,1)} %copy-done.26, bf16[256,2048]{1,0:T(8,128)(2,1)} %copy-done.25, bf16[2048,2048]{1,0:T(8,128)(2,1)} %all-gather.9.cloned.1.call-done.refs_1_.refs_2_.refs_14_, ...), custom_call_target="tpu_custom_call" | custom-call | flops 4294967 | bytes 16777 | tf_op jit(solution)/shard_map/up_gelu_3/pallas_call | solution.py:311
  309.0 23.2 %down_grad.1 = bf16[2048,2048]{1,0:T(8,128)(2,1)} custom-call(bf16[512,2048]{1,0:T(8,128)(2,1)} %get-tuple-element.116.refs_0_.refs_1_.refs_7_, bf16[512,2048]{1,0:T(8,128)(2,1)} %get-tuple-element.116.refs_0_.refs_1_.refs_7_, bf16[512,2048]{1,0:T(8,128)(2,1)} %get-tuple-element.121.refs_2_.refs_3_, bf16[512,2048]{1,0:T(8,128)(2,1)} %get-tuple-element.121.refs_2_.refs_3_, ...), custom_call_target="tpu_custom_call" | custom-call | flops 17179868 | bytes 25165 | tf_op jit(solution)/shard_map/down_grad/pallas_call | solution.py:384
  332.3 70.5 %feed_back.1 = (bf16[512,2048]{1,0:T(8,128)(2,1)}, bf16[512,2048]{1,0:T(8,128)(2,1)}, bf16[512,2048]{1,0:T(8,128)(2,1)}, bf16[256,2048]{1,0:T(8,128)(2,1)}, bf16...) custom-call(bf16[256,2048]{1,0:T(8,128)(2,1)} %get-tuple-element.105, ...), custom_call_target="tpu_custom_call" | custom-call | flops 34359736 | tf_op jit(solution)/shard_map/feed_back/pallas_call | solution.py:627
  402.8 25.5 %up_back.1 = (bf16[256,2048]{1,0:T(8,128)(2,1)S(1)}, bf16[256,2048]{1,0:T(8,128)(2,1)}, bf16[2048,2048]{1,0:T(8,128)(2,1)}) custom-call(bf16[256,2048]{1,0:T(8,128)(2,1)} %get-tuple-element.135.refs_0_, bf16[256,2048]{1,0:T(8,128)(2,1)} %get-tuple-element.136.refs_1_, bf16[512,2048]{1,0:T(8,128)(2,1)} %copy-done.13, ...), custom_call_target="tpu_custom_call" | custom-call | flops 17179868 | tf_op jit(solution)/shard_map/up_back/pallas_call | solution.py:499
  428.4 9.4 %mix_far.1 = (bf16[256,2048]{1,0:T(8,128)(2,1)S(1)}, bf16[256,2048]{1,0:T(8,128)(2,1)}) custom-call(bf16[256,2048]{1,0:T(8,128)(2,1)} %copy-done.1, bf16[256,2048]{1,0:T(8,128)(2,1)} %get-tuple-element.147.refs_7_.refs_1_, bf16[2048,2048]{1,0:T(8,128)(2,1)} %all-gather.11.cloned.1.call-done.refs_13_.refs_2_.refs_5_.refs_8_), custom_call_target="tpu_custom_call" | custom-call | flops 4294967 | bytes 16777 | tf_op jit(solution)/shard_map/mix_far/pallas_call | solution.py:311
  450.4 6.0 convolution_convert_fusion.refs_0_
  456.4 4.2 collective-permute-done.15.refs_6_
  461.6 27.9 %heads_back.1 = (bf16[2048,512]{1,0:T(8,128)(2,1)}, bf16[2048,2048]{1,0:T(8,128)(2,1)}, bf16[256,2048]{1,0:T(8,128)(2,1)}, bf16[256,2048]{1,0:T(8,128)(2,1)}, bf...) custom-call(bf16[512,2048]{1,0:T(8,128)(2,1)} %convolution_convert_fusion.refs_0_, ...), custom_call_target="tpu_custom_call" | custom-call | flops 21474836 | tf_op jit(solution)/shard_map/heads_back/pallas_call | solution.py:701
  493.7 36.2 %attn_backward.1.refs_0_ = bf16[2048,1536]{1,0:T(8,128)(2,1)} custom-call(s32[16]{0:T(128)S(1)} %select_reduce_fusion.inv_ref, f32[4]{0:T(128)S(1)} %multiply_power_fusion.slope_ref, ...), custom_call_target="tpu_custom_call" | custom-call | flops 40000000 | bytes 14680 | tf_op jit(solution)/shard_map/attn_backward/pallas_call | solution.py:233
  530.0 75.8 %qkv_back.1 = (f32[512,2048]{1,0:T(8,128)}, bf16[512,2048]{1,0:T(8,128)(2,1)}, bf16[512,2048]{1,0:T(8,128)(2,1)}, bf16[512,2048]{1,0:T(8,128)(2,1)}, bf16[256,20...) custom-call(bf16[2048,1536]{1,0:T(8,128)(2,1)} %attn_backward.1.refs, ...), custom_call_target="tpu_custom_call" | custom-call | flops 30064772 | tf_op jit(solution)/shard_map/qkv_back/pallas_call | solution.py:499
  605.9 5.2 fusion.16
  625.6 14.4 %collective-permute-done.28.refs_2_ = bf16[256,2048]{1,0:T(8,128)(2,1)S(1)} collective-permute-done((bf16[256,2048]{1,0:T(8,128)(2,1)}, bf16[256,2048]{1,0:T(8,128)(2,1)S(1)}, u32[]{:S(2)}, u32[]{:S(2)}) %collective-permute-start.28) | collective-permute-done | bytes 1048608 | tf_op jit(solution)/shard_map/ppermute | solution.py:60
  650.0 5.0 collective-permute-done.30.refs_4_
  660.4 7.0 add_add_fusion
  668.3 37.3 %collective-permute-done.31 = bf16[256,2048]{1,0:T(8,128)(2,1)S(1)} collective-permute-done((bf16[256,2048]{1,0:T(8,128)(2,1)}, bf16[256,2048]{1,0:T(8,128)(2,1)S(1)}, u32[]{:S(2)}, u32[]{:S(2)}) %collective-permute-start.31) | collective-permute-done | bytes 1048608 | tf_op jit(solution)/shard_map/ppermute | solution.py:60
  709.7 6.0 lay_out.5
  721.5 6.6 lay_out.4
  734.1 11.4 %reduce_small.1 = f32[24,128]{1,0:T(8,128)} custom-call(f32[8,24,128]{2,1,0:T(8,128)} %bitcast.79), custom_call_target="tpu_custom_call" | custom-call | tf_op jit(solution)/shard_map/reduce_small/pallas_call | solution.py:912
  750.5 5.4 collective-permute-done.26.refs_4_
  (345 shorter events, 145.9 us)
Async XLA Ops:
  7.3 90.9 %all-gather.5.cloned.1.call-start = ((), (), s32[]{:S(2)}) async-start(), calls=%async_computation.4 | async-start | bytes 7077888 | tf_op jit(solution)/shard_map/all_gather | solution.py:976
  9.9 174.5 %all-gather.7.cloned.1.call-start = ((), (), s32[]{:S(2)}) async-start(), calls=%async_computation.5 | async-start | bytes 9437184 | tf_op jit(solution)/shard_map/all_gather | solution.py:976
  12.7 231.5 %all-gather.9.cloned.1.call-start = ((), (), s32[]{:S(2)}) async-start(), calls=%async_computation.6 | async-start | bytes 9437184 | tf_op jit(solution)/shard_map/all_gather | solution.py:976
  12.7 48.7 %collective-permute-start = (bf16[512,2048]{1,0:T(8,128)(2,1)S(1)}, bf16[512,2048]{1,0:T(8,128)(2,1)}, u32[]{:S(2)}, u32[]{:S(2)}) collective-permute-start(bf16[512,2048]{1,0:T(8,128)(2,1)S(1)} %copy-done.9), channel_id=1, source_target_pairs={{0,8},{8,0},{16,24},{24,16},{1,9},{9,1},{17,25},{25,17},{2,10},{10... | collective-permute-start | bytes 6291464 | tf_op jit(solution)/shard_map/ppermute | solution.py:60
  15.8 47.2 %collective-permute-start.1 = (bf16[512,2048]{1,0:T(8,128)(2,1)S(1)}, bf16[512,2048]{1,0:T(8,128)(2,1)}, u32[]{:S(2)}, u32[]{:S(2)}) collective-permute-start(bf16[512,2048]{1,0:T(8,128)(2,1)S(1)} %copy-done.9), channel_id=1, source_target_pairs={{0,16},{8,24},{16,0},{24,8},{1,17},{9,25},{17,1},{25,9},{2,18},{10... | collective-permute-start | bytes 6291464 | tf_op jit(solution)/shard_map/ppermute | solution.py:60
  65.6 23.9 %collective-permute-start.3 = (bf16[256,2048]{1,0:T(8,128)(2,1)S(1)}, bf16[256,2048]{1,0:T(8,128)(2,1)}, u32[]{:S(2)}, u32[]{:S(2)}) collective-permute-start(bf16[256,2048]{1,0:T(8,128)(2,1)S(1)} %slice.166), channel_id=1, source_target_pairs={{0,8},{8,0},{16,24},{24,16},{1,9},{9,1},{17,25},{25,17},{2,10},{10... | collective-permute-start | bytes 3145736 | tf_op jit(solution)/shard_map/ppermute | solution.py:60
  66.0 23.9 %collective-permute-start.2 = (bf16[256,2048]{1,0:T(8,128)(2,1)S(1)}, bf16[256,2048]{1,0:T(8,128)(2,1)}, u32[]{:S(2)}, u32[]{:S(2)}) collective-permute-start(bf16[256,2048]{1,0:T(8,128)(2,1)S(1)} %slice.165), channel_id=1, source_target_pairs={{0,16},{8,24},{16,0},{24,8},{1,17},{9,25},{17,1},{25,9},{2,18},{10... | collective-permute-start | bytes 3145736 | tf_op jit(solution)/shard_map/ppermute | solution.py:60
  89.9 242.4 %all-gather.11.cloned.1.call-start = ((), (), s32[]{:S(2)}) async-start(), calls=%async_computation.7 | async-start | bytes 9437184 | tf_op jit(solution)/shard_map/all_gather | solution.py:976
  128.1 364.0 %reduce-scatter.7.cloned.1.call-start = ((), (), s32[]{:S(2)}) async-start(), calls=%async_computation.9 | async-start | bytes 9437184 | tf_op jit(solution)/shard_map/reduce_scatter | solution.py:1011
  128.1 27.8 %collective-permute-start.4 = (bf16[256,2048]{1,0:T(8,128)(2,1)S(1)}, bf16[256,2048]{1,0:T(8,128)(2,1)S(1)}, u32[]{:S(2)}, u32[]{:S(2)}) collective-permute-start(bf16[256,2048]{1,0:T(8,128)(2,1)S(1)} %copy-done.15), channel_id=1, source_target_pairs={{0,8},{8,0},{16,24},{24,16},{1,9},{9,1},{17,25},{25,17},{2,10},{10... | collective-permute-start | bytes 3145736 | tf_op jit(solution)/shard_map/ppermute | solution.py:60
  129.6 27.4 %collective-permute-start.5 = (bf16[256,2048]{1,0:T(8,128)(2,1)}, bf16[256,2048]{1,0:T(8,128)(2,1)S(1)}, u32[]{:S(2)}, u32[]{:S(2)}) collective-permute-start(bf16[256,2048]{1,0:T(8,128)(2,1)} %get-tuple-element.105.refs_9_.refs_8_.refs_0_), channel_id=1, source_target_pairs={{0,16},{8,24},{16,0},{24,8},{1,17},{9,25},{17,1},{25,9},{2,18},{10... | collective-permute-start | bytes 3145736 | tf_op jit(solution)/shard_map/ppermute | solution.py:60
  194.3 60.9 %collective-permute-start.12 = (bf16[512,2048]{1,0:T(8,128)(2,1)S(1)}, bf16[512,2048]{1,0:T(8,128)(2,1)}, u32[]{:S(2)}, u32[]{:S(2)}) collective-permute-start(bf16[512,2048]{1,0:T(8,128)(2,1)S(1)} %add_convert_fusion.refs_0_.refs_2_), channel_id=1, source_target_pairs={{0,16},{8,24},{16,0},{24,8},{1,17},{9,25},{17,1},{25,9},{2,18},{10... | collective-permute-start | bytes 6291464 | tf_op jit(solution)/shard_map/ppermute | solution.py:60
  195.7 59.4 %collective-permute-start.11 = (bf16[512,2048]{1,0:T(8,128)(2,1)S(1)}, bf16[512,2048]{1,0:T(8,128)(2,1)}, u32[]{:S(2)}, u32[]{:S(2)}) collective-permute-start(bf16[512,2048]{1,0:T(8,128)(2,1)S(1)} %add_convert_fusion.refs_0_.refs_2_), channel_id=1, source_target_pairs={{0,8},{8,0},{16,24},{24,16},{1,9},{9,1},{17,25},{25,17},{2,10},{10... | collective-permute-start | bytes 6291464 | tf_op jit(solution)/shard_map/ppermute | solution.py:60
  258.0 27.7 %collective-permute-start.14 = (bf16[256,2048]{1,0:T(8,128)(2,1)S(1)}, bf16[256,2048]{1,0:T(8,128)(2,1)S(1)}, u32[]{:S(2)}, u32[]{:S(2)}) collective-permute-start(bf16[256,2048]{1,0:T(8,128)(2,1)S(1)} %slice.183), channel_id=1, source_target_pairs={{0,8},{8,0},{16,24},{24,16},{1,9},{9,1},{17,25},{25,17},{2,10},{10... | collective-permute-start | bytes 3145736 | tf_op jit(solution)/shard_map/ppermute | solution.py:60
  259.6 26.1 %collective-permute-start.13 = (bf16[256,2048]{1,0:T(8,128)(2,1)S(1)}, bf16[256,2048]{1,0:T(8,128)(2,1)S(1)}, u32[]{:S(2)}, u32[]{:S(2)}) collective-permute-start(bf16[256,2048]{1,0:T(8,128)(2,1)S(1)} %slice.182), channel_id=1, source_target_pairs={{0,16},{8,24},{16,0},{24,8},{1,17},{9,25},{17,1},{25,9},{2,18},{10... | collective-permute-start | bytes 3145736 | tf_op jit(solution)/shard_map/ppermute | solution.py:60
  262.7 44.9 %collective-permute-start.9 = (bf16[256,2048]{1,0:T(8,128)(2,1)S(1)}, bf16[256,2048]{1,0:T(8,128)(2,1)S(1)}, u32[]{:S(2)}, u32[]{:S(2)}) collective-permute-start(bf16[256,2048]{1,0:T(8,128)(2,1)S(1)} %copy-done.21), channel_id=1, source_target_pairs={{0,16},{8,24},{16,0},{24,8},{1,17},{9,25},{17,1},{25,9},{2,18},{10... | collective-permute-start | bytes 3145736 | tf_op jit(solution)/shard_map/ppermute | solution.py:60
  263.2 44.3 %collective-permute-start.10 = (bf16[256,2048]{1,0:T(8,128)(2,1)S(1)}, bf16[256,2048]{1,0:T(8,128)(2,1)S(1)}, u32[]{:S(2)}, u32[]{:S(2)}) collective-permute-start(bf16[256,2048]{1,0:T(8,128)(2,1)S(1)} %copy-done.22), channel_id=1, source_target_pairs={{0,8},{8,0},{16,24},{24,16},{1,9},{9,1},{17,25},{25,17},{2,10},{10... | collective-permute-start | bytes 3145736 | tf_op jit(solution)/shard_map/ppermute | solution.py:60
  332.2 197.8 %reduce-scatter.5.cloned.1.call-start = ((), (), s32[]{:S(2)}) async-start(), calls=%async_computation.8 | async-start | bytes 9437184 | tf_op jit(solution)/shard_map/reduce_scatter | solution.py:1011
  428.3 228.0 %reduce-scatter.11.cloned.1.call-start = ((), (), s32[]{:S(2)}) async-start(), calls=%async_computation.11 | async-start | bytes 9437184 | tf_op jit(solution)/shard_map/reduce_scatter | solution.py:1011
  437.8 22.8 %collective-permute-start.15 = (bf16[256,2048]{1,0:T(8,128)(2,1)S(1)}, bf16[256,2048]{1,0:T(8,128)(2,1)S(1)}, u32[]{:S(2)}, u32[]{:S(2)}) collective-permute-start(bf16[256,2048]{1,0:T(8,128)(2,1)S(1)} %get-tuple-element.148), channel_id=1, source_target_pairs={{0,8},{8,0},{16,24},{24,16},{1,9},{9,1},{17,25},{25,17},{2,10},{10... | collective-permute-start | bytes 3145736 | tf_op jit(solution)/shard_map/ppermute | solution.py:60
  489.6 238.6 %reduce-scatter.9.cloned.1.call-start = ((), (), s32[]{:S(2)}) async-start(), calls=%async_computation.10 | async-start | bytes 7077888 | tf_op jit(solution)/shard_map/reduce_scatter | solution.py:1011
  489.6 40.3 %collective-permute-start.17 = (bf16[256,2048]{1,0:T(8,128)(2,1)}, bf16[256,2048]{1,0:T(8,128)(2,1)}, u32[]{:S(2)}, u32[]{:S(2)}) collective-permute-start(bf16[256,2048]{1,0:T(8,128)(2,1)} %get-tuple-element.152), channel_id=1, source_target_pairs={{0,8},{8,0},{16,24},{24,16},{1,9},{9,1},{17,25},{25,17},{2,10},{10... | collective-permute-start | bytes 3145736 | tf_op jit(solution)/shard_map/ppermute | solution.py:60
  490.6 39.4 %collective-permute-start.18 = (bf16[256,2048]{1,0:T(8,128)(2,1)}, bf16[256,2048]{1,0:T(8,128)(2,1)}, u32[]{:S(2)}, u32[]{:S(2)}) collective-permute-start(bf16[256,2048]{1,0:T(8,128)(2,1)} %get-tuple-element.153), channel_id=1, source_target_pairs={{0,16},{8,24},{16,0},{24,8},{1,17},{9,25},{17,1},{25,9},{2,18},{10... | collective-permute-start | bytes 3145736 | tf_op jit(solution)/shard_map/ppermute | solution.py:60
  492.0 113.8 %collective-permute-start.20 = (bf16[256,2048]{1,0:T(8,128)(2,1)}, bf16[256,2048]{1,0:T(8,128)(2,1)S(1)}, u32[]{:S(2)}, u32[]{:S(2)}) collective-permute-start(bf16[256,2048]{1,0:T(8,128)(2,1)} %reduce-scatter.7.cloned.1.call-done.refs_0_), channel_id=1, source_target_pairs={{0,16},{8,24},{16,0},{24,8},{1,17},{9,25},{17,1},{25,9},{2,18},{10... | collective-permute-start | bytes 3145736 | tf_op jit(solution)/shard_map/ppermute | solution.py:60
  492.6 113.3 %collective-permute-start.19 = (bf16[256,2048]{1,0:T(8,128)(2,1)}, bf16[256,2048]{1,0:T(8,128)(2,1)}, u32[]{:S(2)}, u32[]{:S(2)}) collective-permute-start(bf16[256,2048]{1,0:T(8,128)(2,1)} %reduce-scatter.7.cloned.1.call-done.refs_0_), channel_id=1, source_target_pairs={{0,8},{8,0},{16,24},{24,16},{1,9},{9,1},{17,25},{25,17},{2,10},{10... | collective-permute-start | bytes 3145736 | tf_op jit(solution)/shard_map/ppermute | solution.py:60
  618.6 23.4 %collective-permute-start.27 = (bf16[256,2048]{1,0:T(8,128)(2,1)}, bf16[256,2048]{1,0:T(8,128)(2,1)S(1)}, u32[]{:S(2)}, u32[]{:S(2)}) collective-permute-start(bf16[256,2048]{1,0:T(8,128)(2,1)} %reduce-scatter.5.cloned.1.call-done.refs_0_), channel_id=1, source_target_pairs={{0,8},{8,0},{16,24},{24,16},{1,9},{9,1},{17,25},{25,17},{2,10},{10... | collective-permute-start | bytes 3145736 | tf_op jit(solution)/shard_map/ppermute | solution.py:60
  647.9 60.6 %collective-permute-start.34 = (bf16[128,2048]{1,0:T(8,128)(2,1)}, bf16[128,2048]{1,0:T(8,128)(2,1)}, u32[]{:S(2)}, u32[]{:S(2)}) collective-permute-start(bf16[128,2048]{1,0:T(8,128)(2,1)} %slice.213), channel_id=1, source_target_pairs={{0,8},{8,0},{16,24},{24,16},{1,9},{9,1},{17,25},{25,17},{2,10},{10... | collective-permute-start | bytes 1572872 | tf_op jit(solution)/shard_map/ppermute | solution.py:60
  648.0 60.5 %collective-permute-start.33 = (bf16[128,2048]{1,0:T(8,128)(2,1)}, bf16[128,2048]{1,0:T(8,128)(2,1)}, u32[]{:S(2)}, u32[]{:S(2)}) collective-permute-start(bf16[128,2048]{1,0:T(8,128)(2,1)} %slice.212), channel_id=1, source_target_pairs={{0,16},{8,24},{16,0},{24,8},{1,17},{9,25},{17,1},{25,9},{2,18},{10... | collective-permute-start | bytes 1572872 | tf_op jit(solution)/shard_map/ppermute | solution.py:60
  650.0 65.7 %collective-permute-start.21 = (bf16[256,2048]{1,0:T(8,128)(2,1)}, bf16[256,2048]{1,0:T(8,128)(2,1)}, u32[]{:S(2)}, u32[]{:S(2)}) collective-permute-start(bf16[256,2048]{1,0:T(8,128)(2,1)} %get-tuple-element.165), channel_id=1, source_target_pairs={{0,8},{8,0},{16,24},{24,16},{1,9},{9,1},{17,25},{25,17},{2,10},{10... | collective-permute-start | bytes 3145736 | tf_op jit(solution)/shard_map/ppermute | solution.py:60
  655.8 59.9 %collective-permute-start.22 = (bf16[256,2048]{1,0:T(8,128)(2,1)}, bf16[256,2048]{1,0:T(8,128)(2,1)}, u32[]{:S(2)}, u32[]{:S(2)}) collective-permute-start(bf16[256,2048]{1,0:T(8,128)(2,1)} %get-tuple-element.166), channel_id=1, source_target_pairs={{0,16},{8,24},{16,0},{24,8},{1,17},{9,25},{17,1},{25,9},{2,18},{10... | collective-permute-start | bytes 3145736 | tf_op jit(solution)/shard_map/ppermute | solution.py:60
  658.3 47.3 %collective-permute-start.31 = (bf16[256,2048]{1,0:T(8,128)(2,1)}, bf16[256,2048]{1,0:T(8,128)(2,1)S(1)}, u32[]{:S(2)}, u32[]{:S(2)}) collective-permute-start(bf16[256,2048]{1,0:T(8,128)(2,1)} %reduce-scatter.11.cloned.1.call-done), channel_id=1, source_target_pairs={{0,8},{8,0},{16,24},{24,16},{1,9},{9,1},{17,25},{25,17},{2,10},{10... | collective-permute-start | bytes 3145736 | tf_op jit(solution)/shard_map/ppermute | solution.py:60
  706.9 23.3 %collective-permute-start.32 = (bf16[256,2048]{1,0:T(8,128)(2,1)}, bf16[256,2048]{1,0:T(8,128)(2,1)}, u32[]{:S(2)}, u32[]{:S(2)}) collective-permute-start(bf16[256,2048]{1,0:T(8,128)(2,1)} %add_convert_fusion.1), channel_id=1, source_target_pairs={{0,16},{8,24},{16,0},{24,8},{1,17},{9,25},{17,1},{25,9},{2,18},{10... | collective-permute-start | bytes 3145736 | tf_op jit(solution)/shard_map/ppermute | solution.py:60
  (75 other events, 1106.3 us)
Sparse Core Ops, SparseCore 0:
  10.3 68.1 all-gather.4
  80.7 80.6 all-gather.6
  163.6 80.5 all-gather.8
  245.6 80.6 all-gather.10
  332.3 88.4 reduce-scatter.6
  428.4 86.9 reduce-scatter.4
  517.7 87.9 reduce-scatter.10
  614.3 67.5 reduce-scatter.8
where the time goes:
time: 779 us; the launch traced here: 767 us
  Pallas kernels  411 us (53%)
  waiting for transfers between devices  172 us (22%)
  other arithmetic  69.6 us (9%)
  local copies, waits for them, and re-layouts  44.5 us (6%)
  starting transfers between devices  39.8 us (5%)
  between operations  15.7 us (2%)
  matrix products  13.7 us (2%)
    pallas_call x3, Pallas kernels, moving_call(): pl.pallas_call(kernel, in_specs=[anywhere] * len(operands), out_specs=[an...  130 us
    ppermute x35, waiting for transfers between devices, swap(): return lax.ppermute(x, 'ctx', [(i, i ^ mask) for i in range(n)])  124 us
    pallas_call x1, Pallas kernels, feed_back(): pl.pallas_call(feed_back_kernel, in_specs=[anywhere] * 15, out_specs=[any...  70.5 us
    pallas_call x5, Pallas kernels, rows_matmul(): pl.pallas_call(functools.partial(rows_kernel, dot_nt if transposed else d...  62.7 us
    pallas_call x2, Pallas kernels, attn_call(): pl.pallas_call(kernel, grid_spec=pltpu.PrefetchScalarGridSpec(num_scalar_...  60.5 us
    all_gather x4, waiting for transfers between devices, gather_f(): return lax.all_gather(x, 'fsdp', axis=0, tiled=True)  47.7 us
    ppermute x35, starting transfers between devices, swap(): return lax.ppermute(x, 'ctx', [(i, i ^ mask) for i in range(n)])  39.5 us
    pallas_call x1, Pallas kernels, heads_back(): pl.pallas_call(functools.partial(heads_back_kernel, part), in_specs=[anyw...  27.9 us
  transfers between devices with their start and end apart: 43, of which 16 were waited for; matrix products, arithmetic and copies ran while one was open for 14% of the time, Pallas kernels for 53%

commit v1 on v0

--- a/solution.py
+++ b/solution.py
@@ -584,14 +584,16 @@
 
 def feed_back_kernel(*refs):
     dz, slope, (w_down, w_up) = refs[0:8], refs[8:13], refs[13:15]
-    du, own, p1_hi, p2_lo, land1_lo, land2_hi = refs[15:20], *refs[20:25]
-    total, far, near, rest, from_x, from_y = refs[25:31]
-    moves = Moves(*refs[31:33])
-    local = refs[33]
+    a2, gb_far = refs[15:20], refs[20:22]
+    du, own, land1, land2, up_grad, mix_x, mix_y = refs[22:27], *refs[27:33]
+    total, far, near, rest, from_x, from_y = refs[33:39]
+    moves = Moves(*refs[39:41])
+    local = refs[41]
     n = from_x.shape[0]
     lo, hi = pl.ds(0, n), pl.ds(n, n)
     (s1_lo, s1_hi), (s2_lo, s2_hi) = halves(slope[1]), halves(slope[2])
     (d1_lo, d1_hi), (d2_lo, d2_hi) = halves(du[1]), halves(du[2])
+    (land1_lo, land1_hi), (land2_lo, land2_hi) = halves(land1), halves(land2)
     greet((1, 2))
     feed_pass(dz[6:8], slope[3:5], w_down, w_up, du[3:5], total)
     far[...] = total[...].astype(half)
@@ -604,81 +606,108 @@
         copy.wait()
     rest[lo] = (total[lo] + from_y[...].astype(single)).astype(half)
     rest[hi] = (total[hi] + from_x[...].astype(single)).astype(half)
-    stores = [
-        pltpu.make_async_copy(rest.at[lo], p1_hi, local.at[0]),
-        pltpu.make_async_copy(rest.at[hi], p2_lo, local.at[1]),
-    ]
-    for copy in stores:
-        copy.start()
+    second += [moves.start(rest.at[lo], land1_hi, 1), moves.start(rest.at[hi], land2_lo, 2)]
+    wide, width = w_down.shape
+    t = math.gcd(width, 512)
+
+    def mix(x_lo, x_hi, w):
+        at = pl.ds(pl.multiple_of(pl.program_id(0) * t, t), t)
+        far[0:n, at] = dot_nn(x_lo[...], w[...]).astype(half)
+        far[n : 2 * n, at] = dot_nn(x_hi[...], w[...]).astype(half)
+
+    pltpu.emit_pipeline(
+        mix,
+        grid=(width // t,),
+        in_specs=[pl.BlockSpec((n, wide), lambda i: (0, 0))] * 2
+        + [pl.BlockSpec((wide, t), lambda i: (0, i))],
+    )(*gb_far, w_down)
+    second += [moves.start(far.at[lo], mix_x, 1), moves.start(far.at[hi], mix_y, 2)]
     feed_pass(dz[0:2], halves(slope[0]), w_down, w_up, halves(du[0]), total)
-    stores.append(pltpu.make_async_copy(total, own, local.at[2]))
-    stores[-1].start()
-    for copy in second + stores:
+    store_own = pltpu.make_async_copy(total, own, local)
+    store_own.start()
+    outer_on(a2, du, up_grad)
+    store_own.wait()
+    for copy in second:
         copy.wait()
 
 
-def feed_back(dz, slope, w_down, w_up):
+def feed_back(dz, slope, w_down, w_up, a2, gb_far):
     n, width = dz[0].shape
     rows, wide = 2 * n, w_down.shape[0]
     anywhere = pl.BlockSpec(memory_space=pl.ANY)
     outs = [((r, wide), half) for r in (rows, rows, rows, n, n)]
-    outs += [((rows, width), single)] + [((n, width), half)] * 4
-    sems = pltpu.SemaphoreType.DMA((4,))
+    outs += [((rows, width), single)] + [((rows, width), half)] * 2
+    outs += [((width, wide), half)] + [((n, width), half)] * 2
+    sems = pltpu.SemaphoreType.DMA((8,))
     out = pl.pallas_call(
         feed_back_kernel,
-        in_specs=[anywhere] * 15,
+        in_specs=[anywhere] * 22,
         out_specs=[anywhere] * len(outs),
         out_shape=[jax.ShapeDtypeStruct(shape, dtype) for shape, dtype in outs],
         scratch_shapes=[pltpu.VMEM((rows, width), single)]
         + [pltpu.VMEM((rows, width), half)] * 3
         + [pltpu.VMEM((n, width), half)] * 2
-        + [sems, sems, pltpu.SemaphoreType.DMA((3,))],
+        + [sems, sems, pltpu.SemaphoreType.DMA],
         compiler_params=pltpu.CompilerParams(
             collective_id=3, has_side_effects=True, vmem_limit_bytes=56 * 1024 * 1024
         ),
-        cost_estimate=hint(16 * rows * width * wide, 0),
+        cost_estimate=hint(26 * rows * width * wide, 0),
         name="feed_back",
-    )(*dz, *slope, w_down, w_up)
-    return out[0:5], out[5], out[6:8], out[8:10]
-
-
-def up_back_kernel(*refs):
-    p1_hi, p2_lo, a2, du = refs[0], refs[1], refs[2:7], refs[7:12]
-    land1_hi, land2_lo, up_grad = refs[12:15]
-    moves = Moves(*refs[15:17])
-    greet((1, 2))
-    copies = [moves.start(p1_hi, land1_hi, 1), moves.start(p2_lo, land2_lo, 2)]
-    outer_on(a2, du, up_grad)
-    for copy in copies:
-        copy.wait()
-
-
-def up_back(p1_hi, p2_lo, a2, du):
-    m, n = a2[0].shape[1], du[0].shape[1]
-    outs = [(p1_hi.shape, half)] * 2 + [((m, n), half)]
-    flops = 8 * a2[0].shape[0] * m * n
-    return moving_call(up_back_kernel, [p1_hi, p2_lo, *a2, *du], outs, 2, 6, flops, "up_back")
+    )(*dz, *slope, w_down, w_up, *a2, *gb_far)
+    return out[0:5], out[5:8], out[8], out[9:11]
 
 
 def heads_back_kernel(part, *refs):
-    dattn, ob, dz1, gb1, gb2, w_down, mix_x, mix_y = refs[0:8]
-    got, out_grad = refs[8:10]
-    mix = refs[10:14]
-    moves = Moves(*refs[14:16])
-    local = refs[16]
-    rows = dattn.shape[0]
-    c = lax.axis_index("ctx")
-
-    def columns(of):
-        return dattn.at[:, pl.ds(pl.multiple_of(of * part, part), part)]
-
+    own, land1, land2, cot, y1, gain, w_out = refs[0:7]
+    ob, gb1, gb2, w_down, mix_x, mix_y, down = refs[7:14]
+    dy1, dz1, sums, got, out_grad = refs[14:19]
+    mix, down1, down2 = refs[19:23], refs[23], refs[24]
+    dz, w, stage = refs[25:28]
+    moves = Moves(*refs[28:30])
+    local = refs[30]
+    rows, width = own.shape
     greet((1, 2, 3))
-    copies = []
-    for mask in (3, 1, 2):
+    load = pltpu.make_async_copy(w_out, w, local.at[0])
+    load.start()
+    copies = [moves.start(down, down1, 1), moves.start(down, down2, 2)]
+    t = math.gcd(rows, 64)
+
+    def norm(own, one, two, cot, y1, gain, dy1, dz1, sums):
+        step = pl.program_id(0)
+        grad = own[...] + one[...].astype(single) + two[...].astype(single)
+        normed, inv = norm_parts(y1[...])
+        dy = cot[...] + norm_back(normed, inv, gain[...], grad)
+        low = dy.astype(half)
+        dy1[...] = dy
+        dz1[...] = low
+        dz[pl.ds(pl.multiple_of(step * t, t), t), :] = low
+
+        @pl.when(step == 0)
+        def _():
+            sums[...] = jnp.zeros_like(sums)
+
+        sums[0:1] += jnp.sum(grad * normed, axis=0, keepdims=True)
+        sums[1:2] += jnp.sum(grad, axis=0, keepdims=True)
+        sums[2:3] += jnp.sum(low.astype(single), axis=0, keepdims=True)
+
+    block = pl.BlockSpec((t, width), lambda i: (i, 0))
+    pltpu.emit_pipeline(
+        norm,
+        grid=(rows // t,),
+        in_specs=[block] * 5 + [pl.BlockSpec((1, width), lambda i: (0, 0))],
+        out_specs=[block] * 2 + [pl.BlockSpec((8, width), lambda i: (0, 0))],
+    )(own, land1, land2, cot, y1, gain, dy1, dz1, sums)
+    load.wait()
+    for mask in (3, 1, 2, 0):
+        of = partner(mask) if mask else lax.axis_index("ctx")
+        heads = w[pl.ds(pl.multiple_of(of * part, part), part), :]
+        stage[mask] = dot_nt(dz[...], heads).astype(half)
         at = got.at[pl.ds(mask * rows, rows)]
-        copies.append(moves.start(columns(partner(mask)), at, mask))
-    own = pltpu.make_async_copy(columns(c), got.at[pl.ds(0, rows)], local)
-    own.start()
+        if mask:
+            copies.append(moves.start(stage.at[mask], at, mask))
+        else:
+            keep = pltpu.make_async_copy(stage.at[0], at, local.at[1])
+            keep.start()
     outer_on([ob], [dz1], out_grad)
     multiply(
         [*halves(gb1), *halves(gb2)],
@@ -688,28 +717,39 @@
         mix,
         store_passed,
     )
-    own.wait()
+    keep.wait()
     for copy in copies:
         copy.wait()
 
 
-def heads_back(dattn, ob, dz1, gb1, gb2, w_down, mix_x, mix_y, part):
-    rows, width = dattn.shape
+def heads_back(terms, cot, y1, gain, w_out, ob, gb1, gb2, w_down, mix_first, down):
+    rows, width = cot.shape
+    part = width // 4
     anywhere = pl.BlockSpec(memory_space=pl.ANY)
-    sems = pltpu.SemaphoreType.DMA((3,))
-    outs = [((4 * rows, part), half), ((width, width), half)] + [((rows // 2, width), half)] * 4
-    return pl.pallas_call(
+    sems = pltpu.SemaphoreType.DMA((5,))
+    outs = [((rows, width), single), ((rows, width), half), ((8, width), single)]
+    outs += [((4 * rows, part), half), ((width, width), half)]
+    outs += [((rows // 2, width), half)] * 4 + [(down.shape, half)] * 2
+    out = pl.pallas_call(
         functools.partial(heads_back_kernel, part),
-        in_specs=[anywhere] * 8,
+        in_specs=[anywhere] * 14,
         out_specs=[anywhere] * len(outs),
         out_shape=[jax.ShapeDtypeStruct(shape, dtype) for shape, dtype in outs],
-        scratch_shapes=[sems, sems, pltpu.SemaphoreType.DMA],
+        scratch_shapes=[
+            pltpu.VMEM((rows, width), half),
+            pltpu.VMEM((width, width), half),
+            pltpu.VMEM((4, rows, part), half),
+            sems,
+            sems,
+            pltpu.SemaphoreType.DMA((2,)),
+        ],
         compiler_params=pltpu.CompilerParams(
-            collective_id=4, has_side_effects=True, vmem_limit_bytes=52 * 1024 * 1024
+            collective_id=4, has_side_effects=True, vmem_limit_bytes=56 * 1024 * 1024
         ),
         cost_estimate=hint(10 * rows * width * width, 0),
         name="heads_back",
-    )(dattn, ob, dz1, gb1, gb2, w_down, mix_x, mix_y)
+    )(*terms, cot, y1, gain.reshape(1, -1), w_out, ob, gb1, gb2, w_down, *mix_first, down)
+    return out[0], out[2], out[3], out[4], out[5:9], out[9:11]
 
 
 def qkv_back_kernel(*refs):
@@ -849,7 +889,12 @@
     )(x)
 
 
-def reduce_small_kernel(nf, nc, x_ref, o_ref, land, stage, send_sem, recv_sem):
+def reduce_small_kernel(nf, nc, moving, x_ref, *refs):
+    if moving:
+        piece, o_ref, one, two, far_lo, far_hi, land, stage, send_sem, recv_sem = refs[:10]
+        moves = Moves(refs[10], refs[11])
+    else:
+        o_ref, land, stage, send_sem, recv_sem = refs
     f = lax.axis_index("fsdp")
     c = lax.axis_index("ctx")
     barrier = pltpu.get_barrier_semaphore()
@@ -868,6 +913,11 @@
             device_id_type=pl.DeviceIdType.MESH,
         )
     pl.semaphore_wait(barrier, nf + nc - 2)
+    if moving:
+        lo, hi = halves(piece)
+        (one_lo, one_hi), (two_lo, two_hi) = halves(one), halves(two)
+        first = [moves.start(lo, one_lo, 1), moves.start(hi, two_hi, 2)]
+        rest = [moves.start(hi, one_hi, 1), moves.start(lo, two_lo, 2)]
     copies = []
     for d in range(1, nf):
         to = lax.rem(f + d, nf)
@@ -882,6 +932,10 @@
             )
         )
         copies[-1].start()
+    if moving:
+        for copy in first:
+            copy.wait()
+        rest += [moves.start(one_lo, far_lo, 2), moves.start(two_hi, far_hi, 1)]
     total = x_ref[f]
     for d in range(1, nf):
         copies[d - 1].wait()
@@ -904,25 +958,39 @@
         copies[d - 1].wait()
         total = total + stage[d]
     o_ref[...] = total
-
-
-def reduce_small(x, nf, nc, call):
+    if moving:
+        for copy in rest:
+            copy.wait()
+
+
+def reduce_small(x, nf, nc, call, piece=None):
     block = x.shape[1:]
     sems = pltpu.SemaphoreType.DMA((nf + nc,))
-    return pl.pallas_call(
-        functools.partial(reduce_small_kernel, nf, nc),
-        out_shape=jax.ShapeDtypeStruct(block, single),
-        in_specs=[pl.BlockSpec(memory_space=pltpu.VMEM)],
-        out_specs=pl.BlockSpec(memory_space=pltpu.VMEM),
-        scratch_shapes=[
-            pltpu.VMEM((nf,) + block, single),
-            pltpu.VMEM((nc,) + block, single),
-            sems,
-            sems,
-        ],
+    moving = piece is not None
+    vmem = pl.BlockSpec(memory_space=pltpu.VMEM)
+    anywhere = pl.BlockSpec(memory_space=pl.ANY)
+    outs = [jax.ShapeDtypeStruct(block, single)]
+    scratch = [
+        pltpu.VMEM((nf,) + block, single),
+        pltpu.VMEM((nc,) + block, single),
+        sems,
+        sems,
+    ]
+    if moving:
+        n = piece.shape[0] // 2
+        shapes = [piece.shape, piece.shape, (n, piece.shape[1]), (n, piece.shape[1])]
+        outs += [jax.ShapeDtypeStruct(shape, half) for shape in shapes]
+        scratch += [pltpu.SemaphoreType.DMA((6,))] * 2
+    out = pl.pallas_call(
+        functools.partial(reduce_small_kernel, nf, nc, moving),
+        out_shape=outs,
+        in_specs=[vmem] + [anywhere] * moving,
+        out_specs=[vmem] + [anywhere] * (len(outs) - 1),
+        scratch_shapes=scratch,
         compiler_params=pltpu.CompilerParams(collective_id=call, has_side_effects=True),
         name="reduce_small",
-    )(x)
+    )(x, *([piece] if moving else []))
+    return out[0], [[piece], [out[1]], [out[2]], [out[3], out[4]]] if moving else None
 
 
 def per_device(
@@ -1072,13 +1140,9 @@
 
     du, dh2, mix = [None] * CTX, [None] * CTX, [None] * CTX
     if CTX == 4:
-        du, dh2, (p1_hi, p2_lo), (x_lo, y_hi) = feed_back(flat(dz2), flat(slope), w_down, w_up)
-        x_hi, y_lo, up_grad = up_back(p1_hi, p2_lo, flat(a2), du)
-        mix_far = plain(after(gb[far], up_grad), w_down, False, half, "mix_far")
-        mix_first = swap(mix_far[0], 1), swap(mix_far[1], 2)
-        lows = total_of(dh2[:n], [x_lo, y_lo])
-        dh2 = jnp.concatenate([lows, total_of(dh2[n:], [x_hi, y_hi])], axis=0)
-        dh2 = after(dh2, mix_far)
+        du, dh2, up_grad, mix_first = feed_back(
+            flat(dz2), flat(slope), w_down, w_up, flat(a2), gb[far]
+        )
         du = [du]
     else:
         for j in range(CTX):
@@ -1092,32 +1156,36 @@
     up_part = scatter_f(up_grad)
     up_bias_grad = sum(jnp.sum(x.astype(single), axis=0) for x in flat(du))
     down_bias_grad = sum(jnp.sum(x.astype(single), axis=0) for x in dz2[0])
-    gain2_grad = jnp.sum(dh2 * normed2, axis=0)
-    shift2_grad = jnp.sum(dh2, axis=0)
-    dy1 = cotangent + norm_back(normed2, inv2, gain2, dh2)
-
-    dz1 = dy1.astype(half)
-    dattn = dot_nt(dz1, w_out).astype(half)
-    out_bias_grad = jnp.sum(dz1.astype(single), axis=0)
     if CTX == 4:
-        dattn, out_grad, one_lo, one_hi, two_lo, two_hi = heads_back(
-            dattn, ob, dz1, gb[1][0], gb[2][0], w_down, *mix_first, part
+        dy1, sums2, dattn, out_grad, mix, down_near = heads_back(
+            dh2, cotangent, y1, gain2, w_out, ob, gb[1][0], gb[2][0], w_down, mix_first, down_part
         )
+        one_lo, one_hi, two_lo, two_hi = mix
+        gain2_grad, shift2_grad, out_bias_grad = sums2[0], sums2[1], sums2[2]
     else:
+        gain2_grad = jnp.sum(dh2 * normed2, axis=0)
+        shift2_grad = jnp.sum(dh2, axis=0)
+        dy1 = cotangent + norm_back(normed2, inv2, gain2, dh2)
+        dz1 = dy1.astype(half)
+        dattn = dot_nt(dz1, w_out).astype(half)
+        out_bias_grad = jnp.sum(dz1.astype(single), axis=0)
         dattn = xor_order([dattn[:, s * part : (s + 1) * part] for s in range(CTX)], c)
         dattn = [dattn[0]] + [swap(dattn[j], j) for j in range(1, CTX)]
         dattn = jnp.concatenate(dattn, axis=0)
         out_grad = outer([ob], [dz1], "out_grad")
         for j in mid:
             mix[j] = plain(gb[j], w_down, False, half, f"mix_{j}")[0]
+        down_near = gather_first(down_part)
     out_part = scatter_f(out_grad)
-    down_own = after(down_part, dattn)
-    down_near = gather_first(down_own)
     dqkv = attn_backward(joined, dattn, inv, slopes, heads, scale)
     if CTX == 4:
         lows = [swap(one_lo, 1), swap(two_lo, 2)]
         dqkv = after(dqkv, lows, up_part)
-        dh1, arrived, qkv_grad, mix[0] = qkv_back(dqkv, w_qkv, a1, gb[0][0], w_down)
+        highs = [swap(one_hi, 1), swap(two_hi, 2)]
+        dh1, arrived, qkv_grad, mix_own = qkv_back(dqkv, w_qkv, a1, gb[0][0], w_down)
+        dh1 = after(dh1, highs)
+        mixed = y1 + bias_d + mix_own
+        mixed = jnp.concatenate([total_of(mixed[:n], lows), total_of(mixed[n:], highs)])
     else:
         dh1 = [
             plain([(dqkv, rows, j)], w_qkv, True, half if j else single, f"dh1_{j}")[0]
@@ -1126,20 +1194,12 @@
         arrived = scatter_send(dh1[1:])
         dh1 = dh1[0]
         qkv_grad = outer(a1, [(dqkv, rows, j) for j in range(CTX)], "qkv_grad")
-        mix[0] = plain(gb[0], w_down, False, single, "mix_0")[0]
-    dh1 = total_of(after(dh1, down_near), arrived)
-    down_out = gather_second(down_own, after(down_near, dh1))
-    mixed = y1 + bias_d + mix[0]
-    if CTX == 4:
-        one_hi, two_hi = after((one_hi, two_hi), dh1)
-        lows = total_of(mixed[:n], lows)
-        mixed = jnp.concatenate([lows, total_of(mixed[n:], [swap(one_hi, 1), swap(two_hi, 2)])])
-    else:
-        mixed = total_of(mixed, scatter_send(mix[1:]))
+        mix_own = plain(gb[0], w_down, False, single, "mix_0")[0]
+        mixed = total_of(y1 + bias_d + mix_own, scatter_send(mix[1:]))
+    dh1 = total_of(dh1, arrived)
+    down_out = gather_second(down_part, after(down_near, dh1))
     down_out = lay_out(0, down_out, c, width // min(width, 512))
-    up_out = gather_ctx(after(up_part, dh1))
-    out_part = after(out_part, up_out)
-    up_out = lay_out(1, up_out, c, nf)
+    up_out = lay_out(1, gather_ctx(after(up_part, dh1)), c, nf)
     sums = jnp.sum(dqkv.astype(single), axis=0)
     normed1_own, inv1_own = norm_parts(tokens.astype(single))
     gain1_grad = jnp.sum(dh1 * normed1_own, axis=0)
@@ -1153,7 +1213,6 @@
         out_part = out_part.astype(single) + swap(out_part, bit).astype(single)
         bit *= 2
     out_out = out_part
-    qkv_out = lay_out(1, gather_ctx(qkv_part), c, 3)
 
     def spread(x, inner):
         x = x.reshape(-1, 1, inner)
@@ -1164,17 +1223,19 @@
         sizes = [x.shape[0] // nf for x in items]
         x = jnp.concatenate([x.reshape(nf, -1) for x in items], axis=1)
         x = jnp.pad(x, ((0, 0), (0, -x.shape[1] % 1024))).reshape(nf, -1, 128)
-        x = reduce_small(x, nf, CTX, call).reshape(-1)
+        x, qkv_all = reduce_small(x, nf, CTX, call, qkv_part if CTX == 4 else None)
+        x = x.reshape(-1)
         out, at = [], 0
         for n in sizes:
             out.append(x[at : at + n])
             at += n
-        return out
+        return out, qkv_all
 
     sums_in = [out_bias_grad, gain2_grad, shift2_grad, down_bias_grad, spread(up_bias_grad, fpart)]
     gain1_grad = after(gain1_grad, qkv_part)
     sums_in += [gain1_grad, shift1_grad, spread(sums[:part], part), spread(sums[2 * part :], part)]
-    sums_out = reduced(sums_in, 2)
+    sums_out, qkv_all = reduced(sums_in, 2)
+    qkv_out = lay_out(1, qkv_all or gather_ctx(qkv_part), c, 3)
     out_bias_out, gain2_out, shift2_out, down_bias_out, up_bias_out = sums_out[:5]
     gain1_out, shift1_out, q_bias_out, v_bias_out = sums_out[5:]
     return (

time: 779 us -> 766 us (0.983)
  Pallas kernels: 411 us -> 459 us
  waiting for transfers between devices: 172 us -> 134 us
  starting transfers between devices: 39.8 us -> 31.1 us
    pallas_call x2, Pallas kernels: 81.9 us -> 142 us  [the longest x1 110 us: feed_back(): pl.pallas_call(feed_back_kernel, in_specs=[anywhere] * 22, out_specs=[any...]
    ppermute x35 -> x27, waiting for transfers between devices: 124 us -> 86.3 us  [swap(): return lax.ppermute(x, 'ctx', [(i, i ^ mask) for i in range(n)])]
    pallas_call x3 -> x2, Pallas kernels: 130 us -> 105 us  [moving_call(): pl.pallas_call(kernel, in_specs=[anywhere] * len(operands), out_specs=[an...]
    pallas_call x1, Pallas kernels: 27.9 us -> 49.9 us  [heads_back(): pl.pallas_call(functools.partial(heads_back_kernel, part), in_specs=[anyw...]
    pallas_call x5 -> x4, Pallas kernels: 62.7 us -> 53.8 us  [rows_matmul(): pl.pallas_call(functools.partial(rows_kernel, dot_nt if transposed else d...]
    ppermute x35 -> x27, starting transfers between devices: 39.5 us -> 30.8 us  [swap(): return lax.ppermute(x, 'ctx', [(i, i ^ mask) for i in range(n)])]
    unnamed x162 -> x165, local copies, waits for them, and re-layouts: 24.1 us -> 25.3 us
  transfers between devices with their start and end apart: 43 -> 35, of which waited for: 16 -> 12; matrix products, arithmetic and copies ran while one was open for 14% -> 13% of each run, Pallas kernels for 53% -> 56%
where the time goes in v1:
time: 766 us; the launch traced here: 756 us
  Pallas kernels  459 us (60%)
  waiting for transfers between devices  134 us (17%)
  other arithmetic  63.9 us (8%)
  local copies, waits for them, and re-layouts  45.7 us (6%)
  starting transfers between devices  31.1 us (4%)
  between operations  15.6 us (2%)
  matrix products  7.75 us (1%)
    pallas_call x1, Pallas kernels, feed_back(): pl.pallas_call(feed_back_kernel, in_specs=[anywhere] * 22, out_specs=[any...  110 us
    pallas_call x2, Pallas kernels, moving_call(): pl.pallas_call(kernel, in_specs=[anywhere] * len(operands), out_specs=[an...  105 us
    ppermute x27, waiting for transfers between devices, swap(): return lax.ppermute(x, 'ctx', [(i, i ^ mask) for i in range(n)])  86.3 us
    pallas_call x2, Pallas kernels, attn_call(): pl.pallas_call(kernel, grid_spec=pltpu.PrefetchScalarGridSpec(num_scalar_...  60.5 us
    pallas_call x4, Pallas kernels, rows_matmul(): pl.pallas_call(functools.partial(rows_kernel, dot_nt if transposed else d...  53.8 us
    pallas_call x1, Pallas kernels, heads_back(): pl.pallas_call(functools.partial(heads_back_kernel, part), in_specs=[anyw...  49.9 us
    all_gather x4, waiting for transfers between devices, gather_f(): return lax.all_gather(x, 'fsdp', axis=0, tiled=True)  47.2 us
    pallas_call x1, Pallas kernels, reduce_small(): pl.pallas_call(functools.partial(reduce_small_kernel, nf, nc, moving), ou...  31.6 us
  transfers between devices with their start and end apart: 35, of which 12 were waited for; matrix products, arithmetic and copies ran while one was open for 13% of the time, Pallas kernels for 56%

profile of v1, /device:TPU:0, one launch (start us, length us, event | category | flops | bytes accessed | tf_op | source)
XLA Modules:
  0.0 756.2 jit_solution(12719810543279104347)
XLA Ops:
  18.1 9.0 %gather_small.1 = f32[8,24,128]{2,1,0:T(8,128)} custom-call(f32[24,128]{1,0:T(8,128)} %bitcast.93), custom_call_target="tpu_custom_call" | custom-call | tf_op jit(solution)/shard_map/gather_small/pallas_call | solution.py:881
  37.9 23.6 %collective-permute-done = bf16[512,2048]{1,0:T(8,128)(2,1)} collective-permute-done((bf16[512,2048]{1,0:T(8,128)(2,1)S(1)}, bf16[512,2048]{1,0:T(8,128)(2,1)}, u32[]{:S(2)}, u32[]{:S(2)}) %collective-permute-start) | collective-permute-done | bytes 2097184 | tf_op jit(solution)/shard_map/ppermute | solution.py:60
  75.3 5.8 fusion.21
  81.0 8.5 %collective-permute-done.3.refs_1_ = bf16[256,2048]{1,0:T(8,128)(2,1)} collective-permute-done((bf16[256,2048]{1,0:T(8,128)(2,1)S(1)}, bf16[256,2048]{1,0:T(8,128)(2,1)}, u32[]{:S(2)}, u32[]{:S(2)}) %collective-permute-start.3) | collective-permute-done | bytes 1048608 | tf_op jit(solution)/shard_map/ppermute | solution.py:60
  98.2 28.8 %qkv.1 = (bf16[2048,1536]{1,0:T(8,128)(2,1)}, bf16[256,2048]{1,0:T(8,128)(2,1)S(1)}, bf16[256,2048]{1,0:T(8,128)(2,1)}, bf16[256,2048]{1,0:T(8,128)(2,1)}, bf16[256,2048]{1,0:T(8,128)(2,1)}) custom-call(bf16[256,2048]{1,0:T(8,128)(2,1)} %collective-permute-done.2.refs_0_, bf16[256,2048]{1,0:T(8,128)(2,1)} %collective-permute-done.3.refs_1_, ...), custom_call_target="tpu_custom_call" | custom-call | flops 12884901 | tf_op jit(solution)/shard_map/qkv/pallas_call | solution.py:499
  130.1 24.3 %attn_forward.1 = bf16[2048,512]{1,0:T(8,128)(2,1)S(1)} custom-call(s32[16]{0:T(128)S(1)} %select_reduce_fusion.inv_ref, f32[4]{0:T(128)S(1)} %multiply_power_fusion.slope_ref, ...), custom_call_target="tpu_custom_call" | custom-call | flops 20000000 | bytes 8388 | tf_op jit(solution)/shard_map/attn_forward/pallas_call | solution.py:233
  161.3 12.5 %collective-permute-done.6 = bf16[512,512]{1,0:T(8,128)(2,1)S(1)} collective-permute-done((bf16[512,512]{1,0:T(8,128)(2,1)}, bf16[512,512]{1,0:T(8,128)(2,1)S(1)}, u32[]{:S(2)}, u32[]{:S(2)}) %collective-permute-start.6) | collective-permute-done | bytes 524320 | tf_op jit(solution)/shard_map/ppermute | solution.py:60
  173.8 7.0 collective-permute-done.7
  184.4 7.8 %fusion.43 = (f32[512]{0:T(512)S(1)}, f32[512,2048]{1,0:T(8,128)S(1)}) fusion(f32[2048]{0:T(1024)S(1)} %bitcast.96, bf16[2048,2048]{1,0:T(8,128)(2,1)} %all-gather.7.cloned.1.call-done.refs_6_, bf16[512,512]{1,0:T(8,128)(2,1)} %get-tuple-element.189, bf16[512,512]{1,0:T(8,128)(2,1)} %get-tuple-element.188, bf16[512,512]{1,0:T(8,128)(2,1)S(1)} %get-tuple-element.187, ...), kind=kOutput, calls=%fused_computation.158 | convolution fusion | flops 4307549696 | bytes 16787456 | tf_op jit(solution)/shard_map/dot_general | solution.py:24
  197.0 47.2 %all-gather.9.cloned.1.call-done.refs_1_.refs_2_.refs_14_ = bf16[2048,2048]{1,0:T(8,128)(2,1)} async-done(((bf16[256,2048]{1,0:T(8,128)(2,1)}), bf16[2048,2048]{1,0:T(8,128)(2,1)}) %all-gather.9.cloned.1.call-update) | async-done | bytes 8388624 | tf_op jit(solution)/shard_map/all_gather | solution.py:1044
  244.2 11.0 %up_gelu_0.1 = (bf16[512,2048]{1,0:T(8,128)(2,1)}, bf16[512,2048]{1,0:T(8,128)(2,1)}) custom-call(bf16[512,2048]{1,0:T(8,128)(2,1)} %add_convert_fusion.refs_0_.refs_15_, bf16[2048,2048]{1,0:T(8,128)(2,1)} %all-gather.9.cloned.1.call-done.refs_1_.refs_2_.refs_14_, f32[1,2048]{1,0:T(1,128)S(1)} %bitcast.71), custom_call_target="tpu_custom_call" | custom-call | flops 4294967 | bytes 16777 | tf_op jit(solution)/shard_map/up_gelu_0/pallas_call | solution.py:311
  263.3 10.9 %up_gelu_1.1 = (bf16[512,2048]{1,0:T(8,128)(2,1)}, bf16[512,2048]{1,0:T(8,128)(2,1)}) custom-call(bf16[512,2048]{1,0:T(8,128)(2,1)} %collective-permute-done.11.refs_0_.refs_16_, bf16[2048,2048]{1,0:T(8,128)(2,1)} %all-gather.9.cloned.1.call-done.refs_1_.refs_2_.refs_14_, f32[1,2048]{1,0:T(1,128)S(1)} %bitcast.72), custom_call_target="tpu_custom_call" | custom-call | flops 4294967 | bytes 16777 | tf_op jit(solution)/shard_map/up_gelu_1/pallas_call | solution.py:311
  274.2 10.9 %up_gelu_2.1 = (bf16[512,2048]{1,0:T(8,128)(2,1)}, bf16[512,2048]{1,0:T(8,128)(2,1)}) custom-call(bf16[512,2048]{1,0:T(8,128)(2,1)} %copy-done.21, bf16[2048,2048]{1,0:T(8,128)(2,1)} %all-gather.9.cloned.1.call-done.refs_1_.refs_2_.refs_14_, f32[1,2048]{1,0:T(1,128)S(1)} %bitcast.73), custom_call_target="tpu_custom_call" | custom-call | flops 4294967 | bytes 16777 | tf_op jit(solution)/shard_map/up_gelu_2/pallas_call | solution.py:311
  286.4 21.0 %up_gelu_3.1 = (bf16[256,2048]{1,0:T(8,128)(2,1)S(1)}, bf16[256,2048]{1,0:T(8,128)(2,1)}, bf16[256,2048]{1,0:T(8,128)(2,1)}, bf16[256,2048]{1,0:T(8,128)(2,1)}) custom-call(bf16[256,2048]{1,0:T(8,128)(2,1)} %copy-done.27, bf16[256,2048]{1,0:T(8,128)(2,1)} %copy-done.26, bf16[2048,2048]{1,0:T(8,128)(2,1)} %all-gather.9.cloned.1.call-done.refs_1_.refs_2_.refs_14_, ...), custom_call_target="tpu_custom_call" | custom-call | flops 4294967 | bytes 16777 | tf_op jit(solution)/shard_map/up_gelu_3/pallas_call | solution.py:311
  308.9 23.2 %down_grad.1 = bf16[2048,2048]{1,0:T(8,128)(2,1)} custom-call(bf16[512,2048]{1,0:T(8,128)(2,1)} %get-tuple-element.114.refs_0_.refs_1_.refs_7_, bf16[512,2048]{1,0:T(8,128)(2,1)} %get-tuple-element.114.refs_0_.refs_1_.refs_7_, bf16[512,2048]{1,0:T(8,128)(2,1)} %get-tuple-element.119.refs_2_.refs_3_.refs_8_, ...), custom_call_target="tpu_custom_call" | custom-call | flops 17179868 | bytes 25165 | tf_op jit(solution)/shard_map/down_grad/pallas_call | solution.py:384
  332.2 110.0 %feed_back.1 = (bf16[512,2048]{1,0:T(8,128)(2,1)}, bf16[512,2048]{1,0:T(8,128)(2,1)}, bf16[512,2048]{1,0:T(8,128)(2,1)}, bf16[256,2048]{1,0:T(8,128)(2,1)}, bf16...) custom-call(bf16[256,2048]{1,0:T(8,128)(2,1)} %get-tuple-element.103, ...), custom_call_target="tpu_custom_call" | custom-call | flops 55834576 | tf_op jit(solution)/shard_map/feed_back/pallas_call | solution.py:642
  442.9 49.9 %heads_back.1 = (f32[512,2048]{1,0:T(8,128)}, bf16[512,2048]{1,0:T(8,128)(2,1)}, f32[8,2048]{1,0:T(8,128)}, bf16[2048,512]{1,0:T(8,128)(2,1)}, bf16[2048,2048]{1...) custom-call(f32[512,2048]{1,0:T(8,128)} %get-tuple-element.131.refs_, ...), custom_call_target="tpu_custom_call" | custom-call | flops 21474836 | tf_op jit(solution)/shard_map/heads_back/pallas_call | solution.py:733
  497.0 36.2 %attn_backward.1.refs_0_ = bf16[2048,1536]{1,0:T(8,128)(2,1)} custom-call(s32[16]{0:T(128)S(1)} %select_reduce_fusion.inv_ref, f32[4]{0:T(128)S(1)} %multiply_power_fusion.slope_ref, ...), custom_call_target="tpu_custom_call" | custom-call | flops 40000000 | bytes 14680 | tf_op jit(solution)/shard_map/attn_backward/pallas_call | solution.py:233
  533.3 76.6 %qkv_back.1 = (f32[512,2048]{1,0:T(8,128)}, bf16[512,2048]{1,0:T(8,128)(2,1)}, bf16[512,2048]{1,0:T(8,128)(2,1)}, bf16[512,2048]{1,0:T(8,128)(2,1)}, bf16[256,20...) custom-call(bf16[2048,1536]{1,0:T(8,128)(2,1)} %attn_backward.1.refs, ...), custom_call_target="tpu_custom_call" | custom-call | flops 30064772 | tf_op jit(solution)/shard_map/qkv_back/pallas_call | solution.py:499
  610.0 5.5 fusion.16
  615.6 3.0 fusion.15
  635.2 4.5 add_add_fusion
  639.7 14.9 %collective-permute-done.19 = bf16[256,2048]{1,0:T(8,128)(2,1)S(1)} collective-permute-done((bf16[256,2048]{1,0:T(8,128)(2,1)}, bf16[256,2048]{1,0:T(8,128)(2,1)S(1)}, u32[]{:S(2)}, u32[]{:S(2)}) %collective-permute-start.19) | collective-permute-done | bytes 1048608 | tf_op jit(solution)/shard_map/ppermute | solution.py:60
  657.2 4.8 fusion.28
  664.6 12.5 %collective-permute-done.21.refs_1_ = bf16[256,2048]{1,0:T(8,128)(2,1)S(1)} collective-permute-done((bf16[256,2048]{1,0:T(8,128)(2,1)}, bf16[256,2048]{1,0:T(8,128)(2,1)S(1)}, u32[]{:S(2)}, u32[]{:S(2)}) %collective-permute-start.21) | collective-permute-done | bytes 1048608 | tf_op jit(solution)/shard_map/ppermute | solution.py:60
  680.1 4.8 pad_maximum_fusion
  684.9 3.6 collective-permute-done.26.refs_4_
  688.5 5.4 lay_out.5
  695.8 6.6 lay_out.4
  702.4 3.2 convert_add_fusion.2
  706.4 31.6 %reduce_small.1 = (f32[24,128]{1,0:T(8,128)}, bf16[256,1536]{1,0:T(8,128)(2,1)}, bf16[256,1536]{1,0:T(8,128)(2,1)}, bf16[128,1536]{1,0:T(8,128)(2,1)}, bf16[128,1536]{1,0:T(8,128)(2,1)}) custom-call(f32[8,24,128]{2,1,0:T(8,128)} %bitcast.81, bf16[256,1536]{1,0:T(8,128)(2,1)} %reduce-scatter.9.cloned.1.call-done.refs_0_), custom_call_target="tpu_custom_call" | custom-call | tf_op jit(solution)/shard_map/reduce_small/pallas_call | solution.py:984
  746.1 3.1 lay_out.3
  (321 shorter events, 112.9 us)
Async XLA Ops:
  7.3 90.9 %all-gather.5.cloned.1.call-start = ((), (), s32[]{:S(2)}) async-start(), calls=%async_computation.4 | async-start | bytes 7077888 | tf_op jit(solution)/shard_map/all_gather | solution.py:1044
  9.9 174.4 %all-gather.7.cloned.1.call-start = ((), (), s32[]{:S(2)}) async-start(), calls=%async_computation.5 | async-start | bytes 9437184 | tf_op jit(solution)/shard_map/all_gather | solution.py:1044
  12.7 231.5 %all-gather.9.cloned.1.call-start = ((), (), s32[]{:S(2)}) async-start(), calls=%async_computation.6 | async-start | bytes 9437184 | tf_op jit(solution)/shard_map/all_gather | solution.py:1044
  12.7 48.7 %collective-permute-start = (bf16[512,2048]{1,0:T(8,128)(2,1)S(1)}, bf16[512,2048]{1,0:T(8,128)(2,1)}, u32[]{:S(2)}, u32[]{:S(2)}) collective-permute-start(bf16[512,2048]{1,0:T(8,128)(2,1)S(1)} %copy-done.15), channel_id=1, source_target_pairs={{0,8},{8,0},{16,24},{24,16},{1,9},{9,1},{17,25},{25,17},{2,10},{10... | collective-permute-start | bytes 6291464 | tf_op jit(solution)/shard_map/ppermute | solution.py:60
  15.7 47.2 %collective-permute-start.1 = (bf16[512,2048]{1,0:T(8,128)(2,1)S(1)}, bf16[512,2048]{1,0:T(8,128)(2,1)}, u32[]{:S(2)}, u32[]{:S(2)}) collective-permute-start(bf16[512,2048]{1,0:T(8,128)(2,1)S(1)} %copy-done.15), channel_id=1, source_target_pairs={{0,16},{8,24},{16,0},{24,8},{1,17},{9,25},{17,1},{25,9},{2,18},{10... | collective-permute-start | bytes 6291464 | tf_op jit(solution)/shard_map/ppermute | solution.py:60
  65.6 23.9 %collective-permute-start.3 = (bf16[256,2048]{1,0:T(8,128)(2,1)S(1)}, bf16[256,2048]{1,0:T(8,128)(2,1)}, u32[]{:S(2)}, u32[]{:S(2)}) collective-permute-start(bf16[256,2048]{1,0:T(8,128)(2,1)S(1)} %slice.163), channel_id=1, source_target_pairs={{0,8},{8,0},{16,24},{24,16},{1,9},{9,1},{17,25},{25,17},{2,10},{10... | collective-permute-start | bytes 3145736 | tf_op jit(solution)/shard_map/ppermute | solution.py:60
  66.0 23.9 %collective-permute-start.2 = (bf16[256,2048]{1,0:T(8,128)(2,1)S(1)}, bf16[256,2048]{1,0:T(8,128)(2,1)}, u32[]{:S(2)}, u32[]{:S(2)}) collective-permute-start(bf16[256,2048]{1,0:T(8,128)(2,1)S(1)} %slice.162), channel_id=1, source_target_pairs={{0,16},{8,24},{16,0},{24,8},{1,17},{9,25},{17,1},{25,9},{2,18},{10... | collective-permute-start | bytes 3145736 | tf_op jit(solution)/shard_map/ppermute | solution.py:60
  89.9 242.3 %all-gather.11.cloned.1.call-start = ((), (), s32[]{:S(2)}) async-start(), calls=%async_computation.7 | async-start | bytes 9437184 | tf_op jit(solution)/shard_map/all_gather | solution.py:1044
  128.0 314.9 %reduce-scatter.5.cloned.1.call-start = ((), (), s32[]{:S(2)}) async-start(), calls=%async_computation.8 | async-start | bytes 9437184 | tf_op jit(solution)/shard_map/reduce_scatter | solution.py:1079
  128.0 27.8 %collective-permute-start.4 = (bf16[256,2048]{1,0:T(8,128)(2,1)S(1)}, bf16[256,2048]{1,0:T(8,128)(2,1)S(1)}, u32[]{:S(2)}, u32[]{:S(2)}) collective-permute-start(bf16[256,2048]{1,0:T(8,128)(2,1)S(1)} %copy-done.20), channel_id=1, source_target_pairs={{0,8},{8,0},{16,24},{24,16},{1,9},{9,1},{17,25},{25,17},{2,10},{10... | collective-permute-start | bytes 3145736 | tf_op jit(solution)/shard_map/ppermute | solution.py:60
  129.5 27.3 %collective-permute-start.5 = (bf16[256,2048]{1,0:T(8,128)(2,1)}, bf16[256,2048]{1,0:T(8,128)(2,1)S(1)}, u32[]{:S(2)}, u32[]{:S(2)}) collective-permute-start(bf16[256,2048]{1,0:T(8,128)(2,1)} %get-tuple-element.103.refs_9_.refs_8_.refs_0_), channel_id=1, source_target_pairs={{0,16},{8,24},{16,0},{24,8},{1,17},{9,25},{17,1},{25,9},{2,18},{10... | collective-permute-start | bytes 3145736 | tf_op jit(solution)/shard_map/ppermute | solution.py:60
  159.3 21.5 %collective-permute-start.7 = (bf16[512,512]{1,0:T(8,128)(2,1)}, bf16[512,512]{1,0:T(8,128)(2,1)S(1)}, u32[]{:S(2)}, u32[]{:S(2)}) collective-permute-start(bf16[512,512]{1,0:T(8,128)(2,1)} %get-tuple-element.105), channel_id=1, source_target_pairs={{0,16},{8,24},{16,0},{24,8},{1,17},{9,25},{17,1},{25,9},{2,18},{10... | collective-permute-start | bytes 1572872 | tf_op jit(solution)/shard_map/ppermute | solution.py:60
  194.8 60.4 %collective-permute-start.12 = (bf16[512,2048]{1,0:T(8,128)(2,1)}, bf16[512,2048]{1,0:T(8,128)(2,1)S(1)}, u32[]{:S(2)}, u32[]{:S(2)}) collective-permute-start(bf16[512,2048]{1,0:T(8,128)(2,1)} %add_convert_fusion.refs_0_.refs_15_), channel_id=1, source_target_pairs={{0,16},{8,24},{16,0},{24,8},{1,17},{9,25},{17,1},{25,9},{2,18},{10... | collective-permute-start | bytes 6291464 | tf_op jit(solution)/shard_map/ppermute | solution.py:60
  196.3 59.0 %collective-permute-start.11 = (bf16[512,2048]{1,0:T(8,128)(2,1)}, bf16[512,2048]{1,0:T(8,128)(2,1)}, u32[]{:S(2)}, u32[]{:S(2)}) collective-permute-start(bf16[512,2048]{1,0:T(8,128)(2,1)} %add_convert_fusion.refs_0_.refs_15_), channel_id=1, source_target_pairs={{0,8},{8,0},{16,24},{24,16},{1,9},{9,1},{17,25},{25,17},{2,10},{10... | collective-permute-start | bytes 6291464 | tf_op jit(solution)/shard_map/ppermute | solution.py:60
  257.5 27.6 %collective-permute-start.14 = (bf16[256,2048]{1,0:T(8,128)(2,1)S(1)}, bf16[256,2048]{1,0:T(8,128)(2,1)S(1)}, u32[]{:S(2)}, u32[]{:S(2)}) collective-permute-start(bf16[256,2048]{1,0:T(8,128)(2,1)S(1)} %slice.180), channel_id=1, source_target_pairs={{0,8},{8,0},{16,24},{24,16},{1,9},{9,1},{17,25},{25,17},{2,10},{10... | collective-permute-start | bytes 3145736 | tf_op jit(solution)/shard_map/ppermute | solution.py:60
  259.0 26.1 %collective-permute-start.13 = (bf16[256,2048]{1,0:T(8,128)(2,1)S(1)}, bf16[256,2048]{1,0:T(8,128)(2,1)S(1)}, u32[]{:S(2)}, u32[]{:S(2)}) collective-permute-start(bf16[256,2048]{1,0:T(8,128)(2,1)S(1)} %slice.179), channel_id=1, source_target_pairs={{0,16},{8,24},{16,0},{24,8},{1,17},{9,25},{17,1},{25,9},{2,18},{10... | collective-permute-start | bytes 3145736 | tf_op jit(solution)/shard_map/ppermute | solution.py:60
  262.2 45.3 %collective-permute-start.9 = (bf16[256,2048]{1,0:T(8,128)(2,1)S(1)}, bf16[256,2048]{1,0:T(8,128)(2,1)S(1)}, u32[]{:S(2)}, u32[]{:S(2)}) collective-permute-start(bf16[256,2048]{1,0:T(8,128)(2,1)S(1)} %copy-done.22), channel_id=1, source_target_pairs={{0,16},{8,24},{16,0},{24,8},{1,17},{9,25},{17,1},{25,9},{2,18},{10... | collective-permute-start | bytes 3145736 | tf_op jit(solution)/shard_map/ppermute | solution.py:60
  262.7 44.7 %collective-permute-start.10 = (bf16[256,2048]{1,0:T(8,128)(2,1)S(1)}, bf16[256,2048]{1,0:T(8,128)(2,1)S(1)}, u32[]{:S(2)}, u32[]{:S(2)}) collective-permute-start(bf16[256,2048]{1,0:T(8,128)(2,1)S(1)} %copy-done.23), channel_id=1, source_target_pairs={{0,8},{8,0},{16,24},{24,16},{1,9},{9,1},{17,25},{25,17},{2,10},{10... | collective-permute-start | bytes 3145736 | tf_op jit(solution)/shard_map/ppermute | solution.py:60
  332.2 201.1 %reduce-scatter.7.cloned.1.call-start = ((), (), s32[]{:S(2)}) async-start(), calls=%async_computation.9 | async-start | bytes 9437184 | tf_op jit(solution)/shard_map/reduce_scatter | solution.py:1079
  442.2 186.0 %reduce-scatter.11.cloned.1.call-start = ((), (), s32[]{:S(2)}) async-start(), calls=%async_computation.11 | async-start | bytes 9437184 | tf_op jit(solution)/shard_map/reduce_scatter | solution.py:1079
  492.8 212.8 %reduce-scatter.9.cloned.1.call-start = ((), (), s32[]{:S(2)}) async-start(), calls=%async_computation.10 | async-start | bytes 7077888 | tf_op jit(solution)/shard_map/reduce_scatter | solution.py:1079
  492.9 40.3 %collective-permute-start.15 = (bf16[256,2048]{1,0:T(8,128)(2,1)}, bf16[256,2048]{1,0:T(8,128)(2,1)}, u32[]{:S(2)}, u32[]{:S(2)}) collective-permute-start(bf16[256,2048]{1,0:T(8,128)(2,1)} %get-tuple-element.137), channel_id=1, source_target_pairs={{0,8},{8,0},{16,24},{24,16},{1,9},{9,1},{17,25},{25,17},{2,10},{10... | collective-permute-start | bytes 3145736 | tf_op jit(solution)/shard_map/ppermute | solution.py:60
  493.4 39.8 %collective-permute-start.16 = (bf16[256,2048]{1,0:T(8,128)(2,1)}, bf16[256,2048]{1,0:T(8,128)(2,1)}, u32[]{:S(2)}, u32[]{:S(2)}) collective-permute-start(bf16[256,2048]{1,0:T(8,128)(2,1)} %get-tuple-element.138), channel_id=1, source_target_pairs={{0,16},{8,24},{16,0},{24,8},{1,17},{9,25},{17,1},{25,9},{2,18},{10... | collective-permute-start | bytes 3145736 | tf_op jit(solution)/shard_map/ppermute | solution.py:60
  494.8 115.1 %collective-permute-start.17 = (bf16[256,2048]{1,0:T(8,128)(2,1)}, bf16[256,2048]{1,0:T(8,128)(2,1)S(1)}, u32[]{:S(2)}, u32[]{:S(2)}) collective-permute-start(bf16[256,2048]{1,0:T(8,128)(2,1)} %get-tuple-element.144), channel_id=1, source_target_pairs={{0,8},{8,0},{16,24},{24,16},{1,9},{9,1},{17,25},{25,17},{2,10},{10... | collective-permute-start | bytes 3145736 | tf_op jit(solution)/shard_map/ppermute | solution.py:60
  495.5 114.5 %collective-permute-start.18 = (bf16[256,2048]{1,0:T(8,128)(2,1)}, bf16[256,2048]{1,0:T(8,128)(2,1)}, u32[]{:S(2)}, u32[]{:S(2)}) collective-permute-start(bf16[256,2048]{1,0:T(8,128)(2,1)} %get-tuple-element.145), channel_id=1, source_target_pairs={{0,16},{8,24},{16,0},{24,8},{1,17},{9,25},{17,1},{25,9},{2,18},{10... | collective-permute-start | bytes 3145736 | tf_op jit(solution)/shard_map/ppermute | solution.py:60
  628.3 26.4 %collective-permute-start.19 = (bf16[256,2048]{1,0:T(8,128)(2,1)}, bf16[256,2048]{1,0:T(8,128)(2,1)S(1)}, u32[]{:S(2)}, u32[]{:S(2)}) collective-permute-start(bf16[256,2048]{1,0:T(8,128)(2,1)} %reduce-scatter.11.cloned.1.call-done), channel_id=1, source_target_pairs={{0,8},{8,0},{16,24},{24,16},{1,9},{9,1},{17,25},{25,17},{2,10},{10... | collective-permute-start | bytes 3145736 | tf_op jit(solution)/shard_map/ppermute | solution.py:60
  629.4 33.5 %collective-permute-start.22 = (bf16[256,2048]{1,0:T(8,128)(2,1)}, bf16[256,2048]{1,0:T(8,128)(2,1)S(1)}, u32[]{:S(2)}, u32[]{:S(2)}) collective-permute-start(bf16[256,2048]{1,0:T(8,128)(2,1)} %reduce-scatter.7.cloned.1.call-done.refs_0_), channel_id=1, source_target_pairs={{0,16},{8,24},{16,0},{24,8},{1,17},{9,25},{17,1},{25,9},{2,18},{10... | collective-permute-start | bytes 3145736 | tf_op jit(solution)/shard_map/ppermute | solution.py:60
  630.1 47.0 %collective-permute-start.21 = (bf16[256,2048]{1,0:T(8,128)(2,1)}, bf16[256,2048]{1,0:T(8,128)(2,1)S(1)}, u32[]{:S(2)}, u32[]{:S(2)}) collective-permute-start(bf16[256,2048]{1,0:T(8,128)(2,1)} %reduce-scatter.7.cloned.1.call-done.refs_0_), channel_id=1, source_target_pairs={{0,8},{8,0},{16,24},{24,16},{1,9},{9,1},{17,25},{25,17},{2,10},{10... | collective-permute-start | bytes 3145736 | tf_op jit(solution)/shard_map/ppermute | solution.py:60
  633.2 55.3 %collective-permute-start.26 = (bf16[128,2048]{1,0:T(8,128)(2,1)}, bf16[128,2048]{1,0:T(8,128)(2,1)}, u32[]{:S(2)}, u32[]{:S(2)}) collective-permute-start(bf16[128,2048]{1,0:T(8,128)(2,1)} %slice.209), channel_id=1, source_target_pairs={{0,8},{8,0},{16,24},{24,16},{1,9},{9,1},{17,25},{25,17},{2,10},{10... | collective-permute-start | bytes 1572872 | tf_op jit(solution)/shard_map/ppermute | solution.py:60
  633.8 54.7 %collective-permute-start.25 = (bf16[128,2048]{1,0:T(8,128)(2,1)}, bf16[128,2048]{1,0:T(8,128)(2,1)}, u32[]{:S(2)}, u32[]{:S(2)}) collective-permute-start(bf16[128,2048]{1,0:T(8,128)(2,1)} %slice.208), channel_id=1, source_target_pairs={{0,16},{8,24},{16,0},{24,8},{1,17},{9,25},{17,1},{25,9},{2,18},{10... | collective-permute-start | bytes 1572872 | tf_op jit(solution)/shard_map/ppermute | solution.py:60
  656.1 46.3 %collective-permute-start.20 = (bf16[256,2048]{1,0:T(8,128)(2,1)}, bf16[256,2048]{1,0:T(8,128)(2,1)}, u32[]{:S(2)}, u32[]{:S(2)}) collective-permute-start(bf16[256,2048]{1,0:T(8,128)(2,1)} %add_convert_fusion.1), channel_id=1, source_target_pairs={{0,16},{8,24},{16,0},{24,8},{1,17},{9,25},{17,1},{25,9},{2,18},{10... | collective-permute-start | bytes 3145736 | tf_op jit(solution)/shard_map/ppermute | solution.py:60
  663.8 30.5 %collective-permute-start.24 = (bf16[128,2048]{1,0:T(8,128)(2,1)}, bf16[128,2048]{1,0:T(8,128)(2,1)}, u32[]{:S(2)}, u32[]{:S(2)}) collective-permute-start(bf16[128,2048]{1,0:T(8,128)(2,1)} %slice.232), channel_id=1, source_target_pairs={{0,8},{8,0},{16,24},{24,16},{1,9},{9,1},{17,25},{25,17},{2,10},{10... | collective-permute-start | bytes 1572872 | tf_op jit(solution)/shard_map/ppermute | solution.py:60
  (68 other events, 922.7 us)
Sparse Core Ops, SparseCore 0:
  10.3 68.1 all-gather.4
  80.7 80.6 all-gather.6
  163.6 80.5 all-gather.8
  245.6 80.6 all-gather.10
  332.3 88.0 reduce-scatter.4
  442.4 86.8 reduce-scatter.6
  531.5 87.9 reduce-scatter.10
  621.8 68.1 reduce-scatter.8

commit v2 on v1

--- a/solution.py
+++ b/solution.py
@@ -586,42 +586,42 @@
     dz, slope, (w_down, w_up) = refs[0:8], refs[8:13], refs[13:15]
     a2, gb_far = refs[15:20], refs[20:22]
     du, own, land1, land2, up_grad, mix_x, mix_y = refs[22:27], *refs[27:33]
-    total, far, near, rest, from_x, from_y = refs[33:39]
-    moves = Moves(*refs[39:41])
-    local = refs[41]
+    total, far, near, rest, from_x, from_y, mixed = refs[33:40]
+    moves = Moves(*refs[40:42])
+    local = refs[42]
     n = from_x.shape[0]
     lo, hi = pl.ds(0, n), pl.ds(n, n)
     (s1_lo, s1_hi), (s2_lo, s2_hi) = halves(slope[1]), halves(slope[2])
     (d1_lo, d1_hi), (d2_lo, d2_hi) = halves(du[1]), halves(du[2])
     (land1_lo, land1_hi), (land2_lo, land2_hi) = halves(land1), halves(land2)
     greet((1, 2))
+    wide, width = w_down.shape
+    t = math.gcd(width, 512)
+
+    def mix(x_lo, x_hi, w):
+        at = pl.ds(pl.multiple_of(pl.program_id(0) * t, t), t)
+        mixed[0:n, at] = dot_nn(x_lo[...], w[...]).astype(half)
+        mixed[n : 2 * n, at] = dot_nn(x_hi[...], w[...]).astype(half)
+
+    pltpu.emit_pipeline(
+        mix,
+        grid=(width // t,),
+        in_specs=[pl.BlockSpec((n, wide), lambda i: (0, 0))] * 2
+        + [pl.BlockSpec((wide, t), lambda i: (0, i))],
+    )(*gb_far, w_down)
+    second = [moves.start(mixed.at[lo], mix_x, 1), moves.start(mixed.at[hi], mix_y, 2)]
     feed_pass(dz[6:8], slope[3:5], w_down, w_up, du[3:5], total)
     far[...] = total[...].astype(half)
     first = [moves.start(far.at[lo], from_x, 1), moves.start(far.at[hi], from_y, 2)]
     feed_pass([dz[2], dz[5]], [s1_lo, s2_hi], w_down, w_up, [d1_lo, d2_hi], total)
     near[...] = total[...].astype(half)
-    second = [moves.start(near.at[lo], land1_lo, 1), moves.start(near.at[hi], land2_hi, 2)]
+    second += [moves.start(near.at[lo], land1_lo, 1), moves.start(near.at[hi], land2_hi, 2)]
     feed_pass([dz[3], dz[4]], [s1_hi, s2_lo], w_down, w_up, [d1_hi, d2_lo], total)
     for copy in first:
         copy.wait()
     rest[lo] = (total[lo] + from_y[...].astype(single)).astype(half)
     rest[hi] = (total[hi] + from_x[...].astype(single)).astype(half)
     second += [moves.start(rest.at[lo], land1_hi, 1), moves.start(rest.at[hi], land2_lo, 2)]
-    wide, width = w_down.shape
-    t = math.gcd(width, 512)
-
-    def mix(x_lo, x_hi, w):
-        at = pl.ds(pl.multiple_of(pl.program_id(0) * t, t), t)
-        far[0:n, at] = dot_nn(x_lo[...], w[...]).astype(half)
-        far[n : 2 * n, at] = dot_nn(x_hi[...], w[...]).astype(half)
-
-    pltpu.emit_pipeline(
-        mix,
-        grid=(width // t,),
-        in_specs=[pl.BlockSpec((n, wide), lambda i: (0, 0))] * 2
-        + [pl.BlockSpec((wide, t), lambda i: (0, i))],
-    )(*gb_far, w_down)
-    second += [moves.start(far.at[lo], mix_x, 1), moves.start(far.at[hi], mix_y, 2)]
     feed_pass(dz[0:2], halves(slope[0]), w_down, w_up, halves(du[0]), total)
     store_own = pltpu.make_async_copy(total, own, local)
     store_own.start()
@@ -647,6 +647,7 @@
         scratch_shapes=[pltpu.VMEM((rows, width), single)]
         + [pltpu.VMEM((rows, width), half)] * 3
         + [pltpu.VMEM((n, width), half)] * 2
+        + [pltpu.VMEM((rows, width), half)]
         + [sems, sems, pltpu.SemaphoreType.DMA],
         compiler_params=pltpu.CompilerParams(
             collective_id=3, has_side_effects=True, vmem_limit_bytes=56 * 1024 * 1024
@@ -754,9 +755,10 @@
 
 def qkv_back_kernel(*refs):
     dqkv, w_qkv = refs[0:2]
-    a1, gb_own, w_down = refs[2:7], refs[7], refs[8]
-    own, p3, p1, p2, from_x, from_y, land1, land2, qkv_grad, mix_own = refs[9:19]
-    moves = Moves(*refs[19:21])
+    a1, gb_own, w_down, one_hi, two_hi = refs[2:7], *refs[7:11]
+    own, p3, p1, p2, from_x, from_y, land1, land2, qkv_grad, mix_own = refs[11:21]
+    x_hi, y_hi = refs[21:23]
+    moves = Moves(*refs[23:25])
     rows = own.shape[0]
     n = rows // 2
 
@@ -764,6 +766,7 @@
         return dqkv.at[pl.ds(k * n, n)]
 
     greet((1, 2))
+    output = [moves.start(one_hi, x_hi, 1), moves.start(two_hi, y_hi, 2)]
     (p3_lo, p3_hi), (p1_lo, p1_hi), (p2_lo, p2_hi) = halves(p3), halves(p1), halves(p2)
     (land1_lo, land1_hi), (land2_lo, land2_hi) = halves(land1), halves(land2)
     multiply([block(6), block(7)], w_qkv, True, [], [p3_lo, p3_hi], store)
@@ -781,27 +784,27 @@
         rights.append(dqkv.at[pl.ds(at, x.shape[0])])
         at += x.shape[0]
     outer_on(a1, rights, qkv_grad)
-    for copy in second:
+    for copy in output + second:
         copy.wait()
 
 
-def qkv_back(dqkv, w_qkv, a1, gb_own, w_down):
+def qkv_back(dqkv, w_qkv, a1, gb_own, w_down, one_hi, two_hi):
     rows, width = a1[0].shape
     wide = gb_own.shape[1]
     n = rows // 2
     outs = [((rows, width), single)] + [((rows, width), half)] * 3
     outs += [((n, width), half)] * 2 + [((rows, width), half)] * 2
-    outs += [((width, dqkv.shape[1]), half), ((rows, width), single)]
+    outs += [((width, dqkv.shape[1]), half), ((rows, width), single)] + [((n, width), half)] * 2
     out = moving_call(
         qkv_back_kernel,
-        [dqkv, w_qkv, *a1, gb_own, w_down],
+        [dqkv, w_qkv, *a1, gb_own, w_down, one_hi, two_hi],
         outs,
-        6,
+        8,
         5,
         16 * rows * width * dqkv.shape[1] + 2 * rows * width * wide,
         "qkv_back",
     )
-    return out[0], out[6:8], out[8], out[9]
+    return out[0], out[6:8], out[8], out[9], out[10:12]
 
 
 def lay_out_kernel(axis, layout, c_ref, *refs):
@@ -889,12 +892,7 @@
     )(x)
 
 
-def reduce_small_kernel(nf, nc, moving, x_ref, *refs):
-    if moving:
-        piece, o_ref, one, two, far_lo, far_hi, land, stage, send_sem, recv_sem = refs[:10]
-        moves = Moves(refs[10], refs[11])
-    else:
-        o_ref, land, stage, send_sem, recv_sem = refs
+def reduce_small_kernel(nf, nc, x_ref, o_ref, land, stage, send_sem, recv_sem):
     f = lax.axis_index("fsdp")
     c = lax.axis_index("ctx")
     barrier = pltpu.get_barrier_semaphore()
@@ -913,11 +911,6 @@
             device_id_type=pl.DeviceIdType.MESH,
         )
     pl.semaphore_wait(barrier, nf + nc - 2)
-    if moving:
-        lo, hi = halves(piece)
-        (one_lo, one_hi), (two_lo, two_hi) = halves(one), halves(two)
-        first = [moves.start(lo, one_lo, 1), moves.start(hi, two_hi, 2)]
-        rest = [moves.start(hi, one_hi, 1), moves.start(lo, two_lo, 2)]
     copies = []
     for d in range(1, nf):
         to = lax.rem(f + d, nf)
@@ -932,10 +925,6 @@
             )
         )
         copies[-1].start()
-    if moving:
-        for copy in first:
-            copy.wait()
-        rest += [moves.start(one_lo, far_lo, 2), moves.start(two_hi, far_hi, 1)]
     total = x_ref[f]
     for d in range(1, nf):
         copies[d - 1].wait()
@@ -958,39 +947,25 @@
         copies[d - 1].wait()
         total = total + stage[d]
     o_ref[...] = total
-    if moving:
-        for copy in rest:
-            copy.wait()
-
-
-def reduce_small(x, nf, nc, call, piece=None):
+
+
+def reduce_small(x, nf, nc, call):
     block = x.shape[1:]
     sems = pltpu.SemaphoreType.DMA((nf + nc,))
-    moving = piece is not None
-    vmem = pl.BlockSpec(memory_space=pltpu.VMEM)
-    anywhere = pl.BlockSpec(memory_space=pl.ANY)
-    outs = [jax.ShapeDtypeStruct(block, single)]
-    scratch = [
-        pltpu.VMEM((nf,) + block, single),
-        pltpu.VMEM((nc,) + block, single),
-        sems,
-        sems,
-    ]
-    if moving:
-        n = piece.shape[0] // 2
-        shapes = [piece.shape, piece.shape, (n, piece.shape[1]), (n, piece.shape[1])]
-        outs += [jax.ShapeDtypeStruct(shape, half) for shape in shapes]
-        scratch += [pltpu.SemaphoreType.DMA((6,))] * 2
-    out = pl.pallas_call(
-        functools.partial(reduce_small_kernel, nf, nc, moving),
-        out_shape=outs,
-        in_specs=[vmem] + [anywhere] * moving,
-        out_specs=[vmem] + [anywhere] * (len(outs) - 1),
-        scratch_shapes=scratch,
+    return pl.pallas_call(
+        functools.partial(reduce_small_kernel, nf, nc),
+        out_shape=jax.ShapeDtypeStruct(block, single),
+        in_specs=[pl.BlockSpec(memory_space=pltpu.VMEM)],
+        out_specs=pl.BlockSpec(memory_space=pltpu.VMEM),
+        scratch_shapes=[
+            pltpu.VMEM((nf,) + block, single),
+            pltpu.VMEM((nc,) + block, single),
+            sems,
+            sems,
+        ],
         compiler_params=pltpu.CompilerParams(collective_id=call, has_side_effects=True),
         name="reduce_small",
-    )(x, *([piece] if moving else []))
-    return out[0], [[piece], [out[1]], [out[2]], [out[3], out[4]]] if moving else None
+    )(x)
 
 
 def per_device(
@@ -1047,6 +1022,7 @@
     up_own = columns(up_weight, fpart, wide // nf, nf)
     down_own = lax.dynamic_slice_in_dim(down_weight, c * fpart, fpart, axis=0)
     w_qkv = gather_f(qkv_own.astype(half))
+    up_own, down_own = up_own.astype(half), down_own.astype(half)
     small = jnp.concatenate(
         [ln1_gain, ln1_shift, q_bias, v_bias, out_bias, ln2_gain, ln2_shift, down_bias, up_bias]
     )
@@ -1085,18 +1061,18 @@
         normed, _ = norm_parts(x.astype(single))
         return (normed * gain1 + shift1).astype(half)
 
-    tok_near = after(gather_first(tokens), small_all, place, inv, slopes)
+    n = rows // 2
+    dz2_lo, dz2_hi = cotangent[:n].astype(half), cotangent[n:].astype(half)
+    early = (small_all, place, inv, slopes, up_own, down_own, dz2_lo, dz2_hi)
+    early, tok_near = after((early, gather_first(tokens)))
+    small_all, place, inv, slopes, up_own, down_own, dz2_lo, dz2_hi = early
     tok = gather_second(tokens, tok_near)
     near = [[first_norm(x) for x in p] for p in tok[:far]]
     tok = after(tok, near)
-    n = rows // 2
-    if CTX == 4:
-        cot = after(cotangent, tok)
-        dz2_lo, dz2_hi = cot[:n].astype(half), cot[n:].astype(half)
-    else:
-        dz2_own = after(cotangent, tok).astype(half)
+    if CTX != 4:
+        dz2_own = jnp.concatenate([dz2_lo, dz2_hi], axis=0)
         dz2_rest = gather_first(dz2_own)
-    w_up = gather_f(after(up_own.astype(half), tok))
+    w_up = gather_f(after(up_own, tok))
     a1 = flat(near)
     if CTX == 4:
         joined, a1_far, dz2_first = qkv_forward(
@@ -1108,7 +1084,7 @@
     else:
         a1 = a1 + [first_norm(x) for x in tok[far]]
         joined = joined_rows(a1, w_qkv, bias_qkv, "qkv")
-    w_down = gather_f(after(down_own.astype(half), joined))
+    w_down = gather_f(after(down_own, joined))
     attended = attn_forward(joined, inv, slopes, heads, scale)
     mine = [attended[j * rows : (j + 1) * rows] for j in range(CTX)]
     mine = after(mine, dz2_rest)
@@ -1181,9 +1157,9 @@
     if CTX == 4:
         lows = [swap(one_lo, 1), swap(two_lo, 2)]
         dqkv = after(dqkv, lows, up_part)
-        highs = [swap(one_hi, 1), swap(two_hi, 2)]
-        dh1, arrived, qkv_grad, mix_own = qkv_back(dqkv, w_qkv, a1, gb[0][0], w_down)
-        dh1 = after(dh1, highs)
+        dh1, arrived, qkv_grad, mix_own, highs = qkv_back(
+            dqkv, w_qkv, a1, gb[0][0], w_down, one_hi, two_hi
+        )
         mixed = y1 + bias_d + mix_own
         mixed = jnp.concatenate([total_of(mixed[:n], lows), total_of(mixed[n:], highs)])
     else:
@@ -1196,23 +1172,34 @@
         qkv_grad = outer(a1, [(dqkv, rows, j) for j in range(CTX)], "qkv_grad")
         mix_own = plain(gb[0], w_down, False, single, "mix_0")[0]
         mixed = total_of(y1 + bias_d + mix_own, scatter_send(mix[1:]))
-    dh1 = total_of(dh1, arrived)
-    down_out = gather_second(down_part, after(down_near, dh1))
-    down_out = lay_out(0, down_out, c, width // min(width, 512))
-    up_out = lay_out(1, gather_ctx(after(up_part, dh1)), c, nf)
+    qkv_part = scatter_f(qkv_grad)
+    up_own = after(up_part, arrived)
+    up_near = gather_first(up_own)
+    down_out = gather_second(down_part, after(down_near, arrived))
+    dh1 = total_of(after(dh1, up_near), arrived)
+    up_out = gather_second(up_own, up_near)
     sums = jnp.sum(dqkv.astype(single), axis=0)
     normed1_own, inv1_own = norm_parts(tokens.astype(single))
     gain1_grad = jnp.sum(dh1 * normed1_own, axis=0)
     shift1_grad = jnp.sum(dh1, axis=0)
+    dy1 = after(dy1, up_out)
     input_grad = dy1 + norm_back(normed1_own, inv1_own, gain1, dh1)
 
-    qkv_part = scatter_f(after(qkv_grad, input_grad))
-    bit = 1
-    while bit < CTX:
-        out_part = out_part.astype(half)
-        out_part = out_part.astype(single) + swap(out_part, bit).astype(single)
-        bit *= 2
-    out_out = out_part
+    def add_swapped(x, mask):
+        return (x.astype(single) + swap(x, mask).astype(single)).astype(half)
+
+    if CTX == 4:
+        k = out_part.shape[0] // 2
+        out_lo, out_hi = add_swapped(out_part[:k], 1), add_swapped(out_part[k:], 2)
+        out_lo, out_hi = (out_lo, swap(out_lo, 2)), (out_hi, swap(out_hi, 1))
+        out_out = [x.astype(single) + y.astype(single) for x, y in (out_lo, out_hi)]
+        out_out = jnp.concatenate(out_out, axis=0)
+    else:
+        bit = 1
+        while bit < CTX:
+            out_out = out_part.astype(single) + swap(out_part, bit).astype(single)
+            out_part = out_out.astype(half)
+            bit *= 2
 
     def spread(x, inner):
         x = x.reshape(-1, 1, inner)
@@ -1223,19 +1210,21 @@
         sizes = [x.shape[0] // nf for x in items]
         x = jnp.concatenate([x.reshape(nf, -1) for x in items], axis=1)
         x = jnp.pad(x, ((0, 0), (0, -x.shape[1] % 1024))).reshape(nf, -1, 128)
-        x, qkv_all = reduce_small(x, nf, CTX, call, qkv_part if CTX == 4 else None)
-        x = x.reshape(-1)
+        x = reduce_small(x, nf, CTX, call).reshape(-1)
         out, at = [], 0
         for n in sizes:
             out.append(x[at : at + n])
             at += n
-        return out, qkv_all
+        return out
 
     sums_in = [out_bias_grad, gain2_grad, shift2_grad, down_bias_grad, spread(up_bias_grad, fpart)]
-    gain1_grad = after(gain1_grad, qkv_part)
     sums_in += [gain1_grad, shift1_grad, spread(sums[:part], part), spread(sums[2 * part :], part)]
-    sums_out, qkv_all = reduced(sums_in, 2)
-    qkv_out = lay_out(1, qkv_all or gather_ctx(qkv_part), c, 3)
+    qkv_near = gather_first(qkv_part)
+    sums_in[5] = after(sums_in[5], qkv_near)
+    sums_out = reduced(sums_in, 2)
+    qkv_out = lay_out(1, gather_second(qkv_part, qkv_near), c, 3)
+    down_out = lay_out(0, after(down_out, qkv_part), c, width // min(width, 512))
+    up_out = lay_out(1, after(up_out, qkv_part), c, nf)
     out_bias_out, gain2_out, shift2_out, down_bias_out, up_bias_out = sums_out[:5]
     gain1_out, shift1_out, q_bias_out, v_bias_out = sums_out[5:]
     return (

time: 766 us -> 759 us (level)
  Pallas kernels: 459 us -> 447 us
  waiting for transfers between devices: 134 us -> 125 us
    pallas_call x1, Pallas kernels: 31.6 us -> 13.6 us  [reduce_small(): pl.pallas_call(functools.partial(reduce_small_kernel, nf, nc), out_shape=...]
    ppermute x27 -> x31, waiting for transfers between devices: 86.3 us -> 69.3 us  [swap(): return lax.ppermute(x, 'ctx', [(i, i ^ mask) for i in range(n)])]
    pallas_call x2, Pallas kernels: 105 us -> 118 us  [moving_call(): pl.pallas_call(kernel, in_specs=[anywhere] * len(operands), out_specs=[an...]
    all_gather x4, waiting for transfers between devices: 47.2 us -> 55.9 us  [gather_f(): return lax.all_gather(x, 'fsdp', axis=0, tiled=True)]
    ppermute x27 -> x31, starting transfers between devices: 30.8 us -> 35.3 us  [swap(): return lax.ppermute(x, 'ctx', [(i, i ^ mask) for i in range(n)])]
    unnamed x165 -> x155, local copies, waits for them, and re-layouts: 25.3 us -> 22.8 us
  transfers between devices with their start and end apart: 35 -> 39, of which waited for: 12 -> 13; matrix products, arithmetic and copies ran while one was open for 13% -> 15% of each run, Pallas kernels for 56% -> 59%
where the time goes in v2:
time: 759 us; the launch traced here: 749 us
  Pallas kernels  447 us (59%)
  waiting for transfers between devices  125 us (16%)
  other arithmetic  70.9 us (9%)
  local copies, waits for them, and re-layouts  46.4 us (6%)
  starting transfers between devices  35.7 us (5%)
  between operations  15.5 us (2%)
  matrix products  7.85 us (1%)
    pallas_call x2, Pallas kernels, moving_call(): pl.pallas_call(kernel, in_specs=[anywhere] * len(operands), out_specs=[an...  118 us
    pallas_call x1, Pallas kernels, feed_back(): pl.pallas_call(feed_back_kernel, in_specs=[anywhere] * 22, out_specs=[any...  103 us
    ppermute x31, waiting for transfers between devices, swap(): return lax.ppermute(x, 'ctx', [(i, i ^ mask) for i in range(n)])  69.3 us
    pallas_call x2, Pallas kernels, attn_call(): pl.pallas_call(kernel, grid_spec=pltpu.PrefetchScalarGridSpec(num_scalar_...  60.5 us
    all_gather x4, waiting for transfers between devices, gather_f(): return lax.all_gather(x, 'fsdp', axis=0, tiled=True)  55.9 us
    pallas_call x4, Pallas kernels, rows_matmul(): pl.pallas_call(functools.partial(rows_kernel, dot_nt if transposed else d...  53.9 us
    pallas_call x1, Pallas kernels, heads_back(): pl.pallas_call(functools.partial(heads_back_kernel, part), in_specs=[anyw...  50 us
    ppermute x31, starting transfers between devices, swap(): return lax.ppermute(x, 'ctx', [(i, i ^ mask) for i in range(n)])  35.3 us
  transfers between devices with their start and end apart: 39, of which 13 were waited for; matrix products, arithmetic and copies ran while one was open for 15% of the time, Pallas kernels for 59%

profile of v2, /device:TPU:0, one launch (start us, length us, event | category | flops | bytes accessed | tf_op | source)
XLA Modules:
  0.0 748.6 jit_solution(14861241579095570227)
XLA Ops:
  18.1 9.0 %gather_small.1 = f32[8,24,128]{2,1,0:T(8,128)} custom-call(f32[24,128]{1,0:T(8,128)} %bitcast.91), custom_call_target="tpu_custom_call" | custom-call | tf_op jit(solution)/shard_map/gather_small/pallas_call | solution.py:884
  31.9 3.9 convert.46
  46.1 15.4 %collective-permute-done = bf16[512,2048]{1,0:T(8,128)(2,1)} collective-permute-done((bf16[512,2048]{1,0:T(8,128)(2,1)S(1)}, bf16[512,2048]{1,0:T(8,128)(2,1)}, u32[]{:S(2)}, u32[]{:S(2)}) %collective-permute-start) | collective-permute-done | bytes 2097184 | tf_op jit(solution)/shard_map/ppermute | solution.py:60
  76.3 5.7 fusion.21
  82.0 6.1 collective-permute-done.2.refs_0_
  91.0 28.0 %qkv.1 = (bf16[2048,1536]{1,0:T(8,128)(2,1)}, bf16[256,2048]{1,0:T(8,128)(2,1)S(1)}, bf16[256,2048]{1,0:T(8,128)(2,1)}, bf16[256,2048]{1,0:T(8,128)(2,1)}, bf16[256,2048]{1,0:T(8,128)(2,1)}) custom-call(bf16[256,2048]{1,0:T(8,128)(2,1)} %collective-permute-done.2.refs_0_, bf16[256,2048]{1,0:T(8,128)(2,1)} %collective-permute-done.3.refs_1_, ...), custom_call_target="tpu_custom_call" | custom-call | flops 12884901 | tf_op jit(solution)/shard_map/qkv/pallas_call | solution.py:499
  122.2 24.4 %attn_forward.1 = bf16[2048,512]{1,0:T(8,128)(2,1)S(1)} custom-call(s32[16]{0:T(128)S(1)} %select_reduce_fusion.inv_ref, f32[4]{0:T(128)S(1)} %multiply_power_fusion.slope_ref, ...), custom_call_target="tpu_custom_call" | custom-call | flops 20000000 | bytes 8388 | tf_op jit(solution)/shard_map/attn_forward/pallas_call | solution.py:233
  153.4 12.5 %collective-permute-done.6 = bf16[512,512]{1,0:T(8,128)(2,1)S(1)} collective-permute-done((bf16[512,512]{1,0:T(8,128)(2,1)}, bf16[512,512]{1,0:T(8,128)(2,1)S(1)}, u32[]{:S(2)}, u32[]{:S(2)}) %collective-permute-start.6) | collective-permute-done | bytes 524320 | tf_op jit(solution)/shard_map/ppermute | solution.py:60
  165.8 6.9 collective-permute-done.7
  176.2 7.9 %fusion.44 = (f32[512]{0:T(512)S(1)}, f32[512,2048]{1,0:T(8,128)S(1)}) fusion(f32[2048]{0:T(1024)S(1)} %bitcast.94, bf16[2048,2048]{1,0:T(8,128)(2,1)} %all-gather.7.cloned.1.call-done.refs_6_, bf16[512,512]{1,0:T(8,128)(2,1)} %get-tuple-element.205, bf16[512,512]{1,0:T(8,128)(2,1)} %get-tuple-element.204, bf16[512,512]{1,0:T(8,128)(2,1)S(1)} %get-tuple-element.203, ...), kind=kOutput, calls=%fused_computation.162 | convolution fusion | flops 4307549696 | bytes 16787456 | tf_op jit(solution)/shard_map/dot_general | solution.py:24
  188.4 55.8 %all-gather.9.cloned.1.call-done.refs_1_.refs_2_.refs_14_ = bf16[2048,2048]{1,0:T(8,128)(2,1)} async-done(((bf16[256,2048]{1,0:T(8,128)(2,1)}), bf16[2048,2048]{1,0:T(8,128)(2,1)}) %all-gather.9.cloned.1.call-update) | async-done | bytes 8388624 | tf_op jit(solution)/shard_map/all_gather | solution.py:1019
  244.2 11.0 %up_gelu_0.1 = (bf16[512,2048]{1,0:T(8,128)(2,1)}, bf16[512,2048]{1,0:T(8,128)(2,1)}) custom-call(bf16[512,2048]{1,0:T(8,128)(2,1)} %copy-done.20, bf16[2048,2048]{1,0:T(8,128)(2,1)} %all-gather.9.cloned.1.call-done.refs_1_.refs_2_.refs_14_, f32[1,2048]{1,0:T(1,128)S(1)} %bitcast.71), custom_call_target="tpu_custom_call" | custom-call | flops 4294967 | bytes 16777 | tf_op jit(solution)/shard_map/up_gelu_0/pallas_call | solution.py:311
  263.9 10.9 %up_gelu_1.1 = (bf16[512,2048]{1,0:T(8,128)(2,1)}, bf16[512,2048]{1,0:T(8,128)(2,1)}) custom-call(bf16[512,2048]{1,0:T(8,128)(2,1)} %collective-permute-done.11.refs_0_.refs_16_, bf16[2048,2048]{1,0:T(8,128)(2,1)} %all-gather.9.cloned.1.call-done.refs_1_.refs_2_.refs_14_, f32[1,2048]{1,0:T(1,128)S(1)} %bitcast.72), custom_call_target="tpu_custom_call" | custom-call | flops 4294967 | bytes 16777 | tf_op jit(solution)/shard_map/up_gelu_1/pallas_call | solution.py:311
  274.8 11.0 %up_gelu_2.1 = (bf16[512,2048]{1,0:T(8,128)(2,1)}, bf16[512,2048]{1,0:T(8,128)(2,1)}) custom-call(bf16[512,2048]{1,0:T(8,128)(2,1)} %collective-permute-done.12.refs_0_.refs_17_, bf16[2048,2048]{1,0:T(8,128)(2,1)} %all-gather.9.cloned.1.call-done.refs_1_.refs_2_.refs_14_, f32[1,2048]{1,0:T(1,128)S(1)} %bitcast.73), custom_call_target="tpu_custom_call" | custom-call | flops 4294967 | bytes 16777 | tf_op jit(solution)/shard_map/up_gelu_2/pallas_call | solution.py:311
  287.3 21.0 %up_gelu_3.1 = (bf16[256,2048]{1,0:T(8,128)(2,1)S(1)}, bf16[256,2048]{1,0:T(8,128)(2,1)}, bf16[256,2048]{1,0:T(8,128)(2,1)}, bf16[256,2048]{1,0:T(8,128)(2,1)}) custom-call(bf16[256,2048]{1,0:T(8,128)(2,1)} %copy-done.26, bf16[256,2048]{1,0:T(8,128)(2,1)} %copy-done.27, bf16[2048,2048]{1,0:T(8,128)(2,1)} %all-gather.9.cloned.1.call-done.refs_1_.refs_2_.refs_14_, ...), custom_call_target="tpu_custom_call" | custom-call | flops 4294967 | bytes 16777 | tf_op jit(solution)/shard_map/up_gelu_3/pallas_call | solution.py:311
  309.6 23.2 %down_grad.1 = bf16[2048,2048]{1,0:T(8,128)(2,1)} custom-call(bf16[512,2048]{1,0:T(8,128)(2,1)} %get-tuple-element.124.refs_0_.refs_1_.refs_7_, bf16[512,2048]{1,0:T(8,128)(2,1)} %get-tuple-element.124.refs_0_.refs_1_.refs_7_, bf16[512,2048]{1,0:T(8,128)(2,1)} %get-tuple-element.129.refs_2_.refs_3_.refs_8_, ...), custom_call_target="tpu_custom_call" | custom-call | flops 17179868 | bytes 25165 | tf_op jit(solution)/shard_map/down_grad/pallas_call | solution.py:384
  332.9 102.7 %feed_back.1 = (bf16[512,2048]{1,0:T(8,128)(2,1)}, bf16[512,2048]{1,0:T(8,128)(2,1)}, bf16[512,2048]{1,0:T(8,128)(2,1)}, bf16[256,2048]{1,0:T(8,128)(2,1)}, bf16...) custom-call(bf16[256,2048]{1,0:T(8,128)(2,1)} %get-tuple-element.112, ...), custom_call_target="tpu_custom_call" | custom-call | flops 55834576 | tf_op jit(solution)/shard_map/feed_back/pallas_call | solution.py:642
  436.2 50.0 %heads_back.1 = (f32[512,2048]{1,0:T(8,128)}, bf16[512,2048]{1,0:T(8,128)(2,1)}, f32[8,2048]{1,0:T(8,128)}, bf16[2048,512]{1,0:T(8,128)(2,1)}, bf16[2048,2048]{1...) custom-call(f32[512,2048]{1,0:T(8,128)} %get-tuple-element.142.refs_, ...), custom_call_target="tpu_custom_call" | custom-call | flops 21474836 | tf_op jit(solution)/shard_map/heads_back/pallas_call | solution.py:734
  489.0 36.2 %attn_backward.1.refs_0_ = bf16[2048,1536]{1,0:T(8,128)(2,1)} custom-call(s32[16]{0:T(128)S(1)} %select_reduce_fusion.inv_ref, f32[4]{0:T(128)S(1)} %multiply_power_fusion.slope_ref, ...), custom_call_target="tpu_custom_call" | custom-call | flops 40000000 | bytes 14680 | tf_op jit(solution)/shard_map/attn_backward/pallas_call | solution.py:233
  525.2 90.4 %qkv_back.1 = (f32[512,2048]{1,0:T(8,128)}, bf16[512,2048]{1,0:T(8,128)(2,1)}, bf16[512,2048]{1,0:T(8,128)(2,1)}, bf16[512,2048]{1,0:T(8,128)(2,1)}, bf16[256,20...) custom-call(bf16[2048,1536]{1,0:T(8,128)(2,1)} %attn_backward.1.refs, ...), custom_call_target="tpu_custom_call" | custom-call | flops 30064772 | tf_op jit(solution)/shard_map/qkv_back/pallas_call | solution.py:499
  628.8 3.8 convert_reduce_fusion
  632.6 5.2 add_add_fusion
  638.7 4.4 fusion.28
  648.1 4.2 collective-permute-done.18.refs_2_
  659.5 6.6 fusion.16
  666.1 8.7 %collective-permute-done.19.refs_3_ = bf16[128,2048]{1,0:T(8,128)(2,1)} collective-permute-done((bf16[128,2048]{1,0:T(8,128)(2,1)}, bf16[128,2048]{1,0:T(8,128)(2,1)}, u32[]{:S(2)}, u32[]{:S(2)}) %collective-permute-start.19) | collective-permute-done | bytes 524320 | tf_op jit(solution)/shard_map/ppermute | solution.py:60
  675.5 5.3 collective-permute-done.27
  685.7 5.6 fusion.15
  692.2 4.2 collective-permute-done.26
  702.7 5.4 lay_out.5
  708.1 7.2 lay_out.4
  719.8 13.6 %reduce_small.1 = f32[24,128]{1,0:T(8,128)} custom-call(f32[8,24,128]{2,1,0:T(8,128)} %bitcast.79), custom_call_target="tpu_custom_call" | custom-call | tf_op jit(solution)/shard_map/reduce_small/pallas_call | solution.py:955
  (324 shorter events, 127.0 us)
Async XLA Ops:
  7.3 83.7 %all-gather.5.cloned.1.call-start = ((), (), s32[]{:S(2)}) async-start(), calls=%async_computation.4 | async-start | bytes 7077888 | tf_op jit(solution)/shard_map/all_gather | solution.py:1019
  9.9 166.3 %all-gather.7.cloned.1.call-start = ((), (), s32[]{:S(2)}) async-start(), calls=%async_computation.5 | async-start | bytes 9437184 | tf_op jit(solution)/shard_map/all_gather | solution.py:1019
  12.7 231.5 %all-gather.9.cloned.1.call-start = ((), (), s32[]{:S(2)}) async-start(), calls=%async_computation.6 | async-start | bytes 9437184 | tf_op jit(solution)/shard_map/all_gather | solution.py:1019
  12.7 48.7 %collective-permute-start = (bf16[512,2048]{1,0:T(8,128)(2,1)S(1)}, bf16[512,2048]{1,0:T(8,128)(2,1)}, u32[]{:S(2)}, u32[]{:S(2)}) collective-permute-start(bf16[512,2048]{1,0:T(8,128)(2,1)S(1)} %copy-done.15), channel_id=1, source_target_pairs={{0,8},{8,0},{16,24},{24,16},{1,9},{9,1},{17,25},{25,17},{2,10},{10... | collective-permute-start | bytes 6291464 | tf_op jit(solution)/shard_map/ppermute | solution.py:60
  15.7 47.2 %collective-permute-start.1 = (bf16[512,2048]{1,0:T(8,128)(2,1)S(1)}, bf16[512,2048]{1,0:T(8,128)(2,1)}, u32[]{:S(2)}, u32[]{:S(2)}) collective-permute-start(bf16[512,2048]{1,0:T(8,128)(2,1)S(1)} %copy-done.15), channel_id=1, source_target_pairs={{0,16},{8,24},{16,0},{24,8},{1,17},{9,25},{17,1},{25,9},{2,18},{10... | collective-permute-start | bytes 6291464 | tf_op jit(solution)/shard_map/ppermute | solution.py:60
  64.3 23.9 %collective-permute-start.2 = (bf16[256,2048]{1,0:T(8,128)(2,1)S(1)}, bf16[256,2048]{1,0:T(8,128)(2,1)}, u32[]{:S(2)}, u32[]{:S(2)}) collective-permute-start(bf16[256,2048]{1,0:T(8,128)(2,1)S(1)} %slice.176), channel_id=1, source_target_pairs={{0,16},{8,24},{16,0},{24,8},{1,17},{9,25},{17,1},{25,9},{2,18},{10... | collective-permute-start | bytes 3145736 | tf_op jit(solution)/shard_map/ppermute | solution.py:60
  67.2 23.6 %collective-permute-start.3 = (bf16[256,2048]{1,0:T(8,128)(2,1)S(1)}, bf16[256,2048]{1,0:T(8,128)(2,1)}, u32[]{:S(2)}, u32[]{:S(2)}) collective-permute-start(bf16[256,2048]{1,0:T(8,128)(2,1)S(1)} %slice.177), channel_id=1, source_target_pairs={{0,8},{8,0},{16,24},{24,16},{1,9},{9,1},{17,25},{25,17},{2,10},{10... | collective-permute-start | bytes 3145736 | tf_op jit(solution)/shard_map/ppermute | solution.py:60
  90.8 242.0 %all-gather.11.cloned.1.call-start = ((), (), s32[]{:S(2)}) async-start(), calls=%async_computation.7 | async-start | bytes 9437184 | tf_op jit(solution)/shard_map/all_gather | solution.py:1019
  120.0 316.2 %reduce-scatter.5.cloned.1.call-start = ((), (), s32[]{:S(2)}) async-start(), calls=%async_computation.8 | async-start | bytes 9437184 | tf_op jit(solution)/shard_map/reduce_scatter | solution.py:1055
  120.1 27.8 %collective-permute-start.4 = (bf16[256,2048]{1,0:T(8,128)(2,1)S(1)}, bf16[256,2048]{1,0:T(8,128)(2,1)S(1)}, u32[]{:S(2)}, u32[]{:S(2)}) collective-permute-start(bf16[256,2048]{1,0:T(8,128)(2,1)S(1)} %copy-done.17), channel_id=1, source_target_pairs={{0,8},{8,0},{16,24},{24,16},{1,9},{9,1},{17,25},{25,17},{2,10},{10... | collective-permute-start | bytes 3145736 | tf_op jit(solution)/shard_map/ppermute | solution.py:60
  121.6 27.3 %collective-permute-start.5 = (bf16[256,2048]{1,0:T(8,128)(2,1)}, bf16[256,2048]{1,0:T(8,128)(2,1)S(1)}, u32[]{:S(2)}, u32[]{:S(2)}) collective-permute-start(bf16[256,2048]{1,0:T(8,128)(2,1)} %get-tuple-element.112.refs_9_.refs_8_.refs_0_), channel_id=1, source_target_pairs={{0,16},{8,24},{16,0},{24,8},{1,17},{9,25},{17,1},{25,9},{2,18},{10... | collective-permute-start | bytes 3145736 | tf_op jit(solution)/shard_map/ppermute | solution.py:60
  151.3 21.4 %collective-permute-start.7 = (bf16[512,512]{1,0:T(8,128)(2,1)}, bf16[512,512]{1,0:T(8,128)(2,1)S(1)}, u32[]{:S(2)}, u32[]{:S(2)}) collective-permute-start(bf16[512,512]{1,0:T(8,128)(2,1)} %get-tuple-element.114), channel_id=1, source_target_pairs={{0,16},{8,24},{16,0},{24,8},{1,17},{9,25},{17,1},{25,9},{2,18},{10... | collective-permute-start | bytes 1572872 | tf_op jit(solution)/shard_map/ppermute | solution.py:60
  152.7 20.8 %collective-permute-start.8 = (bf16[512,512]{1,0:T(8,128)(2,1)}, bf16[512,512]{1,0:T(8,128)(2,1)}, u32[]{:S(2)}, u32[]{:S(2)}) collective-permute-start(bf16[512,512]{1,0:T(8,128)(2,1)} %get-tuple-element.115), channel_id=1, source_target_pairs={{0,8},{8,0},{16,24},{24,16},{1,9},{9,1},{17,25},{25,17},{2,10},{10... | collective-permute-start | bytes 1572872 | tf_op jit(solution)/shard_map/ppermute | solution.py:60
  186.1 69.1 %collective-permute-start.11 = (bf16[512,2048]{1,0:T(8,128)(2,1)S(1)}, bf16[512,2048]{1,0:T(8,128)(2,1)}, u32[]{:S(2)}, u32[]{:S(2)}) collective-permute-start(bf16[512,2048]{1,0:T(8,128)(2,1)S(1)} %add_convert_fusion.refs_0_.refs_15_), channel_id=1, source_target_pairs={{0,8},{8,0},{16,24},{24,16},{1,9},{9,1},{17,25},{25,17},{2,10},{10... | collective-permute-start | bytes 6291464 | tf_op jit(solution)/shard_map/ppermute | solution.py:60
  187.6 67.6 %collective-permute-start.12 = (bf16[512,2048]{1,0:T(8,128)(2,1)S(1)}, bf16[512,2048]{1,0:T(8,128)(2,1)}, u32[]{:S(2)}, u32[]{:S(2)}) collective-permute-start(bf16[512,2048]{1,0:T(8,128)(2,1)S(1)} %add_convert_fusion.refs_0_.refs_15_), channel_id=1, source_target_pairs={{0,16},{8,24},{16,0},{24,8},{1,17},{9,25},{17,1},{25,9},{2,18},{10... | collective-permute-start | bytes 6291464 | tf_op jit(solution)/shard_map/ppermute | solution.py:60
  256.7 29.1 %collective-permute-start.13 = (bf16[256,2048]{1,0:T(8,128)(2,1)S(1)}, bf16[256,2048]{1,0:T(8,128)(2,1)S(1)}, u32[]{:S(2)}, u32[]{:S(2)}) collective-permute-start(bf16[256,2048]{1,0:T(8,128)(2,1)S(1)} %slice.191), channel_id=1, source_target_pairs={{0,16},{8,24},{16,0},{24,8},{1,17},{9,25},{17,1},{25,9},{2,18},{10... | collective-permute-start | bytes 3145736 | tf_op jit(solution)/shard_map/ppermute | solution.py:60
  259.6 26.2 %collective-permute-start.14 = (bf16[256,2048]{1,0:T(8,128)(2,1)S(1)}, bf16[256,2048]{1,0:T(8,128)(2,1)S(1)}, u32[]{:S(2)}, u32[]{:S(2)}) collective-permute-start(bf16[256,2048]{1,0:T(8,128)(2,1)S(1)} %slice.192), channel_id=1, source_target_pairs={{0,8},{8,0},{16,24},{24,16},{1,9},{9,1},{17,25},{25,17},{2,10},{10... | collective-permute-start | bytes 3145736 | tf_op jit(solution)/shard_map/ppermute | solution.py:60
  262.8 45.4 %collective-permute-start.10 = (bf16[256,2048]{1,0:T(8,128)(2,1)S(1)}, bf16[256,2048]{1,0:T(8,128)(2,1)S(1)}, u32[]{:S(2)}, u32[]{:S(2)}) collective-permute-start(bf16[256,2048]{1,0:T(8,128)(2,1)S(1)} %copy-done.23), channel_id=1, source_target_pairs={{0,8},{8,0},{16,24},{24,16},{1,9},{9,1},{17,25},{25,17},{2,10},{10... | collective-permute-start | bytes 3145736 | tf_op jit(solution)/shard_map/ppermute | solution.py:60
  263.4 44.9 %collective-permute-start.9 = (bf16[256,2048]{1,0:T(8,128)(2,1)S(1)}, bf16[256,2048]{1,0:T(8,128)(2,1)S(1)}, u32[]{:S(2)}, u32[]{:S(2)}) collective-permute-start(bf16[256,2048]{1,0:T(8,128)(2,1)S(1)} %copy-done.22), channel_id=1, source_target_pairs={{0,16},{8,24},{16,0},{24,8},{1,17},{9,25},{17,1},{25,9},{2,18},{10... | collective-permute-start | bytes 3145736 | tf_op jit(solution)/shard_map/ppermute | solution.py:60
  332.8 192.4 %reduce-scatter.7.cloned.1.call-start = ((), (), s32[]{:S(2)}) async-start(), calls=%async_computation.9 | async-start | bytes 9437184 | tf_op jit(solution)/shard_map/reduce_scatter | solution.py:1055
  435.6 219.3 %reduce-scatter.11.cloned.1.call-start = ((), (), s32[]{:S(2)}) async-start(), calls=%async_computation.11 | async-start | bytes 9437184 | tf_op jit(solution)/shard_map/reduce_scatter | solution.py:1055
  486.3 204.9 %reduce-scatter.9.cloned.1.call-start = ((), (), s32[]{:S(2)}) async-start(), calls=%async_computation.10 | async-start | bytes 7077888 | tf_op jit(solution)/shard_map/reduce_scatter | solution.py:1055
  486.4 38.8 %collective-permute-start.15 = (bf16[256,2048]{1,0:T(8,128)(2,1)}, bf16[256,2048]{1,0:T(8,128)(2,1)}, u32[]{:S(2)}, u32[]{:S(2)}) collective-permute-start(bf16[256,2048]{1,0:T(8,128)(2,1)} %get-tuple-element.148), channel_id=1, source_target_pairs={{0,8},{8,0},{16,24},{24,16},{1,9},{9,1},{17,25},{25,17},{2,10},{10... | collective-permute-start | bytes 3145736 | tf_op jit(solution)/shard_map/ppermute | solution.py:60
  487.9 37.3 %collective-permute-start.16 = (bf16[256,2048]{1,0:T(8,128)(2,1)S(1)}, bf16[256,2048]{1,0:T(8,128)(2,1)}, u32[]{:S(2)}, u32[]{:S(2)}) collective-permute-start(bf16[256,2048]{1,0:T(8,128)(2,1)S(1)} %copy-done.58), channel_id=1, source_target_pairs={{0,16},{8,24},{16,0},{24,8},{1,17},{9,25},{17,1},{25,9},{2,18},{10... | collective-permute-start | bytes 3145736 | tf_op jit(solution)/shard_map/ppermute | solution.py:60
  624.5 21.7 %collective-permute-start.17 = (bf16[256,2048]{1,0:T(8,128)(2,1)}, bf16[256,2048]{1,0:T(8,128)(2,1)S(1)}, u32[]{:S(2)}, u32[]{:S(2)}) collective-permute-start(bf16[256,2048]{1,0:T(8,128)(2,1)} %reduce-scatter.7.cloned.1.call-done.refs_0_), channel_id=1, source_target_pairs={{0,8},{8,0},{16,24},{24,16},{1,9},{9,1},{17,25},{25,17},{2,10},{10... | collective-permute-start | bytes 3145736 | tf_op jit(solution)/shard_map/ppermute | solution.py:60
  625.9 26.4 %collective-permute-start.18 = (bf16[256,2048]{1,0:T(8,128)(2,1)}, bf16[256,2048]{1,0:T(8,128)(2,1)}, u32[]{:S(2)}, u32[]{:S(2)}) collective-permute-start(bf16[256,2048]{1,0:T(8,128)(2,1)} %reduce-scatter.7.cloned.1.call-done.refs_0_), channel_id=1, source_target_pairs={{0,16},{8,24},{16,0},{24,8},{1,17},{9,25},{17,1},{25,9},{2,18},{10... | collective-permute-start | bytes 3145736 | tf_op jit(solution)/shard_map/ppermute | solution.py:60
  627.6 75.0 %collective-permute-start.29 = (bf16[128,2048]{1,0:T(8,128)(2,1)}, bf16[128,2048]{1,0:T(8,128)(2,1)}, u32[]{:S(2)}, u32[]{:S(2)}) collective-permute-start(bf16[128,2048]{1,0:T(8,128)(2,1)} %slice.224), channel_id=1, source_target_pairs={{0,16},{8,24},{16,0},{24,8},{1,17},{9,25},{17,1},{25,9},{2,18},{10... | collective-permute-start | bytes 1572872 | tf_op jit(solution)/shard_map/ppermute | solution.py:60
  647.1 27.7 %collective-permute-start.19 = (bf16[128,2048]{1,0:T(8,128)(2,1)}, bf16[128,2048]{1,0:T(8,128)(2,1)}, u32[]{:S(2)}, u32[]{:S(2)}) collective-permute-start(bf16[128,2048]{1,0:T(8,128)(2,1)} %slice.245), channel_id=1, source_target_pairs={{0,16},{8,24},{16,0},{24,8},{1,17},{9,25},{17,1},{25,9},{2,18},{10... | collective-permute-start | bytes 1572872 | tf_op jit(solution)/shard_map/ppermute | solution.py:60
  654.2 21.2 %collective-permute-start.20 = (bf16[128,2048]{1,0:T(8,128)(2,1)}, bf16[128,2048]{1,0:T(8,128)(2,1)}, u32[]{:S(2)}, u32[]{:S(2)}) collective-permute-start(bf16[128,2048]{1,0:T(8,128)(2,1)} %slice.246), channel_id=1, source_target_pairs={{0,8},{8,0},{16,24},{24,16},{1,9},{9,1},{17,25},{25,17},{2,10},{10... | collective-permute-start | bytes 1572872 | tf_op jit(solution)/shard_map/ppermute | solution.py:60
  658.5 22.2 %collective-permute-start.27 = (bf16[128,2048]{1,0:T(8,128)(2,1)}, bf16[128,2048]{1,0:T(8,128)(2,1)}, u32[]{:S(2)}, u32[]{:S(2)}) collective-permute-start(bf16[128,2048]{1,0:T(8,128)(2,1)} %get-tuple-element.215), channel_id=1, source_target_pairs={{0,16},{8,24},{16,0},{24,8},{1,17},{9,25},{17,1},{25,9},{2,18},{10... | collective-permute-start | bytes 1572872 | tf_op jit(solution)/shard_map/ppermute | solution.py:60
  674.8 27.9 %collective-permute-start.30 = (bf16[128,2048]{1,0:T(8,128)(2,1)}, bf16[128,2048]{1,0:T(8,128)(2,1)}, u32[]{:S(2)}, u32[]{:S(2)}) collective-permute-start(bf16[128,2048]{1,0:T(8,128)(2,1)} %slice.225), channel_id=1, source_target_pairs={{0,8},{8,0},{16,24},{24,16},{1,9},{9,1},{17,25},{25,17},{2,10},{10... | collective-permute-start | bytes 1572872 | tf_op jit(solution)/shard_map/ppermute | solution.py:60
  691.3 24.0 %collective-permute-start.21 = (bf16[256,1536]{1,0:T(8,128)(2,1)}, bf16[256,1536]{1,0:T(8,128)(2,1)S(1)}, u32[]{:S(2)}, u32[]{:S(2)}) collective-permute-start(bf16[256,1536]{1,0:T(8,128)(2,1)} %reduce-scatter.9.cloned.1.call-done.refs_0_), channel_id=1, source_target_pairs={{0,8},{8,0},{16,24},{24,16},{1,9},{9,1},{17,25},{25,17},{2,10},{10... | collective-permute-start | bytes 2359304 | tf_op jit(solution)/shard_map/ppermute | solution.py:60
  (67 other events, 711.9 us)
Sparse Core Ops, SparseCore 0:
  10.3 68.1 all-gather.4
  80.7 80.6 all-gather.6
  163.6 80.5 all-gather.8
  245.6 80.6 all-gather.10
  332.9 88.1 reduce-scatter.4
  435.7 87.4 reduce-scatter.6
  525.5 87.9 reduce-scatter.10
  615.8 68.4 reduce-scatter.8

commit v3 on v2

--- a/solution.py
+++ b/solution.py
@@ -1093,17 +1093,18 @@
     y1 = tokens.astype(single) + dot_nn(ob, w_out) + bias_o
 
     normed2, inv2 = norm_parts(y1)
+    a2_own = (normed2 * gain2 + shift2).astype(half)
+    gb, slope = [None] * CTX, [None] * CTX
+    gb[0], slope[0] = up_gelu([a2_own], w_up, bias_u, "up_gelu_0")
+    last = gb[0]
+    a2_near = gather_first(a2_own)
+    a2 = gather_second(a2_own, a2_near)
     if CTX == 4:
-        one_lo, two_hi = after(dz2_first, ob)
+        one_lo, two_hi = after(dz2_first, a2_near)
         one_hi, two_lo = dz2_rest
         dz2 = [[dz2_lo, dz2_hi], [one_lo, one_hi], [two_lo, two_hi], [swap(one_lo, 2), swap(two_hi, 1)]]
     else:
         dz2 = [[dz2_own]] + [[x] for x in dz2_rest]
-    a2_own = (normed2 * gain2 + shift2).astype(half)
-    gb, slope = [None] * CTX, [None] * CTX
-    gb[0], slope[0] = up_gelu([a2_own], w_up, bias_u, "up_gelu_0")
-    last = gb[0]
-    a2 = gather_second(a2_own, after(gather_first(a2_own), last))
     for j in range(1, CTX):
         gb[j], slope[j] = up_gelu(after(a2[j], last), w_up, bias_u, f"up_gelu_{j}")
         last = gb[j]
@@ -1130,8 +1131,6 @@
         mix[far] = plain(gb[far], w_down, False, half, "mix_far")[0]
         dh2 = total_of(dh2, arrived)
     up_part = scatter_f(up_grad)
-    up_bias_grad = sum(jnp.sum(x.astype(single), axis=0) for x in flat(du))
-    down_bias_grad = sum(jnp.sum(x.astype(single), axis=0) for x in dz2[0])
     if CTX == 4:
         dy1, sums2, dattn, out_grad, mix, down_near = heads_back(
             dh2, cotangent, y1, gain2, w_out, ob, gb[1][0], gb[2][0], w_down, mix_first, down_part
@@ -1160,8 +1159,6 @@
         dh1, arrived, qkv_grad, mix_own, highs = qkv_back(
             dqkv, w_qkv, a1, gb[0][0], w_down, one_hi, two_hi
         )
-        mixed = y1 + bias_d + mix_own
-        mixed = jnp.concatenate([total_of(mixed[:n], lows), total_of(mixed[n:], highs)])
     else:
         dh1 = [
             plain([(dqkv, rows, j)], w_qkv, True, half if j else single, f"dh1_{j}")[0]
@@ -1171,28 +1168,40 @@
         dh1 = dh1[0]
         qkv_grad = outer(a1, [(dqkv, rows, j) for j in range(CTX)], "qkv_grad")
         mix_own = plain(gb[0], w_down, False, single, "mix_0")[0]
-        mixed = total_of(y1 + bias_d + mix_own, scatter_send(mix[1:]))
     qkv_part = scatter_f(qkv_grad)
     up_own = after(up_part, arrived)
     up_near = gather_first(up_own)
-    down_out = gather_second(down_part, after(down_near, arrived))
-    dh1 = total_of(after(dh1, up_near), arrived)
+    out_first = []
+    if CTX == 4:
+        k = out_part.shape[0] // 2
+        out_lo, out_hi = after(out_part, arrived)[:k], after(out_part, arrived)[k:]
+        out_first = [swap(out_lo, 1), swap(out_hi, 2)]
+    waiting = (dh1, dqkv, mix_own, flat(du), flat(dz2[:1]))
+    dh1, dqkv, mix_own, du, dz2_own = after(waiting, up_near, out_first)
+    up_bias_grad = sum(jnp.sum(x.astype(single), axis=0) for x in du)
+    down_bias_grad = sum(jnp.sum(x.astype(single), axis=0) for x in dz2_own)
+    dh1 = total_of(dh1, arrived)
+    down_near, up_near, out_first = after((down_near, up_near, out_first))
+    down_out = gather_second(down_part, down_near)
     up_out = gather_second(up_own, up_near)
+    out_second = []
+    if CTX == 4:
+        out_lo = (out_lo.astype(single) + out_first[0].astype(single)).astype(half)
+        out_hi = (out_hi.astype(single) + out_first[1].astype(single)).astype(half)
+        out_second = [(out_lo, swap(out_lo, 2)), (out_hi, swap(out_hi, 1))]
+        mixed = y1 + bias_d + mix_own
+        mixed = jnp.concatenate([total_of(mixed[:n], lows), total_of(mixed[n:], highs)])
+    else:
+        mixed = total_of(y1 + bias_d + mix_own, scatter_send(mix[1:]))
     sums = jnp.sum(dqkv.astype(single), axis=0)
     normed1_own, inv1_own = norm_parts(tokens.astype(single))
     gain1_grad = jnp.sum(dh1 * normed1_own, axis=0)
     shift1_grad = jnp.sum(dh1, axis=0)
-    dy1 = after(dy1, up_out)
+    dy1 = after(dy1, up_out, down_out, out_second)
     input_grad = dy1 + norm_back(normed1_own, inv1_own, gain1, dh1)
 
-    def add_swapped(x, mask):
-        return (x.astype(single) + swap(x, mask).astype(single)).astype(half)
-
     if CTX == 4:
-        k = out_part.shape[0] // 2
-        out_lo, out_hi = add_swapped(out_part[:k], 1), add_swapped(out_part[k:], 2)
-        out_lo, out_hi = (out_lo, swap(out_lo, 2)), (out_hi, swap(out_hi, 1))
-        out_out = [x.astype(single) + y.astype(single) for x, y in (out_lo, out_hi)]
+        out_out = [x.astype(single) + y.astype(single) for x, y in out_second]
         out_out = jnp.concatenate(out_out, axis=0)
     else:
         bit = 1

time: 759 us -> 759 us (level)
  waiting for transfers between devices: 125 us -> 133 us
    ppermute x31, waiting for transfers between devices: 69.3 us -> 125 us  [swap(): return lax.ppermute(x, 'ctx', [(i, i ^ mask) for i in range(n)])]
    all_gather x4, waiting for transfers between devices: 55.9 us -> 8.16 us  [gather_f(): return lax.all_gather(x, 'fsdp', axis=0, tiled=True)]
    pallas_call x4, Pallas kernels: 53.9 us -> 43.3 us  [rows_matmul(): pl.pallas_call(functools.partial(rows_kernel, dot_nt if transposed else d...]
    pallas_call x1, Pallas kernels: 23.2 us -> 33.6 us  [outer(): pl.pallas_call(functools.partial(outer_kernel, len(left)), grid=(m // tm,...]
    unnamed x155 -> x153, local copies, waits for them, and re-layouts: 22.8 us -> 21.1 us
  transfers between devices with their start and end apart: 39 -> 39, of which waited for: 13 -> 14; matrix products, arithmetic and copies ran while one was open for 15% -> 14% of each run, Pallas kernels for 59% -> 59%
where the time goes in v3:
time: 759 us; the launch traced here: 748 us
  Pallas kernels  446 us (59%)
  waiting for transfers between devices  133 us (18%)
  other arithmetic  65.7 us (9%)
  local copies, waits for them, and re-layouts  44.3 us (6%)
  starting transfers between devices  35.2 us (5%)
  between operations  15.5 us (2%)
  matrix products  7.84 us (1%)
    ppermute x31, waiting for transfers between devices, swap(): return lax.ppermute(x, 'ctx', [(i, i ^ mask) for i in range(n)])  125 us
    pallas_call x2, Pallas kernels, moving_call(): pl.pallas_call(kernel, in_specs=[anywhere] * len(operands), out_specs=[an...  121 us
    pallas_call x1, Pallas kernels, feed_back(): pl.pallas_call(feed_back_kernel, in_specs=[anywhere] * 22, out_specs=[any...  104 us
    pallas_call x2, Pallas kernels, attn_call(): pl.pallas_call(kernel, grid_spec=pltpu.PrefetchScalarGridSpec(num_scalar_...  60.6 us
    pallas_call x1, Pallas kernels, heads_back(): pl.pallas_call(functools.partial(heads_back_kernel, part), in_specs=[anyw...  49.1 us
    pallas_call x4, Pallas kernels, rows_matmul(): pl.pallas_call(functools.partial(rows_kernel, dot_nt if transposed else d...  43.3 us
    ppermute x31, starting transfers between devices, swap(): return lax.ppermute(x, 'ctx', [(i, i ^ mask) for i in range(n)])  34.9 us
    pallas_call x1, Pallas kernels, outer(): pl.pallas_call(functools.partial(outer_kernel, len(left)), grid=(m // tm,...  33.6 us
  transfers between devices with their start and end apart: 39, of which 14 were waited for; matrix products, arithmetic and copies ran while one was open for 14% of the time, Pallas kernels for 59%

profile of v3, /device:TPU:0, one launch (start us, length us, event | category | flops | bytes accessed | tf_op | source)
XLA Modules:
  0.0 748.0 jit_solution(17271368554164626837)
XLA Ops:
  18.1 9.0 %gather_small.1 = f32[8,24,128]{2,1,0:T(8,128)} custom-call(f32[24,128]{1,0:T(8,128)} %bitcast.91), custom_call_target="tpu_custom_call" | custom-call | tf_op jit(solution)/shard_map/gather_small/pallas_call | solution.py:884
  31.9 3.9 convert.46
  46.3 15.2 %collective-permute-done = bf16[512,2048]{1,0:T(8,128)(2,1)} collective-permute-done((bf16[512,2048]{1,0:T(8,128)(2,1)S(1)}, bf16[512,2048]{1,0:T(8,128)(2,1)}, u32[]{:S(2)}, u32[]{:S(2)}) %collective-permute-start) | collective-permute-done | bytes 2097184 | tf_op jit(solution)/shard_map/ppermute | solution.py:60
  76.3 5.7 fusion.21
  82.0 6.1 collective-permute-done.2.refs_0_
  91.0 28.0 %qkv.1 = (bf16[2048,1536]{1,0:T(8,128)(2,1)}, bf16[256,2048]{1,0:T(8,128)(2,1)S(1)}, bf16[256,2048]{1,0:T(8,128)(2,1)}, bf16[256,2048]{1,0:T(8,128)(2,1)}, bf16[256,2048]{1,0:T(8,128)(2,1)}) custom-call(bf16[256,2048]{1,0:T(8,128)(2,1)} %collective-permute-done.2.refs_0_, bf16[256,2048]{1,0:T(8,128)(2,1)} %collective-permute-done.3.refs_1_, ...), custom_call_target="tpu_custom_call" | custom-call | flops 12884901 | tf_op jit(solution)/shard_map/qkv/pallas_call | solution.py:499
  122.2 24.4 %attn_forward.1 = bf16[2048,512]{1,0:T(8,128)(2,1)S(1)} custom-call(s32[16]{0:T(128)S(1)} %select_reduce_fusion.inv_ref, f32[4]{0:T(128)S(1)} %multiply_power_fusion.slope_ref, ...), custom_call_target="tpu_custom_call" | custom-call | flops 20000000 | bytes 8388 | tf_op jit(solution)/shard_map/attn_forward/pallas_call | solution.py:233
  153.4 12.5 %collective-permute-done.6 = bf16[512,512]{1,0:T(8,128)(2,1)S(1)} collective-permute-done((bf16[512,512]{1,0:T(8,128)(2,1)}, bf16[512,512]{1,0:T(8,128)(2,1)S(1)}, u32[]{:S(2)}, u32[]{:S(2)}) %collective-permute-start.6) | collective-permute-done | bytes 524320 | tf_op jit(solution)/shard_map/ppermute | solution.py:60
  165.9 6.9 collective-permute-done.7
  176.3 7.8 %fusion.44 = (f32[512]{0:T(512)S(1)}, f32[512,2048]{1,0:T(8,128)S(1)}) fusion(f32[2048]{0:T(1024)S(1)} %bitcast.94, bf16[2048,2048]{1,0:T(8,128)(2,1)} %all-gather.7.cloned.1.call-done.refs_6_, bf16[512,512]{1,0:T(8,128)(2,1)} %get-tuple-element.229, bf16[512,512]{1,0:T(8,128)(2,1)} %get-tuple-element.228, bf16[512,512]{1,0:T(8,128)(2,1)S(1)} %get-tuple-element.227, ...), kind=kOutput, calls=%fused_computation.162 | convolution fusion | flops 4307549696 | bytes 16787456 | tf_op jit(solution)/shard_map/dot_general | solution.py:24
  188.4 45.3 %collective-permute-done.9.refs_0_.refs_16_ = bf16[512,2048]{1,0:T(8,128)(2,1)S(1)} collective-permute-done((bf16[512,2048]{1,0:T(8,128)(2,1)S(1)}, bf16[512,2048]{1,0:T(8,128)(2,1)S(1)}, u32[]{:S(2)}, u32[]{:S(2)}) %collective-permute-start.9) | collective-permute-done | bytes 2097184 | tf_op jit(solution)/shard_map/ppermute | solution.py:60
  240.1 4.1 all-gather.9.cloned.1.call-done.refs_1_.refs_2_.refs_14_
  244.2 11.0 %up_gelu_0.1 = (bf16[512,2048]{1,0:T(8,128)(2,1)}, bf16[512,2048]{1,0:T(8,128)(2,1)}) custom-call(bf16[512,2048]{1,0:T(8,128)(2,1)} %copy-done.15, bf16[2048,2048]{1,0:T(8,128)(2,1)} %all-gather.9.cloned.1.call-done.refs_1_.refs_2_.refs_14_, f32[1,2048]{1,0:T(1,128)S(1)} %bitcast.71), custom_call_target="tpu_custom_call" | custom-call | flops 4294967 | bytes 16777 | tf_op jit(solution)/shard_map/up_gelu_0/pallas_call | solution.py:311
  255.2 10.8 %up_gelu_1.1 = (bf16[512,2048]{1,0:T(8,128)(2,1)}, bf16[512,2048]{1,0:T(8,128)(2,1)}) custom-call(bf16[512,2048]{1,0:T(8,128)(2,1)} %copy-done.16, bf16[2048,2048]{1,0:T(8,128)(2,1)} %all-gather.9.cloned.1.call-done.refs_1_.refs_2_.refs_14_, f32[1,2048]{1,0:T(1,128)S(1)} %bitcast.72), custom_call_target="tpu_custom_call" | custom-call | flops 4294967 | bytes 16777 | tf_op jit(solution)/shard_map/up_gelu_1/pallas_call | solution.py:311
  266.0 10.9 %up_gelu_2.1 = (bf16[512,2048]{1,0:T(8,128)(2,1)}, bf16[512,2048]{1,0:T(8,128)(2,1)}) custom-call(bf16[512,2048]{1,0:T(8,128)(2,1)} %copy-done.17, bf16[2048,2048]{1,0:T(8,128)(2,1)} %all-gather.9.cloned.1.call-done.refs_1_.refs_2_.refs_14_, f32[1,2048]{1,0:T(1,128)S(1)} %bitcast.73), custom_call_target="tpu_custom_call" | custom-call | flops 4294967 | bytes 16777 | tf_op jit(solution)/shard_map/up_gelu_2/pallas_call | solution.py:311
  277.8 10.7 %up_gelu_3.1 = (bf16[256,2048]{1,0:T(8,128)(2,1)S(1)}, bf16[256,2048]{1,0:T(8,128)(2,1)}, bf16[256,2048]{1,0:T(8,128)(2,1)}, bf16[256,2048]{1,0:T(8,128)(2,1)}) custom-call(bf16[256,2048]{1,0:T(8,128)(2,1)} %copy-done.21, bf16[256,2048]{1,0:T(8,128)(2,1)} %collective-permute-done.14.refs_1_.refs_19_, ...), custom_call_target="tpu_custom_call" | custom-call | flops 4294967 | bytes 16777 | tf_op jit(solution)/shard_map/up_gelu_3/pallas_call | solution.py:311
  288.6 33.6 %down_grad.1 = bf16[2048,2048]{1,0:T(8,128)(2,1)} custom-call(bf16[512,2048]{1,0:T(8,128)(2,1)} %get-tuple-element.136.refs_0_.refs_1_.refs_7_, bf16[512,2048]{1,0:T(8,128)(2,1)} %get-tuple-element.136.refs_0_.refs_1_.refs_7_, bf16[512,2048]{1,0:T(8,128)(2,1)} %get-tuple-element.139.refs_2_.refs_3_.refs_8_, ...), custom_call_target="tpu_custom_call" | custom-call | flops 17179868 | bytes 25165 | tf_op jit(solution)/shard_map/down_grad/pallas_call | solution.py:384
  322.2 4.1 all-gather.11.cloned.1.call-done.refs_13_.refs_10_.refs_8_
  326.3 104.0 %feed_back.1 = (bf16[512,2048]{1,0:T(8,128)(2,1)}, bf16[512,2048]{1,0:T(8,128)(2,1)}, bf16[512,2048]{1,0:T(8,128)(2,1)}, bf16[256,2048]{1,0:T(8,128)(2,1)}, bf16...) custom-call(bf16[256,2048]{1,0:T(8,128)(2,1)} %get-tuple-element.193, ...), custom_call_target="tpu_custom_call" | custom-call | flops 55834576 | tf_op jit(solution)/shard_map/feed_back/pallas_call | solution.py:642
  433.5 49.1 %heads_back.1 = (f32[512,2048]{1,0:T(8,128)}, bf16[512,2048]{1,0:T(8,128)(2,1)}, f32[8,2048]{1,0:T(8,128)}, bf16[2048,512]{1,0:T(8,128)(2,1)}, bf16[2048,2048]{1...) custom-call(f32[512,2048]{1,0:T(8,128)} %get-tuple-element.152.refs_, ...), custom_call_target="tpu_custom_call" | custom-call | flops 21474836 | tf_op jit(solution)/shard_map/heads_back/pallas_call | solution.py:734
  485.0 36.2 %attn_backward.1.refs_0_ = bf16[2048,1536]{1,0:T(8,128)(2,1)} custom-call(s32[16]{0:T(128)S(1)} %select_reduce_fusion.inv_ref, f32[4]{0:T(128)S(1)} %multiply_power_fusion.slope_ref, ...), custom_call_target="tpu_custom_call" | custom-call | flops 40000000 | bytes 14680 | tf_op jit(solution)/shard_map/attn_backward/pallas_call | solution.py:233
  521.2 92.5 %qkv_back.1 = (f32[512,2048]{1,0:T(8,128)}, bf16[512,2048]{1,0:T(8,128)(2,1)}, bf16[512,2048]{1,0:T(8,128)(2,1)}, bf16[512,2048]{1,0:T(8,128)(2,1)}, bf16[256,20...) custom-call(bf16[2048,1536]{1,0:T(8,128)(2,1)} %attn_backward.1.refs, ...), custom_call_target="tpu_custom_call" | custom-call | flops 30064772 | tf_op jit(solution)/shard_map/qkv_back/pallas_call | solution.py:499
  621.5 18.7 %collective-permute-done.17.refs_1_ = bf16[256,2048]{1,0:T(8,128)(2,1)S(1)} collective-permute-done((bf16[256,2048]{1,0:T(8,128)(2,1)}, bf16[256,2048]{1,0:T(8,128)(2,1)S(1)}, u32[]{:S(2)}, u32[]{:S(2)}) %collective-permute-start.17) | collective-permute-done | bytes 1048608 | tf_op jit(solution)/shard_map/ppermute | solution.py:60
  641.3 7.9 %collective-permute-done.19 = bf16[128,2048]{1,0:T(8,128)(2,1)} collective-permute-done((bf16[128,2048]{1,0:T(8,128)(2,1)}, bf16[128,2048]{1,0:T(8,128)(2,1)}, u32[]{:S(2)}, u32[]{:S(2)}) %collective-permute-start.19) | collective-permute-done | bytes 524320 | tf_op jit(solution)/shard_map/ppermute | solution.py:60
  666.4 6.6 fusion.16
  673.0 3.8 convert_reduce_fusion
  676.9 4.5 add_add_fusion
  687.6 6.6 collective-permute-done.26
  699.2 6.2 fusion.15
  705.5 5.4 lay_out.5
  710.9 6.9 lay_out.4
  722.3 10.5 %reduce_small.1 = f32[24,128]{1,0:T(8,128)} custom-call(f32[8,24,128]{2,1,0:T(8,128)} %bitcast.79), custom_call_target="tpu_custom_call" | custom-call | tf_op jit(solution)/shard_map/reduce_small/pallas_call | solution.py:955
  (322 shorter events, 123.5 us)
Async XLA Ops:
  7.3 83.7 %all-gather.5.cloned.1.call-start = ((), (), s32[]{:S(2)}) async-start(), calls=%async_computation.4 | async-start | bytes 7077888 | tf_op jit(solution)/shard_map/all_gather | solution.py:1019
  9.9 166.4 %all-gather.7.cloned.1.call-start = ((), (), s32[]{:S(2)}) async-start(), calls=%async_computation.5 | async-start | bytes 9437184 | tf_op jit(solution)/shard_map/all_gather | solution.py:1019
  12.7 231.5 %all-gather.9.cloned.1.call-start = ((), (), s32[]{:S(2)}) async-start(), calls=%async_computation.6 | async-start | bytes 9437184 | tf_op jit(solution)/shard_map/all_gather | solution.py:1019
  12.7 48.7 %collective-permute-start = (bf16[512,2048]{1,0:T(8,128)(2,1)S(1)}, bf16[512,2048]{1,0:T(8,128)(2,1)}, u32[]{:S(2)}, u32[]{:S(2)}) collective-permute-start(bf16[512,2048]{1,0:T(8,128)(2,1)S(1)} %copy-done.13), channel_id=1, source_target_pairs={{0,8},{8,0},{16,24},{24,16},{1,9},{9,1},{17,25},{25,17},{2,10},{10... | collective-permute-start | bytes 6291464 | tf_op jit(solution)/shard_map/ppermute | solution.py:60
  15.7 47.2 %collective-permute-start.1 = (bf16[512,2048]{1,0:T(8,128)(2,1)S(1)}, bf16[512,2048]{1,0:T(8,128)(2,1)}, u32[]{:S(2)}, u32[]{:S(2)}) collective-permute-start(bf16[512,2048]{1,0:T(8,128)(2,1)S(1)} %copy-done.13), channel_id=1, source_target_pairs={{0,16},{8,24},{16,0},{24,8},{1,17},{9,25},{17,1},{25,9},{2,18},{10... | collective-permute-start | bytes 6291464 | tf_op jit(solution)/shard_map/ppermute | solution.py:60
  64.3 23.9 %collective-permute-start.2 = (bf16[256,2048]{1,0:T(8,128)(2,1)S(1)}, bf16[256,2048]{1,0:T(8,128)(2,1)}, u32[]{:S(2)}, u32[]{:S(2)}) collective-permute-start(bf16[256,2048]{1,0:T(8,128)(2,1)S(1)} %slice.176), channel_id=1, source_target_pairs={{0,16},{8,24},{16,0},{24,8},{1,17},{9,25},{17,1},{25,9},{2,18},{10... | collective-permute-start | bytes 3145736 | tf_op jit(solution)/shard_map/ppermute | solution.py:60
  67.2 23.6 %collective-permute-start.3 = (bf16[256,2048]{1,0:T(8,128)(2,1)S(1)}, bf16[256,2048]{1,0:T(8,128)(2,1)}, u32[]{:S(2)}, u32[]{:S(2)}) collective-permute-start(bf16[256,2048]{1,0:T(8,128)(2,1)S(1)} %slice.177), channel_id=1, source_target_pairs={{0,8},{8,0},{16,24},{24,16},{1,9},{9,1},{17,25},{25,17},{2,10},{10... | collective-permute-start | bytes 3145736 | tf_op jit(solution)/shard_map/ppermute | solution.py:60
  90.8 235.5 %all-gather.11.cloned.1.call-start = ((), (), s32[]{:S(2)}) async-start(), calls=%async_computation.7 | async-start | bytes 9437184 | tf_op jit(solution)/shard_map/all_gather | solution.py:1019
  120.0 313.5 %reduce-scatter.5.cloned.1.call-start = ((), (), s32[]{:S(2)}) async-start(), calls=%async_computation.8 | async-start | bytes 9437184 | tf_op jit(solution)/shard_map/reduce_scatter | solution.py:1055
  120.1 27.8 %collective-permute-start.4 = (bf16[256,2048]{1,0:T(8,128)(2,1)S(1)}, bf16[256,2048]{1,0:T(8,128)(2,1)S(1)}, u32[]{:S(2)}, u32[]{:S(2)}) collective-permute-start(bf16[256,2048]{1,0:T(8,128)(2,1)S(1)} %copy-done.14), channel_id=1, source_target_pairs={{0,8},{8,0},{16,24},{24,16},{1,9},{9,1},{17,25},{25,17},{2,10},{10... | collective-permute-start | bytes 3145736 | tf_op jit(solution)/shard_map/ppermute | solution.py:60
  121.5 27.4 %collective-permute-start.5 = (bf16[256,2048]{1,0:T(8,128)(2,1)}, bf16[256,2048]{1,0:T(8,128)(2,1)S(1)}, u32[]{:S(2)}, u32[]{:S(2)}) collective-permute-start(bf16[256,2048]{1,0:T(8,128)(2,1)} %get-tuple-element.193.refs_9_.refs_8_.refs_0_), channel_id=1, source_target_pairs={{0,16},{8,24},{16,0},{24,8},{1,17},{9,25},{17,1},{25,9},{2,18},{10... | collective-permute-start | bytes 3145736 | tf_op jit(solution)/shard_map/ppermute | solution.py:60
  186.1 47.6 %collective-permute-start.9 = (bf16[512,2048]{1,0:T(8,128)(2,1)S(1)}, bf16[512,2048]{1,0:T(8,128)(2,1)S(1)}, u32[]{:S(2)}, u32[]{:S(2)}) collective-permute-start(bf16[512,2048]{1,0:T(8,128)(2,1)S(1)} %add_convert_fusion.refs_0_.refs_15_), channel_id=1, source_target_pairs={{0,8},{8,0},{16,24},{24,16},{1,9},{9,1},{17,25},{25,17},{2,10},{10... | collective-permute-start | bytes 6291464 | tf_op jit(solution)/shard_map/ppermute | solution.py:60
  187.7 48.6 %collective-permute-start.10 = (bf16[512,2048]{1,0:T(8,128)(2,1)S(1)}, bf16[512,2048]{1,0:T(8,128)(2,1)S(1)}, u32[]{:S(2)}, u32[]{:S(2)}) collective-permute-start(bf16[512,2048]{1,0:T(8,128)(2,1)S(1)} %add_convert_fusion.refs_0_.refs_15_), channel_id=1, source_target_pairs={{0,16},{8,24},{16,0},{24,8},{1,17},{9,25},{17,1},{25,9},{2,18},{10... | collective-permute-start | bytes 6291464 | tf_op jit(solution)/shard_map/ppermute | solution.py:60
  234.9 42.0 %collective-permute-start.13 = (bf16[256,2048]{1,0:T(8,128)(2,1)}, bf16[256,2048]{1,0:T(8,128)(2,1)S(1)}, u32[]{:S(2)}, u32[]{:S(2)}) collective-permute-start(bf16[256,2048]{1,0:T(8,128)(2,1)} %slice.243), channel_id=1, source_target_pairs={{0,16},{8,24},{16,0},{24,8},{1,17},{9,25},{17,1},{25,9},{2,18},{10... | collective-permute-start | bytes 3145736 | tf_op jit(solution)/shard_map/ppermute | solution.py:60
  237.5 39.4 %collective-permute-start.14 = (bf16[256,2048]{1,0:T(8,128)(2,1)}, bf16[256,2048]{1,0:T(8,128)(2,1)}, u32[]{:S(2)}, u32[]{:S(2)}) collective-permute-start(bf16[256,2048]{1,0:T(8,128)(2,1)} %slice.244), channel_id=1, source_target_pairs={{0,8},{8,0},{16,24},{24,16},{1,9},{9,1},{17,25},{25,17},{2,10},{10... | collective-permute-start | bytes 3145736 | tf_op jit(solution)/shard_map/ppermute | solution.py:60
  238.3 50.3 %collective-permute-start.11 = (bf16[256,2048]{1,0:T(8,128)(2,1)}, bf16[256,2048]{1,0:T(8,128)(2,1)}, u32[]{:S(2)}, u32[]{:S(2)}) collective-permute-start(bf16[256,2048]{1,0:T(8,128)(2,1)} %get-tuple-element.131.refs_10_.refs_2_), channel_id=1, source_target_pairs={{0,16},{8,24},{16,0},{24,8},{1,17},{9,25},{17,1},{25,9},{2,18},{10... | collective-permute-start | bytes 3145736 | tf_op jit(solution)/shard_map/ppermute | solution.py:60
  239.5 49.1 %collective-permute-start.12 = (bf16[256,2048]{1,0:T(8,128)(2,1)}, bf16[256,2048]{1,0:T(8,128)(2,1)}, u32[]{:S(2)}, u32[]{:S(2)}) collective-permute-start(bf16[256,2048]{1,0:T(8,128)(2,1)} %get-tuple-element.132.refs_13_.refs_5_), channel_id=1, source_target_pairs={{0,8},{8,0},{16,24},{24,16},{1,9},{9,1},{17,25},{25,17},{2,10},{10... | collective-permute-start | bytes 3145736 | tf_op jit(solution)/shard_map/ppermute | solution.py:60
  322.2 199.0 %reduce-scatter.7.cloned.1.call-start = ((), (), s32[]{:S(2)}) async-start(), calls=%async_computation.9 | async-start | bytes 9437184 | tf_op jit(solution)/shard_map/reduce_scatter | solution.py:1055
  430.4 185.6 %reduce-scatter.9.cloned.1.call-start = ((), (), s32[]{:S(2)}) async-start(), calls=%async_computation.10 | async-start | bytes 9437184 | tf_op jit(solution)/shard_map/reduce_scatter | solution.py:1055
  482.6 214.5 %reduce-scatter.11.cloned.1.call-start = ((), (), s32[]{:S(2)}) async-start(), calls=%async_computation.11 | async-start | bytes 7077888 | tf_op jit(solution)/shard_map/reduce_scatter | solution.py:1055
  482.7 38.5 %collective-permute-start.15 = (bf16[256,2048]{1,0:T(8,128)(2,1)}, bf16[256,2048]{1,0:T(8,128)(2,1)}, u32[]{:S(2)}, u32[]{:S(2)}) collective-permute-start(bf16[256,2048]{1,0:T(8,128)(2,1)} %get-tuple-element.158), channel_id=1, source_target_pairs={{0,8},{8,0},{16,24},{24,16},{1,9},{9,1},{17,25},{25,17},{2,10},{10... | collective-permute-start | bytes 3145736 | tf_op jit(solution)/shard_map/ppermute | solution.py:60
  483.8 37.4 %collective-permute-start.16 = (bf16[256,2048]{1,0:T(8,128)(2,1)S(1)}, bf16[256,2048]{1,0:T(8,128)(2,1)}, u32[]{:S(2)}, u32[]{:S(2)}) collective-permute-start(bf16[256,2048]{1,0:T(8,128)(2,1)S(1)} %copy-done.57), channel_id=1, source_target_pairs={{0,16},{8,24},{16,0},{24,8},{1,17},{9,25},{17,1},{25,9},{2,18},{10... | collective-permute-start | bytes 3145736 | tf_op jit(solution)/shard_map/ppermute | solution.py:60
  613.8 26.4 %collective-permute-start.17 = (bf16[256,2048]{1,0:T(8,128)(2,1)}, bf16[256,2048]{1,0:T(8,128)(2,1)S(1)}, u32[]{:S(2)}, u32[]{:S(2)}) collective-permute-start(bf16[256,2048]{1,0:T(8,128)(2,1)} %reduce-scatter.7.cloned.1.call-done.refs_0_), channel_id=1, source_target_pairs={{0,8},{8,0},{16,24},{24,16},{1,9},{9,1},{17,25},{25,17},{2,10},{10... | collective-permute-start | bytes 3145736 | tf_op jit(solution)/shard_map/ppermute | solution.py:60
  614.9 26.4 %collective-permute-start.18 = (bf16[256,2048]{1,0:T(8,128)(2,1)}, bf16[256,2048]{1,0:T(8,128)(2,1)}, u32[]{:S(2)}, u32[]{:S(2)}) collective-permute-start(bf16[256,2048]{1,0:T(8,128)(2,1)} %reduce-scatter.7.cloned.1.call-done.refs_0_), channel_id=1, source_target_pairs={{0,16},{8,24},{16,0},{24,8},{1,17},{9,25},{17,1},{25,9},{2,18},{10... | collective-permute-start | bytes 3145736 | tf_op jit(solution)/shard_map/ppermute | solution.py:60
  618.3 30.9 %collective-permute-start.19 = (bf16[128,2048]{1,0:T(8,128)(2,1)}, bf16[128,2048]{1,0:T(8,128)(2,1)}, u32[]{:S(2)}, u32[]{:S(2)}) collective-permute-start(bf16[128,2048]{1,0:T(8,128)(2,1)} %get-tuple-element.239), channel_id=1, source_target_pairs={{0,8},{8,0},{16,24},{24,16},{1,9},{9,1},{17,25},{25,17},{2,10},{10... | collective-permute-start | bytes 1572872 | tf_op jit(solution)/shard_map/ppermute | solution.py:60
  619.2 30.6 %collective-permute-start.20 = (bf16[128,2048]{1,0:T(8,128)(2,1)}, bf16[128,2048]{1,0:T(8,128)(2,1)}, u32[]{:S(2)}, u32[]{:S(2)}) collective-permute-start(bf16[128,2048]{1,0:T(8,128)(2,1)} %get-tuple-element.238), channel_id=1, source_target_pairs={{0,16},{8,24},{16,0},{24,8},{1,17},{9,25},{17,1},{25,9},{2,18},{10... | collective-permute-start | bytes 1572872 | tf_op jit(solution)/shard_map/ppermute | solution.py:60
  650.6 33.6 %collective-permute-start.23 = (bf16[128,2048]{1,0:T(8,128)(2,1)}, bf16[128,2048]{1,0:T(8,128)(2,1)}, u32[]{:S(2)}, u32[]{:S(2)}) collective-permute-start(bf16[128,2048]{1,0:T(8,128)(2,1)} %slice.199), channel_id=1, source_target_pairs={{0,16},{8,24},{16,0},{24,8},{1,17},{9,25},{17,1},{25,9},{2,18},{10... | collective-permute-start | bytes 1572872 | tf_op jit(solution)/shard_map/ppermute | solution.py:60
  652.6 35.0 %collective-permute-start.24 = (bf16[128,2048]{1,0:T(8,128)(2,1)}, bf16[128,2048]{1,0:T(8,128)(2,1)}, u32[]{:S(2)}, u32[]{:S(2)}) collective-permute-start(bf16[128,2048]{1,0:T(8,128)(2,1)} %slice.200), channel_id=1, source_target_pairs={{0,8},{8,0},{16,24},{24,16},{1,9},{9,1},{17,25},{25,17},{2,10},{10... | collective-permute-start | bytes 1572872 | tf_op jit(solution)/shard_map/ppermute | solution.py:60
  654.4 33.2 %collective-permute-start.21 = (bf16[128,2048]{1,0:T(8,128)(2,1)}, bf16[128,2048]{1,0:T(8,128)(2,1)}, u32[]{:S(2)}, u32[]{:S(2)}) collective-permute-start(bf16[128,2048]{1,0:T(8,128)(2,1)} %slice.197), channel_id=1, source_target_pairs={{0,16},{8,24},{16,0},{24,8},{1,17},{9,25},{17,1},{25,9},{2,18},{10... | collective-permute-start | bytes 1572872 | tf_op jit(solution)/shard_map/ppermute | solution.py:60
  657.4 30.2 %collective-permute-start.22 = (bf16[128,2048]{1,0:T(8,128)(2,1)}, bf16[128,2048]{1,0:T(8,128)(2,1)}, u32[]{:S(2)}, u32[]{:S(2)}) collective-permute-start(bf16[128,2048]{1,0:T(8,128)(2,1)} %slice.198), channel_id=1, source_target_pairs={{0,8},{8,0},{16,24},{24,16},{1,9},{9,1},{17,25},{25,17},{2,10},{10... | collective-permute-start | bytes 1572872 | tf_op jit(solution)/shard_map/ppermute | solution.py:60
  660.9 26.7 %collective-permute-start.25 = (bf16[128,2048]{1,0:T(8,128)(2,1)}, bf16[128,2048]{1,0:T(8,128)(2,1)}, u32[]{:S(2)}, u32[]{:S(2)}) collective-permute-start(bf16[128,2048]{1,0:T(8,128)(2,1)} %get-tuple-element.237), channel_id=1, source_target_pairs={{0,16},{8,24},{16,0},{24,8},{1,17},{9,25},{17,1},{25,9},{2,18},{10... | collective-permute-start | bytes 1572872 | tf_op jit(solution)/shard_map/ppermute | solution.py:60
  698.1 21.5 %collective-permute-start.28 = (bf16[256,1536]{1,0:T(8,128)(2,1)}, bf16[256,1536]{1,0:T(8,128)(2,1)S(1)}, u32[]{:S(2)}, u32[]{:S(2)}) collective-permute-start(bf16[256,1536]{1,0:T(8,128)(2,1)} %reduce-scatter.11.cloned.1.call-done.refs_0_), channel_id=1, source_target_pairs={{0,16},{8,24},{16,0},{24,8},{1,17},{9,25},{17,1},{25,9},{2,18},{10... | collective-permute-start | bytes 2359304 | tf_op jit(solution)/shard_map/ppermute | solution.py:60
  (66 other events, 784.4 us)
Sparse Core Ops, SparseCore 0:
  10.3 68.1 all-gather.4
  80.7 80.6 all-gather.6
  163.6 80.5 all-gather.8
  245.6 80.6 all-gather.10
  329.0 88.0 reduce-scatter.4
  430.5 87.0 reduce-scatter.6
  519.9 87.9 reduce-scatter.8
  614.0 66.9 reduce-scatter.10

commit v4 on v3

--- a/solution.py
+++ b/solution.py
@@ -1176,11 +1176,9 @@
         k = out_part.shape[0] // 2
         out_lo, out_hi = after(out_part, arrived)[:k], after(out_part, arrived)[k:]
         out_first = [swap(out_lo, 1), swap(out_hi, 2)]
-    waiting = (dh1, dqkv, mix_own, flat(du), flat(dz2[:1]))
-    dh1, dqkv, mix_own, du, dz2_own = after(waiting, up_near, out_first)
+    mix_own, du, dz2_own = after((mix_own, flat(du), flat(dz2[:1])), out_part)
     up_bias_grad = sum(jnp.sum(x.astype(single), axis=0) for x in du)
     down_bias_grad = sum(jnp.sum(x.astype(single), axis=0) for x in dz2_own)
-    dh1 = total_of(dh1, arrived)
     down_near, up_near, out_first = after((down_near, up_near, out_first))
     down_out = gather_second(down_part, down_near)
     up_out = gather_second(up_own, up_near)
@@ -1188,11 +1186,14 @@
     if CTX == 4:
         out_lo = (out_lo.astype(single) + out_first[0].astype(single)).astype(half)
         out_hi = (out_hi.astype(single) + out_first[1].astype(single)).astype(half)
+        out_lo, out_hi = after((out_lo, out_hi))
+        dh1, dqkv = after((dh1, dqkv), out_lo, out_hi)
         out_second = [(out_lo, swap(out_lo, 2)), (out_hi, swap(out_hi, 1))]
         mixed = y1 + bias_d + mix_own
         mixed = jnp.concatenate([total_of(mixed[:n], lows), total_of(mixed[n:], highs)])
     else:
         mixed = total_of(y1 + bias_d + mix_own, scatter_send(mix[1:]))
+    dh1 = total_of(dh1, arrived)
     sums = jnp.sum(dqkv.astype(single), axis=0)
     normed1_own, inv1_own = norm_parts(tokens.astype(single))
     gain1_grad = jnp.sum(dh1 * normed1_own, axis=0)
@@ -1229,11 +1230,12 @@
     sums_in = [out_bias_grad, gain2_grad, shift2_grad, down_bias_grad, spread(up_bias_grad, fpart)]
     sums_in += [gain1_grad, shift1_grad, spread(sums[:part], part), spread(sums[2 * part :], part)]
     qkv_near = gather_first(qkv_part)
-    sums_in[5] = after(sums_in[5], qkv_near)
+    sums_in[5] = after(sums_in[5], qkv_part)
     sums_out = reduced(sums_in, 2)
+    down_out = lay_out(0, after(down_out, sums_out), c, width // min(width, 512))
+    qkv_near = after(qkv_near, down_out)
     qkv_out = lay_out(1, gather_second(qkv_part, qkv_near), c, 3)
-    down_out = lay_out(0, after(down_out, qkv_part), c, width // min(width, 512))
-    up_out = lay_out(1, after(up_out, qkv_part), c, nf)
+    up_out = lay_out(1, after(up_out, qkv_near), c, nf)
     out_bias_out, gain2_out, shift2_out, down_bias_out, up_bias_out = sums_out[:5]
     gain1_out, shift1_out, q_bias_out, v_bias_out = sums_out[5:]
     return (

time: 759 us -> 760 us (level)
    unnamed x153 -> x175, local copies, waits for them, and re-layouts: 21.1 us -> 19.4 us
  transfers between devices with their start and end apart: 39 -> 39, of which waited for: 14 -> 16; matrix products, arithmetic and copies ran while one was open for 14% -> 13% of each run, Pallas kernels for 59% -> 59%
where the time goes in v4:
time: 760 us; the launch traced here: 749 us
  Pallas kernels  449 us (59%)
  waiting for transfers between devices  133 us (18%)
  other arithmetic  64.4 us (8%)
  local copies, waits for them, and re-layouts  43 us (6%)
  starting transfers between devices  36.2 us (5%)
  between operations  15.6 us (2%)
  matrix products  7.85 us (1%)
    ppermute x31, waiting for transfers between devices, swap(): return lax.ppermute(x, 'ctx', [(i, i ^ mask) for i in range(n)])  125 us
    pallas_call x2, Pallas kernels, moving_call(): pl.pallas_call(kernel, in_specs=[anywhere] * len(operands), out_specs=[an...  120 us
    pallas_call x1, Pallas kernels, feed_back(): pl.pallas_call(feed_back_kernel, in_specs=[anywhere] * 22, out_specs=[any...  104 us
    pallas_call x2, Pallas kernels, attn_call(): pl.pallas_call(kernel, grid_spec=pltpu.PrefetchScalarGridSpec(num_scalar_...  60.6 us
    pallas_call x1, Pallas kernels, heads_back(): pl.pallas_call(functools.partial(heads_back_kernel, part), in_specs=[anyw...  48.9 us
    pallas_call x4, Pallas kernels, rows_matmul(): pl.pallas_call(functools.partial(rows_kernel, dot_nt if transposed else d...  43.4 us
    ppermute x31, starting transfers between devices, swap(): return lax.ppermute(x, 'ctx', [(i, i ^ mask) for i in range(n)])  35.9 us
    pallas_call x1, Pallas kernels, outer(): pl.pallas_call(functools.partial(outer_kernel, len(left)), grid=(m // tm,...  33.6 us
  transfers between devices with their start and end apart: 39, of which 16 were waited for; matrix products, arithmetic and copies ran while one was open for 13% of the time, Pallas kernels for 59%

profile of v4, /device:TPU:0, one launch (start us, length us, event | category | flops | bytes accessed | tf_op | source)
XLA Modules:
  0.0 749.2 jit_solution(6782488022557912740)
XLA Ops:
  18.1 9.0 %gather_small.1 = f32[8,24,128]{2,1,0:T(8,128)} custom-call(f32[24,128]{1,0:T(8,128)} %bitcast.93), custom_call_target="tpu_custom_call" | custom-call | tf_op jit(solution)/shard_map/gather_small/pallas_call | solution.py:884
  31.9 3.9 convert.46
  46.3 15.1 %collective-permute-done = bf16[512,2048]{1,0:T(8,128)(2,1)} collective-permute-done((bf16[512,2048]{1,0:T(8,128)(2,1)S(1)}, bf16[512,2048]{1,0:T(8,128)(2,1)}, u32[]{:S(2)}, u32[]{:S(2)}) %collective-permute-start) | collective-permute-done | bytes 2097184 | tf_op jit(solution)/shard_map/ppermute | solution.py:60
  76.3 5.7 fusion.21
  82.0 6.1 collective-permute-done.2.refs_0_
  91.0 27.9 %qkv.1 = (bf16[2048,1536]{1,0:T(8,128)(2,1)}, bf16[256,2048]{1,0:T(8,128)(2,1)S(1)}, bf16[256,2048]{1,0:T(8,128)(2,1)}, bf16[256,2048]{1,0:T(8,128)(2,1)}, bf16[256,2048]{1,0:T(8,128)(2,1)}) custom-call(bf16[256,2048]{1,0:T(8,128)(2,1)} %collective-permute-done.2.refs_0_, bf16[256,2048]{1,0:T(8,128)(2,1)} %collective-permute-done.3.refs_1_, ...), custom_call_target="tpu_custom_call" | custom-call | flops 12884901 | tf_op jit(solution)/shard_map/qkv/pallas_call | solution.py:499
  122.1 24.4 %attn_forward.1 = bf16[2048,512]{1,0:T(8,128)(2,1)S(1)} custom-call(s32[16]{0:T(128)S(1)} %select_reduce_fusion.inv_ref, f32[4]{0:T(128)S(1)} %multiply_power_fusion.slope_ref, ...), custom_call_target="tpu_custom_call" | custom-call | flops 20000000 | bytes 8388 | tf_op jit(solution)/shard_map/attn_forward/pallas_call | solution.py:233
  153.4 12.5 %collective-permute-done.6 = bf16[512,512]{1,0:T(8,128)(2,1)S(1)} collective-permute-done((bf16[512,512]{1,0:T(8,128)(2,1)}, bf16[512,512]{1,0:T(8,128)(2,1)S(1)}, u32[]{:S(2)}, u32[]{:S(2)}) %collective-permute-start.6) | collective-permute-done | bytes 524320 | tf_op jit(solution)/shard_map/ppermute | solution.py:60
  165.9 6.9 collective-permute-done.7
  176.2 7.9 %fusion.44 = (f32[512]{0:T(512)S(1)}, f32[512,2048]{1,0:T(8,128)S(1)}) fusion(f32[2048]{0:T(1024)S(1)} %bitcast.96, bf16[2048,2048]{1,0:T(8,128)(2,1)} %all-gather.7.cloned.1.call-done.refs_6_, bf16[512,512]{1,0:T(8,128)(2,1)} %get-tuple-element.237, bf16[512,512]{1,0:T(8,128)(2,1)} %get-tuple-element.236, bf16[512,512]{1,0:T(8,128)(2,1)S(1)} %get-tuple-element.235, ...), kind=kOutput, calls=%fused_computation.162 | convolution fusion | flops 4307549696 | bytes 16787456 | tf_op jit(solution)/shard_map/dot_general | solution.py:24
  188.4 45.3 %collective-permute-done.9.refs_0_.refs_16_ = bf16[512,2048]{1,0:T(8,128)(2,1)S(1)} collective-permute-done((bf16[512,2048]{1,0:T(8,128)(2,1)S(1)}, bf16[512,2048]{1,0:T(8,128)(2,1)S(1)}, u32[]{:S(2)}, u32[]{:S(2)}) %collective-permute-start.9) | collective-permute-done | bytes 2097184 | tf_op jit(solution)/shard_map/ppermute | solution.py:60
  240.1 4.1 all-gather.9.cloned.1.call-done.refs_1_.refs_2_.refs_14_
  244.2 10.9 %up_gelu_0.1 = (bf16[512,2048]{1,0:T(8,128)(2,1)}, bf16[512,2048]{1,0:T(8,128)(2,1)}) custom-call(bf16[512,2048]{1,0:T(8,128)(2,1)} %copy-done.23, bf16[2048,2048]{1,0:T(8,128)(2,1)} %all-gather.9.cloned.1.call-done.refs_1_.refs_2_.refs_14_, f32[1,2048]{1,0:T(1,128)S(1)} %bitcast.71), custom_call_target="tpu_custom_call" | custom-call | flops 4294967 | bytes 16777 | tf_op jit(solution)/shard_map/up_gelu_0/pallas_call | solution.py:311
  255.1 10.9 %up_gelu_1.1 = (bf16[512,2048]{1,0:T(8,128)(2,1)}, bf16[512,2048]{1,0:T(8,128)(2,1)}) custom-call(bf16[512,2048]{1,0:T(8,128)(2,1)} %copy-done.24, bf16[2048,2048]{1,0:T(8,128)(2,1)} %all-gather.9.cloned.1.call-done.refs_1_.refs_2_.refs_14_, f32[1,2048]{1,0:T(1,128)S(1)} %bitcast.72), custom_call_target="tpu_custom_call" | custom-call | flops 4294967 | bytes 16777 | tf_op jit(solution)/shard_map/up_gelu_1/pallas_call | solution.py:311
  266.0 10.8 %up_gelu_2.1 = (bf16[512,2048]{1,0:T(8,128)(2,1)}, bf16[512,2048]{1,0:T(8,128)(2,1)}) custom-call(bf16[512,2048]{1,0:T(8,128)(2,1)} %copy-done.25, bf16[2048,2048]{1,0:T(8,128)(2,1)} %all-gather.9.cloned.1.call-done.refs_1_.refs_2_.refs_14_, f32[1,2048]{1,0:T(1,128)S(1)} %bitcast.73), custom_call_target="tpu_custom_call" | custom-call | flops 4294967 | bytes 16777 | tf_op jit(solution)/shard_map/up_gelu_2/pallas_call | solution.py:311
  277.9 10.7 %up_gelu_3.1 = (bf16[256,2048]{1,0:T(8,128)(2,1)S(1)}, bf16[256,2048]{1,0:T(8,128)(2,1)}, bf16[256,2048]{1,0:T(8,128)(2,1)}, bf16[256,2048]{1,0:T(8,128)(2,1)}) custom-call(bf16[256,2048]{1,0:T(8,128)(2,1)} %copy-done.30, bf16[256,2048]{1,0:T(8,128)(2,1)} %collective-permute-done.14.refs_1_.refs_19_, ...), custom_call_target="tpu_custom_call" | custom-call | flops 4294967 | bytes 16777 | tf_op jit(solution)/shard_map/up_gelu_3/pallas_call | solution.py:311
  288.6 33.6 %down_grad.1 = bf16[2048,2048]{1,0:T(8,128)(2,1)} custom-call(bf16[512,2048]{1,0:T(8,128)(2,1)} %get-tuple-element.140.refs_0_.refs_1_.refs_7_, bf16[512,2048]{1,0:T(8,128)(2,1)} %get-tuple-element.140.refs_0_.refs_1_.refs_7_, bf16[512,2048]{1,0:T(8,128)(2,1)} %get-tuple-element.143.refs_2_.refs_3_.refs_8_, ...), custom_call_target="tpu_custom_call" | custom-call | flops 17179868 | bytes 25165 | tf_op jit(solution)/shard_map/down_grad/pallas_call | solution.py:384
  322.3 4.1 all-gather.11.cloned.1.call-done.refs_13_.refs_10_.refs_8_
  326.3 104.0 %feed_back.1 = (bf16[512,2048]{1,0:T(8,128)(2,1)}, bf16[512,2048]{1,0:T(8,128)(2,1)}, bf16[512,2048]{1,0:T(8,128)(2,1)}, bf16[256,2048]{1,0:T(8,128)(2,1)}, bf16...) custom-call(bf16[256,2048]{1,0:T(8,128)(2,1)} %get-tuple-element.199, ...), custom_call_target="tpu_custom_call" | custom-call | flops 55834576 | tf_op jit(solution)/shard_map/feed_back/pallas_call | solution.py:642
  433.5 48.9 %heads_back.1 = (f32[512,2048]{1,0:T(8,128)}, bf16[512,2048]{1,0:T(8,128)(2,1)}, f32[8,2048]{1,0:T(8,128)}, bf16[2048,512]{1,0:T(8,128)(2,1)}, bf16[2048,2048]{1...) custom-call(f32[512,2048]{1,0:T(8,128)} %get-tuple-element.156.refs_, ...), custom_call_target="tpu_custom_call" | custom-call | flops 21474836 | tf_op jit(solution)/shard_map/heads_back/pallas_call | solution.py:734
  484.9 36.2 %attn_backward.1.refs_0_ = bf16[2048,1536]{1,0:T(8,128)(2,1)} custom-call(s32[16]{0:T(128)S(1)} %select_reduce_fusion.inv_ref, f32[4]{0:T(128)S(1)} %multiply_power_fusion.slope_ref, ...), custom_call_target="tpu_custom_call" | custom-call | flops 40000000 | bytes 14680 | tf_op jit(solution)/shard_map/attn_backward/pallas_call | solution.py:233
  521.2 92.5 %qkv_back.1 = (f32[512,2048]{1,0:T(8,128)}, bf16[512,2048]{1,0:T(8,128)(2,1)}, bf16[512,2048]{1,0:T(8,128)(2,1)}, bf16[512,2048]{1,0:T(8,128)(2,1)}, bf16[256,20...) custom-call(bf16[2048,1536]{1,0:T(8,128)(2,1)} %attn_backward.1.refs, ...), custom_call_target="tpu_custom_call" | custom-call | flops 30064772 | tf_op jit(solution)/shard_map/qkv_back/pallas_call | solution.py:499
  628.4 4.5 add_add_fusion
  642.9 7.9 %collective-permute-done.19 = bf16[128,2048]{1,0:T(8,128)(2,1)} collective-permute-done((bf16[128,2048]{1,0:T(8,128)(2,1)}, bf16[128,2048]{1,0:T(8,128)(2,1)}, u32[]{:S(2)}, u32[]{:S(2)}) %collective-permute-start.19) | collective-permute-done | bytes 524320 | tf_op jit(solution)/shard_map/ppermute | solution.py:60
  657.4 4.0 fusion.16
  666.9 13.5 %collective-permute-done.23.refs_3_ = bf16[128,2048]{1,0:T(8,128)(2,1)S(1)} collective-permute-done((bf16[128,2048]{1,0:T(8,128)(2,1)S(1)}, bf16[128,2048]{1,0:T(8,128)(2,1)S(1)}, u32[]{:S(2)}, u32[]{:S(2)}) %collective-permute-start.23) | collective-permute-done | bytes 524320 | tf_op jit(solution)/shard_map/ppermute | solution.py:60
  682.4 5.5 collective-permute-done.21.refs_3_
  693.1 6.3 fusion.15
  702.1 13.2 %reduce_small.1 = f32[24,128]{1,0:T(8,128)} custom-call(f32[8,24,128]{2,1,0:T(8,128)} %bitcast.81), custom_call_target="tpu_custom_call" | custom-call | tf_op jit(solution)/shard_map/reduce_small/pallas_call | solution.py:955
  719.1 5.0 lay_out.3
  731.4 6.6 lay_out.5
  738.0 4.1 lay_out.4
  (345 shorter events, 131.4 us)
Async XLA Ops:
  7.3 83.7 %all-gather.5.cloned.1.call-start = ((), (), s32[]{:S(2)}) async-start(), calls=%async_computation.4 | async-start | bytes 7077888 | tf_op jit(solution)/shard_map/all_gather | solution.py:1019
  9.9 166.3 %all-gather.7.cloned.1.call-start = ((), (), s32[]{:S(2)}) async-start(), calls=%async_computation.5 | async-start | bytes 9437184 | tf_op jit(solution)/shard_map/all_gather | solution.py:1019
  12.7 231.5 %all-gather.9.cloned.1.call-start = ((), (), s32[]{:S(2)}) async-start(), calls=%async_computation.6 | async-start | bytes 9437184 | tf_op jit(solution)/shard_map/all_gather | solution.py:1019
  12.7 48.7 %collective-permute-start = (bf16[512,2048]{1,0:T(8,128)(2,1)S(1)}, bf16[512,2048]{1,0:T(8,128)(2,1)}, u32[]{:S(2)}, u32[]{:S(2)}) collective-permute-start(bf16[512,2048]{1,0:T(8,128)(2,1)S(1)} %copy-done.19), channel_id=1, source_target_pairs={{0,8},{8,0},{16,24},{24,16},{1,9},{9,1},{17,25},{25,17},{2,10},{10... | collective-permute-start | bytes 6291464 | tf_op jit(solution)/shard_map/ppermute | solution.py:60
  15.8 47.2 %collective-permute-start.1 = (bf16[512,2048]{1,0:T(8,128)(2,1)S(1)}, bf16[512,2048]{1,0:T(8,128)(2,1)}, u32[]{:S(2)}, u32[]{:S(2)}) collective-permute-start(bf16[512,2048]{1,0:T(8,128)(2,1)S(1)} %copy-done.19), channel_id=1, source_target_pairs={{0,16},{8,24},{16,0},{24,8},{1,17},{9,25},{17,1},{25,9},{2,18},{10... | collective-permute-start | bytes 6291464 | tf_op jit(solution)/shard_map/ppermute | solution.py:60
  64.3 23.9 %collective-permute-start.2 = (bf16[256,2048]{1,0:T(8,128)(2,1)S(1)}, bf16[256,2048]{1,0:T(8,128)(2,1)}, u32[]{:S(2)}, u32[]{:S(2)}) collective-permute-start(bf16[256,2048]{1,0:T(8,128)(2,1)S(1)} %slice.176), channel_id=1, source_target_pairs={{0,16},{8,24},{16,0},{24,8},{1,17},{9,25},{17,1},{25,9},{2,18},{10... | collective-permute-start | bytes 3145736 | tf_op jit(solution)/shard_map/ppermute | solution.py:60
  67.2 23.6 %collective-permute-start.3 = (bf16[256,2048]{1,0:T(8,128)(2,1)S(1)}, bf16[256,2048]{1,0:T(8,128)(2,1)}, u32[]{:S(2)}, u32[]{:S(2)}) collective-permute-start(bf16[256,2048]{1,0:T(8,128)(2,1)S(1)} %slice.177), channel_id=1, source_target_pairs={{0,8},{8,0},{16,24},{24,16},{1,9},{9,1},{17,25},{25,17},{2,10},{10... | collective-permute-start | bytes 3145736 | tf_op jit(solution)/shard_map/ppermute | solution.py:60
  90.8 235.5 %all-gather.11.cloned.1.call-start = ((), (), s32[]{:S(2)}) async-start(), calls=%async_computation.7 | async-start | bytes 9437184 | tf_op jit(solution)/shard_map/all_gather | solution.py:1019
  119.9 313.5 %reduce-scatter.5.cloned.1.call-start = ((), (), s32[]{:S(2)}) async-start(), calls=%async_computation.8 | async-start | bytes 9437184 | tf_op jit(solution)/shard_map/reduce_scatter | solution.py:1055
  120.0 27.8 %collective-permute-start.4 = (bf16[256,2048]{1,0:T(8,128)(2,1)S(1)}, bf16[256,2048]{1,0:T(8,128)(2,1)S(1)}, u32[]{:S(2)}, u32[]{:S(2)}) collective-permute-start(bf16[256,2048]{1,0:T(8,128)(2,1)S(1)} %copy-done.21), channel_id=1, source_target_pairs={{0,8},{8,0},{16,24},{24,16},{1,9},{9,1},{17,25},{25,17},{2,10},{10... | collective-permute-start | bytes 3145736 | tf_op jit(solution)/shard_map/ppermute | solution.py:60
  121.5 27.4 %collective-permute-start.5 = (bf16[256,2048]{1,0:T(8,128)(2,1)}, bf16[256,2048]{1,0:T(8,128)(2,1)S(1)}, u32[]{:S(2)}, u32[]{:S(2)}) collective-permute-start(bf16[256,2048]{1,0:T(8,128)(2,1)} %get-tuple-element.199.refs_9_.refs_8_.refs_0_), channel_id=1, source_target_pairs={{0,16},{8,24},{16,0},{24,8},{1,17},{9,25},{17,1},{25,9},{2,18},{10... | collective-permute-start | bytes 3145736 | tf_op jit(solution)/shard_map/ppermute | solution.py:60
  186.1 47.6 %collective-permute-start.9 = (bf16[512,2048]{1,0:T(8,128)(2,1)S(1)}, bf16[512,2048]{1,0:T(8,128)(2,1)S(1)}, u32[]{:S(2)}, u32[]{:S(2)}) collective-permute-start(bf16[512,2048]{1,0:T(8,128)(2,1)S(1)} %add_convert_fusion.refs_0_.refs_15_), channel_id=1, source_target_pairs={{0,8},{8,0},{16,24},{24,16},{1,9},{9,1},{17,25},{25,17},{2,10},{10... | collective-permute-start | bytes 6291464 | tf_op jit(solution)/shard_map/ppermute | solution.py:60
  187.6 48.6 %collective-permute-start.10 = (bf16[512,2048]{1,0:T(8,128)(2,1)S(1)}, bf16[512,2048]{1,0:T(8,128)(2,1)S(1)}, u32[]{:S(2)}, u32[]{:S(2)}) collective-permute-start(bf16[512,2048]{1,0:T(8,128)(2,1)S(1)} %add_convert_fusion.refs_0_.refs_15_), channel_id=1, source_target_pairs={{0,16},{8,24},{16,0},{24,8},{1,17},{9,25},{17,1},{25,9},{2,18},{10... | collective-permute-start | bytes 6291464 | tf_op jit(solution)/shard_map/ppermute | solution.py:60
  234.8 42.0 %collective-permute-start.13 = (bf16[256,2048]{1,0:T(8,128)(2,1)}, bf16[256,2048]{1,0:T(8,128)(2,1)S(1)}, u32[]{:S(2)}, u32[]{:S(2)}) collective-permute-start(bf16[256,2048]{1,0:T(8,128)(2,1)} %slice.243), channel_id=1, source_target_pairs={{0,16},{8,24},{16,0},{24,8},{1,17},{9,25},{17,1},{25,9},{2,18},{10... | collective-permute-start | bytes 3145736 | tf_op jit(solution)/shard_map/ppermute | solution.py:60
  237.4 39.5 %collective-permute-start.14 = (bf16[256,2048]{1,0:T(8,128)(2,1)}, bf16[256,2048]{1,0:T(8,128)(2,1)}, u32[]{:S(2)}, u32[]{:S(2)}) collective-permute-start(bf16[256,2048]{1,0:T(8,128)(2,1)} %slice.244), channel_id=1, source_target_pairs={{0,8},{8,0},{16,24},{24,16},{1,9},{9,1},{17,25},{25,17},{2,10},{10... | collective-permute-start | bytes 3145736 | tf_op jit(solution)/shard_map/ppermute | solution.py:60
  238.3 50.3 %collective-permute-start.11 = (bf16[256,2048]{1,0:T(8,128)(2,1)}, bf16[256,2048]{1,0:T(8,128)(2,1)}, u32[]{:S(2)}, u32[]{:S(2)}) collective-permute-start(bf16[256,2048]{1,0:T(8,128)(2,1)} %get-tuple-element.135.refs_10_.refs_2_), channel_id=1, source_target_pairs={{0,16},{8,24},{16,0},{24,8},{1,17},{9,25},{17,1},{25,9},{2,18},{10... | collective-permute-start | bytes 3145736 | tf_op jit(solution)/shard_map/ppermute | solution.py:60
  239.5 49.1 %collective-permute-start.12 = (bf16[256,2048]{1,0:T(8,128)(2,1)}, bf16[256,2048]{1,0:T(8,128)(2,1)}, u32[]{:S(2)}, u32[]{:S(2)}) collective-permute-start(bf16[256,2048]{1,0:T(8,128)(2,1)} %get-tuple-element.136.refs_13_.refs_5_), channel_id=1, source_target_pairs={{0,8},{8,0},{16,24},{24,16},{1,9},{9,1},{17,25},{25,17},{2,10},{10... | collective-permute-start | bytes 3145736 | tf_op jit(solution)/shard_map/ppermute | solution.py:60
  322.2 199.0 %reduce-scatter.7.cloned.1.call-start = ((), (), s32[]{:S(2)}) async-start(), calls=%async_computation.9 | async-start | bytes 9437184 | tf_op jit(solution)/shard_map/reduce_scatter | solution.py:1055
  430.4 187.2 %reduce-scatter.9.cloned.1.call-start = ((), (), s32[]{:S(2)}) async-start(), calls=%async_computation.10 | async-start | bytes 9437184 | tf_op jit(solution)/shard_map/reduce_scatter | solution.py:1055
  482.5 216.9 %reduce-scatter.11.cloned.1.call-start = ((), (), s32[]{:S(2)}) async-start(), calls=%async_computation.11 | async-start | bytes 7077888 | tf_op jit(solution)/shard_map/reduce_scatter | solution.py:1055
  482.5 38.6 %collective-permute-start.15 = (bf16[256,2048]{1,0:T(8,128)(2,1)}, bf16[256,2048]{1,0:T(8,128)(2,1)}, u32[]{:S(2)}, u32[]{:S(2)}) collective-permute-start(bf16[256,2048]{1,0:T(8,128)(2,1)} %get-tuple-element.162), channel_id=1, source_target_pairs={{0,8},{8,0},{16,24},{24,16},{1,9},{9,1},{17,25},{25,17},{2,10},{10... | collective-permute-start | bytes 3145736 | tf_op jit(solution)/shard_map/ppermute | solution.py:60
  483.6 37.5 %collective-permute-start.16 = (bf16[256,2048]{1,0:T(8,128)(2,1)S(1)}, bf16[256,2048]{1,0:T(8,128)(2,1)}, u32[]{:S(2)}, u32[]{:S(2)}) collective-permute-start(bf16[256,2048]{1,0:T(8,128)(2,1)S(1)} %copy-done.66), channel_id=1, source_target_pairs={{0,16},{8,24},{16,0},{24,8},{1,17},{9,25},{17,1},{25,9},{2,18},{10... | collective-permute-start | bytes 3145736 | tf_op jit(solution)/shard_map/ppermute | solution.py:60
  615.5 26.4 %collective-permute-start.17 = (bf16[256,2048]{1,0:T(8,128)(2,1)}, bf16[256,2048]{1,0:T(8,128)(2,1)S(1)}, u32[]{:S(2)}, u32[]{:S(2)}) collective-permute-start(bf16[256,2048]{1,0:T(8,128)(2,1)} %reduce-scatter.7.cloned.1.call-done.refs_0_), channel_id=1, source_target_pairs={{0,8},{8,0},{16,24},{24,16},{1,9},{9,1},{17,25},{25,17},{2,10},{10... | collective-permute-start | bytes 3145736 | tf_op jit(solution)/shard_map/ppermute | solution.py:60
  616.6 26.3 %collective-permute-start.18 = (bf16[256,2048]{1,0:T(8,128)(2,1)}, bf16[256,2048]{1,0:T(8,128)(2,1)S(1)}, u32[]{:S(2)}, u32[]{:S(2)}) collective-permute-start(bf16[256,2048]{1,0:T(8,128)(2,1)} %reduce-scatter.7.cloned.1.call-done.refs_0_), channel_id=1, source_target_pairs={{0,16},{8,24},{16,0},{24,8},{1,17},{9,25},{17,1},{25,9},{2,18},{10... | collective-permute-start | bytes 3145736 | tf_op jit(solution)/shard_map/ppermute | solution.py:60
  620.0 30.8 %collective-permute-start.19 = (bf16[128,2048]{1,0:T(8,128)(2,1)}, bf16[128,2048]{1,0:T(8,128)(2,1)}, u32[]{:S(2)}, u32[]{:S(2)}) collective-permute-start(bf16[128,2048]{1,0:T(8,128)(2,1)} %get-tuple-element.247), channel_id=1, source_target_pairs={{0,8},{8,0},{16,24},{24,16},{1,9},{9,1},{17,25},{25,17},{2,10},{10... | collective-permute-start | bytes 1572872 | tf_op jit(solution)/shard_map/ppermute | solution.py:60
  621.2 30.3 %collective-permute-start.20 = (bf16[128,2048]{1,0:T(8,128)(2,1)}, bf16[128,2048]{1,0:T(8,128)(2,1)}, u32[]{:S(2)}, u32[]{:S(2)}) collective-permute-start(bf16[128,2048]{1,0:T(8,128)(2,1)} %get-tuple-element.246), channel_id=1, source_target_pairs={{0,16},{8,24},{16,0},{24,8},{1,17},{9,25},{17,1},{25,9},{2,18},{10... | collective-permute-start | bytes 1572872 | tf_op jit(solution)/shard_map/ppermute | solution.py:60
  654.0 36.5 %collective-permute-start.25 = (bf16[128,2048]{1,0:T(8,128)(2,1)}, bf16[128,2048]{1,0:T(8,128)(2,1)}, u32[]{:S(2)}, u32[]{:S(2)}) collective-permute-start(bf16[128,2048]{1,0:T(8,128)(2,1)} %get-tuple-element.193), channel_id=1, source_target_pairs={{0,16},{8,24},{16,0},{24,8},{1,17},{9,25},{17,1},{25,9},{2,18},{10... | collective-permute-start | bytes 1572872 | tf_op jit(solution)/shard_map/ppermute | solution.py:60
  655.2 35.4 %collective-permute-start.26 = (bf16[128,2048]{1,0:T(8,128)(2,1)}, bf16[128,2048]{1,0:T(8,128)(2,1)}, u32[]{:S(2)}, u32[]{:S(2)}) collective-permute-start(bf16[128,2048]{1,0:T(8,128)(2,1)} %get-tuple-element.194), channel_id=1, source_target_pairs={{0,8},{8,0},{16,24},{24,16},{1,9},{9,1},{17,25},{25,17},{2,10},{10... | collective-permute-start | bytes 1572872 | tf_op jit(solution)/shard_map/ppermute | solution.py:60
  656.1 24.2 %collective-permute-start.23 = (bf16[128,2048]{1,0:T(8,128)(2,1)S(1)}, bf16[128,2048]{1,0:T(8,128)(2,1)S(1)}, u32[]{:S(2)}, u32[]{:S(2)}) collective-permute-start(bf16[128,2048]{1,0:T(8,128)(2,1)S(1)} %slice.199), channel_id=1, source_target_pairs={{0,16},{8,24},{16,0},{24,8},{1,17},{9,25},{17,1},{25,9},{2,18},{10... | collective-permute-start | bytes 1572872 | tf_op jit(solution)/shard_map/ppermute | solution.py:60
  663.9 24.0 %collective-permute-start.21 = (bf16[128,2048]{1,0:T(8,128)(2,1)}, bf16[128,2048]{1,0:T(8,128)(2,1)S(1)}, u32[]{:S(2)}, u32[]{:S(2)}) collective-permute-start(bf16[128,2048]{1,0:T(8,128)(2,1)} %slice.197), channel_id=1, source_target_pairs={{0,16},{8,24},{16,0},{24,8},{1,17},{9,25},{17,1},{25,9},{2,18},{10... | collective-permute-start | bytes 1572872 | tf_op jit(solution)/shard_map/ppermute | solution.py:60
  699.3 24.8 %collective-permute-start.27 = (bf16[256,1536]{1,0:T(8,128)(2,1)}, bf16[256,1536]{1,0:T(8,128)(2,1)}, u32[]{:S(2)}, u32[]{:S(2)}) collective-permute-start(bf16[256,1536]{1,0:T(8,128)(2,1)} %reduce-scatter.11.cloned.1.call-done.refs_0_), channel_id=1, source_target_pairs={{0,8},{8,0},{16,24},{24,16},{1,9},{9,1},{17,25},{25,17},{2,10},{10... | collective-permute-start | bytes 2359304 | tf_op jit(solution)/shard_map/ppermute | solution.py:60
  700.6 23.6 %collective-permute-start.28 = (bf16[256,1536]{1,0:T(8,128)(2,1)}, bf16[256,1536]{1,0:T(8,128)(2,1)}, u32[]{:S(2)}, u32[]{:S(2)}) collective-permute-start(bf16[256,1536]{1,0:T(8,128)(2,1)} %reduce-scatter.11.cloned.1.call-done.refs_0_), channel_id=1, source_target_pairs={{0,16},{8,24},{16,0},{24,8},{1,17},{9,25},{17,1},{25,9},{2,18},{10... | collective-permute-start | bytes 2359304 | tf_op jit(solution)/shard_map/ppermute | solution.py:60
  (77 other events, 885.1 us)
Sparse Core Ops, SparseCore 0:
  10.3 68.1 all-gather.4
  80.7 80.6 all-gather.6
  163.6 80.5 all-gather.8
  245.6 80.6 all-gather.10
  329.0 88.0 reduce-scatter.4
  430.5 87.0 reduce-scatter.6
  519.9 87.9 reduce-scatter.8
  613.9 67.0 reduce-scatter.10

commit v5 on v3

--- a/solution.py
+++ b/solution.py
@@ -755,10 +755,10 @@
 
 def qkv_back_kernel(*refs):
     dqkv, w_qkv = refs[0:2]
-    a1, gb_own, w_down, one_hi, two_hi = refs[2:7], *refs[7:11]
-    own, p3, p1, p2, from_x, from_y, land1, land2, qkv_grad, mix_own = refs[11:21]
-    x_hi, y_hi = refs[21:23]
-    moves = Moves(*refs[23:25])
+    a1, gb_own, w_down, one_hi, two_hi, down1, down2 = refs[2:7], *refs[7:13]
+    own, p3, p1, p2, from_x, from_y, land1, land2, qkv_grad, mix_own = refs[13:23]
+    x_hi, y_hi, down_lo, down_hi = refs[23:27]
+    moves = Moves(*refs[27:29])
     rows = own.shape[0]
     n = rows // 2
 
@@ -779,6 +779,8 @@
         copy.wait()
     multiply([block(3), block(4)], w_qkv, True, [from_y, from_x], [p1_hi, p2_lo], store_sum)
     second += [moves.start(p1_hi, land1_hi, 1), moves.start(p2_lo, land2_lo, 2)]
+    second += [moves.start(halves(down1)[0], down_lo, 2)]
+    second += [moves.start(halves(down2)[1], down_hi, 1)]
     rights, at = [], 0
     for x in a1:
         rights.append(dqkv.at[pl.ds(at, x.shape[0])])
@@ -788,23 +790,24 @@
         copy.wait()
 
 
-def qkv_back(dqkv, w_qkv, a1, gb_own, w_down, one_hi, two_hi):
+def qkv_back(dqkv, w_qkv, a1, gb_own, w_down, one_hi, two_hi, down_near):
     rows, width = a1[0].shape
     wide = gb_own.shape[1]
     n = rows // 2
     outs = [((rows, width), single)] + [((rows, width), half)] * 3
     outs += [((n, width), half)] * 2 + [((rows, width), half)] * 2
     outs += [((width, dqkv.shape[1]), half), ((rows, width), single)] + [((n, width), half)] * 2
+    outs += [((down_near[0].shape[0] // 2, width), half)] * 2
     out = moving_call(
         qkv_back_kernel,
-        [dqkv, w_qkv, *a1, gb_own, w_down, one_hi, two_hi],
+        [dqkv, w_qkv, *a1, gb_own, w_down, one_hi, two_hi, *down_near],
         outs,
-        8,
+        10,
         5,
         16 * rows * width * dqkv.shape[1] + 2 * rows * width * wide,
         "qkv_back",
     )
-    return out[0], out[6:8], out[8], out[9], out[10:12]
+    return out[0], out[6:8], out[8], out[9], out[10:12], out[12:14]
 
 
 def lay_out_kernel(axis, layout, c_ref, *refs):
@@ -1156,9 +1159,10 @@
     if CTX == 4:
         lows = [swap(one_lo, 1), swap(two_lo, 2)]
         dqkv = after(dqkv, lows, up_part)
-        dh1, arrived, qkv_grad, mix_own, highs = qkv_back(
-            dqkv, w_qkv, a1, gb[0][0], w_down, one_hi, two_hi
+        dh1, arrived, qkv_grad, mix_own, highs, down_far = qkv_back(
+            dqkv, w_qkv, a1, gb[0][0], w_down, one_hi, two_hi, down_near
         )
+        down_out = [[down_part], [down_near[0]], [down_near[1]], down_far]
     else:
         dh1 = [
             plain([(dqkv, rows, j)], w_qkv, True, half if j else single, f"dh1_{j}")[0]
@@ -1168,7 +1172,9 @@
         dh1 = dh1[0]
         qkv_grad = outer(a1, [(dqkv, rows, j) for j in range(CTX)], "qkv_grad")
         mix_own = plain(gb[0], w_down, False, single, "mix_0")[0]
+        down_out = gather_second(down_part, down_near)
     qkv_part = scatter_f(qkv_grad)
+
     up_own = after(up_part, arrived)
     up_near = gather_first(up_own)
     out_first = []
@@ -1176,31 +1182,34 @@
         k = out_part.shape[0] // 2
         out_lo, out_hi = after(out_part, arrived)[:k], after(out_part, arrived)[k:]
         out_first = [swap(out_lo, 1), swap(out_hi, 2)]
-    waiting = (dh1, dqkv, mix_own, flat(du), flat(dz2[:1]))
-    dh1, dqkv, mix_own, du, dz2_own = after(waiting, up_near, out_first)
-    up_bias_grad = sum(jnp.sum(x.astype(single), axis=0) for x in du)
-    down_bias_grad = sum(jnp.sum(x.astype(single), axis=0) for x in dz2_own)
+    waiting = (dh1, dqkv, mix_own, flat(du), flat(dz2[:1]), down_out)
+    dh1, dqkv, mix_own, du, dz2_own, down_out = after(waiting, out_part)
+    down_out = lay_out(0, down_out, c, width // min(width, 512))
     dh1 = total_of(dh1, arrived)
-    down_near, up_near, out_first = after((down_near, up_near, out_first))
-    down_out = gather_second(down_part, down_near)
-    up_out = gather_second(up_own, up_near)
-    out_second = []
     if CTX == 4:
-        out_lo = (out_lo.astype(single) + out_first[0].astype(single)).astype(half)
-        out_hi = (out_hi.astype(single) + out_first[1].astype(single)).astype(half)
-        out_second = [(out_lo, swap(out_lo, 2)), (out_hi, swap(out_hi, 1))]
         mixed = y1 + bias_d + mix_own
         mixed = jnp.concatenate([total_of(mixed[:n], lows), total_of(mixed[n:], highs)])
     else:
         mixed = total_of(y1 + bias_d + mix_own, scatter_send(mix[1:]))
+    up_bias_grad = sum(jnp.sum(x.astype(single), axis=0) for x in du)
+    down_bias_grad = sum(jnp.sum(x.astype(single), axis=0) for x in dz2_own)
     sums = jnp.sum(dqkv.astype(single), axis=0)
     normed1_own, inv1_own = norm_parts(tokens.astype(single))
     gain1_grad = jnp.sum(dh1 * normed1_own, axis=0)
     shift1_grad = jnp.sum(dh1, axis=0)
-    dy1 = after(dy1, up_out, down_out, out_second)
     input_grad = dy1 + norm_back(normed1_own, inv1_own, gain1, dh1)
 
+    done = (down_out, input_grad, mixed, sums, up_bias_grad, down_bias_grad, gain1_grad, shift1_grad)
+    up_near, out_first = after((up_near, out_first), done)
     if CTX == 4:
+        out_lo = (out_lo.astype(single) + out_first[0].astype(single)).astype(half)
+        out_hi = (out_hi.astype(single) + out_first[1].astype(single)).astype(half)
+        out_lo, out_hi, up_near = after((out_lo, out_hi, up_near))
+        out_second = [(out_lo, swap(out_lo, 2)), (out_hi, swap(out_hi, 1))]
+    up_out = gather_second(up_own, up_near)
+    up_out = lay_out(1, up_out, c, nf)
+    if CTX == 4:
+        out_second = after(out_second, up_out)
         out_out = [x.astype(single) + y.astype(single) for x, y in out_second]
         out_out = jnp.concatenate(out_out, axis=0)
     else:
@@ -1228,12 +1237,12 @@
 
     sums_in = [out_bias_grad, gain2_grad, shift2_grad, down_bias_grad, spread(up_bias_grad, fpart)]
     sums_in += [gain1_grad, shift1_grad, spread(sums[:part], part), spread(sums[2 * part :], part)]
+    qkv_part = after(qkv_part, out_out)
     qkv_near = gather_first(qkv_part)
-    sums_in[5] = after(sums_in[5], qkv_near)
+    sums_in[5] = after(sums_in[5], qkv_part)
     sums_out = reduced(sums_in, 2)
+    qkv_near = after(qkv_near, sums_out)
     qkv_out = lay_out(1, gather_second(qkv_part, qkv_near), c, 3)
-    down_out = lay_out(0, after(down_out, qkv_part), c, width // min(width, 512))
-    up_out = lay_out(1, after(up_out, qkv_part), c, nf)
     out_bias_out, gain2_out, shift2_out, down_bias_out, up_bias_out = sums_out[:5]
     gain1_out, shift1_out, q_bias_out, v_bias_out = sums_out[5:]
     return (

time: 759 us -> 751 us (0.989)
  waiting for transfers between devices: 133 us -> 117 us
  Pallas kernels: 446 us -> 460 us
    ppermute x31 -> x29, waiting for transfers between devices: 125 us -> 108 us  [swap(): return lax.ppermute(x, 'ctx', [(i, i ^ mask) for i in range(n)])]
    pallas_call x2, Pallas kernels: 121 us -> 131 us  [moving_call(): pl.pallas_call(kernel, in_specs=[anywhere] * len(operands), out_specs=[an...]
    unnamed x153 -> x151, local copies, waits for them, and re-layouts: 21.1 us -> 23.7 us
    ppermute x31 -> x29, starting transfers between devices: 34.9 us -> 33.4 us  [swap(): return lax.ppermute(x, 'ctx', [(i, i ^ mask) for i in range(n)])]
  transfers between devices with their start and end apart: 39 -> 37, of which waited for: 14 -> 13; matrix products, arithmetic and copies ran while one was open for 14% -> 13% of each run, Pallas kernels for 59% -> 62%
where the time goes in v5:
time: 751 us; the launch traced here: 740 us
  Pallas kernels  460 us (61%)
  waiting for transfers between devices  117 us (16%)
  other arithmetic  60.7 us (8%)
  local copies, waits for them, and re-layouts  44.6 us (6%)
  starting transfers between devices  33.8 us (5%)
  between operations  15.5 us (2%)
  matrix products  7.86 us (1%)
    pallas_call x2, Pallas kernels, moving_call(): pl.pallas_call(kernel, in_specs=[anywhere] * len(operands), out_specs=[an...  131 us
    ppermute x29, waiting for transfers between devices, swap(): return lax.ppermute(x, 'ctx', [(i, i ^ mask) for i in range(n)])  108 us
    pallas_call x1, Pallas kernels, feed_back(): pl.pallas_call(feed_back_kernel, in_specs=[anywhere] * 22, out_specs=[any...  104 us
    pallas_call x2, Pallas kernels, attn_call(): pl.pallas_call(kernel, grid_spec=pltpu.PrefetchScalarGridSpec(num_scalar_...  60.6 us
    pallas_call x1, Pallas kernels, heads_back(): pl.pallas_call(functools.partial(heads_back_kernel, part), in_specs=[anyw...  48.9 us
    pallas_call x4, Pallas kernels, rows_matmul(): pl.pallas_call(functools.partial(rows_kernel, dot_nt if transposed else d...  43.5 us
    pallas_call x1, Pallas kernels, outer(): pl.pallas_call(functools.partial(outer_kernel, len(left)), grid=(m // tm,...  33.7 us
    ppermute x29, starting transfers between devices, swap(): return lax.ppermute(x, 'ctx', [(i, i ^ mask) for i in range(n)])  33.4 us
  transfers between devices with their start and end apart: 37, of which 13 were waited for; matrix products, arithmetic and copies ran while one was open for 13% of the time, Pallas kernels for 62%

profile of v5, /device:TPU:0, one launch (start us, length us, event | category | flops | bytes accessed | tf_op | source)
XLA Modules:
  0.0 740.1 jit_solution(3651100381284531300)
XLA Ops:
  12.7 3.0 collective-permute-start
  18.1 9.0 %gather_small.1 = f32[8,24,128]{2,1,0:T(8,128)} custom-call(f32[24,128]{1,0:T(8,128)} %bitcast.91), custom_call_target="tpu_custom_call" | custom-call | tf_op jit(solution)/shard_map/gather_small/pallas_call | solution.py:887
  31.9 3.9 convert.46
  42.8 3.4 fusion.41
  46.2 15.2 %collective-permute-done = bf16[512,2048]{1,0:T(8,128)(2,1)} collective-permute-done((bf16[512,2048]{1,0:T(8,128)(2,1)S(1)}, bf16[512,2048]{1,0:T(8,128)(2,1)}, u32[]{:S(2)}, u32[]{:S(2)}) %collective-permute-start) | collective-permute-done | bytes 2097184 | tf_op jit(solution)/shard_map/ppermute | solution.py:60
  76.3 5.7 fusion.21
  82.0 6.1 collective-permute-done.2.refs_0_
  91.0 28.0 %qkv.1 = (bf16[2048,1536]{1,0:T(8,128)(2,1)}, bf16[256,2048]{1,0:T(8,128)(2,1)S(1)}, bf16[256,2048]{1,0:T(8,128)(2,1)}, bf16[256,2048]{1,0:T(8,128)(2,1)}, bf16[256,2048]{1,0:T(8,128)(2,1)}) custom-call(bf16[256,2048]{1,0:T(8,128)(2,1)} %collective-permute-done.2.refs_0_, bf16[256,2048]{1,0:T(8,128)(2,1)} %collective-permute-done.3.refs_1_, ...), custom_call_target="tpu_custom_call" | custom-call | flops 12884901 | tf_op jit(solution)/shard_map/qkv/pallas_call | solution.py:499
  122.2 24.4 %attn_forward.1 = bf16[2048,512]{1,0:T(8,128)(2,1)S(1)} custom-call(s32[16]{0:T(128)S(1)} %select_reduce_fusion.inv_ref, f32[4]{0:T(128)S(1)} %multiply_power_fusion.slope_ref, ...), custom_call_target="tpu_custom_call" | custom-call | flops 20000000 | bytes 8388 | tf_op jit(solution)/shard_map/attn_forward/pallas_call | solution.py:233
  153.4 12.5 %collective-permute-done.6 = bf16[512,512]{1,0:T(8,128)(2,1)S(1)} collective-permute-done((bf16[512,512]{1,0:T(8,128)(2,1)}, bf16[512,512]{1,0:T(8,128)(2,1)S(1)}, u32[]{:S(2)}, u32[]{:S(2)}) %collective-permute-start.6) | collective-permute-done | bytes 524320 | tf_op jit(solution)/shard_map/ppermute | solution.py:60
  165.9 6.9 collective-permute-done.7
  176.3 7.9 %fusion.44 = (f32[512]{0:T(512)S(1)}, f32[512,2048]{1,0:T(8,128)S(1)}) fusion(f32[2048]{0:T(1024)S(1)} %bitcast.94, bf16[2048,2048]{1,0:T(8,128)(2,1)} %all-gather.7.cloned.1.call-done.refs_6_, bf16[512,512]{1,0:T(8,128)(2,1)} %get-tuple-element.239, bf16[512,512]{1,0:T(8,128)(2,1)} %get-tuple-element.238, bf16[512,512]{1,0:T(8,128)(2,1)S(1)} %get-tuple-element.237, ...), kind=kOutput, calls=%fused_computation.162 | convolution fusion | flops 4307549696 | bytes 16787456 | tf_op jit(solution)/shard_map/dot_general | solution.py:24
  188.5 45.3 %collective-permute-done.9.refs_0_.refs_16_ = bf16[512,2048]{1,0:T(8,128)(2,1)S(1)} collective-permute-done((bf16[512,2048]{1,0:T(8,128)(2,1)S(1)}, bf16[512,2048]{1,0:T(8,128)(2,1)S(1)}, u32[]{:S(2)}, u32[]{:S(2)}) %collective-permute-start.9) | collective-permute-done | bytes 2097184 | tf_op jit(solution)/shard_map/ppermute | solution.py:60
  240.1 4.1 all-gather.9.cloned.1.call-done.refs_1_.refs_2_.refs_14_
  244.2 11.0 %up_gelu_0.1 = (bf16[512,2048]{1,0:T(8,128)(2,1)}, bf16[512,2048]{1,0:T(8,128)(2,1)}) custom-call(bf16[512,2048]{1,0:T(8,128)(2,1)} %copy-done.18, bf16[2048,2048]{1,0:T(8,128)(2,1)} %all-gather.9.cloned.1.call-done.refs_1_.refs_2_.refs_14_, f32[1,2048]{1,0:T(1,128)S(1)} %bitcast.71), custom_call_target="tpu_custom_call" | custom-call | flops 4294967 | bytes 16777 | tf_op jit(solution)/shard_map/up_gelu_0/pallas_call | solution.py:311
  255.2 10.9 %up_gelu_1.1 = (bf16[512,2048]{1,0:T(8,128)(2,1)}, bf16[512,2048]{1,0:T(8,128)(2,1)}) custom-call(bf16[512,2048]{1,0:T(8,128)(2,1)} %copy-done.19, bf16[2048,2048]{1,0:T(8,128)(2,1)} %all-gather.9.cloned.1.call-done.refs_1_.refs_2_.refs_14_, f32[1,2048]{1,0:T(1,128)S(1)} %bitcast.72), custom_call_target="tpu_custom_call" | custom-call | flops 4294967 | bytes 16777 | tf_op jit(solution)/shard_map/up_gelu_1/pallas_call | solution.py:311
  266.1 10.8 %up_gelu_2.1 = (bf16[512,2048]{1,0:T(8,128)(2,1)}, bf16[512,2048]{1,0:T(8,128)(2,1)}) custom-call(bf16[512,2048]{1,0:T(8,128)(2,1)} %copy-done.20, bf16[2048,2048]{1,0:T(8,128)(2,1)} %all-gather.9.cloned.1.call-done.refs_1_.refs_2_.refs_14_, f32[1,2048]{1,0:T(1,128)S(1)} %bitcast.73), custom_call_target="tpu_custom_call" | custom-call | flops 4294967 | bytes 16777 | tf_op jit(solution)/shard_map/up_gelu_2/pallas_call | solution.py:311
  276.9 10.8 %up_gelu_3.1 = (bf16[256,2048]{1,0:T(8,128)(2,1)S(1)}, bf16[256,2048]{1,0:T(8,128)(2,1)}, bf16[256,2048]{1,0:T(8,128)(2,1)}, bf16[256,2048]{1,0:T(8,128)(2,1)}) custom-call(bf16[256,2048]{1,0:T(8,128)(2,1)} %collective-permute-done.13.refs_0_.refs_18_, bf16[256,2048]{1,0:T(8,128)(2,1)} %collective-permute-done.14.refs_1_.refs_19_, ...), custom_call_target="tpu_custom_call" | custom-call | flops 4294967 | bytes 16777 | tf_op jit(solution)/shard_map/up_gelu_3/pallas_call | solution.py:311
  287.7 33.7 %down_grad.1 = bf16[2048,2048]{1,0:T(8,128)(2,1)} custom-call(bf16[512,2048]{1,0:T(8,128)(2,1)} %get-tuple-element.141.refs_0_.refs_1_.refs_7_, bf16[512,2048]{1,0:T(8,128)(2,1)} %get-tuple-element.141.refs_0_.refs_1_.refs_7_, bf16[512,2048]{1,0:T(8,128)(2,1)} %get-tuple-element.144.refs_2_.refs_3_.refs_8_, ...), custom_call_target="tpu_custom_call" | custom-call | flops 17179868 | bytes 25165 | tf_op jit(solution)/shard_map/down_grad/pallas_call | solution.py:384
  321.4 4.9 all-gather.11.cloned.1.call-done.refs_13_.refs_10_.refs_8_
  326.3 104.0 %feed_back.1 = (bf16[512,2048]{1,0:T(8,128)(2,1)}, bf16[512,2048]{1,0:T(8,128)(2,1)}, bf16[512,2048]{1,0:T(8,128)(2,1)}, bf16[256,2048]{1,0:T(8,128)(2,1)}, bf16...) custom-call(bf16[256,2048]{1,0:T(8,128)(2,1)} %get-tuple-element.191, ...), custom_call_target="tpu_custom_call" | custom-call | flops 55834576 | tf_op jit(solution)/shard_map/feed_back/pallas_call | solution.py:642
  433.5 48.9 %heads_back.1 = (f32[512,2048]{1,0:T(8,128)}, bf16[512,2048]{1,0:T(8,128)(2,1)}, f32[8,2048]{1,0:T(8,128)}, bf16[2048,512]{1,0:T(8,128)(2,1)}, bf16[2048,2048]{1...) custom-call(f32[512,2048]{1,0:T(8,128)} %get-tuple-element.157.refs_, ...), custom_call_target="tpu_custom_call" | custom-call | flops 21474836 | tf_op jit(solution)/shard_map/heads_back/pallas_call | solution.py:734
  484.9 36.2 %attn_backward.1.refs_0_ = bf16[2048,1536]{1,0:T(8,128)(2,1)} custom-call(s32[16]{0:T(128)S(1)} %select_reduce_fusion.inv_ref, f32[4]{0:T(128)S(1)} %multiply_power_fusion.slope_ref, ...), custom_call_target="tpu_custom_call" | custom-call | flops 40000000 | bytes 14680 | tf_op jit(solution)/shard_map/attn_backward/pallas_call | solution.py:233
  521.1 103.3 %qkv_back.1 = (f32[512,2048]{1,0:T(8,128)}, bf16[512,2048]{1,0:T(8,128)(2,1)}, bf16[512,2048]{1,0:T(8,128)(2,1)}, bf16[512,2048]{1,0:T(8,128)(2,1)}, bf16[256,20...) custom-call(bf16[2048,1536]{1,0:T(8,128)(2,1)} %attn_backward.1.refs, ...), custom_call_target="tpu_custom_call" | custom-call | flops 30064772 | tf_op jit(solution)/shard_map/qkv_back/pallas_call | solution.py:499
  642.1 5.0 fusion.16
  661.3 3.8 lay_out.3
  665.1 3.9 convert_reduce_fusion
  677.1 9.5 %collective-permute-done.23.refs_3_ = bf16[128,2048]{1,0:T(8,128)(2,1)S(1)} collective-permute-done((bf16[128,2048]{1,0:T(8,128)(2,1)S(1)}, bf16[128,2048]{1,0:T(8,128)(2,1)S(1)}, u32[]{:S(2)}, u32[]{:S(2)}) %collective-permute-start.23) | collective-permute-done | bytes 524320 | tf_op jit(solution)/shard_map/ppermute | solution.py:60
  688.3 7.3 lay_out.4
  702.1 15.1 %reduce_small.1 = f32[24,128]{1,0:T(8,128)} custom-call(f32[8,24,128]{2,1,0:T(8,128)} %bitcast.79), custom_call_target="tpu_custom_call" | custom-call | tf_op jit(solution)/shard_map/reduce_small/pallas_call | solution.py:958
  721.9 5.9 collective-permute-done.27.refs_3_
  730.0 3.1 lay_out.5
  (314 shorter events, 121.0 us)
Async XLA Ops:
  7.3 83.7 %all-gather.5.cloned.1.call-start = ((), (), s32[]{:S(2)}) async-start(), calls=%async_computation.4 | async-start | bytes 7077888 | tf_op jit(solution)/shard_map/all_gather | solution.py:1022
  9.9 166.4 %all-gather.7.cloned.1.call-start = ((), (), s32[]{:S(2)}) async-start(), calls=%async_computation.5 | async-start | bytes 9437184 | tf_op jit(solution)/shard_map/all_gather | solution.py:1022
  12.7 231.5 %all-gather.9.cloned.1.call-start = ((), (), s32[]{:S(2)}) async-start(), calls=%async_computation.6 | async-start | bytes 9437184 | tf_op jit(solution)/shard_map/all_gather | solution.py:1022
  12.7 48.7 %collective-permute-start = (bf16[512,2048]{1,0:T(8,128)(2,1)S(1)}, bf16[512,2048]{1,0:T(8,128)(2,1)}, u32[]{:S(2)}, u32[]{:S(2)}) collective-permute-start(bf16[512,2048]{1,0:T(8,128)(2,1)S(1)} %copy-done.13), channel_id=1, source_target_pairs={{0,8},{8,0},{16,24},{24,16},{1,9},{9,1},{17,25},{25,17},{2,10},{10... | collective-permute-start | bytes 6291464 | tf_op jit(solution)/shard_map/ppermute | solution.py:60
  15.7 47.2 %collective-permute-start.1 = (bf16[512,2048]{1,0:T(8,128)(2,1)S(1)}, bf16[512,2048]{1,0:T(8,128)(2,1)}, u32[]{:S(2)}, u32[]{:S(2)}) collective-permute-start(bf16[512,2048]{1,0:T(8,128)(2,1)S(1)} %copy-done.13), channel_id=1, source_target_pairs={{0,16},{8,24},{16,0},{24,8},{1,17},{9,25},{17,1},{25,9},{2,18},{10... | collective-permute-start | bytes 6291464 | tf_op jit(solution)/shard_map/ppermute | solution.py:60
  64.3 23.9 %collective-permute-start.2 = (bf16[256,2048]{1,0:T(8,128)(2,1)S(1)}, bf16[256,2048]{1,0:T(8,128)(2,1)}, u32[]{:S(2)}, u32[]{:S(2)}) collective-permute-start(bf16[256,2048]{1,0:T(8,128)(2,1)S(1)} %slice.170), channel_id=1, source_target_pairs={{0,16},{8,24},{16,0},{24,8},{1,17},{9,25},{17,1},{25,9},{2,18},{10... | collective-permute-start | bytes 3145736 | tf_op jit(solution)/shard_map/ppermute | solution.py:60
  67.2 23.6 %collective-permute-start.3 = (bf16[256,2048]{1,0:T(8,128)(2,1)S(1)}, bf16[256,2048]{1,0:T(8,128)(2,1)}, u32[]{:S(2)}, u32[]{:S(2)}) collective-permute-start(bf16[256,2048]{1,0:T(8,128)(2,1)S(1)} %slice.171), channel_id=1, source_target_pairs={{0,8},{8,0},{16,24},{24,16},{1,9},{9,1},{17,25},{25,17},{2,10},{10... | collective-permute-start | bytes 3145736 | tf_op jit(solution)/shard_map/ppermute | solution.py:60
  90.8 235.5 %all-gather.11.cloned.1.call-start = ((), (), s32[]{:S(2)}) async-start(), calls=%async_computation.7 | async-start | bytes 9437184 | tf_op jit(solution)/shard_map/all_gather | solution.py:1022
  120.0 313.5 %reduce-scatter.5.cloned.1.call-start = ((), (), s32[]{:S(2)}) async-start(), calls=%async_computation.8 | async-start | bytes 9437184 | tf_op jit(solution)/shard_map/reduce_scatter | solution.py:1058
  120.1 27.8 %collective-permute-start.4 = (bf16[256,2048]{1,0:T(8,128)(2,1)S(1)}, bf16[256,2048]{1,0:T(8,128)(2,1)S(1)}, u32[]{:S(2)}, u32[]{:S(2)}) collective-permute-start(bf16[256,2048]{1,0:T(8,128)(2,1)S(1)} %copy-done.15), channel_id=1, source_target_pairs={{0,8},{8,0},{16,24},{24,16},{1,9},{9,1},{17,25},{25,17},{2,10},{10... | collective-permute-start | bytes 3145736 | tf_op jit(solution)/shard_map/ppermute | solution.py:60
  121.5 27.3 %collective-permute-start.5 = (bf16[256,2048]{1,0:T(8,128)(2,1)}, bf16[256,2048]{1,0:T(8,128)(2,1)S(1)}, u32[]{:S(2)}, u32[]{:S(2)}) collective-permute-start(bf16[256,2048]{1,0:T(8,128)(2,1)} %get-tuple-element.191.refs_9_.refs_8_.refs_0_), channel_id=1, source_target_pairs={{0,16},{8,24},{16,0},{24,8},{1,17},{9,25},{17,1},{25,9},{2,18},{10... | collective-permute-start | bytes 3145736 | tf_op jit(solution)/shard_map/ppermute | solution.py:60
  151.4 21.4 %collective-permute-start.7 = (bf16[512,512]{1,0:T(8,128)(2,1)}, bf16[512,512]{1,0:T(8,128)(2,1)S(1)}, u32[]{:S(2)}, u32[]{:S(2)}) collective-permute-start(bf16[512,512]{1,0:T(8,128)(2,1)} %get-tuple-element.131), channel_id=1, source_target_pairs={{0,16},{8,24},{16,0},{24,8},{1,17},{9,25},{17,1},{25,9},{2,18},{10... | collective-permute-start | bytes 1572872 | tf_op jit(solution)/shard_map/ppermute | solution.py:60
  152.7 20.8 %collective-permute-start.8 = (bf16[512,512]{1,0:T(8,128)(2,1)}, bf16[512,512]{1,0:T(8,128)(2,1)}, u32[]{:S(2)}, u32[]{:S(2)}) collective-permute-start(bf16[512,512]{1,0:T(8,128)(2,1)} %get-tuple-element.132), channel_id=1, source_target_pairs={{0,8},{8,0},{16,24},{24,16},{1,9},{9,1},{17,25},{25,17},{2,10},{10... | collective-permute-start | bytes 1572872 | tf_op jit(solution)/shard_map/ppermute | solution.py:60
  186.2 47.6 %collective-permute-start.9 = (bf16[512,2048]{1,0:T(8,128)(2,1)S(1)}, bf16[512,2048]{1,0:T(8,128)(2,1)S(1)}, u32[]{:S(2)}, u32[]{:S(2)}) collective-permute-start(bf16[512,2048]{1,0:T(8,128)(2,1)S(1)} %add_convert_fusion.refs_0_.refs_15_), channel_id=1, source_target_pairs={{0,8},{8,0},{16,24},{24,16},{1,9},{9,1},{17,25},{25,17},{2,10},{10... | collective-permute-start | bytes 6291464 | tf_op jit(solution)/shard_map/ppermute | solution.py:60
  187.7 48.6 %collective-permute-start.10 = (bf16[512,2048]{1,0:T(8,128)(2,1)S(1)}, bf16[512,2048]{1,0:T(8,128)(2,1)S(1)}, u32[]{:S(2)}, u32[]{:S(2)}) collective-permute-start(bf16[512,2048]{1,0:T(8,128)(2,1)S(1)} %add_convert_fusion.refs_0_.refs_15_), channel_id=1, source_target_pairs={{0,16},{8,24},{16,0},{24,8},{1,17},{9,25},{17,1},{25,9},{2,18},{10... | collective-permute-start | bytes 6291464 | tf_op jit(solution)/shard_map/ppermute | solution.py:60
  234.9 42.0 %collective-permute-start.13 = (bf16[256,2048]{1,0:T(8,128)(2,1)}, bf16[256,2048]{1,0:T(8,128)(2,1)}, u32[]{:S(2)}, u32[]{:S(2)}) collective-permute-start(bf16[256,2048]{1,0:T(8,128)(2,1)} %slice.235), channel_id=1, source_target_pairs={{0,16},{8,24},{16,0},{24,8},{1,17},{9,25},{17,1},{25,9},{2,18},{10... | collective-permute-start | bytes 3145736 | tf_op jit(solution)/shard_map/ppermute | solution.py:60
  237.4 39.5 %collective-permute-start.14 = (bf16[256,2048]{1,0:T(8,128)(2,1)}, bf16[256,2048]{1,0:T(8,128)(2,1)}, u32[]{:S(2)}, u32[]{:S(2)}) collective-permute-start(bf16[256,2048]{1,0:T(8,128)(2,1)} %slice.236), channel_id=1, source_target_pairs={{0,8},{8,0},{16,24},{24,16},{1,9},{9,1},{17,25},{25,17},{2,10},{10... | collective-permute-start | bytes 3145736 | tf_op jit(solution)/shard_map/ppermute | solution.py:60
  238.3 49.4 %collective-permute-start.11 = (bf16[256,2048]{1,0:T(8,128)(2,1)S(1)}, bf16[256,2048]{1,0:T(8,128)(2,1)}, u32[]{:S(2)}, u32[]{:S(2)}) collective-permute-start(bf16[256,2048]{1,0:T(8,128)(2,1)S(1)} %copy-done.22), channel_id=1, source_target_pairs={{0,16},{8,24},{16,0},{24,8},{1,17},{9,25},{17,1},{25,9},{2,18},{10... | collective-permute-start | bytes 3145736 | tf_op jit(solution)/shard_map/ppermute | solution.py:60
  239.5 48.2 %collective-permute-start.12 = (bf16[256,2048]{1,0:T(8,128)(2,1)}, bf16[256,2048]{1,0:T(8,128)(2,1)}, u32[]{:S(2)}, u32[]{:S(2)}) collective-permute-start(bf16[256,2048]{1,0:T(8,128)(2,1)} %get-tuple-element.137.refs_13_.refs_5_), channel_id=1, source_target_pairs={{0,8},{8,0},{16,24},{24,16},{1,9},{9,1},{17,25},{25,17},{2,10},{10... | collective-permute-start | bytes 3145736 | tf_op jit(solution)/shard_map/ppermute | solution.py:60
  321.4 199.7 %reduce-scatter.7.cloned.1.call-start = ((), (), s32[]{:S(2)}) async-start(), calls=%async_computation.9 | async-start | bytes 9437184 | tf_op jit(solution)/shard_map/reduce_scatter | solution.py:1058
  430.4 199.7 %reduce-scatter.9.cloned.1.call-start = ((), (), s32[]{:S(2)}) async-start(), calls=%async_computation.10 | async-start | bytes 9437184 | tf_op jit(solution)/shard_map/reduce_scatter | solution.py:1058
  482.4 216.9 %reduce-scatter.11.cloned.1.call-start = ((), (), s32[]{:S(2)}) async-start(), calls=%async_computation.11 | async-start | bytes 7077888 | tf_op jit(solution)/shard_map/reduce_scatter | solution.py:1058
  482.5 38.6 %collective-permute-start.15 = (bf16[256,2048]{1,0:T(8,128)(2,1)}, bf16[256,2048]{1,0:T(8,128)(2,1)S(1)}, u32[]{:S(2)}, u32[]{:S(2)}) collective-permute-start(bf16[256,2048]{1,0:T(8,128)(2,1)} %get-tuple-element.163), channel_id=1, source_target_pairs={{0,8},{8,0},{16,24},{24,16},{1,9},{9,1},{17,25},{25,17},{2,10},{10... | collective-permute-start | bytes 3145736 | tf_op jit(solution)/shard_map/ppermute | solution.py:60
  483.4 37.7 %collective-permute-start.16 = (bf16[256,2048]{1,0:T(8,128)(2,1)}, bf16[256,2048]{1,0:T(8,128)(2,1)}, u32[]{:S(2)}, u32[]{:S(2)}) collective-permute-start(bf16[256,2048]{1,0:T(8,128)(2,1)} %get-tuple-element.164), channel_id=1, source_target_pairs={{0,16},{8,24},{16,0},{24,8},{1,17},{9,25},{17,1},{25,9},{2,18},{10... | collective-permute-start | bytes 3145736 | tf_op jit(solution)/shard_map/ppermute | solution.py:60
  628.0 41.0 %collective-permute-start.17 = (bf16[256,2048]{1,0:T(8,128)(2,1)}, bf16[256,2048]{1,0:T(8,128)(2,1)}, u32[]{:S(2)}, u32[]{:S(2)}) collective-permute-start(bf16[256,2048]{1,0:T(8,128)(2,1)} %reduce-scatter.7.cloned.1.call-done.refs_0_), channel_id=1, source_target_pairs={{0,8},{8,0},{16,24},{24,16},{1,9},{9,1},{17,25},{25,17},{2,10},{10... | collective-permute-start | bytes 3145736 | tf_op jit(solution)/shard_map/ppermute | solution.py:60
  628.6 40.3 %collective-permute-start.18 = (bf16[256,2048]{1,0:T(8,128)(2,1)}, bf16[256,2048]{1,0:T(8,128)(2,1)}, u32[]{:S(2)}, u32[]{:S(2)}) collective-permute-start(bf16[256,2048]{1,0:T(8,128)(2,1)} %reduce-scatter.7.cloned.1.call-done.refs_0_), channel_id=1, source_target_pairs={{0,16},{8,24},{16,0},{24,8},{1,17},{9,25},{17,1},{25,9},{2,18},{10... | collective-permute-start | bytes 3145736 | tf_op jit(solution)/shard_map/ppermute | solution.py:60
  632.5 36.5 %collective-permute-start.19 = (bf16[128,2048]{1,0:T(8,128)(2,1)}, bf16[128,2048]{1,0:T(8,128)(2,1)}, u32[]{:S(2)}, u32[]{:S(2)}) collective-permute-start(bf16[128,2048]{1,0:T(8,128)(2,1)} %get-tuple-element.249), channel_id=1, source_target_pairs={{0,8},{8,0},{16,24},{24,16},{1,9},{9,1},{17,25},{25,17},{2,10},{10... | collective-permute-start | bytes 1572872 | tf_op jit(solution)/shard_map/ppermute | solution.py:60
  633.3 35.7 %collective-permute-start.20 = (bf16[128,2048]{1,0:T(8,128)(2,1)}, bf16[128,2048]{1,0:T(8,128)(2,1)}, u32[]{:S(2)}, u32[]{:S(2)}) collective-permute-start(bf16[128,2048]{1,0:T(8,128)(2,1)} %get-tuple-element.248), channel_id=1, source_target_pairs={{0,16},{8,24},{16,0},{24,8},{1,17},{9,25},{17,1},{25,9},{2,18},{10... | collective-permute-start | bytes 1572872 | tf_op jit(solution)/shard_map/ppermute | solution.py:60
  674.7 20.8 %collective-permute-start.21 = (bf16[128,2048]{1,0:T(8,128)(2,1)S(1)}, bf16[128,2048]{1,0:T(8,128)(2,1)}, u32[]{:S(2)}, u32[]{:S(2)}) collective-permute-start(bf16[128,2048]{1,0:T(8,128)(2,1)S(1)} %get-tuple-element.215), channel_id=1, source_target_pairs={{0,16},{8,24},{16,0},{24,8},{1,17},{9,25},{17,1},{25,9},{2,18},{10... | collective-permute-start | bytes 1572872 | tf_op jit(solution)/shard_map/ppermute | solution.py:60
  675.4 20.1 %collective-permute-start.22 = (bf16[128,2048]{1,0:T(8,128)(2,1)S(1)}, bf16[128,2048]{1,0:T(8,128)(2,1)}, u32[]{:S(2)}, u32[]{:S(2)}) collective-permute-start(bf16[128,2048]{1,0:T(8,128)(2,1)S(1)} %get-tuple-element.217), channel_id=1, source_target_pairs={{0,8},{8,0},{16,24},{24,16},{1,9},{9,1},{17,25},{25,17},{2,10},{10... | collective-permute-start | bytes 1572872 | tf_op jit(solution)/shard_map/ppermute | solution.py:60
  699.4 20.6 %collective-permute-start.25 = (bf16[256,1536]{1,0:T(8,128)(2,1)}, bf16[256,1536]{1,0:T(8,128)(2,1)S(1)}, u32[]{:S(2)}, u32[]{:S(2)}) collective-permute-start(bf16[256,1536]{1,0:T(8,128)(2,1)} %reduce-scatter.11.cloned.1.call-done.refs_0_), channel_id=1, source_target_pairs={{0,8},{8,0},{16,24},{24,16},{1,9},{9,1},{17,25},{25,17},{2,10},{10... | collective-permute-start | bytes 2359304 | tf_op jit(solution)/shard_map/ppermute | solution.py:60
  700.6 19.3 %collective-permute-start.26 = (bf16[256,1536]{1,0:T(8,128)(2,1)}, bf16[256,1536]{1,0:T(8,128)(2,1)S(1)}, u32[]{:S(2)}, u32[]{:S(2)}) collective-permute-start(bf16[256,1536]{1,0:T(8,128)(2,1)} %reduce-scatter.11.cloned.1.call-done.refs_0_), channel_id=1, source_target_pairs={{0,16},{8,24},{16,0},{24,8},{1,17},{9,25},{17,1},{25,9},{2,18},{10... | collective-permute-start | bytes 2359304 | tf_op jit(solution)/shard_map/ppermute | solution.py:60
  (63 other events, 604.2 us)
Sparse Core Ops, SparseCore 0:
  10.3 68.1 all-gather.4
  80.7 80.6 all-gather.6
  163.6 80.5 all-gather.8
  245.6 80.6 all-gather.10
  329.0 88.0 reduce-scatter.4
  430.5 87.0 reduce-scatter.6
  519.9 87.9 reduce-scatter.8
  626.2 67.0 reduce-scatter.10

commit v6 on v3

--- a/solution.py
+++ b/solution.py
@@ -189,10 +189,11 @@
 
 def attn_bwd_kernel(scale, inv_ref, slope_ref, *refs):
     q_refs, k_refs, v_refs, g_refs = refs[:8], refs[8:16], refs[16:24], refs[24:32]
-    out, stage, sems, dk_acc, dv_acc = refs[32:]
+    out, sum_q, sum_v, stage, sems, dk_acc, dv_acc = refs[32:]
     slope = slope_ref[pl.program_id(1)]
     rows = Rows(inv_ref, stage, out, sems, 3)
     rows.open()
+    total_q = jnp.zeros((1, 128), single)
     for i in (3, 2, 1, 0):
         q, k, e, r = attn_scores(q_refs, k_refs, i, scale, slope)
         n = TILE * (i + 1)
@@ -205,6 +206,7 @@
         pb = p.astype(half)
         dq = (dot_nn(ds, k) * scale).astype(half)
         stage[rows.slot, 0, TILE * i : TILE * (i + 1), :] = dq
+        total_q = total_q + jnp.sum(dq.astype(single), axis=0, keepdims=True)
         dk = dot_tn(ds, q)
         dv = dot_tn(pb, g)
         if i == 3:
@@ -214,7 +216,11 @@
             dk_acc[:n, :] += dk
             dv_acc[:n, :] += dv
     stage[rows.slot, 1] = (dk_acc[...] * scale).astype(half)
-    stage[rows.slot, 2] = dv_acc[...].astype(half)
+    dv = dv_acc[...].astype(half)
+    stage[rows.slot, 2] = dv
+    total_v = jnp.sum(dv.astype(single), axis=0, keepdims=True)
+    sum_q[...] = jnp.broadcast_to(total_q, sum_q.shape)
+    sum_v[...] = jnp.broadcast_to(total_v, sum_v.shape)
     rows.close()
 
 
@@ -229,6 +235,7 @@
 
 def attn_call(kernel, kinds, joined, extra, extra_specs, scratch, inv, slopes, heads, cost, name):
     rows = joined.shape[0]
+    tops = [pl.BlockSpec((8, 128), lambda s, h, inv, slope: (s, h))] * (2 if kinds == 3 else 0)
     specs = block_specs(0) + block_specs(heads) + block_specs(2 * heads) + extra_specs
     return pl.pallas_call(
         kernel,
@@ -236,14 +243,15 @@
             num_scalar_prefetch=2,
             grid=(2, heads),
             in_specs=specs,
-            out_specs=pl.BlockSpec(memory_space=pl.ANY),
+            out_specs=[pl.BlockSpec(memory_space=pl.ANY)] + tops,
             scratch_shapes=[
                 pltpu.VMEM((2, kinds, rows // 2, 128), half),
                 pltpu.SemaphoreType.DMA((2, kinds * SEQ_BLOCKS)),
             ]
             + scratch,
         ),
-        out_shape=jax.ShapeDtypeStruct((rows, kinds * heads * 128), half),
+        out_shape=[jax.ShapeDtypeStruct((rows, kinds * heads * 128), half)]
+        + [jax.ShapeDtypeStruct((16, heads * 128), single)] * len(tops),
         compiler_params=pltpu.CompilerParams(vmem_limit_bytes=48 * 1024 * 1024),
         cost_estimate=cost,
         name=name,
@@ -255,7 +263,7 @@
     cost = hint(20 * 10**9, joined.shape[0] * heads * 128 * 8)
     return attn_call(
         kernel, 1, joined, [], [], [], inv, slopes, heads, cost, "attn_forward"
-    )
+    )[0]
 
 
 def attn_backward(joined, grad, inv, slopes, heads, scale):
@@ -559,7 +567,7 @@
     return out[0], out[1:3], out[3:5]
 
 
-def feed_pass(dz, slope, w_down, w_up, du, total):
+def feed_pass(dz, slope, w_down, w_up, du, total, sums):
     n, width = dz[0].shape
     wide = w_down.shape[0]
     t = math.gcd(wide, 512)
@@ -570,6 +578,8 @@
             grad = dot_nt(x[...], down[...]).astype(half).astype(single)
             grad = (grad * s[...].astype(single)).astype(half)
             d[...] = grad
+            at = pl.ds(pl.multiple_of(pl.program_id(0) * t, t), t)
+            sums[0:1, at] += jnp.sum(grad.astype(single), axis=0, keepdims=True)
             total[i * n : (i + 1) * n, :] += dot_nt(grad, up[...])
 
     pltpu.emit_pipeline(
@@ -585,10 +595,11 @@
 def feed_back_kernel(*refs):
     dz, slope, (w_down, w_up) = refs[0:8], refs[8:13], refs[13:15]
     a2, gb_far = refs[15:20], refs[20:22]
-    du, own, land1, land2, up_grad, mix_x, mix_y = refs[22:27], *refs[27:33]
-    total, far, near, rest, from_x, from_y, mixed = refs[33:40]
-    moves = Moves(*refs[40:42])
-    local = refs[42]
+    du, own, land1, land2, up_grad, mix_x, mix_y, bias = refs[22:27], *refs[27:34]
+    total, far, near, rest, from_x, from_y, mixed, sums = refs[34:42]
+    moves = Moves(*refs[42:44])
+    local = refs[44]
+    sums[...] = jnp.zeros_like(sums)
     n = from_x.shape[0]
     lo, hi = pl.ds(0, n), pl.ds(n, n)
     (s1_lo, s1_hi), (s2_lo, s2_hi) = halves(slope[1]), halves(slope[2])
@@ -610,24 +621,27 @@
         + [pl.BlockSpec((wide, t), lambda i: (0, i))],
     )(*gb_far, w_down)
     second = [moves.start(mixed.at[lo], mix_x, 1), moves.start(mixed.at[hi], mix_y, 2)]
-    feed_pass(dz[6:8], slope[3:5], w_down, w_up, du[3:5], total)
+    feed_pass(dz[6:8], slope[3:5], w_down, w_up, du[3:5], total, sums)
     far[...] = total[...].astype(half)
     first = [moves.start(far.at[lo], from_x, 1), moves.start(far.at[hi], from_y, 2)]
-    feed_pass([dz[2], dz[5]], [s1_lo, s2_hi], w_down, w_up, [d1_lo, d2_hi], total)
+    feed_pass([dz[2], dz[5]], [s1_lo, s2_hi], w_down, w_up, [d1_lo, d2_hi], total, sums)
     near[...] = total[...].astype(half)
     second += [moves.start(near.at[lo], land1_lo, 1), moves.start(near.at[hi], land2_hi, 2)]
-    feed_pass([dz[3], dz[4]], [s1_hi, s2_lo], w_down, w_up, [d1_hi, d2_lo], total)
+    feed_pass([dz[3], dz[4]], [s1_hi, s2_lo], w_down, w_up, [d1_hi, d2_lo], total, sums)
     for copy in first:
         copy.wait()
     rest[lo] = (total[lo] + from_y[...].astype(single)).astype(half)
     rest[hi] = (total[hi] + from_x[...].astype(single)).astype(half)
     second += [moves.start(rest.at[lo], land1_hi, 1), moves.start(rest.at[hi], land2_lo, 2)]
-    feed_pass(dz[0:2], halves(slope[0]), w_down, w_up, halves(du[0]), total)
-    store_own = pltpu.make_async_copy(total, own, local)
-    store_own.start()
+    feed_pass(dz[0:2], halves(slope[0]), w_down, w_up, halves(du[0]), total, sums)
+    stores = [
+        pltpu.make_async_copy(total, own, local.at[0]),
+        pltpu.make_async_copy(sums, bias, local.at[1]),
+    ]
+    for copy in stores:
+        copy.start()
     outer_on(a2, du, up_grad)
-    store_own.wait()
-    for copy in second:
+    for copy in stores + second:
         copy.wait()
 
 
@@ -637,7 +651,7 @@
     anywhere = pl.BlockSpec(memory_space=pl.ANY)
     outs = [((r, wide), half) for r in (rows, rows, rows, n, n)]
     outs += [((rows, width), single)] + [((rows, width), half)] * 2
-    outs += [((width, wide), half)] + [((n, width), half)] * 2
+    outs += [((width, wide), half)] + [((n, width), half)] * 2 + [((8, wide), single)]
     sems = pltpu.SemaphoreType.DMA((8,))
     out = pl.pallas_call(
         feed_back_kernel,
@@ -647,15 +661,15 @@
         scratch_shapes=[pltpu.VMEM((rows, width), single)]
         + [pltpu.VMEM((rows, width), half)] * 3
         + [pltpu.VMEM((n, width), half)] * 2
-        + [pltpu.VMEM((rows, width), half)]
-        + [sems, sems, pltpu.SemaphoreType.DMA],
+        + [pltpu.VMEM((rows, width), half), pltpu.VMEM((8, wide), single)]
+        + [sems, sems, pltpu.SemaphoreType.DMA((2,))],
         compiler_params=pltpu.CompilerParams(
             collective_id=3, has_side_effects=True, vmem_limit_bytes=56 * 1024 * 1024
         ),
         cost_estimate=hint(26 * rows * width * wide, 0),
         name="feed_back",
     )(*dz, *slope, w_down, w_up, *a2, *gb_far)
-    return out[0:5], out[5:8], out[8], out[9:11]
+    return out[5:8], out[8], out[9:11], out[11][0]
 
 
 def heads_back_kernel(part, *refs):
@@ -1117,10 +1131,9 @@
 
     du, dh2, mix = [None] * CTX, [None] * CTX, [None] * CTX
     if CTX == 4:
-        du, dh2, up_grad, mix_first = feed_back(
+        dh2, up_grad, mix_first, up_bias_grad = feed_back(
             flat(dz2), flat(slope), w_down, w_up, flat(a2), gb[far]
         )
-        du = [du]
     else:
         for j in range(CTX):
             du[j] = hidden_back(dz2[j], w_down, slope[j], f"du_{j}")
@@ -1128,6 +1141,7 @@
         arrived = scatter_send(dh2[1:])
         dh2 = dh2[0]
         up_grad = outer(flat(a2), flat(du), "up_grad")
+        up_bias_grad = sum(jnp.sum(x.astype(single), axis=0) for x in flat(du))
         mix[far] = plain(gb[far], w_down, False, half, "mix_far")[0]
         dh2 = total_of(dh2, arrived)
     up_part = scatter_f(up_grad)
@@ -1152,10 +1166,12 @@
             mix[j] = plain(gb[j], w_down, False, half, f"mix_{j}")[0]
         down_near = gather_first(down_part)
     out_part = scatter_f(out_grad)
-    dqkv = attn_backward(joined, dattn, inv, slopes, heads, scale)
+    dqkv, sum_q, sum_v = attn_backward(joined, dattn, inv, slopes, heads, scale)
+    sum_q, sum_v = sum_q[0] + sum_q[8], sum_v[0] + sum_v[8]
     if CTX == 4:
         lows = [swap(one_lo, 1), swap(two_lo, 2)]
-        dqkv = after(dqkv, lows, up_part)
+        down_out = gather_second(down_part, down_near)
+        dqkv = after(dqkv, lows, up_part, down_out)
         dh1, arrived, qkv_grad, mix_own, highs = qkv_back(
             dqkv, w_qkv, a1, gb[0][0], w_down, one_hi, two_hi
         )
@@ -1168,7 +1184,9 @@
         dh1 = dh1[0]
         qkv_grad = outer(a1, [(dqkv, rows, j) for j in range(CTX)], "qkv_grad")
         mix_own = plain(gb[0], w_down, False, single, "mix_0")[0]
+        down_out = gather_second(down_part, down_near)
     qkv_part = scatter_f(qkv_grad)
+
     up_own = after(up_part, arrived)
     up_near = gather_first(up_own)
     out_first = []
@@ -1176,40 +1194,30 @@
         k = out_part.shape[0] // 2
         out_lo, out_hi = after(out_part, arrived)[:k], after(out_part, arrived)[k:]
         out_first = [swap(out_lo, 1), swap(out_hi, 2)]
-    waiting = (dh1, dqkv, mix_own, flat(du), flat(dz2[:1]))
-    dh1, dqkv, mix_own, du, dz2_own = after(waiting, up_near, out_first)
-    up_bias_grad = sum(jnp.sum(x.astype(single), axis=0) for x in du)
-    down_bias_grad = sum(jnp.sum(x.astype(single), axis=0) for x in dz2_own)
+    waiting = (dh1, mix_own, flat(dz2[:1]), down_out)
+    dh1, mix_own, dz2_own, down_out = after(waiting, out_part)
+    down_out = lay_out(0, down_out, c, width // min(width, 512))
     dh1 = total_of(dh1, arrived)
-    down_near, up_near, out_first = after((down_near, up_near, out_first))
-    down_out = gather_second(down_part, down_near)
-    up_out = gather_second(up_own, up_near)
-    out_second = []
     if CTX == 4:
-        out_lo = (out_lo.astype(single) + out_first[0].astype(single)).astype(half)
-        out_hi = (out_hi.astype(single) + out_first[1].astype(single)).astype(half)
-        out_second = [(out_lo, swap(out_lo, 2)), (out_hi, swap(out_hi, 1))]
         mixed = y1 + bias_d + mix_own
         mixed = jnp.concatenate([total_of(mixed[:n], lows), total_of(mixed[n:], highs)])
     else:
         mixed = total_of(y1 + bias_d + mix_own, scatter_send(mix[1:]))
-    sums = jnp.sum(dqkv.astype(single), axis=0)
+    down_bias_grad = sum(jnp.sum(x.astype(single), axis=0) for x in dz2_own)
     normed1_own, inv1_own = norm_parts(tokens.astype(single))
     gain1_grad = jnp.sum(dh1 * normed1_own, axis=0)
     shift1_grad = jnp.sum(dh1, axis=0)
-    dy1 = after(dy1, up_out, down_out, out_second)
     input_grad = dy1 + norm_back(normed1_own, inv1_own, gain1, dh1)
 
+    done = (down_out, input_grad, mixed, down_bias_grad, gain1_grad, shift1_grad)
+    up_near, out_first = after((up_near, out_first), done)
     if CTX == 4:
-        out_out = [x.astype(single) + y.astype(single) for x, y in out_second]
-        out_out = jnp.concatenate(out_out, axis=0)
-    else:
-        bit = 1
-        while bit < CTX:
-            out_out = out_part.astype(single) + swap(out_part, bit).astype(single)
-            out_part = out_out.astype(half)
-            bit *= 2
-
+        out_lo = (out_lo.astype(single) + out_first[0].astype(single)).astype(half)
+        out_hi = (out_hi.astype(single) + out_first[1].astype(single)).astype(half)
+        out_lo, out_hi, up_near = after((out_lo, out_hi, up_near))
+        out_second = [(out_lo, swap(out_lo, 2)), (out_hi, swap(out_hi, 1))]
+    up_out = gather_second(up_own, up_near)
+    up_out = lay_out(1, up_out, c, nf)
     def spread(x, inner):
         x = x.reshape(-1, 1, inner)
         mask = (jnp.arange(CTX) == c)[None, :, None]
@@ -1227,13 +1235,24 @@
         return out
 
     sums_in = [out_bias_grad, gain2_grad, shift2_grad, down_bias_grad, spread(up_bias_grad, fpart)]
-    sums_in += [gain1_grad, shift1_grad, spread(sums[:part], part), spread(sums[2 * part :], part)]
+    sums_in += [gain1_grad, shift1_grad, spread(sum_q, part), spread(sum_v, part)]
+    qkv_part = after(qkv_part, up_out)
     qkv_near = gather_first(qkv_part)
-    sums_in[5] = after(sums_in[5], qkv_near)
+    sums_in[5] = after(sums_in[5], qkv_part)
     sums_out = reduced(sums_in, 2)
+    if CTX == 4:
+        out_second = after(out_second, sums_out)
+        out_out = [x.astype(single) + y.astype(single) for x, y in out_second]
+        out_out = jnp.concatenate(out_out, axis=0)
+    else:
+        bit = 1
+        while bit < CTX:
+            out_out = out_part.astype(single) + swap(out_part, bit).astype(single)
+            out_part = out_out.astype(half)
+            bit *= 2
+
+    qkv_near = after(qkv_near, sums_out)
     qkv_out = lay_out(1, gather_second(qkv_part, qkv_near), c, 3)
-    down_out = lay_out(0, after(down_out, qkv_part), c, width // min(width, 512))
-    up_out = lay_out(1, after(up_out, qkv_part), c, nf)
     out_bias_out, gain2_out, shift2_out, down_bias_out, up_bias_out = sums_out[:5]
     gain1_out, shift1_out, q_bias_out, v_bias_out = sums_out[5:]
     return (

time: 759 us -> 743 us (0.979)
  other arithmetic: 65.7 us -> 53.2 us
  waiting for transfers between devices: 133 us -> 123 us
    ppermute x31, waiting for transfers between devices: 125 us -> 112 us  [swap(): return lax.ppermute(x, 'ctx', [(i, i ^ mask) for i in range(n)])]
    unnamed x153 -> x149, local copies, waits for them, and re-layouts: 21.1 us -> 21.7 us
  transfers between devices with their start and end apart: 39 -> 39, of which waited for: 14 -> 16; matrix products, arithmetic and copies ran while one was open for 14% -> 12% of each run, Pallas kernels for 59% -> 61%
where the time goes in v6:
time: 743 us; the launch traced here: 730 us
  Pallas kernels  450 us (61%)
  waiting for transfers between devices  123 us (17%)
  other arithmetic  53.2 us (7%)
  local copies, waits for them, and re-layouts  44 us (6%)
  starting transfers between devices  36.7 us (5%)
  between operations  15.5 us (2%)
  matrix products  7.85 us (1%)
    pallas_call x2, Pallas kernels, moving_call(): pl.pallas_call(kernel, in_specs=[anywhere] * len(operands), out_specs=[an...  120 us
    ppermute x31, waiting for transfers between devices, swap(): return lax.ppermute(x, 'ctx', [(i, i ^ mask) for i in range(n)])  112 us
    pallas_call x1, Pallas kernels, feed_back(): pl.pallas_call(feed_back_kernel, in_specs=[anywhere] * 22, out_specs=[any...  104 us
    pallas_call x2, Pallas kernels, attn_call(): pl.pallas_call(kernel, grid_spec=pltpu.PrefetchScalarGridSpec(num_scalar_...  61.3 us
    pallas_call x1, Pallas kernels, heads_back(): pl.pallas_call(functools.partial(heads_back_kernel, part), in_specs=[anyw...  48.9 us
    pallas_call x4, Pallas kernels, rows_matmul(): pl.pallas_call(functools.partial(rows_kernel, dot_nt if transposed else d...  43.3 us
    ppermute x31, starting transfers between devices, swap(): return lax.ppermute(x, 'ctx', [(i, i ^ mask) for i in range(n)])  36.3 us
    pallas_call x1, Pallas kernels, outer(): pl.pallas_call(functools.partial(outer_kernel, len(left)), grid=(m // tm,...  33.7 us
  transfers between devices with their start and end apart: 39, of which 16 were waited for; matrix products, arithmetic and copies ran while one was open for 12% of the time, Pallas kernels for 61%

profile of v6, /device:TPU:0, one launch (start us, length us, event | category | flops | bytes accessed | tf_op | source)
XLA Modules:
  0.0 729.9 jit_solution(12402713932556388541)
XLA Ops:
  12.7 3.0 collective-permute-start
  18.1 9.0 %gather_small.1 = f32[8,24,128]{2,1,0:T(8,128)} custom-call(f32[24,128]{1,0:T(8,128)} %bitcast.91), custom_call_target="tpu_custom_call" | custom-call | tf_op jit(solution)/shard_map/gather_small/pallas_call | solution.py:898
  31.9 3.9 convert.46
  42.8 3.5 fusion.41
  46.3 15.2 %collective-permute-done = bf16[512,2048]{1,0:T(8,128)(2,1)} collective-permute-done((bf16[512,2048]{1,0:T(8,128)(2,1)S(1)}, bf16[512,2048]{1,0:T(8,128)(2,1)}, u32[]{:S(2)}, u32[]{:S(2)}) %collective-permute-start) | collective-permute-done | bytes 2097184 | tf_op jit(solution)/shard_map/ppermute | solution.py:60
  76.3 5.7 fusion.21
  82.0 6.1 collective-permute-done.2.refs_0_
  91.0 27.9 %qkv.1 = (bf16[2048,1536]{1,0:T(8,128)(2,1)}, bf16[256,2048]{1,0:T(8,128)(2,1)S(1)}, bf16[256,2048]{1,0:T(8,128)(2,1)}, bf16[256,2048]{1,0:T(8,128)(2,1)}, bf16[256,2048]{1,0:T(8,128)(2,1)}) custom-call(bf16[256,2048]{1,0:T(8,128)(2,1)} %collective-permute-done.2.refs_0_, bf16[256,2048]{1,0:T(8,128)(2,1)} %collective-permute-done.3.refs_1_, ...), custom_call_target="tpu_custom_call" | custom-call | flops 12884901 | tf_op jit(solution)/shard_map/qkv/pallas_call | solution.py:507
  122.1 24.3 %attn_forward.1 = bf16[2048,512]{1,0:T(8,128)(2,1)S(1)} custom-call(s32[16]{0:T(128)S(1)} %select_reduce_fusion.inv_ref, f32[4]{0:T(128)S(1)} %multiply_power_fusion.slope_ref, ...), custom_call_target="tpu_custom_call" | custom-call | flops 20000000 | bytes 8388 | tf_op jit(solution)/shard_map/attn_forward/pallas_call | solution.py:240
  153.3 12.5 %collective-permute-done.6 = bf16[512,512]{1,0:T(8,128)(2,1)S(1)} collective-permute-done((bf16[512,512]{1,0:T(8,128)(2,1)}, bf16[512,512]{1,0:T(8,128)(2,1)S(1)}, u32[]{:S(2)}, u32[]{:S(2)}) %collective-permute-start.6) | collective-permute-done | bytes 524320 | tf_op jit(solution)/shard_map/ppermute | solution.py:60
  165.7 6.9 collective-permute-done.7
  176.1 7.9 %fusion.43 = (f32[512]{0:T(512)S(1)}, f32[512,2048]{1,0:T(8,128)S(1)}) fusion(f32[2048]{0:T(1024)S(1)} %bitcast.94, bf16[2048,2048]{1,0:T(8,128)(2,1)} %all-gather.7.cloned.1.call-done.refs_6_, bf16[512,512]{1,0:T(8,128)(2,1)} %get-tuple-element.221, bf16[512,512]{1,0:T(8,128)(2,1)} %get-tuple-element.220, bf16[512,512]{1,0:T(8,128)(2,1)S(1)} %get-tuple-element.219, ...), kind=kOutput, calls=%fused_computation.157 | convolution fusion | flops 4307549696 | bytes 16787456 | tf_op jit(solution)/shard_map/dot_general | solution.py:24
  188.3 45.3 %collective-permute-done.9.refs_0_.refs_16_ = bf16[512,2048]{1,0:T(8,128)(2,1)S(1)} collective-permute-done((bf16[512,2048]{1,0:T(8,128)(2,1)S(1)}, bf16[512,2048]{1,0:T(8,128)(2,1)S(1)}, u32[]{:S(2)}, u32[]{:S(2)}) %collective-permute-start.9) | collective-permute-done | bytes 2097184 | tf_op jit(solution)/shard_map/ppermute | solution.py:60
  239.9 4.2 all-gather.9.cloned.1.call-done.refs_1_.refs_2_.refs_14_
  244.2 10.9 %up_gelu_0.1 = (bf16[512,2048]{1,0:T(8,128)(2,1)}, bf16[512,2048]{1,0:T(8,128)(2,1)}) custom-call(bf16[512,2048]{1,0:T(8,128)(2,1)} %copy-done.17, bf16[2048,2048]{1,0:T(8,128)(2,1)} %all-gather.9.cloned.1.call-done.refs_1_.refs_2_.refs_14_, f32[1,2048]{1,0:T(1,128)S(1)} %bitcast.71), custom_call_target="tpu_custom_call" | custom-call | flops 4294967 | bytes 16777 | tf_op jit(solution)/shard_map/up_gelu_0/pallas_call | solution.py:319
  255.1 10.8 %up_gelu_1.1 = (bf16[512,2048]{1,0:T(8,128)(2,1)}, bf16[512,2048]{1,0:T(8,128)(2,1)}) custom-call(bf16[512,2048]{1,0:T(8,128)(2,1)} %copy-done.18, bf16[2048,2048]{1,0:T(8,128)(2,1)} %all-gather.9.cloned.1.call-done.refs_1_.refs_2_.refs_14_, f32[1,2048]{1,0:T(1,128)S(1)} %bitcast.72), custom_call_target="tpu_custom_call" | custom-call | flops 4294967 | bytes 16777 | tf_op jit(solution)/shard_map/up_gelu_1/pallas_call | solution.py:319
  266.0 10.8 %up_gelu_2.1 = (bf16[512,2048]{1,0:T(8,128)(2,1)}, bf16[512,2048]{1,0:T(8,128)(2,1)}) custom-call(bf16[512,2048]{1,0:T(8,128)(2,1)} %copy-done.19, bf16[2048,2048]{1,0:T(8,128)(2,1)} %all-gather.9.cloned.1.call-done.refs_1_.refs_2_.refs_14_, f32[1,2048]{1,0:T(1,128)S(1)} %bitcast.73), custom_call_target="tpu_custom_call" | custom-call | flops 4294967 | bytes 16777 | tf_op jit(solution)/shard_map/up_gelu_2/pallas_call | solution.py:319
  277.7 10.7 %up_gelu_3.1 = (bf16[256,2048]{1,0:T(8,128)(2,1)S(1)}, bf16[256,2048]{1,0:T(8,128)(2,1)}, bf16[256,2048]{1,0:T(8,128)(2,1)}, bf16[256,2048]{1,0:T(8,128)(2,1)}) custom-call(bf16[256,2048]{1,0:T(8,128)(2,1)} %copy-done.23, bf16[256,2048]{1,0:T(8,128)(2,1)} %collective-permute-done.14.refs_1_.refs_19_, ...), custom_call_target="tpu_custom_call" | custom-call | flops 4294967 | bytes 16777 | tf_op jit(solution)/shard_map/up_gelu_3/pallas_call | solution.py:319
  288.4 33.7 %down_grad.1 = bf16[2048,2048]{1,0:T(8,128)(2,1)} custom-call(bf16[512,2048]{1,0:T(8,128)(2,1)} %get-tuple-element.132.refs_0_.refs_1_.refs_7_, bf16[512,2048]{1,0:T(8,128)(2,1)} %get-tuple-element.132.refs_0_.refs_1_.refs_7_, bf16[512,2048]{1,0:T(8,128)(2,1)} %get-tuple-element.135.refs_2_.refs_3_.refs_8_, ...), custom_call_target="tpu_custom_call" | custom-call | flops 17179868 | bytes 25165 | tf_op jit(solution)/shard_map/down_grad/pallas_call | solution.py:392
  322.3 4.0 all-gather.11.cloned.1.call-done.refs_13_.refs_10_.refs_8_
  326.3 104.0 %feed_back.1 = (bf16[512,2048]{1,0:T(8,128)(2,1)}, bf16[512,2048]{1,0:T(8,128)(2,1)}, bf16[512,2048]{1,0:T(8,128)(2,1)}, bf16[256,2048]{1,0:T(8,128)(2,1)}, bf16...) custom-call(bf16[256,2048]{1,0:T(8,128)(2,1)} %get-tuple-element.176, ...), custom_call_target="tpu_custom_call" | custom-call | flops 55834576 | tf_op jit(solution)/shard_map/feed_back/pallas_call | solution.py:656
  433.5 48.9 %heads_back.1 = (f32[512,2048]{1,0:T(8,128)}, bf16[512,2048]{1,0:T(8,128)(2,1)}, f32[8,2048]{1,0:T(8,128)}, bf16[2048,512]{1,0:T(8,128)(2,1)}, bf16[2048,2048]{1...) custom-call(f32[512,2048]{1,0:T(8,128)} %get-tuple-element.148.refs_, ...), custom_call_target="tpu_custom_call" | custom-call | flops 21474836 | tf_op jit(solution)/shard_map/heads_back/pallas_call | solution.py:748
  487.9 36.9 %attn_backward.1 = (bf16[2048,1536]{1,0:T(8,128)(2,1)}, f32[16,512]{1,0:T(8,128)S(1)}, f32[16,512]{1,0:T(8,128)S(1)}) custom-call(s32[16]{0:T(128)S(1)} %select_reduce_fusion.inv_ref, f32[4]{0:T(128)S(1)} %multiply_power_fusion.slope_ref, ...), custom_call_target="tpu_custom_call" | custom-call | flops 40000000 | bytes 14680 | tf_op jit(solution)/shard_map/attn_backward/pallas_call | solution.py:240
  526.5 92.1 %qkv_back.1 = (f32[512,2048]{1,0:T(8,128)}, bf16[512,2048]{1,0:T(8,128)(2,1)}, bf16[512,2048]{1,0:T(8,128)(2,1)}, bf16[512,2048]{1,0:T(8,128)(2,1)}, bf16[256,20...) custom-call(bf16[2048,1536]{1,0:T(8,128)(2,1)} %get-tuple-element.16, ...), custom_call_target="tpu_custom_call" | custom-call | flops 30064772 | tf_op jit(solution)/shard_map/qkv_back/pallas_call | solution.py:507
  628.1 6.1 fusion.16
  634.3 3.0 fusion.15
  643.9 3.8 lay_out.3
  650.3 5.8 collective-permute-done.21
  666.6 8.5 %collective-permute-done.23.refs_3_ = bf16[128,2048]{1,0:T(8,128)(2,1)S(1)} collective-permute-done((bf16[128,2048]{1,0:T(8,128)(2,1)}, bf16[128,2048]{1,0:T(8,128)(2,1)S(1)}, u32[]{:S(2)}, u32[]{:S(2)}) %collective-permute-start.23) | collective-permute-done | bytes 524320 | tf_op jit(solution)/shard_map/ppermute | solution.py:60
  677.1 6.5 lay_out.4
  690.0 16.2 %reduce_small.1 = f32[24,128]{1,0:T(8,128)} custom-call(f32[8,24,128]{2,1,0:T(8,128)} %bitcast.79), custom_call_target="tpu_custom_call" | custom-call | tf_op jit(solution)/shard_map/reduce_small/pallas_call | solution.py:969
  719.8 3.1 lay_out.5
  (313 shorter events, 122.9 us)
Async XLA Ops:
  7.3 83.7 %all-gather.5.cloned.1.call-start = ((), (), s32[]{:S(2)}) async-start(), calls=%async_computation.4 | async-start | bytes 7077888 | tf_op jit(solution)/shard_map/all_gather | solution.py:1033
  9.9 166.2 %all-gather.7.cloned.1.call-start = ((), (), s32[]{:S(2)}) async-start(), calls=%async_computation.5 | async-start | bytes 9437184 | tf_op jit(solution)/shard_map/all_gather | solution.py:1033
  12.7 231.5 %all-gather.9.cloned.1.call-start = ((), (), s32[]{:S(2)}) async-start(), calls=%async_computation.6 | async-start | bytes 9437184 | tf_op jit(solution)/shard_map/all_gather | solution.py:1033
  12.7 48.7 %collective-permute-start = (bf16[512,2048]{1,0:T(8,128)(2,1)S(1)}, bf16[512,2048]{1,0:T(8,128)(2,1)}, u32[]{:S(2)}, u32[]{:S(2)}) collective-permute-start(bf16[512,2048]{1,0:T(8,128)(2,1)S(1)} %copy-done.13), channel_id=1, source_target_pairs={{0,8},{8,0},{16,24},{24,16},{1,9},{9,1},{17,25},{25,17},{2,10},{10... | collective-permute-start | bytes 6291464 | tf_op jit(solution)/shard_map/ppermute | solution.py:60
  15.7 47.2 %collective-permute-start.1 = (bf16[512,2048]{1,0:T(8,128)(2,1)S(1)}, bf16[512,2048]{1,0:T(8,128)(2,1)}, u32[]{:S(2)}, u32[]{:S(2)}) collective-permute-start(bf16[512,2048]{1,0:T(8,128)(2,1)S(1)} %copy-done.13), channel_id=1, source_target_pairs={{0,16},{8,24},{16,0},{24,8},{1,17},{9,25},{17,1},{25,9},{2,18},{10... | collective-permute-start | bytes 6291464 | tf_op jit(solution)/shard_map/ppermute | solution.py:60
  64.3 23.9 %collective-permute-start.2 = (bf16[256,2048]{1,0:T(8,128)(2,1)S(1)}, bf16[256,2048]{1,0:T(8,128)(2,1)}, u32[]{:S(2)}, u32[]{:S(2)}) collective-permute-start(bf16[256,2048]{1,0:T(8,128)(2,1)S(1)} %slice.169), channel_id=1, source_target_pairs={{0,16},{8,24},{16,0},{24,8},{1,17},{9,25},{17,1},{25,9},{2,18},{10... | collective-permute-start | bytes 3145736 | tf_op jit(solution)/shard_map/ppermute | solution.py:60
  67.2 23.6 %collective-permute-start.3 = (bf16[256,2048]{1,0:T(8,128)(2,1)S(1)}, bf16[256,2048]{1,0:T(8,128)(2,1)}, u32[]{:S(2)}, u32[]{:S(2)}) collective-permute-start(bf16[256,2048]{1,0:T(8,128)(2,1)S(1)} %slice.170), channel_id=1, source_target_pairs={{0,8},{8,0},{16,24},{24,16},{1,9},{9,1},{17,25},{25,17},{2,10},{10... | collective-permute-start | bytes 3145736 | tf_op jit(solution)/shard_map/ppermute | solution.py:60
  90.8 235.5 %all-gather.11.cloned.1.call-start = ((), (), s32[]{:S(2)}) async-start(), calls=%async_computation.7 | async-start | bytes 9437184 | tf_op jit(solution)/shard_map/all_gather | solution.py:1033
  119.9 313.6 %reduce-scatter.5.cloned.1.call-start = ((), (), s32[]{:S(2)}) async-start(), calls=%async_computation.8 | async-start | bytes 9437184 | tf_op jit(solution)/shard_map/reduce_scatter | solution.py:1069
  120.0 27.8 %collective-permute-start.4 = (bf16[256,2048]{1,0:T(8,128)(2,1)}, bf16[256,2048]{1,0:T(8,128)(2,1)S(1)}, u32[]{:S(2)}, u32[]{:S(2)}) collective-permute-start(bf16[256,2048]{1,0:T(8,128)(2,1)} %get-tuple-element.177.refs_10_.refs_9_.refs_1_), channel_id=1, source_target_pairs={{0,8},{8,0},{16,24},{24,16},{1,9},{9,1},{17,25},{25,17},{2,10},{10... | collective-permute-start | bytes 3145736 | tf_op jit(solution)/shard_map/ppermute | solution.py:60
  121.4 26.4 %collective-permute-start.5 = (bf16[256,2048]{1,0:T(8,128)(2,1)S(1)}, bf16[256,2048]{1,0:T(8,128)(2,1)S(1)}, u32[]{:S(2)}, u32[]{:S(2)}) collective-permute-start(bf16[256,2048]{1,0:T(8,128)(2,1)S(1)} %copy-done.15), channel_id=1, source_target_pairs={{0,16},{8,24},{16,0},{24,8},{1,17},{9,25},{17,1},{25,9},{2,18},{10... | collective-permute-start | bytes 3145736 | tf_op jit(solution)/shard_map/ppermute | solution.py:60
  186.0 47.6 %collective-permute-start.9 = (bf16[512,2048]{1,0:T(8,128)(2,1)S(1)}, bf16[512,2048]{1,0:T(8,128)(2,1)S(1)}, u32[]{:S(2)}, u32[]{:S(2)}) collective-permute-start(bf16[512,2048]{1,0:T(8,128)(2,1)S(1)} %add_convert_fusion.refs_0_.refs_15_), channel_id=1, source_target_pairs={{0,8},{8,0},{16,24},{24,16},{1,9},{9,1},{17,25},{25,17},{2,10},{10... | collective-permute-start | bytes 6291464 | tf_op jit(solution)/shard_map/ppermute | solution.py:60
  187.5 48.6 %collective-permute-start.10 = (bf16[512,2048]{1,0:T(8,128)(2,1)S(1)}, bf16[512,2048]{1,0:T(8,128)(2,1)S(1)}, u32[]{:S(2)}, u32[]{:S(2)}) collective-permute-start(bf16[512,2048]{1,0:T(8,128)(2,1)S(1)} %add_convert_fusion.refs_0_.refs_15_), channel_id=1, source_target_pairs={{0,16},{8,24},{16,0},{24,8},{1,17},{9,25},{17,1},{25,9},{2,18},{10... | collective-permute-start | bytes 6291464 | tf_op jit(solution)/shard_map/ppermute | solution.py:60
  234.7 42.0 %collective-permute-start.13 = (bf16[256,2048]{1,0:T(8,128)(2,1)}, bf16[256,2048]{1,0:T(8,128)(2,1)S(1)}, u32[]{:S(2)}, u32[]{:S(2)}) collective-permute-start(bf16[256,2048]{1,0:T(8,128)(2,1)} %slice.237), channel_id=1, source_target_pairs={{0,16},{8,24},{16,0},{24,8},{1,17},{9,25},{17,1},{25,9},{2,18},{10... | collective-permute-start | bytes 3145736 | tf_op jit(solution)/shard_map/ppermute | solution.py:60
  237.3 39.5 %collective-permute-start.14 = (bf16[256,2048]{1,0:T(8,128)(2,1)}, bf16[256,2048]{1,0:T(8,128)(2,1)}, u32[]{:S(2)}, u32[]{:S(2)}) collective-permute-start(bf16[256,2048]{1,0:T(8,128)(2,1)} %slice.238), channel_id=1, source_target_pairs={{0,8},{8,0},{16,24},{24,16},{1,9},{9,1},{17,25},{25,17},{2,10},{10... | collective-permute-start | bytes 3145736 | tf_op jit(solution)/shard_map/ppermute | solution.py:60
  238.1 50.3 %collective-permute-start.11 = (bf16[256,2048]{1,0:T(8,128)(2,1)}, bf16[256,2048]{1,0:T(8,128)(2,1)}, u32[]{:S(2)}, u32[]{:S(2)}) collective-permute-start(bf16[256,2048]{1,0:T(8,128)(2,1)} %get-tuple-element.127.refs_10_.refs_2_), channel_id=1, source_target_pairs={{0,16},{8,24},{16,0},{24,8},{1,17},{9,25},{17,1},{25,9},{2,18},{10... | collective-permute-start | bytes 3145736 | tf_op jit(solution)/shard_map/ppermute | solution.py:60
  239.3 49.1 %collective-permute-start.12 = (bf16[256,2048]{1,0:T(8,128)(2,1)}, bf16[256,2048]{1,0:T(8,128)(2,1)}, u32[]{:S(2)}, u32[]{:S(2)}) collective-permute-start(bf16[256,2048]{1,0:T(8,128)(2,1)} %get-tuple-element.128.refs_13_.refs_5_), channel_id=1, source_target_pairs={{0,8},{8,0},{16,24},{24,16},{1,9},{9,1},{17,25},{25,17},{2,10},{10... | collective-permute-start | bytes 3145736 | tf_op jit(solution)/shard_map/ppermute | solution.py:60
  322.2 204.2 %reduce-scatter.7.cloned.1.call-start = ((), (), s32[]{:S(2)}) async-start(), calls=%async_computation.9 | async-start | bytes 9437184 | tf_op jit(solution)/shard_map/reduce_scatter | solution.py:1069
  430.4 193.3 %reduce-scatter.9.cloned.1.call-start = ((), (), s32[]{:S(2)}) async-start(), calls=%async_computation.10 | async-start | bytes 9437184 | tf_op jit(solution)/shard_map/reduce_scatter | solution.py:1069
  482.5 203.9 %reduce-scatter.11.cloned.1.call-start = ((), (), s32[]{:S(2)}) async-start(), calls=%async_computation.11 | async-start | bytes 7077888 | tf_op jit(solution)/shard_map/reduce_scatter | solution.py:1069
  482.5 43.9 %collective-permute-start.15 = (bf16[256,2048]{1,0:T(8,128)(2,1)}, bf16[256,2048]{1,0:T(8,128)(2,1)}, u32[]{:S(2)}, u32[]{:S(2)}) collective-permute-start(bf16[256,2048]{1,0:T(8,128)(2,1)} %get-tuple-element.155), channel_id=1, source_target_pairs={{0,8},{8,0},{16,24},{24,16},{1,9},{9,1},{17,25},{25,17},{2,10},{10... | collective-permute-start | bytes 3145736 | tf_op jit(solution)/shard_map/ppermute | solution.py:60
  484.0 42.4 %collective-permute-start.16 = (bf16[256,2048]{1,0:T(8,128)(2,1)}, bf16[256,2048]{1,0:T(8,128)(2,1)}, u32[]{:S(2)}, u32[]{:S(2)}) collective-permute-start(bf16[256,2048]{1,0:T(8,128)(2,1)} %get-tuple-element.156), channel_id=1, source_target_pairs={{0,16},{8,24},{16,0},{24,8},{1,17},{9,25},{17,1},{25,9},{2,18},{10... | collective-permute-start | bytes 3145736 | tf_op jit(solution)/shard_map/ppermute | solution.py:60
  485.1 39.8 %collective-permute-start.17 = (bf16[128,2048]{1,0:T(8,128)(2,1)S(1)}, bf16[128,2048]{1,0:T(8,128)(2,1)S(1)}, u32[]{:S(2)}, u32[]{:S(2)}) collective-permute-start(bf16[128,2048]{1,0:T(8,128)(2,1)S(1)} %slice.186), channel_id=1, source_target_pairs={{0,16},{8,24},{16,0},{24,8},{1,17},{9,25},{17,1},{25,9},{2,18},{10... | collective-permute-start | bytes 1572872 | tf_op jit(solution)/shard_map/ppermute | solution.py:60
  487.3 38.4 %collective-permute-start.18 = (bf16[128,2048]{1,0:T(8,128)(2,1)S(1)}, bf16[128,2048]{1,0:T(8,128)(2,1)S(1)}, u32[]{:S(2)}, u32[]{:S(2)}) collective-permute-start(bf16[128,2048]{1,0:T(8,128)(2,1)S(1)} %slice.187), channel_id=1, source_target_pairs={{0,8},{8,0},{16,24},{24,16},{1,9},{9,1},{17,25},{25,17},{2,10},{10... | collective-permute-start | bytes 1572872 | tf_op jit(solution)/shard_map/ppermute | solution.py:60
  621.6 28.6 %collective-permute-start.19 = (bf16[256,2048]{1,0:T(8,128)(2,1)}, bf16[256,2048]{1,0:T(8,128)(2,1)S(1)}, u32[]{:S(2)}, u32[]{:S(2)}) collective-permute-start(bf16[256,2048]{1,0:T(8,128)(2,1)} %reduce-scatter.7.cloned.1.call-done.refs_0_), channel_id=1, source_target_pairs={{0,8},{8,0},{16,24},{24,16},{1,9},{9,1},{17,25},{25,17},{2,10},{10... | collective-permute-start | bytes 3145736 | tf_op jit(solution)/shard_map/ppermute | solution.py:60
  622.6 27.6 %collective-permute-start.20 = (bf16[256,2048]{1,0:T(8,128)(2,1)}, bf16[256,2048]{1,0:T(8,128)(2,1)S(1)}, u32[]{:S(2)}, u32[]{:S(2)}) collective-permute-start(bf16[256,2048]{1,0:T(8,128)(2,1)} %reduce-scatter.7.cloned.1.call-done.refs_0_), channel_id=1, source_target_pairs={{0,16},{8,24},{16,0},{24,8},{1,17},{9,25},{17,1},{25,9},{2,18},{10... | collective-permute-start | bytes 3145736 | tf_op jit(solution)/shard_map/ppermute | solution.py:60
  626.0 30.1 %collective-permute-start.21 = (bf16[128,2048]{1,0:T(8,128)(2,1)}, bf16[128,2048]{1,0:T(8,128)(2,1)S(1)}, u32[]{:S(2)}, u32[]{:S(2)}) collective-permute-start(bf16[128,2048]{1,0:T(8,128)(2,1)} %get-tuple-element.231), channel_id=1, source_target_pairs={{0,8},{8,0},{16,24},{24,16},{1,9},{9,1},{17,25},{25,17},{2,10},{10... | collective-permute-start | bytes 1572872 | tf_op jit(solution)/shard_map/ppermute | solution.py:60
  626.9 29.8 %collective-permute-start.22 = (bf16[128,2048]{1,0:T(8,128)(2,1)}, bf16[128,2048]{1,0:T(8,128)(2,1)}, u32[]{:S(2)}, u32[]{:S(2)}) collective-permute-start(bf16[128,2048]{1,0:T(8,128)(2,1)} %get-tuple-element.230), channel_id=1, source_target_pairs={{0,16},{8,24},{16,0},{24,8},{1,17},{9,25},{17,1},{25,9},{2,18},{10... | collective-permute-start | bytes 1572872 | tf_op jit(solution)/shard_map/ppermute | solution.py:60
  664.5 44.5 %collective-permute-start.29 = (bf16[128,2048]{1,0:T(8,128)(2,1)}, bf16[128,2048]{1,0:T(8,128)(2,1)}, u32[]{:S(2)}, u32[]{:S(2)}) collective-permute-start(bf16[128,2048]{1,0:T(8,128)(2,1)} %get-tuple-element.201), channel_id=1, source_target_pairs={{0,16},{8,24},{16,0},{24,8},{1,17},{9,25},{17,1},{25,9},{2,18},{10... | collective-permute-start | bytes 1572872 | tf_op jit(solution)/shard_map/ppermute | solution.py:60
  665.7 43.2 %collective-permute-start.30 = (bf16[128,2048]{1,0:T(8,128)(2,1)}, bf16[128,2048]{1,0:T(8,128)(2,1)}, u32[]{:S(2)}, u32[]{:S(2)}) collective-permute-start(bf16[128,2048]{1,0:T(8,128)(2,1)} %get-tuple-element.203), channel_id=1, source_target_pairs={{0,8},{8,0},{16,24},{24,16},{1,9},{9,1},{17,25},{25,17},{2,10},{10... | collective-permute-start | bytes 1572872 | tf_op jit(solution)/shard_map/ppermute | solution.py:60
  686.4 23.9 %collective-permute-start.25 = (bf16[256,1536]{1,0:T(8,128)(2,1)}, bf16[256,1536]{1,0:T(8,128)(2,1)S(1)}, u32[]{:S(2)}, u32[]{:S(2)}) collective-permute-start(bf16[256,1536]{1,0:T(8,128)(2,1)} %reduce-scatter.11.cloned.1.call-done.refs_0_), channel_id=1, source_target_pairs={{0,8},{8,0},{16,24},{24,16},{1,9},{9,1},{17,25},{25,17},{2,10},{10... | collective-permute-start | bytes 2359304 | tf_op jit(solution)/shard_map/ppermute | solution.py:60
  687.8 22.5 %collective-permute-start.26 = (bf16[256,1536]{1,0:T(8,128)(2,1)}, bf16[256,1536]{1,0:T(8,128)(2,1)S(1)}, u32[]{:S(2)}, u32[]{:S(2)}) collective-permute-start(bf16[256,1536]{1,0:T(8,128)(2,1)} %reduce-scatter.11.cloned.1.call-done.refs_0_), channel_id=1, source_target_pairs={{0,16},{8,24},{16,0},{24,8},{1,17},{9,25},{17,1},{25,9},{2,18},{10... | collective-permute-start | bytes 2359304 | tf_op jit(solution)/shard_map/ppermute | solution.py:60
  (64 other events, 641.7 us)
Sparse Core Ops, SparseCore 0:
  10.3 68.1 all-gather.4
  80.7 80.6 all-gather.6
  163.6 80.5 all-gather.8
  245.6 80.6 all-gather.10
  329.0 88.0 reduce-scatter.4
  430.5 87.1 reduce-scatter.6
  520.0 87.9 reduce-scatter.8
  618.8 67.4 reduce-scatter.10

commit v7 on v6

--- a/solution.py
+++ b/solution.py
@@ -568,27 +568,29 @@
 
 
 def feed_pass(dz, slope, w_down, w_up, du, total, sums):
-    n, width = dz[0].shape
+    m, (n, width) = len(dz), dz[0].shape
     wide = w_down.shape[0]
     t = math.gcd(wide, 512)
-    total[...] = jnp.zeros_like(total)
-
-    def body(dz_lo, dz_hi, down, up, slope_lo, slope_hi, du_lo, du_hi):
-        for i, x, s, d in ((0, dz_lo, slope_lo, du_lo), (1, dz_hi, slope_hi, du_hi)):
+    total[0 : m * n] = jnp.zeros((m * n, width), single)
+
+    def body(*refs):
+        down, up = refs[m : m + 2]
+        at = pl.ds(pl.multiple_of(pl.program_id(0) * t, t), t)
+        for i in range(m):
+            x, s, d = refs[i], refs[m + 2 + i], refs[2 * m + 2 + i]
             grad = dot_nt(x[...], down[...]).astype(half).astype(single)
             grad = (grad * s[...].astype(single)).astype(half)
             d[...] = grad
-            at = pl.ds(pl.multiple_of(pl.program_id(0) * t, t), t)
             sums[0:1, at] += jnp.sum(grad.astype(single), axis=0, keepdims=True)
             total[i * n : (i + 1) * n, :] += dot_nt(grad, up[...])
 
     pltpu.emit_pipeline(
         body,
         grid=(wide // t,),
-        in_specs=[pl.BlockSpec((n, width), lambda i: (0, 0))] * 2
+        in_specs=[pl.BlockSpec((n, width), lambda i: (0, 0))] * m
         + [pl.BlockSpec((t, width), lambda i: (i, 0)), pl.BlockSpec((width, t), lambda i: (0, i))]
-        + [pl.BlockSpec((n, t), lambda i: (0, i))] * 2,
-        out_specs=[pl.BlockSpec((n, t), lambda i: (0, i))] * 2,
+        + [pl.BlockSpec((n, t), lambda i: (0, i))] * m,
+        out_specs=[pl.BlockSpec((n, t), lambda i: (0, i))] * m,
     )(*dz, w_down, w_up, *slope, *du)
 
 
@@ -609,33 +611,44 @@
     wide, width = w_down.shape
     t = math.gcd(width, 512)
 
-    def mix(x_lo, x_hi, w):
-        at = pl.ds(pl.multiple_of(pl.program_id(0) * t, t), t)
-        mixed[0:n, at] = dot_nn(x_lo[...], w[...]).astype(half)
-        mixed[n : 2 * n, at] = dot_nn(x_hi[...], w[...]).astype(half)
-
-    pltpu.emit_pipeline(
-        mix,
-        grid=(width // t,),
-        in_specs=[pl.BlockSpec((n, wide), lambda i: (0, 0))] * 2
-        + [pl.BlockSpec((wide, t), lambda i: (0, i))],
-    )(*gb_far, w_down)
-    second = [moves.start(mixed.at[lo], mix_x, 1), moves.start(mixed.at[hi], mix_y, 2)]
+    second = []
+    for part, src, dst, mask in ((lo, gb_far[0], mix_x, 1), (hi, gb_far[1], mix_y, 2)):
+
+        def mix(x, w, part=part):
+            at = pl.ds(pl.multiple_of(pl.program_id(0) * t, t), t)
+            mixed[part, at] = dot_nn(x[...], w[...]).astype(half)
+
+        pltpu.emit_pipeline(
+            mix,
+            grid=(width // t,),
+            in_specs=[
+                pl.BlockSpec((n, wide), lambda i: (0, 0)),
+                pl.BlockSpec((wide, t), lambda i: (0, i)),
+            ],
+        )(src, w_down)
+        second.append(moves.start(mixed.at[part], dst, mask))
     feed_pass(dz[6:8], slope[3:5], w_down, w_up, du[3:5], total, sums)
-    far[...] = total[...].astype(half)
+    far[...] = total[0 : 2 * n].astype(half)
     first = [moves.start(far.at[lo], from_x, 1), moves.start(far.at[hi], from_y, 2)]
     feed_pass([dz[2], dz[5]], [s1_lo, s2_hi], w_down, w_up, [d1_lo, d2_hi], total, sums)
-    near[...] = total[...].astype(half)
+    near[...] = total[0 : 2 * n].astype(half)
     second += [moves.start(near.at[lo], land1_lo, 1), moves.start(near.at[hi], land2_hi, 2)]
-    feed_pass([dz[3], dz[4]], [s1_hi, s2_lo], w_down, w_up, [d1_hi, d2_lo], total, sums)
+    feed_pass(
+        [dz[3], dz[4], dz[0], dz[1]],
+        [s1_hi, s2_lo, *halves(slope[0])],
+        w_down,
+        w_up,
+        [d1_hi, d2_lo, *halves(du[0])],
+        total,
+        sums,
+    )
     for copy in first:
         copy.wait()
     rest[lo] = (total[lo] + from_y[...].astype(single)).astype(half)
     rest[hi] = (total[hi] + from_x[...].astype(single)).astype(half)
     second += [moves.start(rest.at[lo], land1_hi, 1), moves.start(rest.at[hi], land2_lo, 2)]
-    feed_pass(dz[0:2], halves(slope[0]), w_down, w_up, halves(du[0]), total, sums)
     stores = [
-        pltpu.make_async_copy(total, own, local.at[0]),
+        pltpu.make_async_copy(total.at[pl.ds(2 * n, 2 * n)], own, local.at[0]),
         pltpu.make_async_copy(sums, bias, local.at[1]),
     ]
     for copy in stores:
@@ -658,7 +671,7 @@
         in_specs=[anywhere] * 22,
         out_specs=[anywhere] * len(outs),
         out_shape=[jax.ShapeDtypeStruct(shape, dtype) for shape, dtype in outs],
-        scratch_shapes=[pltpu.VMEM((rows, width), single)]
+        scratch_shapes=[pltpu.VMEM((2 * rows, width), single)]
         + [pltpu.VMEM((rows, width), half)] * 3
         + [pltpu.VMEM((n, width), half)] * 2
         + [pltpu.VMEM((rows, width), half), pltpu.VMEM((8, wide), single)]
@@ -676,15 +689,17 @@
     own, land1, land2, cot, y1, gain, w_out = refs[0:7]
     ob, gb1, gb2, w_down, mix_x, mix_y, down = refs[7:14]
     dy1, dz1, sums, got, out_grad = refs[14:19]
-    mix, down1, down2 = refs[19:23], refs[23], refs[24]
-    dz, w, stage = refs[25:28]
-    moves = Moves(*refs[28:30])
-    local = refs[30]
+    mix, (one_lo, one_hi, two_lo, two_hi) = refs[19:23], refs[23:27]
+    dz, w, stage = refs[27:30]
+    moves = Moves(*refs[30:32])
+    local = refs[32]
     rows, width = own.shape
     greet((1, 2, 3))
     load = pltpu.make_async_copy(w_out, w, local.at[0])
     load.start()
-    copies = [moves.start(down, down1, 1), moves.start(down, down2, 2)]
+    down_lo, down_hi = halves(down)
+    copies = [moves.start(down_lo, one_lo, 1), moves.start(down_hi, two_hi, 2)]
+    copies += [moves.start(down_hi, one_hi, 1), moves.start(down_lo, two_lo, 2)]
     t = math.gcd(rows, 64)
 
     def norm(own, one, two, cot, y1, gain, dy1, dz1, sums):
@@ -741,10 +756,10 @@
     rows, width = cot.shape
     part = width // 4
     anywhere = pl.BlockSpec(memory_space=pl.ANY)
-    sems = pltpu.SemaphoreType.DMA((5,))
+    sems = pltpu.SemaphoreType.DMA((7,))
     outs = [((rows, width), single), ((rows, width), half), ((8, width), single)]
     outs += [((4 * rows, part), half), ((width, width), half)]
-    outs += [((rows // 2, width), half)] * 4 + [(down.shape, half)] * 2
+    outs += [((rows // 2, width), half)] * 4 + [((down.shape[0] // 2, width), half)] * 4
     out = pl.pallas_call(
         functools.partial(heads_back_kernel, part),
         in_specs=[anywhere] * 14,
@@ -764,7 +779,7 @@
         cost_estimate=hint(10 * rows * width * width, 0),
         name="heads_back",
     )(*terms, cot, y1, gain.reshape(1, -1), w_out, ob, gb1, gb2, w_down, *mix_first, down)
-    return out[0], out[2], out[3], out[4], out[5:9], out[9:11]
+    return out[0], out[2], out[3], out[4], out[5:9], out[9:13]
 
 
 def qkv_back_kernel(*refs):
@@ -1103,7 +1118,7 @@
     mine = [attended[j * rows : (j + 1) * rows] for j in range(CTX)]
     mine = after(mine, dz2_rest)
     mine = [mine[0]] + [swap(mine[j], j) for j in range(1, CTX)]
-    ob = jnp.concatenate(xor_order(mine, c), axis=1)
+    ob = after(jnp.concatenate(xor_order(mine, c), axis=1))
     y1 = tokens.astype(single) + dot_nn(ob, w_out) + bias_o
 
     normed2, inv2 = norm_parts(y1)
@@ -1170,8 +1185,9 @@
     sum_q, sum_v = sum_q[0] + sum_q[8], sum_v[0] + sum_v[8]
     if CTX == 4:
         lows = [swap(one_lo, 1), swap(two_lo, 2)]
-        down_out = gather_second(down_part, down_near)
-        dqkv = after(dqkv, lows, up_part, down_out)
+        down_far = [swap(down_near[0], 2), swap(down_near[3], 1)]
+        down_out = [[down_part], list(down_near[0:2]), list(down_near[2:4]), down_far]
+        dqkv = after(dqkv, lows, up_part, down_far)
         dh1, arrived, qkv_grad, mix_own, highs = qkv_back(
             dqkv, w_qkv, a1, gb[0][0], w_down, one_hi, two_hi
         )

time: 743 us -> 743 us (level)
    pallas_call x1, Pallas kernels: 33.7 us -> 23.5 us  [outer(): pl.pallas_call(functools.partial(outer_kernel, len(left)), grid=(m // tm,...]
    pallas_call x4, Pallas kernels: 43.3 us -> 53.5 us  [rows_matmul(): pl.pallas_call(functools.partial(rows_kernel, dot_nt if transposed else d...]
    unnamed x149 -> x139, local copies, waits for them, and re-layouts: 21.7 us -> 21.2 us
  transfers between devices with their start and end apart: 39 -> 39, of which waited for: 16 -> 17; matrix products, arithmetic and copies ran while one was open for 12% -> 12% of each run, Pallas kernels for 61% -> 62%
where the time goes in v7:
time: 743 us; the launch traced here: 729 us
  Pallas kernels  453 us (61%)
  waiting for transfers between devices  122 us (16%)
  other arithmetic  52.4 us (7%)
  local copies, waits for them, and re-layouts  42.8 us (6%)
  starting transfers between devices  36.2 us (5%)
  between operations  15.5 us (2%)
  matrix products  7.77 us (1%)
    pallas_call x2, Pallas kernels, moving_call(): pl.pallas_call(kernel, in_specs=[anywhere] * len(operands), out_specs=[an...  118 us
    pallas_call x1, Pallas kernels, feed_back(): pl.pallas_call(feed_back_kernel, in_specs=[anywhere] * 22, out_specs=[any...  108 us
    ppermute x31, waiting for transfers between devices, swap(): return lax.ppermute(x, 'ctx', [(i, i ^ mask) for i in range(n)])  107 us
    pallas_call x2, Pallas kernels, attn_call(): pl.pallas_call(kernel, grid_spec=pltpu.PrefetchScalarGridSpec(num_scalar_...  61.2 us
    pallas_call x4, Pallas kernels, rows_matmul(): pl.pallas_call(functools.partial(rows_kernel, dot_nt if transposed else d...  53.5 us
    pallas_call x1, Pallas kernels, heads_back(): pl.pallas_call(functools.partial(heads_back_kernel, part), in_specs=[anyw...  49.7 us
    ppermute x31, starting transfers between devices, swap(): return lax.ppermute(x, 'ctx', [(i, i ^ mask) for i in range(n)])  35.8 us
    pallas_call x1, Pallas kernels, outer(): pl.pallas_call(functools.partial(outer_kernel, len(left)), grid=(m // tm,...  23.5 us
  transfers between devices with their start and end apart: 39, of which 17 were waited for; matrix products, arithmetic and copies ran while one was open for 12% of the time, Pallas kernels for 62%

profile of v7, /device:TPU:0, one launch (start us, length us, event | category | flops | bytes accessed | tf_op | source)
XLA Modules:
  0.0 729.4 jit_solution(13434245842805797429)
XLA Ops:
  18.1 9.1 %gather_small.1 = f32[8,24,128]{2,1,0:T(8,128)} custom-call(f32[24,128]{1,0:T(8,128)} %bitcast.92), custom_call_target="tpu_custom_call" | custom-call | tf_op jit(solution)/shard_map/gather_small/pallas_call | solution.py:913
  32.9 3.9 convert.46
  46.5 3.3 fusion.41
  49.9 11.6 %collective-permute-done = bf16[512,2048]{1,0:T(8,128)(2,1)} collective-permute-done((bf16[512,2048]{1,0:T(8,128)(2,1)S(1)}, bf16[512,2048]{1,0:T(8,128)(2,1)}, u32[]{:S(2)}, u32[]{:S(2)}) %collective-permute-start) | collective-permute-done | bytes 2097184 | tf_op jit(solution)/shard_map/ppermute | solution.py:60
  76.3 5.7 fusion.21
  82.0 6.1 collective-permute-done.2.refs_0_
  91.0 27.9 %qkv.1 = (bf16[2048,1536]{1,0:T(8,128)(2,1)}, bf16[256,2048]{1,0:T(8,128)(2,1)S(1)}, bf16[256,2048]{1,0:T(8,128)(2,1)}, bf16[256,2048]{1,0:T(8,128)(2,1)}, bf16[256,2048]{1,0:T(8,128)(2,1)}) custom-call(bf16[256,2048]{1,0:T(8,128)(2,1)} %collective-permute-done.2.refs_0_, bf16[256,2048]{1,0:T(8,128)(2,1)} %collective-permute-done.3.refs_1_, ...), custom_call_target="tpu_custom_call" | custom-call | flops 12884901 | tf_op jit(solution)/shard_map/qkv/pallas_call | solution.py:507
  122.1 24.4 %attn_forward.1 = bf16[2048,512]{1,0:T(8,128)(2,1)S(1)} custom-call(s32[16]{0:T(128)S(1)} %select_reduce_fusion.inv_ref, f32[4]{0:T(128)S(1)} %multiply_power_fusion.slope_ref, ...), custom_call_target="tpu_custom_call" | custom-call | flops 20000000 | bytes 8388 | tf_op jit(solution)/shard_map/attn_forward/pallas_call | solution.py:240
  151.2 12.6 %collective-permute-done.6 = bf16[512,512]{1,0:T(8,128)(2,1)} collective-permute-done((bf16[512,512]{1,0:T(8,128)(2,1)}, bf16[512,512]{1,0:T(8,128)(2,1)}, u32[]{:S(2)}, u32[]{:S(2)}) %collective-permute-start.6) | collective-permute-done | bytes 524320 | tf_op jit(solution)/shard_map/ppermute | solution.py:60
  163.8 6.8 collective-permute-done.7
  174.2 7.8 %fusion.43 = (f32[512]{0:T(512)S(1)}, f32[512,2048]{1,0:T(8,128)S(1)}) fusion(f32[2048]{0:T(1024)S(1)} %bitcast.95, bf16[512,2048]{1,0:T(8,128)(2,1)} %pad_maximum_fusion.1.refs_7_, bf16[2048,2048]{1,0:T(8,128)(2,1)} %all-gather.7.cloned.1.call-done.refs_6_, bf16[512,2048]{1,0:T(8,128)(2,1)S(1)} %copy-done.18), kind=kOutput, calls=%fused_computation.157 | convolution fusion | flops 4299161088 | bytes 16787456 | tf_op jit(solution)/shard_map/dot_general | solution.py:24
  185.9 45.4 %collective-permute-done.9.refs_0_.refs_16_ = bf16[512,2048]{1,0:T(8,128)(2,1)S(1)} collective-permute-done((bf16[512,2048]{1,0:T(8,128)(2,1)S(1)}, bf16[512,2048]{1,0:T(8,128)(2,1)S(1)}, u32[]{:S(2)}, u32[]{:S(2)}) %collective-permute-start.9) | collective-permute-done | bytes 2097184 | tf_op jit(solution)/shard_map/ppermute | solution.py:60
  237.6 6.6 all-gather.9.cloned.1.call-done.refs_1_.refs_2_.refs_14_
  244.2 11.0 %up_gelu_0.1 = (bf16[512,2048]{1,0:T(8,128)(2,1)}, bf16[512,2048]{1,0:T(8,128)(2,1)}) custom-call(bf16[512,2048]{1,0:T(8,128)(2,1)} %copy-done.21, bf16[2048,2048]{1,0:T(8,128)(2,1)} %all-gather.9.cloned.1.call-done.refs_1_.refs_2_.refs_14_, f32[1,2048]{1,0:T(1,128)S(1)} %bitcast.72), custom_call_target="tpu_custom_call" | custom-call | flops 4294967 | bytes 16777 | tf_op jit(solution)/shard_map/up_gelu_0/pallas_call | solution.py:319
  255.2 10.8 %up_gelu_1.1 = (bf16[512,2048]{1,0:T(8,128)(2,1)}, bf16[512,2048]{1,0:T(8,128)(2,1)}) custom-call(bf16[512,2048]{1,0:T(8,128)(2,1)} %copy-done.22, bf16[2048,2048]{1,0:T(8,128)(2,1)} %all-gather.9.cloned.1.call-done.refs_1_.refs_2_.refs_14_, f32[1,2048]{1,0:T(1,128)S(1)} %bitcast.73), custom_call_target="tpu_custom_call" | custom-call | flops 4294967 | bytes 16777 | tf_op jit(solution)/shard_map/up_gelu_1/pallas_call | solution.py:319
  265.9 10.8 %up_gelu_2.1 = (bf16[512,2048]{1,0:T(8,128)(2,1)}, bf16[512,2048]{1,0:T(8,128)(2,1)}) custom-call(bf16[512,2048]{1,0:T(8,128)(2,1)} %copy-done.23, bf16[2048,2048]{1,0:T(8,128)(2,1)} %all-gather.9.cloned.1.call-done.refs_1_.refs_2_.refs_14_, f32[1,2048]{1,0:T(1,128)S(1)} %bitcast.74), custom_call_target="tpu_custom_call" | custom-call | flops 4294967 | bytes 16777 | tf_op jit(solution)/shard_map/up_gelu_2/pallas_call | solution.py:319
  277.7 21.0 %up_gelu_3.1 = (bf16[256,2048]{1,0:T(8,128)(2,1)S(1)}, bf16[256,2048]{1,0:T(8,128)(2,1)}, bf16[256,2048]{1,0:T(8,128)(2,1)}, bf16[256,2048]{1,0:T(8,128)(2,1)}) custom-call(bf16[256,2048]{1,0:T(8,128)(2,1)} %copy-done.26, bf16[256,2048]{1,0:T(8,128)(2,1)} %collective-permute-done.14.refs_1_.refs_19_, ...), custom_call_target="tpu_custom_call" | custom-call | flops 4294967 | bytes 16777 | tf_op jit(solution)/shard_map/up_gelu_3/pallas_call | solution.py:319
  298.7 23.5 %down_grad.1 = bf16[2048,2048]{1,0:T(8,128)(2,1)} custom-call(bf16[512,2048]{1,0:T(8,128)(2,1)} %get-tuple-element.136.refs_0_.refs_1_.refs_7_, bf16[512,2048]{1,0:T(8,128)(2,1)} %get-tuple-element.136.refs_0_.refs_1_.refs_7_, bf16[512,2048]{1,0:T(8,128)(2,1)} %get-tuple-element.139.refs_2_.refs_3_.refs_8_, ...), custom_call_target="tpu_custom_call" | custom-call | flops 17179868 | bytes 25165 | tf_op jit(solution)/shard_map/down_grad/pallas_call | solution.py:392
  322.3 4.0 all-gather.11.cloned.1.call-done.refs_13_.refs_10_.refs_8_
  326.3 107.5 %feed_back.1 = (bf16[512,2048]{1,0:T(8,128)(2,1)}, bf16[512,2048]{1,0:T(8,128)(2,1)}, bf16[512,2048]{1,0:T(8,128)(2,1)}, bf16[256,2048]{1,0:T(8,128)(2,1)}, bf16...) custom-call(bf16[256,2048]{1,0:T(8,128)(2,1)} %get-tuple-element.182, ...), custom_call_target="tpu_custom_call" | custom-call | flops 55834576 | tf_op jit(solution)/shard_map/feed_back/pallas_call | solution.py:669
  434.5 49.7 %heads_back.1 = (f32[512,2048]{1,0:T(8,128)}, bf16[512,2048]{1,0:T(8,128)(2,1)}, f32[8,2048]{1,0:T(8,128)}, bf16[2048,512]{1,0:T(8,128)(2,1)}, bf16[2048,2048]{1...) custom-call(f32[512,2048]{1,0:T(8,128)} %get-tuple-element.152.refs_, ...), custom_call_target="tpu_custom_call" | custom-call | flops 21474836 | tf_op jit(solution)/shard_map/heads_back/pallas_call | solution.py:763
  488.5 36.9 %attn_backward.1 = (bf16[2048,1536]{1,0:T(8,128)(2,1)}, f32[16,512]{1,0:T(8,128)S(1)}, f32[16,512]{1,0:T(8,128)S(1)}) custom-call(s32[16]{0:T(128)S(1)} %select_reduce_fusion.inv_ref, f32[4]{0:T(128)S(1)} %multiply_power_fusion.slope_ref, ...), custom_call_target="tpu_custom_call" | custom-call | flops 40000000 | bytes 14680 | tf_op jit(solution)/shard_map/attn_backward/pallas_call | solution.py:240
  527.0 90.6 %qkv_back.1 = (f32[512,2048]{1,0:T(8,128)}, bf16[512,2048]{1,0:T(8,128)(2,1)}, bf16[512,2048]{1,0:T(8,128)(2,1)}, bf16[512,2048]{1,0:T(8,128)(2,1)}, bf16[256,20...) custom-call(bf16[2048,1536]{1,0:T(8,128)(2,1)} %get-tuple-element.16, ...), custom_call_target="tpu_custom_call" | custom-call | flops 30064772 | tf_op jit(solution)/shard_map/qkv_back/pallas_call | solution.py:507
  627.1 6.2 fusion.16
  633.4 3.0 fusion.15
  643.1 3.8 lay_out.3
  649.4 4.3 collective-permute-done.21
  665.1 8.6 %collective-permute-done.23.refs_3_ = bf16[128,2048]{1,0:T(8,128)(2,1)} collective-permute-done((bf16[128,2048]{1,0:T(8,128)(2,1)}, bf16[128,2048]{1,0:T(8,128)(2,1)}, u32[]{:S(2)}, u32[]{:S(2)}) %collective-permute-start.23) | collective-permute-done | bytes 524320 | tf_op jit(solution)/shard_map/ppermute | solution.py:60
  674.9 6.6 lay_out.4
  681.5 4.3 reduce-scatter.11.cloned.1.call-done.refs_0_
  689.4 16.3 %reduce_small.1 = f32[24,128]{1,0:T(8,128)} custom-call(f32[8,24,128]{2,1,0:T(8,128)} %bitcast.80), custom_call_target="tpu_custom_call" | custom-call | tf_op jit(solution)/shard_map/reduce_small/pallas_call | solution.py:984
  719.2 3.1 lay_out.5
  (301 shorter events, 120.9 us)
Async XLA Ops:
  7.3 83.7 %all-gather.5.cloned.1.call-start = ((), (), s32[]{:S(2)}) async-start(), calls=%async_computation.4 | async-start | bytes 7077888 | tf_op jit(solution)/shard_map/all_gather | solution.py:1048
  9.9 164.3 %all-gather.7.cloned.1.call-start = ((), (), s32[]{:S(2)}) async-start(), calls=%async_computation.5 | async-start | bytes 9437184 | tf_op jit(solution)/shard_map/all_gather | solution.py:1048
  12.7 231.5 %all-gather.9.cloned.1.call-start = ((), (), s32[]{:S(2)}) async-start(), calls=%async_computation.6 | async-start | bytes 9437184 | tf_op jit(solution)/shard_map/all_gather | solution.py:1048
  12.7 48.7 %collective-permute-start = (bf16[512,2048]{1,0:T(8,128)(2,1)S(1)}, bf16[512,2048]{1,0:T(8,128)(2,1)}, u32[]{:S(2)}, u32[]{:S(2)}) collective-permute-start(bf16[512,2048]{1,0:T(8,128)(2,1)S(1)} %copy-done.18), channel_id=1, source_target_pairs={{0,8},{8,0},{16,24},{24,16},{1,9},{9,1},{17,25},{25,17},{2,10},{10... | collective-permute-start | bytes 6291464 | tf_op jit(solution)/shard_map/ppermute | solution.py:60
  15.7 47.2 %collective-permute-start.1 = (bf16[512,2048]{1,0:T(8,128)(2,1)S(1)}, bf16[512,2048]{1,0:T(8,128)(2,1)}, u32[]{:S(2)}, u32[]{:S(2)}) collective-permute-start(bf16[512,2048]{1,0:T(8,128)(2,1)S(1)} %copy-done.18), channel_id=1, source_target_pairs={{0,16},{8,24},{16,0},{24,8},{1,17},{9,25},{17,1},{25,9},{2,18},{10... | collective-permute-start | bytes 6291464 | tf_op jit(solution)/shard_map/ppermute | solution.py:60
  64.3 23.9 %collective-permute-start.2 = (bf16[256,2048]{1,0:T(8,128)(2,1)S(1)}, bf16[256,2048]{1,0:T(8,128)(2,1)}, u32[]{:S(2)}, u32[]{:S(2)}) collective-permute-start(bf16[256,2048]{1,0:T(8,128)(2,1)S(1)} %slice.163), channel_id=1, source_target_pairs={{0,16},{8,24},{16,0},{24,8},{1,17},{9,25},{17,1},{25,9},{2,18},{10... | collective-permute-start | bytes 3145736 | tf_op jit(solution)/shard_map/ppermute | solution.py:60
  67.2 23.6 %collective-permute-start.3 = (bf16[256,2048]{1,0:T(8,128)(2,1)S(1)}, bf16[256,2048]{1,0:T(8,128)(2,1)}, u32[]{:S(2)}, u32[]{:S(2)}) collective-permute-start(bf16[256,2048]{1,0:T(8,128)(2,1)S(1)} %slice.164), channel_id=1, source_target_pairs={{0,8},{8,0},{16,24},{24,16},{1,9},{9,1},{17,25},{25,17},{2,10},{10... | collective-permute-start | bytes 3145736 | tf_op jit(solution)/shard_map/ppermute | solution.py:60
  90.8 235.5 %all-gather.11.cloned.1.call-start = ((), (), s32[]{:S(2)}) async-start(), calls=%async_computation.7 | async-start | bytes 9437184 | tf_op jit(solution)/shard_map/all_gather | solution.py:1048
  119.9 314.6 %reduce-scatter.5.cloned.1.call-start = ((), (), s32[]{:S(2)}) async-start(), calls=%async_computation.8 | async-start | bytes 9437184 | tf_op jit(solution)/shard_map/reduce_scatter | solution.py:1084
  120.0 27.7 %collective-permute-start.4 = (bf16[256,2048]{1,0:T(8,128)(2,1)}, bf16[256,2048]{1,0:T(8,128)(2,1)}, u32[]{:S(2)}, u32[]{:S(2)}) collective-permute-start(bf16[256,2048]{1,0:T(8,128)(2,1)} %get-tuple-element.183.refs_10_.refs_9_.refs_1_), channel_id=1, source_target_pairs={{0,8},{8,0},{16,24},{24,16},{1,9},{9,1},{17,25},{25,17},{2,10},{10... | collective-permute-start | bytes 3145736 | tf_op jit(solution)/shard_map/ppermute | solution.py:60
  121.5 26.2 %collective-permute-start.5 = (bf16[256,2048]{1,0:T(8,128)(2,1)}, bf16[256,2048]{1,0:T(8,128)(2,1)}, u32[]{:S(2)}, u32[]{:S(2)}) collective-permute-start(bf16[256,2048]{1,0:T(8,128)(2,1)} %get-tuple-element.182.refs_9_.refs_8_.refs_0_), channel_id=1, source_target_pairs={{0,16},{8,24},{16,0},{24,8},{1,17},{9,25},{17,1},{25,9},{2,18},{10... | collective-permute-start | bytes 3145736 | tf_op jit(solution)/shard_map/ppermute | solution.py:60
  184.0 47.2 %collective-permute-start.9 = (bf16[512,2048]{1,0:T(8,128)(2,1)S(1)}, bf16[512,2048]{1,0:T(8,128)(2,1)S(1)}, u32[]{:S(2)}, u32[]{:S(2)}) collective-permute-start(bf16[512,2048]{1,0:T(8,128)(2,1)S(1)} %add_convert_fusion.refs_0_.refs_15_), channel_id=1, source_target_pairs={{0,8},{8,0},{16,24},{24,16},{1,9},{9,1},{17,25},{25,17},{2,10},{10... | collective-permute-start | bytes 6291464 | tf_op jit(solution)/shard_map/ppermute | solution.py:60
  185.2 48.7 %collective-permute-start.10 = (bf16[512,2048]{1,0:T(8,128)(2,1)S(1)}, bf16[512,2048]{1,0:T(8,128)(2,1)S(1)}, u32[]{:S(2)}, u32[]{:S(2)}) collective-permute-start(bf16[512,2048]{1,0:T(8,128)(2,1)S(1)} %add_convert_fusion.refs_0_.refs_15_), channel_id=1, source_target_pairs={{0,16},{8,24},{16,0},{24,8},{1,17},{9,25},{17,1},{25,9},{2,18},{10... | collective-permute-start | bytes 6291464 | tf_op jit(solution)/shard_map/ppermute | solution.py:60
  232.4 44.3 %collective-permute-start.13 = (bf16[256,2048]{1,0:T(8,128)(2,1)}, bf16[256,2048]{1,0:T(8,128)(2,1)S(1)}, u32[]{:S(2)}, u32[]{:S(2)}) collective-permute-start(bf16[256,2048]{1,0:T(8,128)(2,1)} %slice.229), channel_id=1, source_target_pairs={{0,16},{8,24},{16,0},{24,8},{1,17},{9,25},{17,1},{25,9},{2,18},{10... | collective-permute-start | bytes 3145736 | tf_op jit(solution)/shard_map/ppermute | solution.py:60
  235.0 41.7 %collective-permute-start.14 = (bf16[256,2048]{1,0:T(8,128)(2,1)}, bf16[256,2048]{1,0:T(8,128)(2,1)}, u32[]{:S(2)}, u32[]{:S(2)}) collective-permute-start(bf16[256,2048]{1,0:T(8,128)(2,1)} %slice.230), channel_id=1, source_target_pairs={{0,8},{8,0},{16,24},{24,16},{1,9},{9,1},{17,25},{25,17},{2,10},{10... | collective-permute-start | bytes 3145736 | tf_op jit(solution)/shard_map/ppermute | solution.py:60
  235.6 63.0 %collective-permute-start.11 = (bf16[256,2048]{1,0:T(8,128)(2,1)S(1)}, bf16[256,2048]{1,0:T(8,128)(2,1)}, u32[]{:S(2)}, u32[]{:S(2)}) collective-permute-start(bf16[256,2048]{1,0:T(8,128)(2,1)S(1)} %copy-done.25), channel_id=1, source_target_pairs={{0,16},{8,24},{16,0},{24,8},{1,17},{9,25},{17,1},{25,9},{2,18},{10... | collective-permute-start | bytes 3145736 | tf_op jit(solution)/shard_map/ppermute | solution.py:60
  237.1 61.6 %collective-permute-start.12 = (bf16[256,2048]{1,0:T(8,128)(2,1)}, bf16[256,2048]{1,0:T(8,128)(2,1)}, u32[]{:S(2)}, u32[]{:S(2)}) collective-permute-start(bf16[256,2048]{1,0:T(8,128)(2,1)} %get-tuple-element.132.refs_13_.refs_5_), channel_id=1, source_target_pairs={{0,8},{8,0},{16,24},{24,16},{1,9},{9,1},{17,25},{25,17},{2,10},{10... | collective-permute-start | bytes 3145736 | tf_op jit(solution)/shard_map/ppermute | solution.py:60
  322.2 204.7 %reduce-scatter.7.cloned.1.call-start = ((), (), s32[]{:S(2)}) async-start(), calls=%async_computation.9 | async-start | bytes 9437184 | tf_op jit(solution)/shard_map/reduce_scatter | solution.py:1084
  433.9 188.8 %reduce-scatter.9.cloned.1.call-start = ((), (), s32[]{:S(2)}) async-start(), calls=%async_computation.10 | async-start | bytes 9437184 | tf_op jit(solution)/shard_map/reduce_scatter | solution.py:1084
  484.3 201.5 %reduce-scatter.11.cloned.1.call-start = ((), (), s32[]{:S(2)}) async-start(), calls=%async_computation.11 | async-start | bytes 7077888 | tf_op jit(solution)/shard_map/reduce_scatter | solution.py:1084
  484.3 42.6 %collective-permute-start.15 = (bf16[256,2048]{1,0:T(8,128)(2,1)}, bf16[256,2048]{1,0:T(8,128)(2,1)}, u32[]{:S(2)}, u32[]{:S(2)}) collective-permute-start(bf16[256,2048]{1,0:T(8,128)(2,1)} %get-tuple-element.159), channel_id=1, source_target_pairs={{0,8},{8,0},{16,24},{24,16},{1,9},{9,1},{17,25},{25,17},{2,10},{10... | collective-permute-start | bytes 3145736 | tf_op jit(solution)/shard_map/ppermute | solution.py:60
  484.6 42.4 %collective-permute-start.16 = (bf16[256,2048]{1,0:T(8,128)(2,1)}, bf16[256,2048]{1,0:T(8,128)(2,1)}, u32[]{:S(2)}, u32[]{:S(2)}) collective-permute-start(bf16[256,2048]{1,0:T(8,128)(2,1)} %get-tuple-element.160), channel_id=1, source_target_pairs={{0,16},{8,24},{16,0},{24,8},{1,17},{9,25},{17,1},{25,9},{2,18},{10... | collective-permute-start | bytes 3145736 | tf_op jit(solution)/shard_map/ppermute | solution.py:60
  486.0 39.3 %collective-permute-start.17 = (bf16[128,2048]{1,0:T(8,128)(2,1)S(1)}, bf16[128,2048]{1,0:T(8,128)(2,1)S(1)}, u32[]{:S(2)}, u32[]{:S(2)}) collective-permute-start(bf16[128,2048]{1,0:T(8,128)(2,1)S(1)} %copy-done.6), channel_id=1, source_target_pairs={{0,16},{8,24},{16,0},{24,8},{1,17},{9,25},{17,1},{25,9},{2,18},{10... | collective-permute-start | bytes 1572872 | tf_op jit(solution)/shard_map/ppermute | solution.py:60
  486.6 39.6 %collective-permute-start.18 = (bf16[128,2048]{1,0:T(8,128)(2,1)S(1)}, bf16[128,2048]{1,0:T(8,128)(2,1)S(1)}, u32[]{:S(2)}, u32[]{:S(2)}) collective-permute-start(bf16[128,2048]{1,0:T(8,128)(2,1)S(1)} %copy-done.10), channel_id=1, source_target_pairs={{0,8},{8,0},{16,24},{24,16},{1,9},{9,1},{17,25},{25,17},{2,10},{10... | collective-permute-start | bytes 1572872 | tf_op jit(solution)/shard_map/ppermute | solution.py:60
  620.6 28.8 %collective-permute-start.19 = (bf16[256,2048]{1,0:T(8,128)(2,1)S(1)}, bf16[256,2048]{1,0:T(8,128)(2,1)S(1)}, u32[]{:S(2)}, u32[]{:S(2)}) collective-permute-start(bf16[256,2048]{1,0:T(8,128)(2,1)S(1)} %copy-done.4), channel_id=1, source_target_pairs={{0,8},{8,0},{16,24},{24,16},{1,9},{9,1},{17,25},{25,17},{2,10},{10... | collective-permute-start | bytes 3145736 | tf_op jit(solution)/shard_map/ppermute | solution.py:60
  621.8 27.6 %collective-permute-start.20 = (bf16[256,2048]{1,0:T(8,128)(2,1)S(1)}, bf16[256,2048]{1,0:T(8,128)(2,1)S(1)}, u32[]{:S(2)}, u32[]{:S(2)}) collective-permute-start(bf16[256,2048]{1,0:T(8,128)(2,1)S(1)} %copy-done.4), channel_id=1, source_target_pairs={{0,16},{8,24},{16,0},{24,8},{1,17},{9,25},{17,1},{25,9},{2,18},{10... | collective-permute-start | bytes 3145736 | tf_op jit(solution)/shard_map/ppermute | solution.py:60
  624.9 28.8 %collective-permute-start.21 = (bf16[128,2048]{1,0:T(8,128)(2,1)}, bf16[128,2048]{1,0:T(8,128)(2,1)S(1)}, u32[]{:S(2)}, u32[]{:S(2)}) collective-permute-start(bf16[128,2048]{1,0:T(8,128)(2,1)} %get-tuple-element.239), channel_id=1, source_target_pairs={{0,8},{8,0},{16,24},{24,16},{1,9},{9,1},{17,25},{25,17},{2,10},{10... | collective-permute-start | bytes 1572872 | tf_op jit(solution)/shard_map/ppermute | solution.py:60
  626.2 29.1 %collective-permute-start.22 = (bf16[128,2048]{1,0:T(8,128)(2,1)}, bf16[128,2048]{1,0:T(8,128)(2,1)}, u32[]{:S(2)}, u32[]{:S(2)}) collective-permute-start(bf16[128,2048]{1,0:T(8,128)(2,1)} %get-tuple-element.238), channel_id=1, source_target_pairs={{0,16},{8,24},{16,0},{24,8},{1,17},{9,25},{17,1},{25,9},{2,18},{10... | collective-permute-start | bytes 1572872 | tf_op jit(solution)/shard_map/ppermute | solution.py:60
  663.0 45.3 %collective-permute-start.29 = (bf16[128,2048]{1,0:T(8,128)(2,1)}, bf16[128,2048]{1,0:T(8,128)(2,1)}, u32[]{:S(2)}, u32[]{:S(2)}) collective-permute-start(bf16[128,2048]{1,0:T(8,128)(2,1)} %get-tuple-element.209), channel_id=1, source_target_pairs={{0,16},{8,24},{16,0},{24,8},{1,17},{9,25},{17,1},{25,9},{2,18},{10... | collective-permute-start | bytes 1572872 | tf_op jit(solution)/shard_map/ppermute | solution.py:60
  663.5 44.9 %collective-permute-start.30 = (bf16[128,2048]{1,0:T(8,128)(2,1)}, bf16[128,2048]{1,0:T(8,128)(2,1)}, u32[]{:S(2)}, u32[]{:S(2)}) collective-permute-start(bf16[128,2048]{1,0:T(8,128)(2,1)} %get-tuple-element.211), channel_id=1, source_target_pairs={{0,8},{8,0},{16,24},{24,16},{1,9},{9,1},{17,25},{25,17},{2,10},{10... | collective-permute-start | bytes 1572872 | tf_op jit(solution)/shard_map/ppermute | solution.py:60
  685.8 23.9 %collective-permute-start.25 = (bf16[256,1536]{1,0:T(8,128)(2,1)}, bf16[256,1536]{1,0:T(8,128)(2,1)S(1)}, u32[]{:S(2)}, u32[]{:S(2)}) collective-permute-start(bf16[256,1536]{1,0:T(8,128)(2,1)} %reduce-scatter.11.cloned.1.call-done.refs_0_), channel_id=1, source_target_pairs={{0,8},{8,0},{16,24},{24,16},{1,9},{9,1},{17,25},{25,17},{2,10},{10... | collective-permute-start | bytes 2359304 | tf_op jit(solution)/shard_map/ppermute | solution.py:60
  687.3 22.5 %collective-permute-start.26 = (bf16[256,1536]{1,0:T(8,128)(2,1)}, bf16[256,1536]{1,0:T(8,128)(2,1)S(1)}, u32[]{:S(2)}, u32[]{:S(2)}) collective-permute-start(bf16[256,1536]{1,0:T(8,128)(2,1)} %reduce-scatter.11.cloned.1.call-done.refs_0_), channel_id=1, source_target_pairs={{0,16},{8,24},{16,0},{24,8},{1,17},{9,25},{17,1},{25,9},{2,18},{10... | collective-permute-start | bytes 2359304 | tf_op jit(solution)/shard_map/ppermute | solution.py:60
  (59 other events, 617.5 us)
Sparse Core Ops, SparseCore 0:
  10.3 68.1 all-gather.4
  80.7 80.6 all-gather.6
  163.6 80.5 all-gather.8
  245.6 80.6 all-gather.10
  329.0 88.0 reduce-scatter.4
  434.0 87.6 reduce-scatter.6
  523.9 87.9 reduce-scatter.8
  617.8 67.9 reduce-scatter.10

commit v8 on v6

--- a/solution.py
+++ b/solution.py
@@ -676,15 +676,17 @@
     own, land1, land2, cot, y1, gain, w_out = refs[0:7]
     ob, gb1, gb2, w_down, mix_x, mix_y, down = refs[7:14]
     dy1, dz1, sums, got, out_grad = refs[14:19]
-    mix, down1, down2 = refs[19:23], refs[23], refs[24]
-    dz, w, stage = refs[25:28]
-    moves = Moves(*refs[28:30])
-    local = refs[30]
+    mix, (one_lo, one_hi, two_lo, two_hi) = refs[19:23], refs[23:27]
+    dz, w, stage = refs[27:30]
+    moves = Moves(*refs[30:32])
+    local = refs[32]
     rows, width = own.shape
     greet((1, 2, 3))
     load = pltpu.make_async_copy(w_out, w, local.at[0])
     load.start()
-    copies = [moves.start(down, down1, 1), moves.start(down, down2, 2)]
+    down_lo, down_hi = halves(down)
+    copies = [moves.start(down_lo, one_lo, 1), moves.start(down_hi, two_hi, 2)]
+    copies += [moves.start(down_hi, one_hi, 1), moves.start(down_lo, two_lo, 2)]
     t = math.gcd(rows, 64)
 
     def norm(own, one, two, cot, y1, gain, dy1, dz1, sums):
@@ -741,10 +743,10 @@
     rows, width = cot.shape
     part = width // 4
     anywhere = pl.BlockSpec(memory_space=pl.ANY)
-    sems = pltpu.SemaphoreType.DMA((5,))
+    sems = pltpu.SemaphoreType.DMA((7,))
     outs = [((rows, width), single), ((rows, width), half), ((8, width), single)]
     outs += [((4 * rows, part), half), ((width, width), half)]
-    outs += [((rows // 2, width), half)] * 4 + [(down.shape, half)] * 2
+    outs += [((rows // 2, width), half)] * 4 + [((down.shape[0] // 2, width), half)] * 4
     out = pl.pallas_call(
         functools.partial(heads_back_kernel, part),
         in_specs=[anywhere] * 14,
@@ -764,7 +766,7 @@
         cost_estimate=hint(10 * rows * width * width, 0),
         name="heads_back",
     )(*terms, cot, y1, gain.reshape(1, -1), w_out, ob, gb1, gb2, w_down, *mix_first, down)
-    return out[0], out[2], out[3], out[4], out[5:9], out[9:11]
+    return out[0], out[2], out[3], out[4], out[5:9], out[9:13]
 
 
 def qkv_back_kernel(*refs):
@@ -1103,7 +1105,7 @@
     mine = [attended[j * rows : (j + 1) * rows] for j in range(CTX)]
     mine = after(mine, dz2_rest)
     mine = [mine[0]] + [swap(mine[j], j) for j in range(1, CTX)]
-    ob = jnp.concatenate(xor_order(mine, c), axis=1)
+    ob = after(jnp.concatenate(xor_order(mine, c), axis=1))
     y1 = tokens.astype(single) + dot_nn(ob, w_out) + bias_o
 
     normed2, inv2 = norm_parts(y1)
@@ -1170,8 +1172,9 @@
     sum_q, sum_v = sum_q[0] + sum_q[8], sum_v[0] + sum_v[8]
     if CTX == 4:
         lows = [swap(one_lo, 1), swap(two_lo, 2)]
-        down_out = gather_second(down_part, down_near)
-        dqkv = after(dqkv, lows, up_part, down_out)
+        down_far = [swap(down_near[0], 2), swap(down_near[3], 1)]
+        down_out = [[down_part], list(down_near[0:2]), list(down_near[2:4]), down_far]
+        dqkv = after(dqkv, lows, up_part, down_far)
         dh1, arrived, qkv_grad, mix_own, highs = qkv_back(
             dqkv, w_qkv, a1, gb[0][0], w_down, one_hi, two_hi
         )

time: 743 us -> 739 us (level)
    pallas_call x4, Pallas kernels: 43.3 us -> 53.5 us  [rows_matmul(): pl.pallas_call(functools.partial(rows_kernel, dot_nt if transposed else d...]
    pallas_call x1, Pallas kernels: 33.7 us -> 23.5 us  [outer(): pl.pallas_call(functools.partial(outer_kernel, len(left)), grid=(m // tm,...]
    unnamed x149 -> x139, local copies, waits for them, and re-layouts: 21.7 us -> 21.2 us
  transfers between devices with their start and end apart: 39 -> 39, of which waited for: 16 -> 17; matrix products, arithmetic and copies ran while one was open for 12% -> 12% of each run, Pallas kernels for 61% -> 62%
where the time goes in v8:
time: 739 us; the launch traced here: 726 us
  Pallas kernels  450 us (61%)
  waiting for transfers between devices  121 us (16%)
  other arithmetic  52.3 us (7%)
  local copies, waits for them, and re-layouts  42.8 us (6%)
  starting transfers between devices  36.1 us (5%)
  between operations  15.5 us (2%)
  matrix products  7.77 us (1%)
    pallas_call x2, Pallas kernels, moving_call(): pl.pallas_call(kernel, in_specs=[anywhere] * len(operands), out_specs=[an...  119 us
    ppermute x31, waiting for transfers between devices, swap(): return lax.ppermute(x, 'ctx', [(i, i ^ mask) for i in range(n)])  108 us
    pallas_call x1, Pallas kernels, feed_back(): pl.pallas_call(feed_back_kernel, in_specs=[anywhere] * 22, out_specs=[any...  104 us
    pallas_call x2, Pallas kernels, attn_call(): pl.pallas_call(kernel, grid_spec=pltpu.PrefetchScalarGridSpec(num_scalar_...  61.3 us
    pallas_call x4, Pallas kernels, rows_matmul(): pl.pallas_call(functools.partial(rows_kernel, dot_nt if transposed else d...  53.5 us
    pallas_call x1, Pallas kernels, heads_back(): pl.pallas_call(functools.partial(heads_back_kernel, part), in_specs=[anyw...  49.8 us
    ppermute x31, starting transfers between devices, swap(): return lax.ppermute(x, 'ctx', [(i, i ^ mask) for i in range(n)])  35.7 us
    pallas_call x1, Pallas kernels, outer(): pl.pallas_call(functools.partial(outer_kernel, len(left)), grid=(m // tm,...  23.5 us
  transfers between devices with their start and end apart: 39, of which 17 were waited for; matrix products, arithmetic and copies ran while one was open for 12% of the time, Pallas kernels for 62%

profile of v8, /device:TPU:0, one launch (start us, length us, event | category | flops | bytes accessed | tf_op | source)
XLA Modules:
  0.0 726.0 jit_solution(15170392395816015961)
XLA Ops:
  12.7 3.0 collective-permute-start
  18.1 9.1 %gather_small.1 = f32[8,24,128]{2,1,0:T(8,128)} custom-call(f32[24,128]{1,0:T(8,128)} %bitcast.92), custom_call_target="tpu_custom_call" | custom-call | tf_op jit(solution)/shard_map/gather_small/pallas_call | solution.py:900
  32.9 3.9 convert.46
  46.5 3.3 fusion.41
  49.9 11.6 %collective-permute-done = bf16[512,2048]{1,0:T(8,128)(2,1)} collective-permute-done((bf16[512,2048]{1,0:T(8,128)(2,1)S(1)}, bf16[512,2048]{1,0:T(8,128)(2,1)}, u32[]{:S(2)}, u32[]{:S(2)}) %collective-permute-start) | collective-permute-done | bytes 2097184 | tf_op jit(solution)/shard_map/ppermute | solution.py:60
  76.3 5.7 fusion.21
  82.0 6.1 collective-permute-done.2.refs_0_
  91.0 27.9 %qkv.1 = (bf16[2048,1536]{1,0:T(8,128)(2,1)}, bf16[256,2048]{1,0:T(8,128)(2,1)S(1)}, bf16[256,2048]{1,0:T(8,128)(2,1)}, bf16[256,2048]{1,0:T(8,128)(2,1)}, bf16[256,2048]{1,0:T(8,128)(2,1)}) custom-call(bf16[256,2048]{1,0:T(8,128)(2,1)} %collective-permute-done.2.refs_0_, bf16[256,2048]{1,0:T(8,128)(2,1)} %collective-permute-done.3.refs_1_, ...), custom_call_target="tpu_custom_call" | custom-call | flops 12884901 | tf_op jit(solution)/shard_map/qkv/pallas_call | solution.py:507
  122.1 24.4 %attn_forward.1 = bf16[2048,512]{1,0:T(8,128)(2,1)S(1)} custom-call(s32[16]{0:T(128)S(1)} %select_reduce_fusion.inv_ref, f32[4]{0:T(128)S(1)} %multiply_power_fusion.slope_ref, ...), custom_call_target="tpu_custom_call" | custom-call | flops 20000000 | bytes 8388 | tf_op jit(solution)/shard_map/attn_forward/pallas_call | solution.py:240
  151.2 12.6 %collective-permute-done.6 = bf16[512,512]{1,0:T(8,128)(2,1)} collective-permute-done((bf16[512,512]{1,0:T(8,128)(2,1)}, bf16[512,512]{1,0:T(8,128)(2,1)}, u32[]{:S(2)}, u32[]{:S(2)}) %collective-permute-start.6) | collective-permute-done | bytes 524320 | tf_op jit(solution)/shard_map/ppermute | solution.py:60
  163.8 6.8 collective-permute-done.7
  174.3 7.8 %fusion.43 = (f32[512]{0:T(512)S(1)}, f32[512,2048]{1,0:T(8,128)S(1)}) fusion(f32[2048]{0:T(1024)S(1)} %bitcast.95, bf16[512,2048]{1,0:T(8,128)(2,1)} %pad_maximum_fusion.1.refs_7_, bf16[2048,2048]{1,0:T(8,128)(2,1)} %all-gather.7.cloned.1.call-done.refs_6_, bf16[512,2048]{1,0:T(8,128)(2,1)S(1)} %copy-done.18), kind=kOutput, calls=%fused_computation.157 | convolution fusion | flops 4299161088 | bytes 16787456 | tf_op jit(solution)/shard_map/dot_general | solution.py:24
  185.9 45.4 %collective-permute-done.9.refs_0_.refs_16_ = bf16[512,2048]{1,0:T(8,128)(2,1)S(1)} collective-permute-done((bf16[512,2048]{1,0:T(8,128)(2,1)S(1)}, bf16[512,2048]{1,0:T(8,128)(2,1)S(1)}, u32[]{:S(2)}, u32[]{:S(2)}) %collective-permute-start.9) | collective-permute-done | bytes 2097184 | tf_op jit(solution)/shard_map/ppermute | solution.py:60
  237.6 6.6 all-gather.9.cloned.1.call-done.refs_1_.refs_2_.refs_14_
  244.2 11.0 %up_gelu_0.1 = (bf16[512,2048]{1,0:T(8,128)(2,1)}, bf16[512,2048]{1,0:T(8,128)(2,1)}) custom-call(bf16[512,2048]{1,0:T(8,128)(2,1)} %copy-done.21, bf16[2048,2048]{1,0:T(8,128)(2,1)} %all-gather.9.cloned.1.call-done.refs_1_.refs_2_.refs_14_, f32[1,2048]{1,0:T(1,128)S(1)} %bitcast.72), custom_call_target="tpu_custom_call" | custom-call | flops 4294967 | bytes 16777 | tf_op jit(solution)/shard_map/up_gelu_0/pallas_call | solution.py:319
  255.2 10.8 %up_gelu_1.1 = (bf16[512,2048]{1,0:T(8,128)(2,1)}, bf16[512,2048]{1,0:T(8,128)(2,1)}) custom-call(bf16[512,2048]{1,0:T(8,128)(2,1)} %copy-done.22, bf16[2048,2048]{1,0:T(8,128)(2,1)} %all-gather.9.cloned.1.call-done.refs_1_.refs_2_.refs_14_, f32[1,2048]{1,0:T(1,128)S(1)} %bitcast.73), custom_call_target="tpu_custom_call" | custom-call | flops 4294967 | bytes 16777 | tf_op jit(solution)/shard_map/up_gelu_1/pallas_call | solution.py:319
  265.9 10.8 %up_gelu_2.1 = (bf16[512,2048]{1,0:T(8,128)(2,1)}, bf16[512,2048]{1,0:T(8,128)(2,1)}) custom-call(bf16[512,2048]{1,0:T(8,128)(2,1)} %copy-done.23, bf16[2048,2048]{1,0:T(8,128)(2,1)} %all-gather.9.cloned.1.call-done.refs_1_.refs_2_.refs_14_, f32[1,2048]{1,0:T(1,128)S(1)} %bitcast.74), custom_call_target="tpu_custom_call" | custom-call | flops 4294967 | bytes 16777 | tf_op jit(solution)/shard_map/up_gelu_2/pallas_call | solution.py:319
  277.7 21.0 %up_gelu_3.1 = (bf16[256,2048]{1,0:T(8,128)(2,1)S(1)}, bf16[256,2048]{1,0:T(8,128)(2,1)}, bf16[256,2048]{1,0:T(8,128)(2,1)}, bf16[256,2048]{1,0:T(8,128)(2,1)}) custom-call(bf16[256,2048]{1,0:T(8,128)(2,1)} %copy-done.26, bf16[256,2048]{1,0:T(8,128)(2,1)} %collective-permute-done.14.refs_1_.refs_19_, ...), custom_call_target="tpu_custom_call" | custom-call | flops 4294967 | bytes 16777 | tf_op jit(solution)/shard_map/up_gelu_3/pallas_call | solution.py:319
  298.7 23.5 %down_grad.1 = bf16[2048,2048]{1,0:T(8,128)(2,1)} custom-call(bf16[512,2048]{1,0:T(8,128)(2,1)} %get-tuple-element.136.refs_0_.refs_1_.refs_7_, bf16[512,2048]{1,0:T(8,128)(2,1)} %get-tuple-element.136.refs_0_.refs_1_.refs_7_, bf16[512,2048]{1,0:T(8,128)(2,1)} %get-tuple-element.139.refs_2_.refs_3_.refs_8_, ...), custom_call_target="tpu_custom_call" | custom-call | flops 17179868 | bytes 25165 | tf_op jit(solution)/shard_map/down_grad/pallas_call | solution.py:392
  322.3 4.0 all-gather.11.cloned.1.call-done.refs_13_.refs_10_.refs_8_
  326.3 104.0 %feed_back.1 = (bf16[512,2048]{1,0:T(8,128)(2,1)}, bf16[512,2048]{1,0:T(8,128)(2,1)}, bf16[512,2048]{1,0:T(8,128)(2,1)}, bf16[256,2048]{1,0:T(8,128)(2,1)}, bf16...) custom-call(bf16[256,2048]{1,0:T(8,128)(2,1)} %get-tuple-element.182, ...), custom_call_target="tpu_custom_call" | custom-call | flops 55834576 | tf_op jit(solution)/shard_map/feed_back/pallas_call | solution.py:656
  431.0 49.8 %heads_back.1 = (f32[512,2048]{1,0:T(8,128)}, bf16[512,2048]{1,0:T(8,128)(2,1)}, f32[8,2048]{1,0:T(8,128)}, bf16[2048,512]{1,0:T(8,128)(2,1)}, bf16[2048,2048]{1...) custom-call(f32[512,2048]{1,0:T(8,128)} %get-tuple-element.152.refs_, ...), custom_call_target="tpu_custom_call" | custom-call | flops 21474836 | tf_op jit(solution)/shard_map/heads_back/pallas_call | solution.py:750
  485.0 36.9 %attn_backward.1 = (bf16[2048,1536]{1,0:T(8,128)(2,1)}, f32[16,512]{1,0:T(8,128)S(1)}, f32[16,512]{1,0:T(8,128)S(1)}) custom-call(s32[16]{0:T(128)S(1)} %select_reduce_fusion.inv_ref, f32[4]{0:T(128)S(1)} %multiply_power_fusion.slope_ref, ...), custom_call_target="tpu_custom_call" | custom-call | flops 40000000 | bytes 14680 | tf_op jit(solution)/shard_map/attn_backward/pallas_call | solution.py:240
  523.5 91.6 %qkv_back.1 = (f32[512,2048]{1,0:T(8,128)}, bf16[512,2048]{1,0:T(8,128)(2,1)}, bf16[512,2048]{1,0:T(8,128)(2,1)}, bf16[512,2048]{1,0:T(8,128)(2,1)}, bf16[256,20...) custom-call(bf16[2048,1536]{1,0:T(8,128)(2,1)} %get-tuple-element.16, ...), custom_call_target="tpu_custom_call" | custom-call | flops 30064772 | tf_op jit(solution)/shard_map/qkv_back/pallas_call | solution.py:507
  624.6 6.1 fusion.16
  630.7 3.0 fusion.15
  640.4 3.8 lay_out.3
  646.7 5.5 collective-permute-done.21
  663.3 8.6 %collective-permute-done.23.refs_3_ = bf16[128,2048]{1,0:T(8,128)(2,1)} collective-permute-done((bf16[128,2048]{1,0:T(8,128)(2,1)}, bf16[128,2048]{1,0:T(8,128)(2,1)}, u32[]{:S(2)}, u32[]{:S(2)}) %collective-permute-start.23) | collective-permute-done | bytes 524320 | tf_op jit(solution)/shard_map/ppermute | solution.py:60
  673.3 6.6 lay_out.4
  686.1 16.2 %reduce_small.1 = f32[24,128]{1,0:T(8,128)} custom-call(f32[8,24,128]{2,1,0:T(8,128)} %bitcast.80), custom_call_target="tpu_custom_call" | custom-call | tf_op jit(solution)/shard_map/reduce_small/pallas_call | solution.py:971
  715.9 3.1 lay_out.5
  (301 shorter events, 120.3 us)
Async XLA Ops:
  7.3 83.7 %all-gather.5.cloned.1.call-start = ((), (), s32[]{:S(2)}) async-start(), calls=%async_computation.4 | async-start | bytes 7077888 | tf_op jit(solution)/shard_map/all_gather | solution.py:1035
  9.9 164.4 %all-gather.7.cloned.1.call-start = ((), (), s32[]{:S(2)}) async-start(), calls=%async_computation.5 | async-start | bytes 9437184 | tf_op jit(solution)/shard_map/all_gather | solution.py:1035
  12.7 231.5 %all-gather.9.cloned.1.call-start = ((), (), s32[]{:S(2)}) async-start(), calls=%async_computation.6 | async-start | bytes 9437184 | tf_op jit(solution)/shard_map/all_gather | solution.py:1035
  12.7 48.7 %collective-permute-start = (bf16[512,2048]{1,0:T(8,128)(2,1)S(1)}, bf16[512,2048]{1,0:T(8,128)(2,1)}, u32[]{:S(2)}, u32[]{:S(2)}) collective-permute-start(bf16[512,2048]{1,0:T(8,128)(2,1)S(1)} %copy-done.18), channel_id=1, source_target_pairs={{0,8},{8,0},{16,24},{24,16},{1,9},{9,1},{17,25},{25,17},{2,10},{10... | collective-permute-start | bytes 6291464 | tf_op jit(solution)/shard_map/ppermute | solution.py:60
  15.7 47.2 %collective-permute-start.1 = (bf16[512,2048]{1,0:T(8,128)(2,1)S(1)}, bf16[512,2048]{1,0:T(8,128)(2,1)}, u32[]{:S(2)}, u32[]{:S(2)}) collective-permute-start(bf16[512,2048]{1,0:T(8,128)(2,1)S(1)} %copy-done.18), channel_id=1, source_target_pairs={{0,16},{8,24},{16,0},{24,8},{1,17},{9,25},{17,1},{25,9},{2,18},{10... | collective-permute-start | bytes 6291464 | tf_op jit(solution)/shard_map/ppermute | solution.py:60
  64.3 23.9 %collective-permute-start.2 = (bf16[256,2048]{1,0:T(8,128)(2,1)S(1)}, bf16[256,2048]{1,0:T(8,128)(2,1)}, u32[]{:S(2)}, u32[]{:S(2)}) collective-permute-start(bf16[256,2048]{1,0:T(8,128)(2,1)S(1)} %slice.163), channel_id=1, source_target_pairs={{0,16},{8,24},{16,0},{24,8},{1,17},{9,25},{17,1},{25,9},{2,18},{10... | collective-permute-start | bytes 3145736 | tf_op jit(solution)/shard_map/ppermute | solution.py:60
  67.2 23.6 %collective-permute-start.3 = (bf16[256,2048]{1,0:T(8,128)(2,1)S(1)}, bf16[256,2048]{1,0:T(8,128)(2,1)}, u32[]{:S(2)}, u32[]{:S(2)}) collective-permute-start(bf16[256,2048]{1,0:T(8,128)(2,1)S(1)} %slice.164), channel_id=1, source_target_pairs={{0,8},{8,0},{16,24},{24,16},{1,9},{9,1},{17,25},{25,17},{2,10},{10... | collective-permute-start | bytes 3145736 | tf_op jit(solution)/shard_map/ppermute | solution.py:60
  90.8 235.5 %all-gather.11.cloned.1.call-start = ((), (), s32[]{:S(2)}) async-start(), calls=%async_computation.7 | async-start | bytes 9437184 | tf_op jit(solution)/shard_map/all_gather | solution.py:1035
  119.9 311.1 %reduce-scatter.5.cloned.1.call-start = ((), (), s32[]{:S(2)}) async-start(), calls=%async_computation.8 | async-start | bytes 9437184 | tf_op jit(solution)/shard_map/reduce_scatter | solution.py:1071
  120.0 27.7 %collective-permute-start.4 = (bf16[256,2048]{1,0:T(8,128)(2,1)}, bf16[256,2048]{1,0:T(8,128)(2,1)}, u32[]{:S(2)}, u32[]{:S(2)}) collective-permute-start(bf16[256,2048]{1,0:T(8,128)(2,1)} %get-tuple-element.183.refs_10_.refs_9_.refs_1_), channel_id=1, source_target_pairs={{0,8},{8,0},{16,24},{24,16},{1,9},{9,1},{17,25},{25,17},{2,10},{10... | collective-permute-start | bytes 3145736 | tf_op jit(solution)/shard_map/ppermute | solution.py:60
  121.5 26.2 %collective-permute-start.5 = (bf16[256,2048]{1,0:T(8,128)(2,1)}, bf16[256,2048]{1,0:T(8,128)(2,1)}, u32[]{:S(2)}, u32[]{:S(2)}) collective-permute-start(bf16[256,2048]{1,0:T(8,128)(2,1)} %get-tuple-element.182.refs_9_.refs_8_.refs_0_), channel_id=1, source_target_pairs={{0,16},{8,24},{16,0},{24,8},{1,17},{9,25},{17,1},{25,9},{2,18},{10... | collective-permute-start | bytes 3145736 | tf_op jit(solution)/shard_map/ppermute | solution.py:60
  184.1 47.2 %collective-permute-start.9 = (bf16[512,2048]{1,0:T(8,128)(2,1)S(1)}, bf16[512,2048]{1,0:T(8,128)(2,1)S(1)}, u32[]{:S(2)}, u32[]{:S(2)}) collective-permute-start(bf16[512,2048]{1,0:T(8,128)(2,1)S(1)} %add_convert_fusion.refs_0_.refs_15_), channel_id=1, source_target_pairs={{0,8},{8,0},{16,24},{24,16},{1,9},{9,1},{17,25},{25,17},{2,10},{10... | collective-permute-start | bytes 6291464 | tf_op jit(solution)/shard_map/ppermute | solution.py:60
  185.2 48.7 %collective-permute-start.10 = (bf16[512,2048]{1,0:T(8,128)(2,1)S(1)}, bf16[512,2048]{1,0:T(8,128)(2,1)S(1)}, u32[]{:S(2)}, u32[]{:S(2)}) collective-permute-start(bf16[512,2048]{1,0:T(8,128)(2,1)S(1)} %add_convert_fusion.refs_0_.refs_15_), channel_id=1, source_target_pairs={{0,16},{8,24},{16,0},{24,8},{1,17},{9,25},{17,1},{25,9},{2,18},{10... | collective-permute-start | bytes 6291464 | tf_op jit(solution)/shard_map/ppermute | solution.py:60
  232.4 44.3 %collective-permute-start.13 = (bf16[256,2048]{1,0:T(8,128)(2,1)}, bf16[256,2048]{1,0:T(8,128)(2,1)S(1)}, u32[]{:S(2)}, u32[]{:S(2)}) collective-permute-start(bf16[256,2048]{1,0:T(8,128)(2,1)} %slice.229), channel_id=1, source_target_pairs={{0,16},{8,24},{16,0},{24,8},{1,17},{9,25},{17,1},{25,9},{2,18},{10... | collective-permute-start | bytes 3145736 | tf_op jit(solution)/shard_map/ppermute | solution.py:60
  235.0 41.7 %collective-permute-start.14 = (bf16[256,2048]{1,0:T(8,128)(2,1)}, bf16[256,2048]{1,0:T(8,128)(2,1)}, u32[]{:S(2)}, u32[]{:S(2)}) collective-permute-start(bf16[256,2048]{1,0:T(8,128)(2,1)} %slice.230), channel_id=1, source_target_pairs={{0,8},{8,0},{16,24},{24,16},{1,9},{9,1},{17,25},{25,17},{2,10},{10... | collective-permute-start | bytes 3145736 | tf_op jit(solution)/shard_map/ppermute | solution.py:60
  235.7 63.1 %collective-permute-start.11 = (bf16[256,2048]{1,0:T(8,128)(2,1)S(1)}, bf16[256,2048]{1,0:T(8,128)(2,1)}, u32[]{:S(2)}, u32[]{:S(2)}) collective-permute-start(bf16[256,2048]{1,0:T(8,128)(2,1)S(1)} %copy-done.25), channel_id=1, source_target_pairs={{0,16},{8,24},{16,0},{24,8},{1,17},{9,25},{17,1},{25,9},{2,18},{10... | collective-permute-start | bytes 3145736 | tf_op jit(solution)/shard_map/ppermute | solution.py:60
  237.1 61.7 %collective-permute-start.12 = (bf16[256,2048]{1,0:T(8,128)(2,1)}, bf16[256,2048]{1,0:T(8,128)(2,1)}, u32[]{:S(2)}, u32[]{:S(2)}) collective-permute-start(bf16[256,2048]{1,0:T(8,128)(2,1)} %get-tuple-element.132.refs_13_.refs_5_), channel_id=1, source_target_pairs={{0,8},{8,0},{16,24},{24,16},{1,9},{9,1},{17,25},{25,17},{2,10},{10... | collective-permute-start | bytes 3145736 | tf_op jit(solution)/shard_map/ppermute | solution.py:60
  322.3 201.3 %reduce-scatter.7.cloned.1.call-start = ((), (), s32[]{:S(2)}) async-start(), calls=%async_computation.9 | async-start | bytes 9437184 | tf_op jit(solution)/shard_map/reduce_scatter | solution.py:1071
  430.3 189.9 %reduce-scatter.9.cloned.1.call-start = ((), (), s32[]{:S(2)}) async-start(), calls=%async_computation.10 | async-start | bytes 9437184 | tf_op jit(solution)/shard_map/reduce_scatter | solution.py:1071
  480.8 201.6 %reduce-scatter.11.cloned.1.call-start = ((), (), s32[]{:S(2)}) async-start(), calls=%async_computation.11 | async-start | bytes 7077888 | tf_op jit(solution)/shard_map/reduce_scatter | solution.py:1071
  480.9 42.7 %collective-permute-start.15 = (bf16[256,2048]{1,0:T(8,128)(2,1)}, bf16[256,2048]{1,0:T(8,128)(2,1)}, u32[]{:S(2)}, u32[]{:S(2)}) collective-permute-start(bf16[256,2048]{1,0:T(8,128)(2,1)} %get-tuple-element.159), channel_id=1, source_target_pairs={{0,8},{8,0},{16,24},{24,16},{1,9},{9,1},{17,25},{25,17},{2,10},{10... | collective-permute-start | bytes 3145736 | tf_op jit(solution)/shard_map/ppermute | solution.py:60
  482.4 41.1 %collective-permute-start.16 = (bf16[256,2048]{1,0:T(8,128)(2,1)}, bf16[256,2048]{1,0:T(8,128)(2,1)}, u32[]{:S(2)}, u32[]{:S(2)}) collective-permute-start(bf16[256,2048]{1,0:T(8,128)(2,1)} %get-tuple-element.160), channel_id=1, source_target_pairs={{0,16},{8,24},{16,0},{24,8},{1,17},{9,25},{17,1},{25,9},{2,18},{10... | collective-permute-start | bytes 3145736 | tf_op jit(solution)/shard_map/ppermute | solution.py:60
  482.6 39.3 %collective-permute-start.17 = (bf16[128,2048]{1,0:T(8,128)(2,1)S(1)}, bf16[128,2048]{1,0:T(8,128)(2,1)S(1)}, u32[]{:S(2)}, u32[]{:S(2)}) collective-permute-start(bf16[128,2048]{1,0:T(8,128)(2,1)S(1)} %copy-done.6), channel_id=1, source_target_pairs={{0,16},{8,24},{16,0},{24,8},{1,17},{9,25},{17,1},{25,9},{2,18},{10... | collective-permute-start | bytes 1572872 | tf_op jit(solution)/shard_map/ppermute | solution.py:60
  484.4 38.3 %collective-permute-start.18 = (bf16[128,2048]{1,0:T(8,128)(2,1)S(1)}, bf16[128,2048]{1,0:T(8,128)(2,1)S(1)}, u32[]{:S(2)}, u32[]{:S(2)}) collective-permute-start(bf16[128,2048]{1,0:T(8,128)(2,1)S(1)} %copy-done.10), channel_id=1, source_target_pairs={{0,8},{8,0},{16,24},{24,16},{1,9},{9,1},{17,25},{25,17},{2,10},{10... | collective-permute-start | bytes 1572872 | tf_op jit(solution)/shard_map/ppermute | solution.py:60
  618.2 28.6 %collective-permute-start.19 = (bf16[256,2048]{1,0:T(8,128)(2,1)S(1)}, bf16[256,2048]{1,0:T(8,128)(2,1)S(1)}, u32[]{:S(2)}, u32[]{:S(2)}) collective-permute-start(bf16[256,2048]{1,0:T(8,128)(2,1)S(1)} %copy-done.4), channel_id=1, source_target_pairs={{0,8},{8,0},{16,24},{24,16},{1,9},{9,1},{17,25},{25,17},{2,10},{10... | collective-permute-start | bytes 3145736 | tf_op jit(solution)/shard_map/ppermute | solution.py:60
  619.7 27.1 %collective-permute-start.20 = (bf16[256,2048]{1,0:T(8,128)(2,1)S(1)}, bf16[256,2048]{1,0:T(8,128)(2,1)S(1)}, u32[]{:S(2)}, u32[]{:S(2)}) collective-permute-start(bf16[256,2048]{1,0:T(8,128)(2,1)S(1)} %copy-done.4), channel_id=1, source_target_pairs={{0,16},{8,24},{16,0},{24,8},{1,17},{9,25},{17,1},{25,9},{2,18},{10... | collective-permute-start | bytes 3145736 | tf_op jit(solution)/shard_map/ppermute | solution.py:60
  622.5 29.7 %collective-permute-start.21 = (bf16[128,2048]{1,0:T(8,128)(2,1)}, bf16[128,2048]{1,0:T(8,128)(2,1)S(1)}, u32[]{:S(2)}, u32[]{:S(2)}) collective-permute-start(bf16[128,2048]{1,0:T(8,128)(2,1)} %get-tuple-element.239), channel_id=1, source_target_pairs={{0,8},{8,0},{16,24},{24,16},{1,9},{9,1},{17,25},{25,17},{2,10},{10... | collective-permute-start | bytes 1572872 | tf_op jit(solution)/shard_map/ppermute | solution.py:60
  624.0 29.5 %collective-permute-start.22 = (bf16[128,2048]{1,0:T(8,128)(2,1)}, bf16[128,2048]{1,0:T(8,128)(2,1)}, u32[]{:S(2)}, u32[]{:S(2)}) collective-permute-start(bf16[128,2048]{1,0:T(8,128)(2,1)} %get-tuple-element.238), channel_id=1, source_target_pairs={{0,16},{8,24},{16,0},{24,8},{1,17},{9,25},{17,1},{25,9},{2,18},{10... | collective-permute-start | bytes 1572872 | tf_op jit(solution)/shard_map/ppermute | solution.py:60
  661.2 43.8 %collective-permute-start.29 = (bf16[128,2048]{1,0:T(8,128)(2,1)}, bf16[128,2048]{1,0:T(8,128)(2,1)}, u32[]{:S(2)}, u32[]{:S(2)}) collective-permute-start(bf16[128,2048]{1,0:T(8,128)(2,1)} %get-tuple-element.209), channel_id=1, source_target_pairs={{0,16},{8,24},{16,0},{24,8},{1,17},{9,25},{17,1},{25,9},{2,18},{10... | collective-permute-start | bytes 1572872 | tf_op jit(solution)/shard_map/ppermute | solution.py:60
  661.9 43.1 %collective-permute-start.30 = (bf16[128,2048]{1,0:T(8,128)(2,1)}, bf16[128,2048]{1,0:T(8,128)(2,1)}, u32[]{:S(2)}, u32[]{:S(2)}) collective-permute-start(bf16[128,2048]{1,0:T(8,128)(2,1)} %get-tuple-element.211), channel_id=1, source_target_pairs={{0,8},{8,0},{16,24},{24,16},{1,9},{9,1},{17,25},{25,17},{2,10},{10... | collective-permute-start | bytes 1572872 | tf_op jit(solution)/shard_map/ppermute | solution.py:60
  682.5 23.9 %collective-permute-start.25 = (bf16[256,1536]{1,0:T(8,128)(2,1)}, bf16[256,1536]{1,0:T(8,128)(2,1)S(1)}, u32[]{:S(2)}, u32[]{:S(2)}) collective-permute-start(bf16[256,1536]{1,0:T(8,128)(2,1)} %reduce-scatter.11.cloned.1.call-done.refs_0_), channel_id=1, source_target_pairs={{0,8},{8,0},{16,24},{24,16},{1,9},{9,1},{17,25},{25,17},{2,10},{10... | collective-permute-start | bytes 2359304 | tf_op jit(solution)/shard_map/ppermute | solution.py:60
  683.9 22.5 %collective-permute-start.26 = (bf16[256,1536]{1,0:T(8,128)(2,1)}, bf16[256,1536]{1,0:T(8,128)(2,1)S(1)}, u32[]{:S(2)}, u32[]{:S(2)}) collective-permute-start(bf16[256,1536]{1,0:T(8,128)(2,1)} %reduce-scatter.11.cloned.1.call-done.refs_0_), channel_id=1, source_target_pairs={{0,16},{8,24},{16,0},{24,8},{1,17},{9,25},{17,1},{25,9},{2,18},{10... | collective-permute-start | bytes 2359304 | tf_op jit(solution)/shard_map/ppermute | solution.py:60
  (59 other events, 617.8 us)
Sparse Core Ops, SparseCore 0:
  10.3 68.1 all-gather.4
  80.7 80.6 all-gather.6
  163.6 80.5 all-gather.8
  245.6 80.6 all-gather.10
  329.0 88.0 reduce-scatter.4
  430.5 87.3 reduce-scatter.6
  520.1 87.8 reduce-scatter.8
  615.4 67.0 reduce-scatter.10

commit v9 on v8

--- a/solution.py
+++ b/solution.py
@@ -1230,21 +1230,23 @@
         sizes = [x.shape[0] // nf for x in items]
         x = jnp.concatenate([x.reshape(nf, -1) for x in items], axis=1)
         x = jnp.pad(x, ((0, 0), (0, -x.shape[1] % 1024))).reshape(nf, -1, 128)
-        x = reduce_small(x, nf, CTX, call).reshape(-1)
+        x = reduce_small(x, nf, CTX, call)
+        near = after(qkv_near, x)
+        x = after(x, near).reshape(-1)
         out, at = [], 0
         for n in sizes:
             out.append(x[at : at + n])
             at += n
-        return out
+        return out, near
 
     sums_in = [out_bias_grad, gain2_grad, shift2_grad, down_bias_grad, spread(up_bias_grad, fpart)]
     sums_in += [gain1_grad, shift1_grad, spread(sum_q, part), spread(sum_v, part)]
     qkv_part = after(qkv_part, up_out)
     qkv_near = gather_first(qkv_part)
     sums_in[5] = after(sums_in[5], qkv_part)
-    sums_out = reduced(sums_in, 2)
+    sums_out, qkv_near = reduced(sums_in, 2)
     if CTX == 4:
-        out_second = after(out_second, sums_out)
+        out_second = after(out_second, qkv_near)
         out_out = [x.astype(single) + y.astype(single) for x, y in out_second]
         out_out = jnp.concatenate(out_out, axis=0)
     else:
@@ -1254,7 +1256,6 @@
             out_part = out_out.astype(half)
             bit *= 2
 
-    qkv_near = after(qkv_near, sums_out)
     qkv_out = lay_out(1, gather_second(qkv_part, qkv_near), c, 3)
     out_bias_out, gain2_out, shift2_out, down_bias_out, up_bias_out = sums_out[:5]
     gain1_out, shift1_out, q_bias_out, v_bias_out = sums_out[5:]

time: 739 us -> 746 us (level)
  Pallas kernels: 450 us -> 460 us
    pallas_call x1, Pallas kernels: 16.2 us -> 26.3 us  [reduce_small(): pl.pallas_call(functools.partial(reduce_small_kernel, nf, nc), out_shape=...]
    unnamed x139 -> x141, local copies, waits for them, and re-layouts: 21.2 us -> 21.2 us
  transfers between devices with their start and end apart: 39 -> 39, of which waited for: 17 -> 16; matrix products, arithmetic and copies ran while one was open for 12% -> 12% of each run, Pallas kernels for 62% -> 62%
where the time goes in v9:
time: 746 us; the launch traced here: 733 us
  Pallas kernels  460 us (62%)
  waiting for transfers between devices  122 us (16%)
  other arithmetic  50 us (7%)
  local copies, waits for them, and re-layouts  42.8 us (6%)
  starting transfers between devices  35.1 us (5%)
  between operations  15.5 us (2%)
  matrix products  7.77 us (1%)
    pallas_call x2, Pallas kernels, moving_call(): pl.pallas_call(kernel, in_specs=[anywhere] * len(operands), out_specs=[an...  120 us
    pallas_call x1, Pallas kernels, feed_back(): pl.pallas_call(feed_back_kernel, in_specs=[anywhere] * 22, out_specs=[any...  104 us
    ppermute x31, waiting for transfers between devices, swap(): return lax.ppermute(x, 'ctx', [(i, i ^ mask) for i in range(n)])  104 us
    pallas_call x2, Pallas kernels, attn_call(): pl.pallas_call(kernel, grid_spec=pltpu.PrefetchScalarGridSpec(num_scalar_...  61.2 us
    pallas_call x4, Pallas kernels, rows_matmul(): pl.pallas_call(functools.partial(rows_kernel, dot_nt if transposed else d...  53.6 us
    pallas_call x1, Pallas kernels, heads_back(): pl.pallas_call(functools.partial(heads_back_kernel, part), in_specs=[anyw...  49.7 us
    ppermute x31, starting transfers between devices, swap(): return lax.ppermute(x, 'ctx', [(i, i ^ mask) for i in range(n)])  34.8 us
    pallas_call x1, Pallas kernels, reduce_small(): pl.pallas_call(functools.partial(reduce_small_kernel, nf, nc), out_shape=...  26.3 us
  transfers between devices with their start and end apart: 39, of which 16 were waited for; matrix products, arithmetic and copies ran while one was open for 12% of the time, Pallas kernels for 62%

profile of v9, /device:TPU:0, one launch (start us, length us, event | category | flops | bytes accessed | tf_op | source)
XLA Modules:
  0.0 733.2 jit_solution(1301074207384648055)
XLA Ops:
  18.1 9.0 %gather_small.1 = f32[8,24,128]{2,1,0:T(8,128)} custom-call(f32[24,128]{1,0:T(8,128)} %bitcast.92), custom_call_target="tpu_custom_call" | custom-call | tf_op jit(solution)/shard_map/gather_small/pallas_call | solution.py:900
  32.9 3.9 convert.46
  46.5 3.3 fusion.41
  49.9 11.6 %collective-permute-done = bf16[512,2048]{1,0:T(8,128)(2,1)} collective-permute-done((bf16[512,2048]{1,0:T(8,128)(2,1)S(1)}, bf16[512,2048]{1,0:T(8,128)(2,1)}, u32[]{:S(2)}, u32[]{:S(2)}) %collective-permute-start) | collective-permute-done | bytes 2097184 | tf_op jit(solution)/shard_map/ppermute | solution.py:60
  76.3 5.7 fusion.21
  82.0 6.1 collective-permute-done.2.refs_0_
  91.0 28.0 %qkv.1 = (bf16[2048,1536]{1,0:T(8,128)(2,1)}, bf16[256,2048]{1,0:T(8,128)(2,1)S(1)}, bf16[256,2048]{1,0:T(8,128)(2,1)}, bf16[256,2048]{1,0:T(8,128)(2,1)}, bf16[256,2048]{1,0:T(8,128)(2,1)}) custom-call(bf16[256,2048]{1,0:T(8,128)(2,1)} %collective-permute-done.2.refs_0_, bf16[256,2048]{1,0:T(8,128)(2,1)} %collective-permute-done.3.refs_1_, ...), custom_call_target="tpu_custom_call" | custom-call | flops 12884901 | tf_op jit(solution)/shard_map/qkv/pallas_call | solution.py:507
  122.2 24.4 %attn_forward.1 = bf16[2048,512]{1,0:T(8,128)(2,1)S(1)} custom-call(s32[16]{0:T(128)S(1)} %select_reduce_fusion.inv_ref, f32[4]{0:T(128)S(1)} %multiply_power_fusion.slope_ref, ...), custom_call_target="tpu_custom_call" | custom-call | flops 20000000 | bytes 8388 | tf_op jit(solution)/shard_map/attn_forward/pallas_call | solution.py:240
  151.2 12.6 %collective-permute-done.6 = bf16[512,512]{1,0:T(8,128)(2,1)} collective-permute-done((bf16[512,512]{1,0:T(8,128)(2,1)}, bf16[512,512]{1,0:T(8,128)(2,1)}, u32[]{:S(2)}, u32[]{:S(2)}) %collective-permute-start.6) | collective-permute-done | bytes 524320 | tf_op jit(solution)/shard_map/ppermute | solution.py:60
  163.8 6.9 collective-permute-done.7
  174.4 7.8 %fusion.43 = (f32[512]{0:T(512)S(1)}, f32[512,2048]{1,0:T(8,128)S(1)}) fusion(f32[2048]{0:T(1024)S(1)} %bitcast.95, bf16[512,2048]{1,0:T(8,128)(2,1)} %pad_maximum_fusion.1.refs_7_, bf16[2048,2048]{1,0:T(8,128)(2,1)} %all-gather.7.cloned.1.call-done.refs_6_, bf16[512,2048]{1,0:T(8,128)(2,1)S(1)} %copy-done.18), kind=kOutput, calls=%fused_computation.157 | convolution fusion | flops 4299161088 | bytes 16787456 | tf_op jit(solution)/shard_map/dot_general | solution.py:24
  185.9 45.4 %collective-permute-done.9.refs_0_.refs_16_ = bf16[512,2048]{1,0:T(8,128)(2,1)S(1)} collective-permute-done((bf16[512,2048]{1,0:T(8,128)(2,1)S(1)}, bf16[512,2048]{1,0:T(8,128)(2,1)S(1)}, u32[]{:S(2)}, u32[]{:S(2)}) %collective-permute-start.9) | collective-permute-done | bytes 2097184 | tf_op jit(solution)/shard_map/ppermute | solution.py:60
  237.7 6.5 all-gather.9.cloned.1.call-done.refs_1_.refs_2_.refs_14_
  244.2 11.0 %up_gelu_0.1 = (bf16[512,2048]{1,0:T(8,128)(2,1)}, bf16[512,2048]{1,0:T(8,128)(2,1)}) custom-call(bf16[512,2048]{1,0:T(8,128)(2,1)} %copy-done.22, bf16[2048,2048]{1,0:T(8,128)(2,1)} %all-gather.9.cloned.1.call-done.refs_1_.refs_2_.refs_14_, f32[1,2048]{1,0:T(1,128)S(1)} %bitcast.72), custom_call_target="tpu_custom_call" | custom-call | flops 4294967 | bytes 16777 | tf_op jit(solution)/shard_map/up_gelu_0/pallas_call | solution.py:319
  255.2 10.8 %up_gelu_1.1 = (bf16[512,2048]{1,0:T(8,128)(2,1)}, bf16[512,2048]{1,0:T(8,128)(2,1)}) custom-call(bf16[512,2048]{1,0:T(8,128)(2,1)} %copy-done.23, bf16[2048,2048]{1,0:T(8,128)(2,1)} %all-gather.9.cloned.1.call-done.refs_1_.refs_2_.refs_14_, f32[1,2048]{1,0:T(1,128)S(1)} %bitcast.73), custom_call_target="tpu_custom_call" | custom-call | flops 4294967 | bytes 16777 | tf_op jit(solution)/shard_map/up_gelu_1/pallas_call | solution.py:319
  266.0 10.8 %up_gelu_2.1 = (bf16[512,2048]{1,0:T(8,128)(2,1)}, bf16[512,2048]{1,0:T(8,128)(2,1)}) custom-call(bf16[512,2048]{1,0:T(8,128)(2,1)} %copy-done.24, bf16[2048,2048]{1,0:T(8,128)(2,1)} %all-gather.9.cloned.1.call-done.refs_1_.refs_2_.refs_14_, f32[1,2048]{1,0:T(1,128)S(1)} %bitcast.74), custom_call_target="tpu_custom_call" | custom-call | flops 4294967 | bytes 16777 | tf_op jit(solution)/shard_map/up_gelu_2/pallas_call | solution.py:319
  277.7 21.0 %up_gelu_3.1 = (bf16[256,2048]{1,0:T(8,128)(2,1)S(1)}, bf16[256,2048]{1,0:T(8,128)(2,1)}, bf16[256,2048]{1,0:T(8,128)(2,1)}, bf16[256,2048]{1,0:T(8,128)(2,1)}) custom-call(bf16[256,2048]{1,0:T(8,128)(2,1)} %copy-done.27, bf16[256,2048]{1,0:T(8,128)(2,1)} %collective-permute-done.14.refs_1_.refs_19_, ...), custom_call_target="tpu_custom_call" | custom-call | flops 4294967 | bytes 16777 | tf_op jit(solution)/shard_map/up_gelu_3/pallas_call | solution.py:319
  298.8 23.5 %down_grad.1 = bf16[2048,2048]{1,0:T(8,128)(2,1)} custom-call(bf16[512,2048]{1,0:T(8,128)(2,1)} %get-tuple-element.137.refs_0_.refs_1_.refs_7_, bf16[512,2048]{1,0:T(8,128)(2,1)} %get-tuple-element.137.refs_0_.refs_1_.refs_7_, bf16[512,2048]{1,0:T(8,128)(2,1)} %get-tuple-element.140.refs_2_.refs_3_.refs_8_, ...), custom_call_target="tpu_custom_call" | custom-call | flops 17179868 | bytes 25165 | tf_op jit(solution)/shard_map/down_grad/pallas_call | solution.py:392
  322.4 3.9 all-gather.11.cloned.1.call-done.refs_13_.refs_10_.refs_8_
  326.3 104.0 %feed_back.1 = (bf16[512,2048]{1,0:T(8,128)(2,1)}, bf16[512,2048]{1,0:T(8,128)(2,1)}, bf16[512,2048]{1,0:T(8,128)(2,1)}, bf16[256,2048]{1,0:T(8,128)(2,1)}, bf16...) custom-call(bf16[256,2048]{1,0:T(8,128)(2,1)} %get-tuple-element.183, ...), custom_call_target="tpu_custom_call" | custom-call | flops 55834576 | tf_op jit(solution)/shard_map/feed_back/pallas_call | solution.py:656
  431.0 49.7 %heads_back.1 = (f32[512,2048]{1,0:T(8,128)}, bf16[512,2048]{1,0:T(8,128)(2,1)}, f32[8,2048]{1,0:T(8,128)}, bf16[2048,512]{1,0:T(8,128)(2,1)}, bf16[2048,2048]{1...) custom-call(f32[512,2048]{1,0:T(8,128)} %get-tuple-element.153.refs_, ...), custom_call_target="tpu_custom_call" | custom-call | flops 21474836 | tf_op jit(solution)/shard_map/heads_back/pallas_call | solution.py:750
  485.0 36.9 %attn_backward.1 = (bf16[2048,1536]{1,0:T(8,128)(2,1)}, f32[16,512]{1,0:T(8,128)S(1)}, f32[16,512]{1,0:T(8,128)S(1)}) custom-call(s32[16]{0:T(128)S(1)} %select_reduce_fusion.inv_ref, f32[4]{0:T(128)S(1)} %multiply_power_fusion.slope_ref, ...), custom_call_target="tpu_custom_call" | custom-call | flops 40000000 | bytes 14680 | tf_op jit(solution)/shard_map/attn_backward/pallas_call | solution.py:240
  523.5 91.6 %qkv_back.1 = (f32[512,2048]{1,0:T(8,128)}, bf16[512,2048]{1,0:T(8,128)(2,1)}, bf16[512,2048]{1,0:T(8,128)(2,1)}, bf16[512,2048]{1,0:T(8,128)(2,1)}, bf16[256,20...) custom-call(bf16[2048,1536]{1,0:T(8,128)(2,1)} %get-tuple-element.16, ...), custom_call_target="tpu_custom_call" | custom-call | flops 30064772 | tf_op jit(solution)/shard_map/qkv_back/pallas_call | solution.py:507
  624.5 6.1 fusion.16
  630.7 3.0 fusion.15
  640.3 3.8 lay_out.3
  646.7 5.5 collective-permute-done.21
  659.9 7.3 collective-permute-done.23.refs_3_
  668.5 6.6 lay_out.4
  675.1 7.4 %reduce-scatter.11.cloned.1.call-done.refs_0_ = bf16[256,1536]{1,0:T(8,128)(2,1)} async-done(((bf16[2048,1536]{1,0:T(8,128)(2,1)}), bf16[256,1536]{1,0:T(8,128)(2,1)}) %reduce-scatter.11.cloned.1.call-update) | async-done | bytes 786448 | tf_op jit(solution)/shard_map/reduce_scatter | solution.py:1071
  687.3 26.3 %reduce_small.1 = f32[24,128]{1,0:T(8,128)} custom-call(f32[8,24,128]{2,1,0:T(8,128)} %bitcast.80), custom_call_target="tpu_custom_call" | custom-call | tf_op jit(solution)/shard_map/reduce_small/pallas_call | solution.py:971
  723.0 3.1 lay_out.5
  (303 shorter events, 114.2 us)
Async XLA Ops:
  7.3 83.7 %all-gather.5.cloned.1.call-start = ((), (), s32[]{:S(2)}) async-start(), calls=%async_computation.4 | async-start | bytes 7077888 | tf_op jit(solution)/shard_map/all_gather | solution.py:1035
  9.9 164.5 %all-gather.7.cloned.1.call-start = ((), (), s32[]{:S(2)}) async-start(), calls=%async_computation.5 | async-start | bytes 9437184 | tf_op jit(solution)/shard_map/all_gather | solution.py:1035
  12.7 231.5 %all-gather.9.cloned.1.call-start = ((), (), s32[]{:S(2)}) async-start(), calls=%async_computation.6 | async-start | bytes 9437184 | tf_op jit(solution)/shard_map/all_gather | solution.py:1035
  12.7 48.7 %collective-permute-start = (bf16[512,2048]{1,0:T(8,128)(2,1)S(1)}, bf16[512,2048]{1,0:T(8,128)(2,1)}, u32[]{:S(2)}, u32[]{:S(2)}) collective-permute-start(bf16[512,2048]{1,0:T(8,128)(2,1)S(1)} %copy-done.18), channel_id=1, source_target_pairs={{0,8},{8,0},{16,24},{24,16},{1,9},{9,1},{17,25},{25,17},{2,10},{10... | collective-permute-start | bytes 6291464 | tf_op jit(solution)/shard_map/ppermute | solution.py:60
  15.7 47.2 %collective-permute-start.1 = (bf16[512,2048]{1,0:T(8,128)(2,1)S(1)}, bf16[512,2048]{1,0:T(8,128)(2,1)}, u32[]{:S(2)}, u32[]{:S(2)}) collective-permute-start(bf16[512,2048]{1,0:T(8,128)(2,1)S(1)} %copy-done.18), channel_id=1, source_target_pairs={{0,16},{8,24},{16,0},{24,8},{1,17},{9,25},{17,1},{25,9},{2,18},{10... | collective-permute-start | bytes 6291464 | tf_op jit(solution)/shard_map/ppermute | solution.py:60
  64.3 23.9 %collective-permute-start.2 = (bf16[256,2048]{1,0:T(8,128)(2,1)S(1)}, bf16[256,2048]{1,0:T(8,128)(2,1)}, u32[]{:S(2)}, u32[]{:S(2)}) collective-permute-start(bf16[256,2048]{1,0:T(8,128)(2,1)S(1)} %slice.163), channel_id=1, source_target_pairs={{0,16},{8,24},{16,0},{24,8},{1,17},{9,25},{17,1},{25,9},{2,18},{10... | collective-permute-start | bytes 3145736 | tf_op jit(solution)/shard_map/ppermute | solution.py:60
  67.2 23.6 %collective-permute-start.3 = (bf16[256,2048]{1,0:T(8,128)(2,1)S(1)}, bf16[256,2048]{1,0:T(8,128)(2,1)}, u32[]{:S(2)}, u32[]{:S(2)}) collective-permute-start(bf16[256,2048]{1,0:T(8,128)(2,1)S(1)} %slice.164), channel_id=1, source_target_pairs={{0,8},{8,0},{16,24},{24,16},{1,9},{9,1},{17,25},{25,17},{2,10},{10... | collective-permute-start | bytes 3145736 | tf_op jit(solution)/shard_map/ppermute | solution.py:60
  90.8 235.5 %all-gather.11.cloned.1.call-start = ((), (), s32[]{:S(2)}) async-start(), calls=%async_computation.7 | async-start | bytes 9437184 | tf_op jit(solution)/shard_map/all_gather | solution.py:1035
  120.0 311.0 %reduce-scatter.5.cloned.1.call-start = ((), (), s32[]{:S(2)}) async-start(), calls=%async_computation.8 | async-start | bytes 9437184 | tf_op jit(solution)/shard_map/reduce_scatter | solution.py:1071
  120.0 27.7 %collective-permute-start.4 = (bf16[256,2048]{1,0:T(8,128)(2,1)}, bf16[256,2048]{1,0:T(8,128)(2,1)}, u32[]{:S(2)}, u32[]{:S(2)}) collective-permute-start(bf16[256,2048]{1,0:T(8,128)(2,1)} %get-tuple-element.184.refs_10_.refs_9_.refs_1_), channel_id=1, source_target_pairs={{0,8},{8,0},{16,24},{24,16},{1,9},{9,1},{17,25},{25,17},{2,10},{10... | collective-permute-start | bytes 3145736 | tf_op jit(solution)/shard_map/ppermute | solution.py:60
  121.5 26.2 %collective-permute-start.5 = (bf16[256,2048]{1,0:T(8,128)(2,1)}, bf16[256,2048]{1,0:T(8,128)(2,1)}, u32[]{:S(2)}, u32[]{:S(2)}) collective-permute-start(bf16[256,2048]{1,0:T(8,128)(2,1)} %get-tuple-element.183.refs_9_.refs_8_.refs_0_), channel_id=1, source_target_pairs={{0,16},{8,24},{16,0},{24,8},{1,17},{9,25},{17,1},{25,9},{2,18},{10... | collective-permute-start | bytes 3145736 | tf_op jit(solution)/shard_map/ppermute | solution.py:60
  184.1 47.2 %collective-permute-start.9 = (bf16[512,2048]{1,0:T(8,128)(2,1)S(1)}, bf16[512,2048]{1,0:T(8,128)(2,1)S(1)}, u32[]{:S(2)}, u32[]{:S(2)}) collective-permute-start(bf16[512,2048]{1,0:T(8,128)(2,1)S(1)} %add_convert_fusion.refs_0_.refs_15_), channel_id=1, source_target_pairs={{0,8},{8,0},{16,24},{24,16},{1,9},{9,1},{17,25},{25,17},{2,10},{10... | collective-permute-start | bytes 6291464 | tf_op jit(solution)/shard_map/ppermute | solution.py:60
  185.3 48.6 %collective-permute-start.10 = (bf16[512,2048]{1,0:T(8,128)(2,1)S(1)}, bf16[512,2048]{1,0:T(8,128)(2,1)S(1)}, u32[]{:S(2)}, u32[]{:S(2)}) collective-permute-start(bf16[512,2048]{1,0:T(8,128)(2,1)S(1)} %add_convert_fusion.refs_0_.refs_15_), channel_id=1, source_target_pairs={{0,16},{8,24},{16,0},{24,8},{1,17},{9,25},{17,1},{25,9},{2,18},{10... | collective-permute-start | bytes 6291464 | tf_op jit(solution)/shard_map/ppermute | solution.py:60
  232.5 44.3 %collective-permute-start.13 = (bf16[256,2048]{1,0:T(8,128)(2,1)}, bf16[256,2048]{1,0:T(8,128)(2,1)S(1)}, u32[]{:S(2)}, u32[]{:S(2)}) collective-permute-start(bf16[256,2048]{1,0:T(8,128)(2,1)} %slice.229), channel_id=1, source_target_pairs={{0,16},{8,24},{16,0},{24,8},{1,17},{9,25},{17,1},{25,9},{2,18},{10... | collective-permute-start | bytes 3145736 | tf_op jit(solution)/shard_map/ppermute | solution.py:60
  235.1 41.7 %collective-permute-start.14 = (bf16[256,2048]{1,0:T(8,128)(2,1)}, bf16[256,2048]{1,0:T(8,128)(2,1)}, u32[]{:S(2)}, u32[]{:S(2)}) collective-permute-start(bf16[256,2048]{1,0:T(8,128)(2,1)} %slice.230), channel_id=1, source_target_pairs={{0,8},{8,0},{16,24},{24,16},{1,9},{9,1},{17,25},{25,17},{2,10},{10... | collective-permute-start | bytes 3145736 | tf_op jit(solution)/shard_map/ppermute | solution.py:60
  235.7 63.0 %collective-permute-start.11 = (bf16[256,2048]{1,0:T(8,128)(2,1)S(1)}, bf16[256,2048]{1,0:T(8,128)(2,1)}, u32[]{:S(2)}, u32[]{:S(2)}) collective-permute-start(bf16[256,2048]{1,0:T(8,128)(2,1)S(1)} %copy-done.26), channel_id=1, source_target_pairs={{0,16},{8,24},{16,0},{24,8},{1,17},{9,25},{17,1},{25,9},{2,18},{10... | collective-permute-start | bytes 3145736 | tf_op jit(solution)/shard_map/ppermute | solution.py:60
  237.1 61.7 %collective-permute-start.12 = (bf16[256,2048]{1,0:T(8,128)(2,1)}, bf16[256,2048]{1,0:T(8,128)(2,1)}, u32[]{:S(2)}, u32[]{:S(2)}) collective-permute-start(bf16[256,2048]{1,0:T(8,128)(2,1)} %get-tuple-element.133.refs_13_.refs_5_), channel_id=1, source_target_pairs={{0,8},{8,0},{16,24},{24,16},{1,9},{9,1},{17,25},{25,17},{2,10},{10... | collective-permute-start | bytes 3145736 | tf_op jit(solution)/shard_map/ppermute | solution.py:60
  322.3 201.2 %reduce-scatter.7.cloned.1.call-start = ((), (), s32[]{:S(2)}) async-start(), calls=%async_computation.9 | async-start | bytes 9437184 | tf_op jit(solution)/shard_map/reduce_scatter | solution.py:1071
  430.3 189.9 %reduce-scatter.9.cloned.1.call-start = ((), (), s32[]{:S(2)}) async-start(), calls=%async_computation.10 | async-start | bytes 9437184 | tf_op jit(solution)/shard_map/reduce_scatter | solution.py:1071
  480.8 201.7 %reduce-scatter.11.cloned.1.call-start = ((), (), s32[]{:S(2)}) async-start(), calls=%async_computation.11 | async-start | bytes 7077888 | tf_op jit(solution)/shard_map/reduce_scatter | solution.py:1071
  480.9 42.6 %collective-permute-start.15 = (bf16[256,2048]{1,0:T(8,128)(2,1)}, bf16[256,2048]{1,0:T(8,128)(2,1)}, u32[]{:S(2)}, u32[]{:S(2)}) collective-permute-start(bf16[256,2048]{1,0:T(8,128)(2,1)} %get-tuple-element.160), channel_id=1, source_target_pairs={{0,8},{8,0},{16,24},{24,16},{1,9},{9,1},{17,25},{25,17},{2,10},{10... | collective-permute-start | bytes 3145736 | tf_op jit(solution)/shard_map/ppermute | solution.py:60
  482.4 41.1 %collective-permute-start.16 = (bf16[256,2048]{1,0:T(8,128)(2,1)}, bf16[256,2048]{1,0:T(8,128)(2,1)}, u32[]{:S(2)}, u32[]{:S(2)}) collective-permute-start(bf16[256,2048]{1,0:T(8,128)(2,1)} %get-tuple-element.161), channel_id=1, source_target_pairs={{0,16},{8,24},{16,0},{24,8},{1,17},{9,25},{17,1},{25,9},{2,18},{10... | collective-permute-start | bytes 3145736 | tf_op jit(solution)/shard_map/ppermute | solution.py:60
  482.7 39.2 %collective-permute-start.17 = (bf16[128,2048]{1,0:T(8,128)(2,1)S(1)}, bf16[128,2048]{1,0:T(8,128)(2,1)S(1)}, u32[]{:S(2)}, u32[]{:S(2)}) collective-permute-start(bf16[128,2048]{1,0:T(8,128)(2,1)S(1)} %copy-done.6), channel_id=1, source_target_pairs={{0,16},{8,24},{16,0},{24,8},{1,17},{9,25},{17,1},{25,9},{2,18},{10... | collective-permute-start | bytes 1572872 | tf_op jit(solution)/shard_map/ppermute | solution.py:60
  484.4 38.3 %collective-permute-start.18 = (bf16[128,2048]{1,0:T(8,128)(2,1)S(1)}, bf16[128,2048]{1,0:T(8,128)(2,1)S(1)}, u32[]{:S(2)}, u32[]{:S(2)}) collective-permute-start(bf16[128,2048]{1,0:T(8,128)(2,1)S(1)} %copy-done.10), channel_id=1, source_target_pairs={{0,8},{8,0},{16,24},{24,16},{1,9},{9,1},{17,25},{25,17},{2,10},{10... | collective-permute-start | bytes 1572872 | tf_op jit(solution)/shard_map/ppermute | solution.py:60
  618.1 28.6 %collective-permute-start.19 = (bf16[256,2048]{1,0:T(8,128)(2,1)S(1)}, bf16[256,2048]{1,0:T(8,128)(2,1)S(1)}, u32[]{:S(2)}, u32[]{:S(2)}) collective-permute-start(bf16[256,2048]{1,0:T(8,128)(2,1)S(1)} %copy-done.4), channel_id=1, source_target_pairs={{0,8},{8,0},{16,24},{24,16},{1,9},{9,1},{17,25},{25,17},{2,10},{10... | collective-permute-start | bytes 3145736 | tf_op jit(solution)/shard_map/ppermute | solution.py:60
  619.6 27.1 %collective-permute-start.20 = (bf16[256,2048]{1,0:T(8,128)(2,1)S(1)}, bf16[256,2048]{1,0:T(8,128)(2,1)S(1)}, u32[]{:S(2)}, u32[]{:S(2)}) collective-permute-start(bf16[256,2048]{1,0:T(8,128)(2,1)S(1)} %copy-done.4), channel_id=1, source_target_pairs={{0,16},{8,24},{16,0},{24,8},{1,17},{9,25},{17,1},{25,9},{2,18},{10... | collective-permute-start | bytes 3145736 | tf_op jit(solution)/shard_map/ppermute | solution.py:60
  622.5 29.7 %collective-permute-start.21 = (bf16[128,2048]{1,0:T(8,128)(2,1)}, bf16[128,2048]{1,0:T(8,128)(2,1)S(1)}, u32[]{:S(2)}, u32[]{:S(2)}) collective-permute-start(bf16[128,2048]{1,0:T(8,128)(2,1)} %get-tuple-element.241), channel_id=1, source_target_pairs={{0,8},{8,0},{16,24},{24,16},{1,9},{9,1},{17,25},{25,17},{2,10},{10... | collective-permute-start | bytes 1572872 | tf_op jit(solution)/shard_map/ppermute | solution.py:60
  623.9 29.5 %collective-permute-start.22 = (bf16[128,2048]{1,0:T(8,128)(2,1)}, bf16[128,2048]{1,0:T(8,128)(2,1)}, u32[]{:S(2)}, u32[]{:S(2)}) collective-permute-start(bf16[128,2048]{1,0:T(8,128)(2,1)} %get-tuple-element.240), channel_id=1, source_target_pairs={{0,16},{8,24},{16,0},{24,8},{1,17},{9,25},{17,1},{25,9},{2,18},{10... | collective-permute-start | bytes 1572872 | tf_op jit(solution)/shard_map/ppermute | solution.py:60
  682.5 31.1 %collective-permute-start.25 = (bf16[256,1536]{1,0:T(8,128)(2,1)}, bf16[256,1536]{1,0:T(8,128)(2,1)S(1)}, u32[]{:S(2)}, u32[]{:S(2)}) collective-permute-start(bf16[256,1536]{1,0:T(8,128)(2,1)} %reduce-scatter.11.cloned.1.call-done.refs_0_), channel_id=1, source_target_pairs={{0,8},{8,0},{16,24},{24,16},{1,9},{9,1},{17,25},{25,17},{2,10},{10... | collective-permute-start | bytes 2359304 | tf_op jit(solution)/shard_map/ppermute | solution.py:60
  683.9 29.7 %collective-permute-start.26 = (bf16[256,1536]{1,0:T(8,128)(2,1)}, bf16[256,1536]{1,0:T(8,128)(2,1)S(1)}, u32[]{:S(2)}, u32[]{:S(2)}) collective-permute-start(bf16[256,1536]{1,0:T(8,128)(2,1)} %reduce-scatter.11.cloned.1.call-done.refs_0_), channel_id=1, source_target_pairs={{0,16},{8,24},{16,0},{24,8},{1,17},{9,25},{17,1},{25,9},{2,18},{10... | collective-permute-start | bytes 2359304 | tf_op jit(solution)/shard_map/ppermute | solution.py:60
  685.4 28.3 %collective-permute-start.29 = (bf16[128,2048]{1,0:T(8,128)(2,1)}, bf16[128,2048]{1,0:T(8,128)(2,1)S(1)}, u32[]{:S(2)}, u32[]{:S(2)}) collective-permute-start(bf16[128,2048]{1,0:T(8,128)(2,1)} %get-tuple-element.211), channel_id=1, source_target_pairs={{0,16},{8,24},{16,0},{24,8},{1,17},{9,25},{17,1},{25,9},{2,18},{10... | collective-permute-start | bytes 1572872 | tf_op jit(solution)/shard_map/ppermute | solution.py:60
  686.1 27.6 %collective-permute-start.30 = (bf16[128,2048]{1,0:T(8,128)(2,1)}, bf16[128,2048]{1,0:T(8,128)(2,1)S(1)}, u32[]{:S(2)}, u32[]{:S(2)}) collective-permute-start(bf16[128,2048]{1,0:T(8,128)(2,1)} %get-tuple-element.213), channel_id=1, source_target_pairs={{0,8},{8,0},{16,24},{24,16},{1,9},{9,1},{17,25},{25,17},{2,10},{10... | collective-permute-start | bytes 1572872 | tf_op jit(solution)/shard_map/ppermute | solution.py:60
  (60 other events, 632.3 us)
Sparse Core Ops, SparseCore 0:
  10.3 68.1 all-gather.4
  80.7 80.6 all-gather.6
  163.6 80.5 all-gather.8
  245.6 80.6 all-gather.10
  329.0 88.0 reduce-scatter.4
  430.5 87.2 reduce-scatter.6
  520.1 87.9 reduce-scatter.8
  615.3 67.1 reduce-scatter.10
